TPU v7x, 512 devices: a whole 4x4x16 slice. The times are simulated.
512 devices in a mesh: row: 16 (over z_lo, core), col: 32 (over y, z_hi, x).
Axes of the slice: x: 4, y: 4, z: 16 (z_hi: 2, z_lo: 8; z = z_hi * 8 + z_lo), core: 2. Of those that a mesh axis runs over, the one named last changes fastest.
Arguments:
- features: bfloat16 [65536, 512], P(('row', 'col')), may hold values from -6 to 6
- weight: bfloat16 [512, 512], replicated, may hold values from -0.25 to 0.25
- cotangent: bfloat16 [65536, 512], P(('row', 'col')), may hold values from -6 to 6
- tile_rows: int32 [16, 32, 8], P('row', 'col'), may hold values from 0 to 31
- tile_cols: int32 [16, 32, 8], P('row', 'col'), may hold values from 0 to 15
- tile_count: int32 [16, 32], P('row', 'col'), may hold values from 2 to 8, as said below
- tile_vals: bfloat16 [16, 32, 8, 128, 128], P('row', 'col'), may hold values from 0 to 3
Outputs:
- output: bfloat16 [65536, 512], P(('row', 'col'))
- weight_grad: float32 [512, 512], replicated
- feature_grad: float32 [65536, 512], P(('row', 'col'))
Inputs may be any that keep to these rules, and one draw needn't show every extreme that they name: `tile_count`: some device has exactly 8 live slots; slots at or past the count are to be ignored. `tile_rows`: block rows of the tiles; tiles may repeat a position. `tile_cols`: block columns of the tiles.
All inputs are finite; a program needn't handle non-finite values.
Results may differ from a plain program's by a relative error of at most 0.015.
Values may be sent and summed in bfloat16 or wider, within the bound.
No kernel may reach another device: no remote copies, remote signals or barrier semaphores. Data moves between devices by JAX's collectives and lax.ppermute only.
A program may use at most 64 MiB of HBM per device.

v0:
```python
import math

import jax
import jax.numpy as jnp
from jax import lax
from jax.sharding import PartitionSpec as P


def layer_rows(row_total, grad_rows, weight):
    inv_rms = lax.rsqrt(jnp.mean(row_total * row_total, axis=1, keepdims=True) + 1e-06)
    norm_f32 = row_total * inv_rms
    normed = norm_f32.astype(jnp.bfloat16)
    pre_act = jnp.dot(normed, weight, preferred_element_type=jnp.float32)
    output = jax.nn.silu(pre_act).astype(jnp.bfloat16)
    sigmoid_pre = jax.nn.sigmoid(pre_act)
    act_slope = sigmoid_pre * (1.0 + pre_act * (1.0 - sigmoid_pre))
    grad_pre = (grad_rows.astype(jnp.float32) * act_slope).astype(jnp.bfloat16)
    grad_norm = jnp.einsum("ng,fg->nf", grad_pre, weight, preferred_element_type=jnp.float32)
    grad_z = (
        inv_rms * (grad_norm - norm_f32 * jnp.mean(grad_norm * norm_f32, axis=1, keepdims=True))
    ).astype(jnp.bfloat16)
    return (output, normed, grad_pre, grad_z)


def local(features, weight, cotangent, tile_rows, tile_cols, tile_count, tile_vals):
    stretch_rows = features.shape[0]
    feat_width = features.shape[1]
    n_rows = lax.axis_size("row")
    n_cols = lax.axis_size("col")
    slot_count = tile_vals.shape[2]
    tile_size = tile_vals.shape[3]
    row_blocks = n_cols * stretch_rows // tile_size
    col_blocks = n_rows * stretch_rows // tile_size
    nodes_total = n_rows * n_cols * stretch_rows
    alive = jnp.arange(slot_count, dtype=jnp.int32) < tile_count[0, 0]
    alive_f32 = alive.astype(jnp.float32)
    weights = tile_vals[0, 0] * alive.astype(jnp.bfloat16)[:, None, None]
    row_index = tile_rows[0, 0]
    col_index = tile_cols[0, 0]
    place_rows = (row_index[:, None] == jnp.arange(row_blocks, dtype=jnp.int32)[None, :]).astype(
        jnp.float32
    )
    place_cols = (col_index[:, None] == jnp.arange(col_blocks, dtype=jnp.int32)[None, :]).astype(
        jnp.float32
    )
    col_sums = jnp.sum(tile_vals[0, 0], axis=1, dtype=jnp.float32) * alive_f32[:, None]
    degree_terms = jnp.einsum(
        "sc,sj->cj", place_cols, col_sums, precision=lax.Precision.HIGHEST
    ).reshape(n_rows * stretch_rows)
    col_degree = 1.0 + lax.psum(degree_terms, "row")
    col_scale = lax.rsqrt(col_degree)
    own_scale = lax.dynamic_slice_in_dim(
        col_scale, lax.axis_index("row") * stretch_rows, stretch_rows
    )
    gathered = lax.all_gather(features, "row", axis=0, tiled=True)
    scaled = (gathered.astype(jnp.float32) * col_scale[:, None]).astype(jnp.bfloat16)
    picked = scaled.reshape(col_blocks, tile_size, feat_width)[col_index]
    products = jnp.einsum("sij,sjf->sif", weights, picked, preferred_element_type=jnp.float32)
    forward_terms = jnp.einsum("sr,sif->rif", place_rows, products, precision=lax.Precision.HIGHEST)
    forward_pieces = forward_terms.astype(jnp.bfloat16)
    arrived = lax.all_to_all(forward_pieces, "col", split_axis=0, concat_axis=0, tiled=True)
    own_total = jnp.sum(arrived.astype(jnp.float32), axis=0)
    output, normed, grad_pre, grad_own = layer_rows(own_total, cotangent, weight)
    grad_group = lax.all_gather(grad_own, "col", axis=0, tiled=True)
    weight_terms = jnp.einsum("nf,ng->fg", normed, grad_pre, preferred_element_type=jnp.float32)
    weight_grad = lax.psum(weight_terms, ("row", "col")) * (1.0 / math.sqrt(nodes_total))
    grad_picked = grad_group.reshape(row_blocks, tile_size, feat_width)[row_index]
    back_products = jnp.einsum(
        "sij,sif->sjf", weights, grad_picked, preferred_element_type=jnp.float32
    )
    backward_terms = jnp.einsum(
        "sc,sjf->cjf", place_cols, back_products, precision=lax.Precision.HIGHEST
    )
    back_rounded = backward_terms.astype(jnp.bfloat16)
    own_grad = lax.psum_scatter(
        back_rounded.astype(jnp.float32)
        .reshape(n_rows * stretch_rows, feat_width)
        .astype(jnp.bfloat16),
        "row",
        scatter_dimension=0,
        tiled=True,
    ).astype(jnp.float32)
    feature_grad = own_grad * own_scale[:, None]
    return (output, weight_grad, feature_grad)


def solution(mesh):
    in_specs = (
        P(("row", "col"), None),
        P(),
        P(("row", "col"), None),
        P("row", "col", None),
        P("row", "col", None),
        P("row", "col"),
        P("row", "col", None, None, None),
    )
    out_specs = (P(("row", "col"), None), P(), P(("row", "col"), None))
    return jax.shard_map(local, mesh=mesh, in_specs=in_specs, out_specs=out_specs, check_vma=False)
```

profile of v0, /device:TPU:24, one launch (start us, length us, event | category | flops | bytes accessed | tf_op | source)
XLA Modules:
  0.0 1063.6 jit_solution(9583429470632935500)
XLA Ops:
  7.2 0.0 all-gather.3.cloned.1.call-start
  7.2 0.7 all-gather.3.cloned.1.call-update
  7.9 0.0 all-gather.5.cloned.1.call-start
  8.6 1.0 convert_reduce_fusion.1
  9.6 0.9 convolution_bitcast_fusion
  10.5 56.9 %psum.14 = f32[2048]{0:T(1024)S(1)} all-reduce(f32[2048]{0:T(1024)S(1)} %convolution_bitcast_fusion), channel_id=1, replica_groups=mesh['row'=16,'col'=32] {'row'}, use_global_device_ids=true, to_apply=%region_1.0 | all-reduce | flops 2048 | bytes 16384 | tf_op jit(solution)/shard_map/psum | solution.py:50
  67.4 0.7 fusion.19
  68.1 46.9 %all-gather.3.cloned.1.call-done = bf16[2048,512]{1,0:T(8,128)(2,1)} async-done(((bf16[128,512]{1,0:T(8,128)(2,1)}), bf16[2048,512]{1,0:T(8,128)(2,1)}) %all-gather.3.cloned.1.call-update) | async-done | bytes 2097168 | tf_op jit(solution)/shard_map/all_gather | solution.py:55
  115.1 2.0 multiply_convert_fusion
  117.1 1.6 gather_fusion
  118.7 1.7 fusion.7
  120.4 3.9 convolution_convert_fusion
  124.3 2.4 copy.12
  126.7 180.7 %all_to_all.5 = bf16[32,128,512]{2,1,0:T(8,128)(2,1)S(1)} all-to-all(bf16[32,128,512]{2,1,0:T(8,128)(2,1)S(1)} %copy.12), channel_id=1, replica_groups=mesh['row'=16,'col'=32] {'col'}, dimensions={0} | all-to-all | bytes 8388608 | tf_op jit(solution)/shard_map/all_to_all | solution.py:61
  307.5 0.6 convert_reduce_fusion
  308.1 0.1 multiply_reduce_fusion.1
  308.2 1.0 multiply_convert_fusion.3
  309.2 0.4 multiply_reduce_fusion
  309.6 0.8 multiply_convert_fusion.1
  310.4 0.0 all-reduce.2.cloned.1.call-start
  310.5 1.4 fusion.21
  311.9 0.0 reduce-scatter.2.cloned.1.call-start
  311.9 162.5 %all-gather.5.cloned.1.call-done = bf16[4096,512]{1,0:T(8,128)(2,1)} async-done(((bf16[128,512]{1,0:T(8,128)(2,1)}), bf16[4096,512]{1,0:T(8,128)(2,1)}) %all-gather.5.cloned.1.call-update) | async-done | bytes 4194320 | tf_op jit(solution)/shard_map/all_gather | solution.py:64
  474.4 2.8 gather_fusion.1
  477.2 0.6 fusion.6
  477.9 2.7 fusion.3
  480.6 2.5 copy.15
  483.1 0.1 dynamic_slice.3
  483.2 462.4 %all-reduce.2.cloned.1.call-done = f32[512,512]{1,0:T(8,128)} async-done(((f32[512,512]{1,0:T(8,128)}), f32[512,512]{1,0:T(8,128)}) %all-reduce.2.cloned.1.call-update) | async-done | bytes 1048592 | tf_op jit(solution)/shard_map/psum | solution.py:66
  945.6 2.3 broadcast_multiply_fusion
  947.9 107.5 %reduce-scatter.2.cloned.1.call-done = bf16[128,512]{1,0:T(8,128)(2,1)} async-done(((bf16[2048,512]{1,0:T(8,128)(2,1)}), bf16[128,512]{1,0:T(8,128)(2,1)}) %reduce-scatter.2.cloned.1.call-update) | async-done | bytes 131088 | tf_op jit(solution)/shard_map/reduce_scatter | solution.py:75
  1055.4 1.7 convert_multiply_fusion
  (21 shorter events, 0.1 us)
Async XLA Ops:
  7.2 301.0 %copy-start = (bf16[512,512]{1,0:T(8,128)(2,1)S(1)}, bf16[512,512]{1,0:T(8,128)(2,1)}, u32[]{:S(2)}) copy-start(bf16[512,512]{1,0:T(8,128)(2,1)} %param.8) | copy-start | bytes 1572868
  7.2 107.9 %all-gather.3.cloned.1.call-start = ((), (), s32[]{:S(2)}) async-start(), calls=%async_computation.2 | async-start | bytes 2228224 | tf_op jit(solution)/shard_map/all_gather | solution.py:55
  7.9 466.5 %all-gather.5.cloned.1.call-start = ((), (), s32[]{:S(2)}) async-start(), calls=%async_computation.4 | async-start | bytes 4325376 | tf_op jit(solution)/shard_map/all_gather | solution.py:64
  117.1 1.6 copy-start.1
  118.7 1.7 copy-start.3
  307.5 1.7 copy-start.2
  310.4 635.3 %all-reduce.2.cloned.1.call-start = ((), (), s32[]{:S(2)}) async-start(), calls=%async_computation.3 | async-start | bytes 2097152 | tf_op jit(solution)/shard_map/psum | solution.py:66
  311.9 743.5 %reduce-scatter.2.cloned.1.call-start = ((), (), s32[]{:S(2)}) async-start(), calls=%async_computation.5 | async-start | bytes 2228224 | tf_op jit(solution)/shard_map/reduce_scatter | solution.py:75
  477.2 0.7 copy-start.4
Sparse Core Ops, SparseCore 0:
  10.1 104.9 all-gather.2
  310.5 163.8 all-gather.4
  480.4 465.1 all-reduce.1
  948.3 107.0 reduce-scatter.1
where the time goes:
time: 1060 us
  waiting for transfers between devices  780 us (74%)
  blocking collectives  238 us (22%)
  between operations  14.6 us (1%)
  matrix products  12.6 us (1%)
    psum x1, waiting for transfers between devices, local(): lax.psum(weight_terms, ('row', 'col')) * (1.0 / math.sqrt(nodes_total))  462 us
    all_to_all x1, blocking collectives, local(): lax.all_to_all(forward_pieces, 'col', split_axis=0, concat_axis=0, tiled=...  181 us
    all_gather x1, waiting for transfers between devices, local(): grad_group = lax.all_gather(grad_own, 'col', axis=0, tiled=True)  162 us
    reduce_scatter x1, waiting for transfers between devices, local(): lax.psum_scatter(back_rounded.astype(jnp.float32).reshape(n_rows * stretc...  107 us
    psum x1, blocking collectives, local(): col_degree = 1.0 + lax.psum(degree_terms, 'row')  56.9 us
    all_gather x1, waiting for transfers between devices, local(): gathered = lax.all_gather(features, 'row', axis=0, tiled=True)  46.9 us
  transfers between devices with their start and end apart: 4, of which 4 were waited for; matrix products, arithmetic and copies ran while one was open for 1% of the time, Pallas kernels for 0%

commit v1 on v0

v1 whole, which is shorter than its diff:
```python
import math

import jax
import jax.numpy as jnp
from jax import lax
from jax.sharding import Mesh
from jax.sharding import PartitionSpec as P

AXES = ("zl", "core", "y", "zh", "x")
ROW = ("zl", "core")
PLANE = ("y", "x")
DEPTH = ("zl", "core", "zh")
BF16 = jnp.bfloat16
F32 = jnp.float32


def layer_rows(row_total, grad_rows, weight):
    inv_rms = lax.rsqrt(jnp.mean(row_total * row_total, axis=1, keepdims=True) + 1e-06)
    norm_f32 = row_total * inv_rms
    normed = norm_f32.astype(BF16)
    pre_act = jnp.dot(normed, weight, preferred_element_type=F32)
    output = jax.nn.silu(pre_act).astype(BF16)
    sigmoid_pre = jax.nn.sigmoid(pre_act)
    act_slope = sigmoid_pre * (1.0 + pre_act * (1.0 - sigmoid_pre))
    grad_pre = (grad_rows.astype(F32) * act_slope).astype(BF16)
    grad_norm = jnp.einsum("ng,fg->nf", grad_pre, weight, preferred_element_type=F32)
    grad_z = (
        inv_rms * (grad_norm - norm_f32 * jnp.mean(grad_norm * norm_f32, axis=1, keepdims=True))
    ).astype(BF16)
    return (output, normed, grad_pre, grad_z)


def exchange(block, axis):
    return lax.ppermute(block, axis, [(0, 1), (1, 0)])


def scatter_parts(parts, axes):
    return lax.all_to_all(parts, axes, split_axis=0, concat_axis=0, tiled=True)


def gather_copies(block, axes):
    count = lax.axis_size(axes)
    copies = jnp.broadcast_to(block[None], (count,) + block.shape)
    return lax.all_to_all(copies, axes, split_axis=0, concat_axis=0, tiled=True)


def local(features, weight, cotangent, tile_rows, tile_cols, tile_count, tile_vals):
    span, width = features.shape
    n_zl, n_core = lax.axis_size("zl"), lax.axis_size("core")
    n_y, n_zh, n_x = lax.axis_size("y"), lax.axis_size("zh"), lax.axis_size("x")
    n_row, n_col = n_zl * n_core, n_y * n_zh * n_x
    n_plane = n_y * n_x
    my_zl, my_core, my_zh = lax.axis_index("zl"), lax.axis_index("core"), lax.axis_index("zh")
    slots = tile_vals.shape[2]
    nodes = n_row * n_col * span
    alive = jnp.arange(slots, dtype=jnp.int32) < tile_count[0, 0]
    weights = tile_vals[0, 0] * alive.astype(BF16)[:, None, None]
    row_index = tile_rows[0, 0]
    col_index = tile_cols[0, 0]
    col_place = ((col_index % n_core) ^ my_core) * n_zl + col_index // n_core
    row_plane = (row_index // (n_zh * n_x)) * n_x + row_index % n_x
    row_place = (((row_index // n_x) % n_zh) ^ my_zh) * n_plane + row_plane
    place_rows = (row_place[:, None] == jnp.arange(n_col, dtype=jnp.int32)[None, :]).astype(F32)
    place_cols = (col_place[:, None] == jnp.arange(n_row, dtype=jnp.int32)[None, :]).astype(F32)
    order_cols = (col_index[:, None] == jnp.arange(n_row, dtype=jnp.int32)[None, :]).astype(F32)

    zl_blocks = lax.all_gather(features, "zl", axis=0, tiled=False)
    other_blocks = exchange(zl_blocks, "core")

    col_sums = jnp.sum(tile_vals[0, 0], axis=1, dtype=F32) * alive.astype(F32)[:, None]
    degree_terms = jnp.einsum("sc,sj->cj", order_cols, col_sums, precision=lax.Precision.HIGHEST)
    col_degree = 1.0 + jnp.sum(gather_copies(degree_terms, ROW), axis=0)
    col_scale = lax.rsqrt(col_degree)
    own_scale = lax.dynamic_index_in_dim(
        col_scale, my_zl * n_core + my_core, axis=0, keepdims=False
    )

    picked = jnp.concatenate([zl_blocks, other_blocks], axis=0)[col_place]
    picked = (picked.astype(F32) * col_scale[col_index][:, :, None]).astype(BF16)
    products = jnp.einsum("sij,sjf->sif", weights, picked, preferred_element_type=F32)

    def forward_terms(half):
        place = place_rows[:, half * n_plane : (half + 1) * n_plane]
        terms = jnp.einsum("sr,sif->rif", place, products, precision=lax.Precision.HIGHEST)
        return terms.astype(BF16)

    far_sum = jnp.sum(scatter_parts(forward_terms(1), PLANE).astype(F32), axis=0)
    from_far = exchange(far_sum.astype(BF16), "zh")
    near_sum = jnp.sum(scatter_parts(forward_terms(0), PLANE).astype(F32), axis=0)
    own_total = near_sum + from_far.astype(F32)

    output, normed, grad_pre, grad_own = layer_rows(own_total, cotangent, weight)

    grad_far = exchange(grad_own, "zh")
    grad_group = jnp.concatenate(
        [gather_copies(grad_own, PLANE), gather_copies(grad_far, PLANE)], axis=0
    )

    weight_terms = jnp.einsum("nf,ng->fg", normed, grad_pre, preferred_element_type=F32)
    plane_part = scatter_parts(
        weight_terms.astype(BF16).reshape(n_plane, width // n_plane, width), PLANE
    )
    plane_sum = jnp.sum(plane_part.astype(F32), axis=0)
    depth = n_row * n_zh
    depth_part = scatter_parts(plane_sum.reshape(depth, -1, 128), DEPTH)
    depth_sum = jnp.sum(depth_part, axis=0) * (1.0 / math.sqrt(nodes))
    plane_rows = gather_copies(depth_sum, DEPTH).reshape(width // n_plane, width)
    weight_grad = gather_copies(plane_rows, PLANE).reshape(width, width)

    grad_picked = grad_group[row_place]
    back_products = jnp.einsum("sij,sif->sjf", weights, grad_picked, preferred_element_type=F32)
    back_terms = jnp.einsum(
        "sc,sjf->cjf", place_cols, back_products, precision=lax.Precision.HIGHEST
    ).astype(BF16)
    core_sum = back_terms[:n_zl].astype(F32) + exchange(back_terms[n_zl:], "core").astype(F32)
    own_grad = jnp.sum(scatter_parts(core_sum.astype(BF16), "zl").astype(F32), axis=0)
    feature_grad = own_grad * own_scale[:, None]
    return (output, weight_grad, feature_grad)


def solution(mesh):
    fine = Mesh(mesh.devices.reshape(8, 2, 4, 2, 4), AXES)
    nodes, row, col = P(AXES, None), ("zl", "core"), ("y", "zh", "x")
    in_specs = (
        nodes,
        P(),
        nodes,
        P(row, col, None),
        P(row, col, None),
        P(row, col),
        P(row, col, None, None, None),
    )
    out_specs = (nodes, P(), nodes)
    return jax.shard_map(local, mesh=fine, in_specs=in_specs, out_specs=out_specs, check_vma=False)
```

time: 1060 us -> 402 us (0.38)
  waiting for transfers between devices: 780 us -> 246 us
  blocking collectives: 238 us -> 23 us
  starting transfers between devices: 0.16 us -> 68.3 us
  local copies, waits for them, and re-layouts: 9.41 us -> 20.2 us
    psum x1 -> x0, waiting for transfers between devices: 462 us -> none  [local(): lax.psum(weight_terms, ('row', 'col')) * (1.0 / math.sqrt(nodes_total))]
    all_to_all x0 -> x9, waiting for transfers between devices: none -> 174 us  [the longest x5 121 us: scatter_parts(): return lax.all_to_all(parts, axes, split_axis=0, concat_axis=0, tiled=True)]
    all_to_all x1, blocking collectives: 181 us -> 23 us  [gather_copies(): return lax.all_to_all(copies, axes, split_axis=0, concat_axis=0, tiled=True)]
    all_gather x2 -> x1, waiting for transfers between devices: 209 us -> 58 us  [local(): zl_blocks = lax.all_gather(features, 'zl', axis=0, tiled=False)]
    reduce_scatter x1 -> x0, waiting for transfers between devices: 107 us -> none  [local(): lax.psum_scatter(back_rounded.astype(jnp.float32).reshape(n_rows * stretc...]
    psum x1 -> x0, blocking collectives: 56.9 us -> none  [local(): col_degree = 1.0 + lax.psum(degree_terms, 'row')]
    all_to_all x0 -> x9, starting transfers between devices: none -> 56.4 us  [the longest x4 30.4 us: gather_copies(): return lax.all_to_all(copies, axes, split_axis=0, concat_axis=0, tiled=True)]
    ppermute x0 -> x4, waiting for transfers between devices: none -> 13.6 us  [exchange(): return lax.ppermute(block, axis, [(0, 1), (1, 0)])]
  transfers between devices with their start and end apart: 4 -> 14, of which waited for: 4 -> 11; matrix products, arithmetic and copies ran while one was open for 1% -> 4% of each run, Pallas kernels for 0% -> 0%
where the time goes in v1:
time: 402 us; the launch traced here: 400 us
  waiting for transfers between devices  246 us (61%)
  starting transfers between devices  68.3 us (17%)
  blocking collectives  23 us (6%)
  local copies, waits for them, and re-layouts  20.2 us (5%)
  between operations  15 us (4%)
  matrix products  13.7 us (3%)
  other arithmetic  13.3 us (3%)
    all_to_all x5, waiting for transfers between devices, scatter_parts(): return lax.all_to_all(parts, axes, split_axis=0, concat_axis=0, tiled=True)  121 us
    all_gather x1, waiting for transfers between devices, local(): zl_blocks = lax.all_gather(features, 'zl', axis=0, tiled=False)  58 us
    all_to_all x4, waiting for transfers between devices, gather_copies(): return lax.all_to_all(copies, axes, split_axis=0, concat_axis=0, tiled=True)  53 us
    all_to_all x4, starting transfers between devices, gather_copies(): return lax.all_to_all(copies, axes, split_axis=0, concat_axis=0, tiled=True)  30.4 us
    all_to_all x5, starting transfers between devices, scatter_parts(): return lax.all_to_all(parts, axes, split_axis=0, concat_axis=0, tiled=True)  26 us
    all_to_all x1, blocking collectives, gather_copies(): return lax.all_to_all(copies, axes, split_axis=0, concat_axis=0, tiled=True)  23 us
    ppermute x4, waiting for transfers between devices, exchange(): return lax.ppermute(block, axis, [(0, 1), (1, 0)])  13.6 us
    ppermute x4, starting transfers between devices, exchange(): return lax.ppermute(block, axis, [(0, 1), (1, 0)])  11.9 us
  transfers between devices with their start and end apart: 14, of which 11 were waited for; matrix products, arithmetic and copies ran while one was open for 4% of the time, Pallas kernels for 0%

profile of v1, /device:TPU:24, one launch (start us, length us, event | category | flops | bytes accessed | tf_op | source)
XLA Modules:
  0.0 399.6 jit_solution(11190666755918117939)
XLA Ops:
  11.2 12.6 %all-to-all-start = ((f32[16,16,128]{2,1,0:T(8,128)}), f32[16,16,128]{2,1,0:T(8,128)S(1)}, u32[]{:S(2)}, u32[]{:S(2)}) async-start(f32[16,16,128]{2,1,0:T(8,128)} %broadcast_in_dim.12), calls=%async_computation | async-start | bytes 262144 | tf_op jit(solution)/shard_map/all_to_all | solution.py:44
  23.8 58.0 %all-gather.3.cloned.1.call-done = bf16[1024,512]{1,0:T(8,128)(2,1)} async-done(((bf16[128,512]{1,0:T(8,128)(2,1)}), bf16[1024,512]{1,0:T(8,128)(2,1)}) %all-gather.3.cloned.1.call-update) | async-done | bytes 1048592 | tf_op jit(solution)/shard_map/all_gather | solution.py:67
  81.8 1.9 collective-permute-start
  91.7 2.7 fusion.9
  94.4 2.5 copy.27
  96.9 7.3 %all-to-all-start.2 = ((bf16[16,128,512]{2,1,0:T(8,128)(2,1)}), bf16[16,128,512]{2,1,0:T(8,128)(2,1)}, u32[]{:S(2)}, u32[]{:S(2)}) async-start(bf16[16,128,512]{2,1,0:T(8,128)(2,1)} %copy.27), calls=%async_computation.2 | async-start | bytes 4194304 | tf_op jit(solution)/shard_map/all_to_all | solution.py:38
  104.2 2.5 fusion.6
  106.7 2.5 copy.25
  109.2 26.4 %all-to-all-done.2 = bf16[16,128,512]{2,1,0:T(8,128)(2,1)} async-done(((bf16[16,128,512]{2,1,0:T(8,128)(2,1)}), bf16[16,128,512]{2,1,0:T(8,128)(2,1)}, u32[]{:S(2)}, u32[]{:S(2)}) %all-to-all-start.2) | async-done | bytes 2097184 | tf_op jit(solution)/shard_map/all_to_all | solution.py:38
  135.6 5.2 %all-to-all-start.1 = ((bf16[16,128,512]{2,1,0:T(8,128)(2,1)}), bf16[16,128,512]{2,1,0:T(8,128)(2,1)S(1)}, u32[]{:S(2)}, u32[]{:S(2)}) async-start(bf16[16,128,512]{2,1,0:T(8,128)(2,1)} %copy.25), calls=%async_computation.1 | async-start | bytes 4194304 | tf_op jit(solution)/shard_map/all_to_all | solution.py:38
  142.8 5.1 %collective-permute-start.1 = (bf16[128,512]{1,0:T(8,128)(2,1)S(1)}, bf16[128,512]{1,0:T(8,128)(2,1)S(1)}, u32[]{:S(2)}, u32[]{:S(2)}) collective-permute-start(bf16[128,512]{1,0:T(8,128)(2,1)S(1)} %reduce_sum.87), channel_id=1, source_target_pairs={{0,4},{4,0},{1,5},{5,1},{2,6},{6,2},{3,7},{7,3},{8,12},{12,8},{9,1... | collective-permute-start | bytes 393224 | tf_op jit(solution)/shard_map/ppermute | solution.py:34
  147.8 21.9 %all-to-all-done.1 = bf16[16,128,512]{2,1,0:T(8,128)(2,1)S(1)} async-done(((bf16[16,128,512]{2,1,0:T(8,128)(2,1)}), bf16[16,128,512]{2,1,0:T(8,128)(2,1)S(1)}, u32[]{:S(2)}, u32[]{:S(2)}) %all-to-all-start.1) | async-done | bytes 2097184 | tf_op jit(solution)/shard_map/all_to_all | solution.py:38
  172.3 5.0 %all-to-all-start.3 = ((bf16[16,32,512]{2,1,0:T(8,128)(2,1)}), bf16[16,32,512]{2,1,0:T(8,128)(2,1)S(1)}, u32[]{:S(2)}, u32[]{:S(2)}) async-start(bf16[16,32,512]{2,1,0:T(8,128)(2,1)} %bitcast.10), calls=%async_computation.3 | async-start | bytes 1048576 | tf_op jit(solution)/shard_map/all_to_all | solution.py:38
  177.8 8.7 %all-to-all-done.3 = bf16[16,32,512]{2,1,0:T(8,128)(2,1)S(1)} async-done(((bf16[16,32,512]{2,1,0:T(8,128)(2,1)}), bf16[16,32,512]{2,1,0:T(8,128)(2,1)S(1)}, u32[]{:S(2)}, u32[]{:S(2)}) %all-to-all-start.3) | async-done | bytes 524320 | tf_op jit(solution)/shard_map/all_to_all | solution.py:38
  187.2 4.9 %all-to-all-start.4 = ((f32[32,4,128]{2,1,0:T(4,128)}), f32[32,4,128]{2,1,0:T(4,128)S(1)}, u32[]{:S(2)}, u32[]{:S(2)}) async-start(f32[32,4,128]{2,1,0:T(4,128)} %reshape.396), calls=%async_computation.4 | async-start | bytes 131072 | tf_op jit(solution)/shard_map/all_to_all | solution.py:38
  192.3 13.6 %all-to-all-done.4 = f32[32,4,128]{2,1,0:T(4,128)S(1)} async-done(((f32[32,4,128]{2,1,0:T(4,128)}), f32[32,4,128]{2,1,0:T(4,128)S(1)}, u32[]{:S(2)}, u32[]{:S(2)}) %all-to-all-start.4) | async-done | bytes 65568 | tf_op jit(solution)/shard_map/all_to_all | solution.py:38
  207.4 6.0 %all-to-all-start.7 = ((bf16[16,128,512]{2,1,0:T(8,128)(2,1)}), bf16[16,128,512]{2,1,0:T(8,128)(2,1)S(1)}, u32[]{:S(2)}, u32[]{:S(2)}) async-start(bf16[16,128,512]{2,1,0:T(8,128)(2,1)} %broadcast_in_dim.16), calls=%async_computation.7 | async-start | bytes 4194304 | tf_op jit(solution)/shard_map/all_to_all | solution.py:44
  213.4 3.0 collective-permute-start.2
  216.4 12.7 %collective-permute-done.2 = bf16[128,512]{1,0:T(8,128)(2,1)S(1)} collective-permute-done((bf16[128,512]{1,0:T(8,128)(2,1)S(1)}, bf16[128,512]{1,0:T(8,128)(2,1)S(1)}, u32[]{:S(2)}, u32[]{:S(2)}) %collective-permute-start.2) | collective-permute-done | bytes 131104 | tf_op jit(solution)/shard_map/ppermute | solution.py:34
  229.1 13.4 %all-to-all-done.7 = bf16[16,128,512]{2,1,0:T(8,128)(2,1)S(1)} async-done(((bf16[16,128,512]{2,1,0:T(8,128)(2,1)}), bf16[16,128,512]{2,1,0:T(8,128)(2,1)S(1)}, u32[]{:S(2)}, u32[]{:S(2)}) %all-to-all-start.7) | async-done | bytes 2097184 | tf_op jit(solution)/shard_map/all_to_all | solution.py:44
  244.0 6.1 %all-to-all-start.8 = ((bf16[16,128,512]{2,1,0:T(8,128)(2,1)}), bf16[16,128,512]{2,1,0:T(8,128)(2,1)}, u32[]{:S(2)}, u32[]{:S(2)}) async-start(bf16[16,128,512]{2,1,0:T(8,128)(2,1)} %broadcast_in_dim.17), calls=%async_computation.8 | async-start | bytes 4194304 | tf_op jit(solution)/shard_map/all_to_all | solution.py:44
  250.3 27.9 %all-to-all-done.8 = bf16[16,128,512]{2,1,0:T(8,128)(2,1)} async-done(((bf16[16,128,512]{2,1,0:T(8,128)(2,1)}), bf16[16,128,512]{2,1,0:T(8,128)(2,1)}, u32[]{:S(2)}, u32[]{:S(2)}) %all-to-all-start.8) | async-done | bytes 2097184 | tf_op jit(solution)/shard_map/all_to_all | solution.py:44
  278.2 3.9 pad_maximum_fusion
  282.1 2.8 gather_fusion.2
  285.5 2.7 fusion.12
  289.4 1.9 collective-permute-start.3
  291.3 23.0 %all_to_all.50 = f32[32,4,128]{2,1,0:T(4,128)S(1)} all-to-all(f32[32,4,128]{2,1,0:T(4,128)S(1)} %broadcast_in_dim.13), channel_id=1, replica_groups=mesh['zl'=8,'core'=2,'y'=4,'zh'=2,'x'=4] {'zl','core','zh'}, dimensions={0} | all-to-all | bytes 131072 | tf_op jit(solution)/shard_map/all_to_all | solution.py:44
  315.4 5.7 %all-to-all-start.6 = ((f32[16,32,512]{2,1,0:T(8,128)}), f32[16,32,512]{2,1,0:T(8,128)}, u32[]{:S(2)}, u32[]{:S(2)}) async-start(f32[16,32,512]{2,1,0:T(8,128)} %broadcast_in_dim.15), calls=%async_computation.6 | async-start | bytes 2097152 | tf_op jit(solution)/shard_map/all_to_all | solution.py:44
  324.0 11.7 %all-to-all-done.6 = f32[16,32,512]{2,1,0:T(8,128)} async-done(((f32[16,32,512]{2,1,0:T(8,128)}), f32[16,32,512]{2,1,0:T(8,128)}, u32[]{:S(2)}, u32[]{:S(2)}) %all-to-all-start.6) | async-done | bytes 1048608 | tf_op jit(solution)/shard_map/all_to_all | solution.py:44
  335.7 3.6 all-to-all-start.9
  339.3 50.2 %all-to-all-done.9 = bf16[8,128,512]{2,1,0:T(8,128)(2,1)S(1)} async-done(((bf16[8,128,512]{2,1,0:T(8,128)(2,1)}), bf16[8,128,512]{2,1,0:T(8,128)(2,1)S(1)}, u32[]{:S(2)}, u32[]{:S(2)}) %all-to-all-start.9) | async-done | bytes 1048608 | tf_op jit(solution)/shard_map/all_to_all | solution.py:38
  390.5 2.3 copy.51
  (60 shorter events, 27.0 us)
Async XLA Ops:
  7.2 163.1 %copy-start = (bf16[512,512]{1,0:T(8,128)(2,1)S(1)}, bf16[512,512]{1,0:T(8,128)(2,1)}, u32[]{:S(2)}) copy-start(bf16[512,512]{1,0:T(8,128)(2,1)} %param.8) | copy-start | bytes 1572868
  7.2 74.6 %all-gather.3.cloned.1.call-start = ((), (), s32[]{:S(2)}) async-start(), calls=%async_computation.10 | async-start | bytes 1179648 | tf_op jit(solution)/shard_map/all_gather | solution.py:67
  11.2 74.0 %all-to-all-start = ((f32[16,16,128]{2,1,0:T(8,128)}), f32[16,16,128]{2,1,0:T(8,128)S(1)}, u32[]{:S(2)}, u32[]{:S(2)}) async-start(f32[16,16,128]{2,1,0:T(8,128)} %broadcast_in_dim.12), calls=%async_computation | async-start | bytes 262144 | tf_op jit(solution)/shard_map/all_to_all | solution.py:44
  81.8 4.9 %collective-permute-start = (bf16[8,128,512]{2,1,0:T(8,128)(2,1)}, bf16[8,128,512]{2,1,0:T(8,128)(2,1)}, u32[]{:S(2)}, u32[]{:S(2)}) collective-permute-start(bf16[8,128,512]{2,1,0:T(8,128)(2,1)} %bitcast.89), channel_id=1, source_target_pairs={{0,32},{32,0},{1,33},{33,1},{2,34},{34,2},{3,35},{35,3},{4,36},{36... | collective-permute-start | bytes 3145736 | tf_op jit(solution)/shard_map/ppermute | solution.py:34
  88.4 1.6 copy-start.1
  96.9 38.7 %all-to-all-start.2 = ((bf16[16,128,512]{2,1,0:T(8,128)(2,1)}), bf16[16,128,512]{2,1,0:T(8,128)(2,1)}, u32[]{:S(2)}, u32[]{:S(2)}) async-start(bf16[16,128,512]{2,1,0:T(8,128)(2,1)} %copy.27), calls=%async_computation.2 | async-start | bytes 4194304 | tf_op jit(solution)/shard_map/all_to_all | solution.py:38
  135.6 34.1 %all-to-all-start.1 = ((bf16[16,128,512]{2,1,0:T(8,128)(2,1)}), bf16[16,128,512]{2,1,0:T(8,128)(2,1)S(1)}, u32[]{:S(2)}, u32[]{:S(2)}) async-start(bf16[16,128,512]{2,1,0:T(8,128)(2,1)} %copy.25), calls=%async_computation.1 | async-start | bytes 4194304 | tf_op jit(solution)/shard_map/all_to_all | solution.py:38
  142.8 28.4 %copy-start.3 = (bf16[128,512]{1,0:T(8,128)(2,1)S(1)}, bf16[128,512]{1,0:T(8,128)(2,1)}, u32[]{:S(2)}) copy-start(bf16[128,512]{1,0:T(8,128)(2,1)} %param.9) | copy-start | bytes 393220
  142.8 27.2 %collective-permute-start.1 = (bf16[128,512]{1,0:T(8,128)(2,1)S(1)}, bf16[128,512]{1,0:T(8,128)(2,1)S(1)}, u32[]{:S(2)}, u32[]{:S(2)}) collective-permute-start(bf16[128,512]{1,0:T(8,128)(2,1)S(1)} %reduce_sum.87), channel_id=1, source_target_pairs={{0,4},{4,0},{1,5},{5,1},{2,6},{6,2},{3,7},{7,3},{8,12},{12,8},{9,1... | collective-permute-start | bytes 393224 | tf_op jit(solution)/shard_map/ppermute | solution.py:34
  172.3 14.1 %all-to-all-start.3 = ((bf16[16,32,512]{2,1,0:T(8,128)(2,1)}), bf16[16,32,512]{2,1,0:T(8,128)(2,1)S(1)}, u32[]{:S(2)}, u32[]{:S(2)}) async-start(bf16[16,32,512]{2,1,0:T(8,128)(2,1)} %bitcast.10), calls=%async_computation.3 | async-start | bytes 1048576 | tf_op jit(solution)/shard_map/all_to_all | solution.py:38
  187.2 18.6 %all-to-all-start.4 = ((f32[32,4,128]{2,1,0:T(4,128)}), f32[32,4,128]{2,1,0:T(4,128)S(1)}, u32[]{:S(2)}, u32[]{:S(2)}) async-start(f32[32,4,128]{2,1,0:T(4,128)} %reshape.396), calls=%async_computation.4 | async-start | bytes 131072 | tf_op jit(solution)/shard_map/all_to_all | solution.py:38
  207.4 35.1 %all-to-all-start.7 = ((bf16[16,128,512]{2,1,0:T(8,128)(2,1)}), bf16[16,128,512]{2,1,0:T(8,128)(2,1)S(1)}, u32[]{:S(2)}, u32[]{:S(2)}) async-start(bf16[16,128,512]{2,1,0:T(8,128)(2,1)} %broadcast_in_dim.16), calls=%async_computation.7 | async-start | bytes 4194304 | tf_op jit(solution)/shard_map/all_to_all | solution.py:44
  213.4 15.7 %collective-permute-start.2 = (bf16[128,512]{1,0:T(8,128)(2,1)S(1)}, bf16[128,512]{1,0:T(8,128)(2,1)S(1)}, u32[]{:S(2)}, u32[]{:S(2)}) collective-permute-start(bf16[128,512]{1,0:T(8,128)(2,1)S(1)} %multiply_convert_fusion.2), channel_id=1, source_target_pairs={{0,4},{4,0},{1,5},{5,1},{2,6},{6,2},{3,7},{7,3},{8,12},{12,8},{9,1... | collective-permute-start | bytes 393224 | tf_op jit(solution)/shard_map/ppermute | solution.py:34
  244.0 6.1 %copy-start.4 = (s32[1,1,8]{2,1,0:T(1,128)S(1)}, s32[1,1,8]{2,1,0:T(1,128)}, u32[]{:S(2)}) copy-start(s32[1,1,8]{2,1,0:T(1,128)} %param.10) | copy-start | bytes 100
  244.0 6.1 %copy-start.2 = (s32[1,1,8]{2,1,0:T(1,128)S(1)}, s32[1,1,8]{2,1,0:T(1,128)}, u32[]{:S(2)}) copy-start(s32[1,1,8]{2,1,0:T(1,128)} %param.11) | copy-start | bytes 100
  244.0 34.1 %all-to-all-start.8 = ((bf16[16,128,512]{2,1,0:T(8,128)(2,1)}), bf16[16,128,512]{2,1,0:T(8,128)(2,1)}, u32[]{:S(2)}, u32[]{:S(2)}) async-start(bf16[16,128,512]{2,1,0:T(8,128)(2,1)} %broadcast_in_dim.17), calls=%async_computation.8 | async-start | bytes 4194304 | tf_op jit(solution)/shard_map/all_to_all | solution.py:44
  289.4 31.7 %collective-permute-start.3 = (bf16[8,128,512]{2,0,1:T(8,128)(2,1)}, bf16[8,128,512]{2,0,1:T(8,128)(2,1)}, u32[]{:S(2)}, u32[]{:S(2)}) collective-permute-start(bf16[8,128,512]{2,0,1:T(8,128)(2,1)} %slice.23), channel_id=1, source_target_pairs={{0,32},{32,0},{1,33},{33,1},{2,34},{34,2},{3,35},{35,3},{4,36},{36... | collective-permute-start | bytes 3145736 | tf_op jit(solution)/shard_map/ppermute | solution.py:34
  315.4 20.3 %all-to-all-start.6 = ((f32[16,32,512]{2,1,0:T(8,128)}), f32[16,32,512]{2,1,0:T(8,128)}, u32[]{:S(2)}, u32[]{:S(2)}) async-start(f32[16,32,512]{2,1,0:T(8,128)} %broadcast_in_dim.15), calls=%async_computation.6 | async-start | bytes 2097152 | tf_op jit(solution)/shard_map/all_to_all | solution.py:44
  335.7 53.8 %all-to-all-start.9 = ((bf16[8,128,512]{2,1,0:T(8,128)(2,1)}), bf16[8,128,512]{2,1,0:T(8,128)(2,1)S(1)}, u32[]{:S(2)}, u32[]{:S(2)}) async-start(bf16[8,128,512]{2,1,0:T(8,128)(2,1)} %copy.31), calls=%async_computation.9 | async-start | bytes 2097152 | tf_op jit(solution)/shard_map/all_to_all | solution.py:38
Sparse Core Ops, SparseCore 0:
  10.1 71.6 all-gather.2

commit v2 on v1

v2 whole, which is shorter than its diff:
```python
import math

import jax
import jax.numpy as jnp
from jax import lax
from jax.sharding import Mesh
from jax.sharding import PartitionSpec as P

AXES = ("zl", "core", "y", "zh", "x")
ROW = ("zl", "core")
PLANE = ("y", "x")
CHUNKS = 2
SHIFT = {1: 0, 2: 1, 4: 2}
BF16 = jnp.bfloat16
F32 = jnp.float32


def layer_rows(row_total, grad_rows, weight):
    inv_rms = lax.rsqrt(jnp.mean(row_total * row_total, axis=1, keepdims=True) + 1e-06)
    norm_f32 = row_total * inv_rms
    normed = norm_f32.astype(BF16)
    pre_act = jnp.dot(normed, weight, preferred_element_type=F32)
    output = jax.nn.silu(pre_act).astype(BF16)
    sigmoid_pre = jax.nn.sigmoid(pre_act)
    act_slope = sigmoid_pre * (1.0 + pre_act * (1.0 - sigmoid_pre))
    grad_pre = (grad_rows.astype(F32) * act_slope).astype(BF16)
    grad_norm = jnp.einsum("ng,fg->nf", grad_pre, weight, preferred_element_type=F32)
    grad_z = (
        inv_rms * (grad_norm - norm_f32 * jnp.mean(grad_norm * norm_f32, axis=1, keepdims=True))
    ).astype(BF16)
    return (output, normed, grad_pre, grad_z)


def flip(block, axis, distance):
    count = lax.axis_size(axis)
    return lax.ppermute(block, axis, [(i, i ^ distance) for i in range(count)])


def scatter_parts(parts, axes):
    return lax.all_to_all(parts, axes, split_axis=0, concat_axis=0, tiled=True)


def gather_copies(block, axes):
    count = lax.axis_size(axes)
    copies = jnp.broadcast_to(block[None], (count,) + block.shape)
    return lax.all_to_all(copies, axes, split_axis=0, concat_axis=0, tiled=True)


def keep_and_send(block, bit):
    halves = block.reshape((2, block.shape[0] // 2) + block.shape[1:])
    keep = lax.dynamic_index_in_dim(halves, bit, axis=0, keepdims=False)
    send = lax.dynamic_index_in_dim(halves, 1 - bit, axis=0, keepdims=False)
    return keep, send


def total_everywhere(block):
    steps = (("x", 1), ("y", 1), ("x", 2), ("y", 2))
    for number, (axis, distance) in enumerate(steps):
        bit = (lax.axis_index(axis) >> SHIFT[distance]) & 1
        keep, send = keep_and_send(block, bit)
        send = send.astype(BF16) if number < 2 else send
        block = keep + flip(send, axis, distance).astype(F32)
    for axis, distance in (("core", 1), ("zl", 1), ("zl", 2), ("zl", 4), ("zh", 1)):
        block = block + flip(block, axis, distance)
    for axis, distance in reversed(steps):
        bit = (lax.axis_index(axis) >> SHIFT[distance]) & 1
        other = flip(block, axis, distance)
        block = jnp.where(
            bit == 0, jnp.concatenate([block, other]), jnp.concatenate([other, block])
        )
    return block


def local(features, weight, cotangent, tile_rows, tile_cols, tile_count, tile_vals):
    span, width = features.shape
    n_zl, n_core = lax.axis_size("zl"), lax.axis_size("core")
    n_y, n_zh, n_x = lax.axis_size("y"), lax.axis_size("zh"), lax.axis_size("x")
    n_row, n_col = n_zl * n_core, n_y * n_zh * n_x
    n_plane = n_y * n_x
    my_zl, my_core, my_zh = lax.axis_index("zl"), lax.axis_index("core"), lax.axis_index("zh")
    slots = tile_vals.shape[2]
    nodes = n_row * n_col * span
    chunk = width // CHUNKS
    alive = jnp.arange(slots, dtype=jnp.int32) < tile_count[0, 0]
    weights = tile_vals[0, 0] * alive.astype(BF16)[:, None, None]
    row_index = tile_rows[0, 0]
    col_index = tile_cols[0, 0]
    zl_bits = (col_index // n_core) ^ my_zl
    zl_place = (zl_bits & 1) * 4 + (zl_bits & 2) + zl_bits // 4
    col_place = ((col_index % n_core) ^ my_core) * n_zl + zl_place
    row_plane = (row_index // (n_zh * n_x)) * n_x + row_index % n_x
    row_place = (((row_index // n_x) % n_zh) ^ my_zh) * n_plane + row_plane
    place_rows = (row_place[:, None] == jnp.arange(n_col, dtype=jnp.int32)[None, :]).astype(F32)
    place_cols = (col_place[:, None] == jnp.arange(n_row, dtype=jnp.int32)[None, :]).astype(F32)
    order_cols = (col_index[:, None] == jnp.arange(n_row, dtype=jnp.int32)[None, :]).astype(F32)
    parts = [slice(c * chunk, (c + 1) * chunk) for c in range(CHUNKS)]

    col_sums = jnp.sum(tile_vals[0, 0], axis=1, dtype=F32) * alive.astype(F32)[:, None]
    degree_terms = jnp.einsum("sc,sj->cj", order_cols, col_sums, precision=lax.Precision.HIGHEST)
    col_degree = 1.0 + jnp.sum(gather_copies(degree_terms, ROW), axis=0)
    col_scale = lax.rsqrt(col_degree)
    own_scale = lax.dynamic_index_in_dim(
        col_scale, my_zl * n_core + my_core, axis=0, keepdims=False
    )
    slot_scale = col_scale[col_index][:, :, None]

    far_sums, near_sums, forward = [], [], []
    for part in parts:
        blocks = features[:, part][None]
        for axis, distance in (("zl", 4), ("zl", 2), ("zl", 1), ("core", 1)):
            blocks = jnp.concatenate([blocks, flip(blocks, axis, distance)])
        picked = (blocks[col_place].astype(F32) * slot_scale).astype(BF16)
        products = jnp.einsum("sij,sjf->sif", weights, picked, preferred_element_type=F32)
        terms = jnp.einsum("sr,sif->rif", place_rows, products, precision=lax.Precision.HIGHEST)
        forward.append(terms.astype(BF16))
    for terms in forward:
        far = jnp.sum(scatter_parts(terms[n_plane:], PLANE).astype(F32), axis=0)
        far_sums.append(flip(far.astype(BF16), "zh", 1))
    for terms in forward:
        near_sums.append(jnp.sum(scatter_parts(terms[:n_plane], PLANE).astype(F32), axis=0))
    own_total = jnp.concatenate(
        [near + far.astype(F32) for near, far in zip(near_sums, far_sums)], axis=1
    )

    output, normed, grad_pre, grad_own = layer_rows(own_total, cotangent, weight)

    grad_far = flip(grad_own, "zh", 1)
    weight_terms = jnp.einsum("nf,ng->fg", normed, grad_pre, preferred_element_type=F32)
    weight_grad = total_everywhere(weight_terms) * (1.0 / math.sqrt(nodes))

    own_grads = []
    for part in parts:
        grad_group = jnp.concatenate(
            [gather_copies(grad_own[:, part], PLANE), gather_copies(grad_far[:, part], PLANE)]
        )
        grad_picked = grad_group[row_place]
        back_products = jnp.einsum("sij,sif->sjf", weights, grad_picked, preferred_element_type=F32)
        total = jnp.einsum(
            "sc,sjf->cjf", place_cols, back_products, precision=lax.Precision.HIGHEST
        )
        for axis, distance in (("core", 1), ("zl", 1), ("zl", 2), ("zl", 4)):
            half = total.shape[0] // 2
            total = total[:half] + flip(total[half:].astype(BF16), axis, distance).astype(F32)
        own_grads.append(total[0])
    feature_grad = jnp.concatenate(own_grads, axis=1) * own_scale[:, None]
    return (output, weight_grad, feature_grad)


def solution(mesh):
    fine = Mesh(mesh.devices.reshape(8, 2, 4, 2, 4), AXES)
    nodes, row, col = P(AXES, None), ("zl", "core"), ("y", "zh", "x")
    in_specs = (
        nodes,
        P(),
        nodes,
        P(row, col, None),
        P(row, col, None),
        P(row, col),
        P(row, col, None, None, None),
    )
    out_specs = (nodes, P(), nodes)
    return jax.shard_map(local, mesh=fine, in_specs=in_specs, out_specs=out_specs, check_vma=False)
```

time: 402 us -> 379 us (0.943)
  waiting for transfers between devices: 246 us -> 129 us
  starting transfers between devices: 68.3 us -> 177 us
  blocking collectives: 23 us -> 0 us
  local copies, waits for them, and re-layouts: 20.2 us -> 34.6 us
  between operations: 15 us -> 2.31 us
  other arithmetic: 13.3 us -> 20.8 us
    ppermute x4 -> x32, starting transfers between devices: 11.9 us -> 116 us  [flip(): return lax.ppermute(block, axis, [(i, i ^ distance) for i in range(count)])]
    all_to_all x5 -> x4, waiting for transfers between devices: 121 us -> 19.3 us  [scatter_parts(): return lax.all_to_all(parts, axes, split_axis=0, concat_axis=0, tiled=True)]
    ppermute x4 -> x32, waiting for transfers between devices: 13.6 us -> 100 us  [flip(): return lax.ppermute(block, axis, [(i, i ^ distance) for i in range(count)])]
    all_gather x1 -> x0, waiting for transfers between devices: 58 us -> none  [local(): zl_blocks = lax.all_gather(features, 'zl', axis=0, tiled=False)]
    all_to_all x4 -> x5, waiting for transfers between devices: 53 us -> 9.54 us  [gather_copies(): return lax.all_to_all(copies, axes, split_axis=0, concat_axis=0, tiled=True)]
    all_to_all x1 -> x0, blocking collectives: 23 us -> none  [gather_copies(): return lax.all_to_all(copies, axes, split_axis=0, concat_axis=0, tiled=True)]
    slice x1 -> x18, local copies, waits for them, and re-layouts: 1.13 us -> 9.21 us  [the longest x4 3.91 us: local(): far = jnp.sum(scatter_parts(terms[n_plane:], PLANE).astype(F32), axis=0)]
    convert_element_type x3 -> x2, local copies, waits for them, and re-layouts: 6.32 us -> 0.71 us  [total_everywhere(): send = send.astype(BF16) if number < 2 else send]
  transfers between devices with their start and end apart: 14 -> 41, of which waited for: 11 -> 23; matrix products, arithmetic and copies ran while one was open for 4% -> 16% of each run, Pallas kernels for 0% -> 0%
where the time goes in v2:
time: 379 us; the launch traced here: 376 us
  starting transfers between devices  177 us (47%)
  waiting for transfers between devices  129 us (34%)
  local copies, waits for them, and re-layouts  34.6 us (9%)
  other arithmetic  20.8 us (5%)
  matrix products  11.9 us (3%)
    ppermute x32, starting transfers between devices, flip(): return lax.ppermute(block, axis, [(i, i ^ distance) for i in range(count)])  116 us
    ppermute x32, waiting for transfers between devices, flip(): return lax.ppermute(block, axis, [(i, i ^ distance) for i in range(count)])  100 us
    all_to_all x5, starting transfers between devices, gather_copies(): return lax.all_to_all(copies, axes, split_axis=0, concat_axis=0, tiled=True)  33.2 us
    all_to_all x4, starting transfers between devices, scatter_parts(): return lax.all_to_all(parts, axes, split_axis=0, concat_axis=0, tiled=True)  28 us
    all_to_all x4, waiting for transfers between devices, scatter_parts(): return lax.all_to_all(parts, axes, split_axis=0, concat_axis=0, tiled=True)  19.3 us
    all_to_all x5, waiting for transfers between devices, gather_copies(): return lax.all_to_all(copies, axes, split_axis=0, concat_axis=0, tiled=True)  9.54 us
  transfers between devices with their start and end apart: 41, of which 23 were waited for; matrix products, arithmetic and copies ran while one was open for 16% of the time, Pallas kernels for 0%

profile of v2, /device:TPU:24, one launch (start us, length us, event | category | flops | bytes accessed | tf_op | source)
XLA Modules:
  0.0 376.2 jit_solution(8136921270154103224)
XLA Ops:
  1.6 9.1 %collective-permute-start = (bf16[1,128,256]{2,1,0:T(8,128)(2,1)S(1)}, bf16[1,128,256]{2,1,0:T(8,128)(2,1)S(1)}, u32[]{:S(2)}, u32[]{:S(2)}) collective-permute-start(bf16[1,128,256]{2,1,0:T(8,128)(2,1)S(1)} %get-tuple-element.11), channel_id=1, source_target_pairs={{0,256},{64,320},{128,384},{192,448},{256,0},{320,64},{384,128},{4... | collective-permute-start | bytes 196616 | tf_op jit(solution)/shard_map/ppermute | solution.py:36
  13.9 6.0 %all-to-all-start = ((f32[16,16,128]{2,1,0:T(8,128)}), f32[16,16,128]{2,1,0:T(8,128)S(1)}, u32[]{:S(2)}, u32[]{:S(2)}) async-start(f32[16,16,128]{2,1,0:T(8,128)} %broadcast_in_dim.15), calls=%async_computation | async-start | bytes 262144 | tf_op jit(solution)/shard_map/all_to_all | solution.py:46
  19.9 7.7 %collective-permute-start.5 = (bf16[1,128,256]{2,1,0:T(8,128)(2,1)S(1)}, bf16[1,128,256]{2,1,0:T(8,128)(2,1)S(1)}, u32[]{:S(2)}, u32[]{:S(2)}) collective-permute-start(bf16[1,128,256]{2,1,0:T(8,128)(2,1)S(1)} %get-tuple-element.12), channel_id=1, source_target_pairs={{0,256},{64,320},{128,384},{192,448},{256,0},{320,64},{384,128},{4... | collective-permute-start | bytes 196616 | tf_op jit(solution)/shard_map/ppermute | solution.py:36
  34.9 8.2 %collective-permute-done.1 = bf16[2,128,256]{2,1,0:T(8,128)(2,1)S(1)} collective-permute-done((bf16[2,128,256]{2,1,0:T(8,128)(2,1)S(1)}, bf16[2,128,256]{2,1,0:T(8,128)(2,1)S(1)}, u32[]{:S(2)}, u32[]{:S(2)}) %collective-permute-start.1) | collective-permute-done | bytes 131104 | tf_op jit(solution)/shard_map/ppermute | solution.py:36
  48.7 6.4 %collective-permute-done.2 = bf16[4,128,256]{2,1,0:T(8,128)(2,1)S(1)} collective-permute-done((bf16[4,128,256]{2,1,0:T(8,128)(2,1)S(1)}, bf16[4,128,256]{2,1,0:T(8,128)(2,1)S(1)}, u32[]{:S(2)}, u32[]{:S(2)}) %collective-permute-start.2) | collective-permute-done | bytes 262176 | tf_op jit(solution)/shard_map/ppermute | solution.py:36
  66.5 7.2 %all-to-all-start.2 = ((bf16[16,128,256]{2,1,0:T(8,128)(2,1)}), bf16[16,128,256]{2,1,0:T(8,128)(2,1)S(1)}, u32[]{:S(2)}, u32[]{:S(2)}) async-start(bf16[16,128,256]{2,1,0:T(8,128)(2,1)} %copy.20), calls=%async_computation.2 | async-start | bytes 2097152 | tf_op jit(solution)/shard_map/all_to_all | solution.py:40
  75.6 8.1 %collective-permute-done.7 = bf16[4,128,256]{2,1,0:T(8,128)(2,1)S(1)} collective-permute-done((bf16[4,128,256]{2,1,0:T(8,128)(2,1)S(1)}, bf16[4,128,256]{2,1,0:T(8,128)(2,1)S(1)}, u32[]{:S(2)}, u32[]{:S(2)}) %collective-permute-start.7) | collective-permute-done | bytes 262176 | tf_op jit(solution)/shard_map/ppermute | solution.py:36
  89.9 7.2 %all-to-all-start.1 = ((bf16[16,128,256]{2,1,0:T(8,128)(2,1)}), bf16[16,128,256]{2,1,0:T(8,128)(2,1)S(1)}, u32[]{:S(2)}, u32[]{:S(2)}) async-start(bf16[16,128,256]{2,1,0:T(8,128)(2,1)} %copy.19), calls=%async_computation.1 | async-start | bytes 2097152 | tf_op jit(solution)/shard_map/all_to_all | solution.py:40
  105.9 7.4 %all-to-all-done.1 = bf16[16,128,256]{2,1,0:T(8,128)(2,1)S(1)} async-done(((bf16[16,128,256]{2,1,0:T(8,128)(2,1)}), bf16[16,128,256]{2,1,0:T(8,128)(2,1)S(1)}, u32[]{:S(2)}, u32[]{:S(2)}) %all-to-all-start.1) | async-done | bytes 1048608 | tf_op jit(solution)/shard_map/all_to_all | solution.py:40
  113.3 6.7 %all-to-all-start.4 = ((bf16[16,128,256]{2,1,0:T(8,128)(2,1)}), bf16[16,128,256]{2,1,0:T(8,128)(2,1)}, u32[]{:S(2)}, u32[]{:S(2)}) async-start(bf16[16,128,256]{2,1,0:T(8,128)(2,1)} %copy.23), calls=%async_computation.4 | async-start | bytes 2097152 | tf_op jit(solution)/shard_map/all_to_all | solution.py:40
  122.5 11.9 %all-to-all-done.4 = bf16[16,128,256]{2,1,0:T(8,128)(2,1)} async-done(((bf16[16,128,256]{2,1,0:T(8,128)(2,1)}), bf16[16,128,256]{2,1,0:T(8,128)(2,1)}, u32[]{:S(2)}, u32[]{:S(2)}) %all-to-all-start.4) | async-done | bytes 1048608 | tf_op jit(solution)/shard_map/all_to_all | solution.py:40
  134.5 6.9 %all-to-all-start.3 = ((bf16[16,128,256]{2,1,0:T(8,128)(2,1)}), bf16[16,128,256]{2,1,0:T(8,128)(2,1)}, u32[]{:S(2)}, u32[]{:S(2)}) async-start(bf16[16,128,256]{2,1,0:T(8,128)(2,1)} %copy.22), calls=%async_computation.3 | async-start | bytes 2097152 | tf_op jit(solution)/shard_map/all_to_all | solution.py:40
  141.5 11.2 %collective-permute-start.4 = (bf16[128,256]{1,0:T(8,128)(2,1)S(1)}, bf16[128,256]{1,0:T(8,128)(2,1)S(1)}, u32[]{:S(2)}, u32[]{:S(2)}) collective-permute-start(bf16[128,256]{1,0:T(8,128)(2,1)S(1)} %reduce_sum.81), channel_id=1, source_target_pairs={{0,4},{4,0},{1,5},{5,1},{2,6},{6,2},{3,7},{7,3},{8,12},{12,8},{9,1... | collective-permute-start | bytes 196616 | tf_op jit(solution)/shard_map/ppermute | solution.py:36
  159.1 10.0 %collective-permute-done.9 = bf16[128,256]{1,0:T(8,128)(2,1)S(1)} collective-permute-done((bf16[128,256]{1,0:T(8,128)(2,1)S(1)}, bf16[128,256]{1,0:T(8,128)(2,1)S(1)}, u32[]{:S(2)}, u32[]{:S(2)}) %collective-permute-start.9) | collective-permute-done | bytes 65568 | tf_op jit(solution)/shard_map/ppermute | solution.py:36
  171.8 7.2 %all-to-all-start.5 = ((bf16[16,128,256]{2,1,0:T(8,128)(2,1)}), bf16[16,128,256]{2,1,0:T(8,128)(2,1)S(1)}, u32[]{:S(2)}, u32[]{:S(2)}) async-start(bf16[16,128,256]{2,1,0:T(8,128)(2,1)} %broadcast_in_dim.17), calls=%async_computation.5 | async-start | bytes 2097152 | tf_op jit(solution)/shard_map/all_to_all | solution.py:46
  183.9 9.5 %all-to-all-done.5 = bf16[16,128,256]{2,1,0:T(8,128)(2,1)S(1)} async-done(((bf16[16,128,256]{2,1,0:T(8,128)(2,1)}), bf16[16,128,256]{2,1,0:T(8,128)(2,1)S(1)}, u32[]{:S(2)}, u32[]{:S(2)}) %all-to-all-start.5) | async-done | bytes 1048608 | tf_op jit(solution)/shard_map/all_to_all | solution.py:46
  194.5 5.9 %all-to-all-start.7 = ((bf16[16,128,256]{2,1,0:T(8,128)(2,1)}), bf16[16,128,256]{2,1,0:T(8,128)(2,1)S(1)}, u32[]{:S(2)}, u32[]{:S(2)}) async-start(bf16[16,128,256]{2,1,0:T(8,128)(2,1)} %broadcast_in_dim.19), calls=%async_computation.7 | async-start | bytes 2097152 | tf_op jit(solution)/shard_map/all_to_all | solution.py:46
  211.8 4.8 %collective-permute-start.12 = (f32[64,512]{1,0:T(8,128)}, f32[64,512]{1,0:T(8,128)}, u32[]{:S(2)}, u32[]{:S(2)}) collective-permute-start(f32[64,512]{1,0:T(8,128)} %dynamic-slice_bitcast_fusion), channel_id=1, source_target_pairs={{0,2},{1,3},{2,0},{3,1},{4,6},{5,7},{6,4},{7,5},{8,10},{9,11},{10,... | collective-permute-start | bytes 393224 | tf_op jit(solution)/shard_map/ppermute | solution.py:36
  216.7 4.5 %collective-permute-done.23 = bf16[128,512]{1,0:T(8,128)(2,1)S(1)} collective-permute-done((bf16[128,512]{1,0:T(8,128)(2,1)S(1)}, bf16[128,512]{1,0:T(8,128)(2,1)S(1)}, u32[]{:S(2)}, u32[]{:S(2)}) %collective-permute-start.23) | collective-permute-done | bytes 131104 | tf_op jit(solution)/shard_map/ppermute | solution.py:36
  222.3 7.6 %all-to-all-start.6 = ((bf16[16,128,256]{2,1,0:T(8,128)(2,1)}), bf16[16,128,256]{2,1,0:T(8,128)(2,1)}, u32[]{:S(2)}, u32[]{:S(2)}) async-start(bf16[16,128,256]{2,1,0:T(8,128)(2,1)} %broadcast_in_dim.18), calls=%async_computation.6 | async-start | bytes 2097152 | tf_op jit(solution)/shard_map/all_to_all | solution.py:46
  234.2 6.3 %collective-permute-done.13 = f32[32,512]{1,0:T(8,128)S(1)} collective-permute-done((f32[32,512]{1,0:T(8,128)S(1)}, f32[32,512]{1,0:T(8,128)S(1)}, u32[]{:S(2)}, u32[]{:S(2)}) %collective-permute-start.13) | collective-permute-done | bytes 65568 | tf_op jit(solution)/shard_map/ppermute | solution.py:36
  243.7 5.4 %collective-permute-start.15 = (f32[32,512]{1,0:T(8,128)S(1)}, f32[32,512]{1,0:T(8,128)S(1)}, u32[]{:S(2)}, u32[]{:S(2)}) collective-permute-start(f32[32,512]{1,0:T(8,128)S(1)} %add.352), channel_id=1, source_target_pairs={{0,64},{64,0},{128,192},{192,128},{256,320},{320,256},{384,448},{4... | collective-permute-start | bytes 196616 | tf_op jit(solution)/shard_map/ppermute | solution.py:36
  253.4 5.2 %collective-permute-done.16 = f32[32,512]{1,0:T(8,128)S(1)} collective-permute-done((f32[32,512]{1,0:T(8,128)S(1)}, f32[32,512]{1,0:T(8,128)S(1)}, u32[]{:S(2)}, u32[]{:S(2)}) %collective-permute-start.16) | collective-permute-done | bytes 65568 | tf_op jit(solution)/shard_map/ppermute | solution.py:36
  260.6 10.3 %collective-permute-done.17 = f32[32,512]{1,0:T(8,128)S(1)} collective-permute-done((f32[32,512]{1,0:T(8,128)S(1)}, f32[32,512]{1,0:T(8,128)S(1)}, u32[]{:S(2)}, u32[]{:S(2)}) %collective-permute-start.17) | collective-permute-done | bytes 65568 | tf_op jit(solution)/shard_map/ppermute | solution.py:36
  270.9 5.1 %collective-permute-start.18 = (f32[32,512]{1,0:T(8,128)S(1)}, f32[32,512]{1,0:T(8,128)S(1)}, u32[]{:S(2)}, u32[]{:S(2)}) collective-permute-start(f32[32,512]{1,0:T(8,128)S(1)} %add.355), channel_id=1, source_target_pairs={{0,4},{4,0},{1,5},{5,1},{2,6},{6,2},{3,7},{7,3},{8,12},{12,8},{9,1... | collective-permute-start | bytes 196616 | tf_op jit(solution)/shard_map/ppermute | solution.py:36
  277.1 6.6 %all-to-all-start.8 = ((bf16[16,128,256]{2,1,0:T(8,128)(2,1)}), bf16[16,128,256]{2,1,0:T(8,128)(2,1)}, u32[]{:S(2)}, u32[]{:S(2)}) async-start(bf16[16,128,256]{2,1,0:T(8,128)(2,1)} %broadcast_in_dim.20), calls=%async_computation.8 | async-start | bytes 2097152 | tf_op jit(solution)/shard_map/all_to_all | solution.py:46
  289.8 7.0 %collective-permute-done.19 = f32[32,512]{1,0:T(8,128)S(1)} collective-permute-done((f32[32,512]{1,0:T(8,128)S(1)}, f32[32,512]{1,0:T(8,128)S(1)}, u32[]{:S(2)}, u32[]{:S(2)}) %collective-permute-start.19) | collective-permute-done | bytes 65568 | tf_op jit(solution)/shard_map/ppermute | solution.py:36
  296.8 5.2 %collective-permute-start.20 = (f32[64,512]{1,0:T(8,128)S(1)}, f32[64,512]{1,0:T(8,128)}, u32[]{:S(2)}, u32[]{:S(2)}) collective-permute-start(f32[64,512]{1,0:T(8,128)S(1)} %maximum_select_fusion.3), channel_id=1, source_target_pairs={{0,2},{1,3},{2,0},{3,1},{4,6},{5,7},{6,4},{7,5},{8,10},{9,11},{10,... | collective-permute-start | bytes 393224 | tf_op jit(solution)/shard_map/ppermute | solution.py:36
  324.5 4.5 %collective-permute-done.21 = f32[128,512]{1,0:T(8,128)S(1)} collective-permute-done((f32[128,512]{1,0:T(8,128)S(1)}, f32[128,512]{1,0:T(8,128)S(1)}, u32[]{:S(2)}, u32[]{:S(2)}) %collective-permute-start.21) | collective-permute-done | bytes 262176 | tf_op jit(solution)/shard_map/ppermute | solution.py:36
  339.3 4.9 %collective-permute-done.25 = bf16[4,128,256]{2,0,1:T(4,128)(2,1)S(1)} collective-permute-done((bf16[4,128,256]{2,0,1:T(4,128)(2,1)S(1)}, bf16[4,128,256]{2,0,1:T(4,128)(2,1)S(1)}, u32[]{:S(2)}, u32[]{:S(2)}) %collective-permute-start.25) | collective-permute-done | bytes 262176 | tf_op jit(solution)/shard_map/ppermute | solution.py:36
  360.8 4.6 %collective-permute-start.31 = (bf16[1,128,256]{2,1,0:T(8,128)(2,1)S(1)}, bf16[1,128,256]{2,1,0:T(8,128)(2,1)S(1)}, u32[]{:S(2)}, u32[]{:S(2)}) collective-permute-start(bf16[1,128,256]{2,1,0:T(8,128)(2,1)S(1)} %slice.173), channel_id=1, source_target_pairs={{0,256},{64,320},{128,384},{192,448},{256,0},{320,64},{384,128},{4... | collective-permute-start | bytes 196616 | tf_op jit(solution)/shard_map/ppermute | solution.py:36
  365.4 9.3 %collective-permute-done.27 = bf16[1,128,256]{2,0,1:T(2,128)(2,1)S(1)} collective-permute-done((bf16[1,128,256]{2,0,1:T(2,128)(2,1)S(1)}, bf16[1,128,256]{2,0,1:T(2,128)(2,1)S(1)}, u32[]{:S(2)}, u32[]{:S(2)}) %collective-permute-start.27) | collective-permute-done | bytes 65568 | tf_op jit(solution)/shard_map/ppermute | solution.py:36
  (182 shorter events, 146.0 us)
Async XLA Ops:
  1.6 28.3 %collective-permute-start = (bf16[1,128,256]{2,1,0:T(8,128)(2,1)S(1)}, bf16[1,128,256]{2,1,0:T(8,128)(2,1)S(1)}, u32[]{:S(2)}, u32[]{:S(2)}) collective-permute-start(bf16[1,128,256]{2,1,0:T(8,128)(2,1)S(1)} %get-tuple-element.11), channel_id=1, source_target_pairs={{0,256},{64,320},{128,384},{192,448},{256,0},{320,64},{384,128},{4... | collective-permute-start | bytes 196616 | tf_op jit(solution)/shard_map/ppermute | solution.py:36
  13.9 45.2 %all-to-all-start = ((f32[16,16,128]{2,1,0:T(8,128)}), f32[16,16,128]{2,1,0:T(8,128)S(1)}, u32[]{:S(2)}, u32[]{:S(2)}) async-start(f32[16,16,128]{2,1,0:T(8,128)} %broadcast_in_dim.15), calls=%async_computation | async-start | bytes 262144 | tf_op jit(solution)/shard_map/all_to_all | solution.py:46
  19.9 25.1 %collective-permute-start.5 = (bf16[1,128,256]{2,1,0:T(8,128)(2,1)S(1)}, bf16[1,128,256]{2,1,0:T(8,128)(2,1)S(1)}, u32[]{:S(2)}, u32[]{:S(2)}) collective-permute-start(bf16[1,128,256]{2,1,0:T(8,128)(2,1)S(1)} %get-tuple-element.12), channel_id=1, source_target_pairs={{0,256},{64,320},{128,384},{192,448},{256,0},{320,64},{384,128},{4... | collective-permute-start | bytes 196616 | tf_op jit(solution)/shard_map/ppermute | solution.py:36
  29.9 13.1 %collective-permute-start.1 = (bf16[2,128,256]{2,1,0:T(8,128)(2,1)S(1)}, bf16[2,128,256]{2,1,0:T(8,128)(2,1)S(1)}, u32[]{:S(2)}, u32[]{:S(2)}) collective-permute-start(bf16[2,128,256]{2,1,0:T(8,128)(2,1)S(1)} %pad_maximum_fusion.7), channel_id=1, source_target_pairs={{0,128},{64,192},{128,0},{192,64},{256,384},{320,448},{384,256},{4... | collective-permute-start | bytes 393224 | tf_op jit(solution)/shard_map/ppermute | solution.py:36
  43.1 12.0 %collective-permute-start.2 = (bf16[4,128,256]{2,1,0:T(8,128)(2,1)S(1)}, bf16[4,128,256]{2,1,0:T(8,128)(2,1)S(1)}, u32[]{:S(2)}, u32[]{:S(2)}) collective-permute-start(bf16[4,128,256]{2,1,0:T(8,128)(2,1)S(1)} %pad_maximum_fusion.4), channel_id=1, source_target_pairs={{0,64},{64,0},{128,192},{192,128},{256,320},{320,256},{384,448},{4... | collective-permute-start | bytes 786440 | tf_op jit(solution)/shard_map/ppermute | solution.py:36
  45.1 28.6 %collective-permute-start.6 = (bf16[2,128,256]{2,1,0:T(8,128)(2,1)S(1)}, bf16[2,128,256]{2,1,0:T(8,128)(2,1)S(1)}, u32[]{:S(2)}, u32[]{:S(2)}) collective-permute-start(bf16[2,128,256]{2,1,0:T(8,128)(2,1)S(1)} %pad_maximum_fusion.8), channel_id=1, source_target_pairs={{0,128},{64,192},{128,0},{192,64},{256,384},{320,448},{384,256},{4... | collective-permute-start | bytes 393224 | tf_op jit(solution)/shard_map/ppermute | solution.py:36
  66.5 23.4 %all-to-all-start.2 = ((bf16[16,128,256]{2,1,0:T(8,128)(2,1)}), bf16[16,128,256]{2,1,0:T(8,128)(2,1)S(1)}, u32[]{:S(2)}, u32[]{:S(2)}) async-start(bf16[16,128,256]{2,1,0:T(8,128)(2,1)} %copy.20), calls=%async_computation.2 | async-start | bytes 2097152 | tf_op jit(solution)/shard_map/all_to_all | solution.py:40
  84.6 12.5 %collective-permute-start.8 = (bf16[8,128,256]{2,1,0:T(8,128)(2,1)}, bf16[8,128,256]{2,1,0:T(8,128)(2,1)}, u32[]{:S(2)}, u32[]{:S(2)}) collective-permute-start(bf16[8,128,256]{2,1,0:T(8,128)(2,1)} %pad_maximum_fusion.3), channel_id=1, source_target_pairs={{0,32},{32,0},{1,33},{33,1},{2,34},{34,2},{3,35},{35,3},{4,36},{36... | collective-permute-start | bytes 1572872 | tf_op jit(solution)/shard_map/ppermute | solution.py:36
  89.9 23.4 %all-to-all-start.1 = ((bf16[16,128,256]{2,1,0:T(8,128)(2,1)}), bf16[16,128,256]{2,1,0:T(8,128)(2,1)S(1)}, u32[]{:S(2)}, u32[]{:S(2)}) async-start(bf16[16,128,256]{2,1,0:T(8,128)(2,1)} %copy.19), calls=%async_computation.1 | async-start | bytes 2097152 | tf_op jit(solution)/shard_map/all_to_all | solution.py:40
  113.3 21.2 %all-to-all-start.4 = ((bf16[16,128,256]{2,1,0:T(8,128)(2,1)}), bf16[16,128,256]{2,1,0:T(8,128)(2,1)}, u32[]{:S(2)}, u32[]{:S(2)}) async-start(bf16[16,128,256]{2,1,0:T(8,128)(2,1)} %copy.23), calls=%async_computation.4 | async-start | bytes 2097152 | tf_op jit(solution)/shard_map/all_to_all | solution.py:40
  134.5 23.2 %all-to-all-start.3 = ((bf16[16,128,256]{2,1,0:T(8,128)(2,1)}), bf16[16,128,256]{2,1,0:T(8,128)(2,1)}, u32[]{:S(2)}, u32[]{:S(2)}) async-start(bf16[16,128,256]{2,1,0:T(8,128)(2,1)} %copy.22), calls=%async_computation.3 | async-start | bytes 2097152 | tf_op jit(solution)/shard_map/all_to_all | solution.py:40
  141.5 17.5 %collective-permute-start.4 = (bf16[128,256]{1,0:T(8,128)(2,1)S(1)}, bf16[128,256]{1,0:T(8,128)(2,1)S(1)}, u32[]{:S(2)}, u32[]{:S(2)}) collective-permute-start(bf16[128,256]{1,0:T(8,128)(2,1)S(1)} %reduce_sum.81), channel_id=1, source_target_pairs={{0,4},{4,0},{1,5},{5,1},{2,6},{6,2},{3,7},{7,3},{8,12},{12,8},{9,1... | collective-permute-start | bytes 196616 | tf_op jit(solution)/shard_map/ppermute | solution.py:36
  154.1 15.0 %collective-permute-start.9 = (bf16[128,256]{1,0:T(8,128)(2,1)S(1)}, bf16[128,256]{1,0:T(8,128)(2,1)S(1)}, u32[]{:S(2)}, u32[]{:S(2)}) collective-permute-start(bf16[128,256]{1,0:T(8,128)(2,1)S(1)} %reduce_sum.83), channel_id=1, source_target_pairs={{0,4},{4,0},{1,5},{5,1},{2,6},{6,2},{3,7},{7,3},{8,12},{12,8},{9,1... | collective-permute-start | bytes 196616 | tf_op jit(solution)/shard_map/ppermute | solution.py:36
  171.8 21.6 %all-to-all-start.5 = ((bf16[16,128,256]{2,1,0:T(8,128)(2,1)}), bf16[16,128,256]{2,1,0:T(8,128)(2,1)S(1)}, u32[]{:S(2)}, u32[]{:S(2)}) async-start(bf16[16,128,256]{2,1,0:T(8,128)(2,1)} %broadcast_in_dim.17), calls=%async_computation.5 | async-start | bytes 2097152 | tf_op jit(solution)/shard_map/all_to_all | solution.py:46
  180.5 19.9 %collective-permute-start.10 = (bf16[256,512]{1,0:T(8,128)(2,1)S(1)}, bf16[256,512]{1,0:T(8,128)(2,1)}, u32[]{:S(2)}, u32[]{:S(2)}) collective-permute-start(bf16[256,512]{1,0:T(8,128)(2,1)S(1)} %fusion.11), channel_id=1, source_target_pairs={{0,1},{1,0},{2,3},{3,2},{4,5},{5,4},{6,7},{7,6},{8,9},{9,8},{10,11... | collective-permute-start | bytes 786440 | tf_op jit(solution)/shard_map/ppermute | solution.py:36
  194.5 26.7 %all-to-all-start.7 = ((bf16[16,128,256]{2,1,0:T(8,128)(2,1)}), bf16[16,128,256]{2,1,0:T(8,128)(2,1)S(1)}, u32[]{:S(2)}, u32[]{:S(2)}) async-start(bf16[16,128,256]{2,1,0:T(8,128)(2,1)} %broadcast_in_dim.19), calls=%async_computation.7 | async-start | bytes 2097152 | tf_op jit(solution)/shard_map/all_to_all | solution.py:46
  205.0 16.1 %collective-permute-start.23 = (bf16[128,512]{1,0:T(8,128)(2,1)S(1)}, bf16[128,512]{1,0:T(8,128)(2,1)S(1)}, u32[]{:S(2)}, u32[]{:S(2)}) collective-permute-start(bf16[128,512]{1,0:T(8,128)(2,1)S(1)} %multiply_convert_fusion.4), channel_id=1, source_target_pairs={{0,4},{4,0},{1,5},{5,1},{2,6},{6,2},{3,7},{7,3},{8,12},{12,8},{9,1... | collective-permute-start | bytes 393224 | tf_op jit(solution)/shard_map/ppermute | solution.py:36
  211.8 18.1 %collective-permute-start.12 = (f32[64,512]{1,0:T(8,128)}, f32[64,512]{1,0:T(8,128)}, u32[]{:S(2)}, u32[]{:S(2)}) collective-permute-start(f32[64,512]{1,0:T(8,128)} %dynamic-slice_bitcast_fusion), channel_id=1, source_target_pairs={{0,2},{1,3},{2,0},{3,1},{4,6},{5,7},{6,4},{7,5},{8,10},{9,11},{10,... | collective-permute-start | bytes 393224 | tf_op jit(solution)/shard_map/ppermute | solution.py:36
  222.3 53.7 %all-to-all-start.6 = ((bf16[16,128,256]{2,1,0:T(8,128)(2,1)}), bf16[16,128,256]{2,1,0:T(8,128)(2,1)}, u32[]{:S(2)}, u32[]{:S(2)}) async-start(bf16[16,128,256]{2,1,0:T(8,128)(2,1)} %broadcast_in_dim.18), calls=%async_computation.6 | async-start | bytes 2097152 | tf_op jit(solution)/shard_map/all_to_all | solution.py:46
  258.6 12.3 %collective-permute-start.17 = (f32[32,512]{1,0:T(8,128)S(1)}, f32[32,512]{1,0:T(8,128)S(1)}, u32[]{:S(2)}, u32[]{:S(2)}) collective-permute-start(f32[32,512]{1,0:T(8,128)S(1)} %add.354), channel_id=1, source_target_pairs={{0,256},{64,320},{128,384},{192,448},{256,0},{320,64},{384,128},{4... | collective-permute-start | bytes 196616 | tf_op jit(solution)/shard_map/ppermute | solution.py:36
  270.9 14.9 %collective-permute-start.18 = (f32[32,512]{1,0:T(8,128)S(1)}, f32[32,512]{1,0:T(8,128)S(1)}, u32[]{:S(2)}, u32[]{:S(2)}) collective-permute-start(f32[32,512]{1,0:T(8,128)S(1)} %add.355), channel_id=1, source_target_pairs={{0,4},{4,0},{1,5},{5,1},{2,6},{6,2},{3,7},{7,3},{8,12},{12,8},{9,1... | collective-permute-start | bytes 196616 | tf_op jit(solution)/shard_map/ppermute | solution.py:36
  277.1 34.6 %all-to-all-start.8 = ((bf16[16,128,256]{2,1,0:T(8,128)(2,1)}), bf16[16,128,256]{2,1,0:T(8,128)(2,1)}, u32[]{:S(2)}, u32[]{:S(2)}) async-start(bf16[16,128,256]{2,1,0:T(8,128)(2,1)} %broadcast_in_dim.20), calls=%async_computation.8 | async-start | bytes 2097152 | tf_op jit(solution)/shard_map/all_to_all | solution.py:46
  285.8 11.0 %collective-permute-start.19 = (f32[32,512]{1,0:T(8,128)S(1)}, f32[32,512]{1,0:T(8,128)S(1)}, u32[]{:S(2)}, u32[]{:S(2)}) collective-permute-start(f32[32,512]{1,0:T(8,128)S(1)} %add.356), channel_id=1, source_target_pairs={{0,16},{8,24},{16,0},{24,8},{1,17},{9,25},{17,1},{25,9},{2,18},{10... | collective-permute-start | bytes 196616 | tf_op jit(solution)/shard_map/ppermute | solution.py:36
  296.8 20.6 %collective-permute-start.20 = (f32[64,512]{1,0:T(8,128)S(1)}, f32[64,512]{1,0:T(8,128)}, u32[]{:S(2)}, u32[]{:S(2)}) collective-permute-start(f32[64,512]{1,0:T(8,128)S(1)} %maximum_select_fusion.3), channel_id=1, source_target_pairs={{0,2},{1,3},{2,0},{3,1},{4,6},{5,7},{6,4},{7,5},{8,10},{9,11},{10,... | collective-permute-start | bytes 393224 | tf_op jit(solution)/shard_map/ppermute | solution.py:36
  309.8 21.9 %collective-permute-start.24 = (bf16[8,128,256]{2,0,1:T(8,128)(2,1)}, bf16[8,128,256]{2,0,1:T(8,128)(2,1)}, u32[]{:S(2)}, u32[]{:S(2)}) collective-permute-start(bf16[8,128,256]{2,0,1:T(8,128)(2,1)} %slice.168), channel_id=1, source_target_pairs={{0,32},{32,0},{1,33},{33,1},{2,34},{34,2},{3,35},{35,3},{4,36},{36... | collective-permute-start | bytes 1572872 | tf_op jit(solution)/shard_map/ppermute | solution.py:36
  322.1 12.9 %collective-permute-start.28 = (bf16[8,128,256]{2,1,0:T(8,128)(2,1)S(1)}, bf16[8,128,256]{2,1,0:T(8,128)(2,1)S(1)}, u32[]{:S(2)}, u32[]{:S(2)}) collective-permute-start(bf16[8,128,256]{2,1,0:T(8,128)(2,1)S(1)} %copy.46), channel_id=1, source_target_pairs={{0,32},{32,0},{1,33},{33,1},{2,34},{34,2},{3,35},{35,3},{4,36},{36... | collective-permute-start | bytes 1572872 | tf_op jit(solution)/shard_map/ppermute | solution.py:36
  329.1 22.2 %collective-permute-start.22 = (f32[256,512]{1,0:T(8,128)S(1)}, f32[256,512]{1,0:T(8,128)S(1)}, u32[]{:S(2)}, u32[]{:S(2)}) collective-permute-start(f32[256,512]{1,0:T(8,128)S(1)} %maximum_select_fusion.1), channel_id=1, source_target_pairs={{0,1},{1,0},{2,3},{3,2},{4,5},{5,4},{6,7},{7,6},{8,9},{9,8},{10,11... | collective-permute-start | bytes 1572872 | tf_op jit(solution)/shard_map/ppermute | solution.py:36
  333.0 11.1 %collective-permute-start.25 = (bf16[4,128,256]{2,0,1:T(4,128)(2,1)S(1)}, bf16[4,128,256]{2,0,1:T(4,128)(2,1)S(1)}, u32[]{:S(2)}, u32[]{:S(2)}) collective-permute-start(bf16[4,128,256]{2,0,1:T(4,128)(2,1)S(1)} %slice.170), channel_id=1, source_target_pairs={{0,64},{64,0},{128,192},{192,128},{256,320},{320,256},{384,448},{4... | collective-permute-start | bytes 786440 | tf_op jit(solution)/shard_map/ppermute | solution.py:36
  335.4 13.0 %collective-permute-start.29 = (bf16[4,128,256]{2,1,0:T(8,128)(2,1)S(1)}, bf16[4,128,256]{2,1,0:T(8,128)(2,1)S(1)}, u32[]{:S(2)}, u32[]{:S(2)}) collective-permute-start(bf16[4,128,256]{2,1,0:T(8,128)(2,1)S(1)} %slice.169), channel_id=1, source_target_pairs={{0,64},{64,0},{128,192},{192,128},{256,320},{320,256},{384,448},{4... | collective-permute-start | bytes 786440 | tf_op jit(solution)/shard_map/ppermute | solution.py:36
  348.4 12.3 %collective-permute-start.30 = (bf16[2,128,256]{2,1,0:T(8,128)(2,1)S(1)}, bf16[2,128,256]{2,1,0:T(8,128)(2,1)S(1)}, u32[]{:S(2)}, u32[]{:S(2)}) collective-permute-start(bf16[2,128,256]{2,1,0:T(8,128)(2,1)S(1)} %slice.171), channel_id=1, source_target_pairs={{0,128},{64,192},{128,0},{192,64},{256,384},{320,448},{384,256},{4... | collective-permute-start | bytes 393224 | tf_op jit(solution)/shard_map/ppermute | solution.py:36
  355.6 19.1 %collective-permute-start.27 = (bf16[1,128,256]{2,0,1:T(2,128)(2,1)S(1)}, bf16[1,128,256]{2,0,1:T(2,128)(2,1)S(1)}, u32[]{:S(2)}, u32[]{:S(2)}) collective-permute-start(bf16[1,128,256]{2,0,1:T(2,128)(2,1)S(1)} %slice.174), channel_id=1, source_target_pairs={{0,256},{64,320},{128,384},{192,448},{256,0},{320,64},{384,128},{4... | collective-permute-start | bytes 196616 | tf_op jit(solution)/shard_map/ppermute | solution.py:36
  360.8 14.6 %collective-permute-start.31 = (bf16[1,128,256]{2,1,0:T(8,128)(2,1)S(1)}, bf16[1,128,256]{2,1,0:T(8,128)(2,1)S(1)}, u32[]{:S(2)}, u32[]{:S(2)}) collective-permute-start(bf16[1,128,256]{2,1,0:T(8,128)(2,1)S(1)} %slice.173), channel_id=1, source_target_pairs={{0,256},{64,320},{128,384},{192,448},{256,0},{320,64},{384,128},{4... | collective-permute-start | bytes 196616 | tf_op jit(solution)/shard_map/ppermute | solution.py:36
  (22 other events, 444.6 us)

commit v3 on v1

v3 whole, which is shorter than its diff:
```python
import functools
import math

import jax
import jax.numpy as jnp
from jax import lax
from jax.experimental import pallas as pl
from jax.experimental.pallas import tpu as pltpu
from jax.sharding import Mesh
from jax.sharding import PartitionSpec as P

AXES = ("z4", "z1", "core", "y", "zh", "x")
LINE = ("z4", "z1")
ROW = ("z4", "z1", "core")
PLANE = ("y", "x")
DEPTH = ("z4", "z1", "core", "zh")
CHUNKS = 2
BF16 = jnp.bfloat16
F32 = jnp.float32


def layer_rows(row_total, grad_rows, weight):
    inv_rms = lax.rsqrt(jnp.mean(row_total * row_total, axis=1, keepdims=True) + 1e-06)
    norm_f32 = row_total * inv_rms
    normed = norm_f32.astype(BF16)
    pre_act = jnp.dot(normed, weight, preferred_element_type=F32)
    output = jax.nn.silu(pre_act).astype(BF16)
    sigmoid_pre = jax.nn.sigmoid(pre_act)
    act_slope = sigmoid_pre * (1.0 + pre_act * (1.0 - sigmoid_pre))
    grad_pre = (grad_rows.astype(F32) * act_slope).astype(BF16)
    grad_norm = jnp.einsum("ng,fg->nf", grad_pre, weight, preferred_element_type=F32)
    grad_z = (
        inv_rms * (grad_norm - norm_f32 * jnp.mean(grad_norm * norm_f32, axis=1, keepdims=True))
    ).astype(BF16)
    return (output, normed, grad_pre, grad_z)


def flip(block, axis):
    return lax.ppermute(block, axis, [(0, 1), (1, 0)])


def after(value, *others):
    return lax.optimization_barrier((value,) + others)[0]


def swap_parts(parts, axes):
    return lax.all_to_all(parts, axes, split_axis=0, concat_axis=0, tiled=True)


def copies_of(block, axes):
    return jnp.broadcast_to(block[None], (lax.axis_size(axes),) + block.shape)


def tile_kernel(
    transposed, slots, source, target, count, tiles, scale, first, second, near, far, total
):
    half = first.shape[0]
    near_blocks = near.shape[0]
    total[...] = jnp.zeros_like(total)
    for slot in range(slots):

        @pl.when(slot < count[0])
        def _():
            place = source[slot]
            tile = tiles[slot]

            def add(block):
                if scale is not None:
                    row = jnp.broadcast_to(scale[slot : slot + 1, :], (tile.shape[1], tile.shape[1]))
                    column = jnp.transpose(row)
                    lanes = column.shape[1]
                    block = jnp.concatenate(
                        [
                            (block[:, i : i + lanes].astype(F32) * column).astype(BF16)
                            for i in range(0, block.shape[1], lanes)
                        ],
                        axis=1,
                    )
                axis = 0 if transposed else 1
                total[target[slot]] += lax.dot_general(
                    tile, block, (((axis,), (0,)), ((), ())), preferred_element_type=F32
                )

            @pl.when(place < half)
            def _():
                add(first[jnp.minimum(place, half - 1), : tile.shape[0], :])

            @pl.when(place >= half)
            def _():
                add(second[jnp.maximum(place - half, 0), : tile.shape[0], :])

    near[...] = total[:near_blocks].astype(BF16)
    far[...] = total[near_blocks:].astype(BF16)


def tile_sums(transposed, source, target, count, tiles, scale, first, second, blocks):
    slots, size, _ = tiles.shape
    width = first.shape[2]
    smem = pl.BlockSpec(memory_space=pltpu.SMEM)
    vmem = pl.BlockSpec(memory_space=pltpu.VMEM)
    half = jax.ShapeDtypeStruct((blocks // 2, size, width), BF16)
    operands = [source, target, count, tiles]
    specs = [smem, smem, smem, vmem]
    kernel = functools.partial(tile_kernel, transposed, slots)
    if scale is None:
        body = lambda s, t, c, w, *refs: kernel(s, t, c, w, None, *refs)
    else:
        body = kernel
        operands, specs = operands + [scale], specs + [vmem]
    return pl.pallas_call(
        body,
        out_shape=(half, half),
        in_specs=specs + [vmem, vmem],
        out_specs=(vmem, vmem),
        scratch_shapes=[pltpu.VMEM((blocks, size, width), F32)],
        compiler_params=pltpu.CompilerParams(vmem_limit_bytes=40 * 1024 * 1024),
        cost_estimate=pl.CostEstimate(
            flops=2 * slots * size * size * width,
            bytes_accessed=6 * blocks * size * width,
            transcendentals=0,
        ),
    )(*operands, first, second)


def local(features, weight, cotangent, tile_rows, tile_cols, tile_count, tile_vals):
    span, width = features.shape
    n_z4, n_z1, n_core = lax.axis_size("z4"), lax.axis_size("z1"), lax.axis_size("core")
    n_y, n_zh, n_x = lax.axis_size("y"), lax.axis_size("zh"), lax.axis_size("x")
    n_line = n_z4 * n_z1
    n_row, n_col = n_line * n_core, n_y * n_zh * n_x
    n_plane = n_y * n_x
    my_row = lax.axis_index(ROW)
    my_z1, my_core, my_zh = lax.axis_index("z1"), lax.axis_index("core"), lax.axis_index("zh")
    slots = tile_vals.shape[2]
    nodes = n_row * n_col * span
    chunk = width // CHUNKS
    parts = [slice(c * chunk, (c + 1) * chunk) for c in range(CHUNKS)]
    tiles = tile_vals[0, 0]
    count = tile_count[0]
    row_index = tile_rows[0, 0]
    col_index = tile_cols[0, 0]
    col_core = (col_index & 1) ^ my_core
    col_from = col_core * n_line + (col_index >> 1)
    col_to = col_core * n_line + (((col_index >> 1) & 1) ^ my_z1) * n_z4 + (col_index >> 2)
    row_plane = (row_index >> 3) * n_x + (row_index & 3)
    row_place = (((row_index >> 2) & 1) ^ my_zh) * n_plane + row_plane

    alive = (jnp.arange(slots, dtype=jnp.int32) < count[0]).astype(F32)
    order_cols = (col_index[:, None] == jnp.arange(n_row, dtype=jnp.int32)[None, :]).astype(F32)
    col_sums = jnp.sum(tiles, axis=1, dtype=F32) * alive[:, None]
    degree_terms = jnp.einsum("sc,sj->cj", order_cols, col_sums, precision=lax.Precision.HIGHEST)
    col_degree = 1.0 + lax.psum(degree_terms.reshape(n_row * span), ROW).reshape(n_row, span)
    col_scale = lax.rsqrt(col_degree)
    own_scale = lax.dynamic_index_in_dim(col_scale, my_row, axis=0, keepdims=False)
    slot_scale = col_scale[col_index]
    first_part, second_part = (features[:, part] for part in parts)
    line_blocks = [
        swap_parts(copies_of(part, LINE), LINE)
        for part in (first_part, after(second_part, col_scale))
    ]

    near_terms, far_terms = [], []
    for blocks in line_blocks:
        near, far = tile_sums(
            False, col_from, row_place, count, tiles, slot_scale, blocks, flip(blocks, "core"), n_col
        )
        near_terms.append(near)
        far_terms.append(far)
    far_sums = [
        jnp.sum(swap_parts(terms, PLANE).astype(F32), axis=0).astype(BF16) for terms in far_terms
    ]
    from_far = [flip(total, "zh") for total in far_sums]
    near_terms[0] = after(near_terms[0], far_sums[0])
    near_terms[1] = after(near_terms[1], far_sums[1], from_far[0])
    near_sums = [jnp.sum(swap_parts(terms, PLANE).astype(F32), axis=0) for terms in near_terms]
    own_total = jnp.concatenate(
        [near + far.astype(F32) for near, far in zip(near_sums, from_far)], axis=1
    )

    output, normed, grad_pre, grad_own = layer_rows(own_total, cotangent, weight)

    weight_terms = jnp.einsum("nf,ng->fg", normed, grad_pre, preferred_element_type=F32)
    weight_parts = weight_terms.astype(BF16).reshape(n_plane, width // n_plane, width)
    near_group = swap_parts(
        jnp.concatenate([copies_of(grad_own, PLANE), weight_parts], axis=1), PLANE
    )
    far_group = swap_parts(copies_of(after(flip(grad_own, "zh"), near_group), PLANE), PLANE)

    depth = n_row * n_zh
    plane_sum = jnp.sum(near_group[:, span:].astype(F32), axis=0)
    plane_sum = after(plane_sum, far_group)
    depth_part = swap_parts(plane_sum.reshape(depth, -1, 128), DEPTH)
    depth_sum = jnp.sum(depth_part, axis=0) * (1.0 / math.sqrt(nodes))

    near, far = tile_sums(
        True, row_place, col_to, count, tiles, None, near_group, far_group, n_row
    )
    core_sum = (near.astype(F32) + flip(far, "core").astype(F32)).astype(BF16)
    pair_far = flip(after(core_sum[n_z4:], depth_sum), "z1")
    pair_sum = (core_sum[:n_z4].astype(F32) + pair_far.astype(F32)).astype(BF16)
    depth_sum = after(depth_sum, pair_sum)
    own_grad = lax.psum_scatter(pair_sum, "z4", scatter_dimension=0, tiled=False)
    feature_grad = own_grad.astype(F32) * own_scale[:, None]

    depth_rows = swap_parts(copies_of(depth_sum, DEPTH), DEPTH).reshape(width // n_plane, width)
    weight_grad = swap_parts(copies_of(depth_rows, PLANE), PLANE).reshape(width, width)
    return (output, weight_grad, feature_grad)


def solution(mesh):
    fine = Mesh(mesh.devices.reshape(4, 2, 2, 4, 2, 4), AXES)
    nodes, row, col = P(AXES, None), ROW, ("y", "zh", "x")
    in_specs = (
        nodes,
        P(),
        nodes,
        P(row, col, None),
        P(row, col, None),
        P(row, col),
        P(row, col, None, None, None),
    )
    out_specs = (nodes, P(), nodes)
    return jax.shard_map(local, mesh=fine, in_specs=in_specs, out_specs=out_specs, check_vma=False)
```

time: 402 us -> 359 us (0.89)
  waiting for transfers between devices: 246 us -> 99.7 us
  blocking collectives: 23 us -> 124 us
  starting transfers between devices: 68.3 us -> 87.4 us
  local copies, waits for them, and re-layouts: 20.2 us -> 8.7 us
  matrix products: 13.7 us -> 2.7 us
  Pallas kernels: 0 us -> 8.63 us
    all_to_all x9 -> x8, waiting for transfers between devices: 174 us -> 51.5 us  [swap_parts(): return lax.all_to_all(parts, axes, split_axis=0, concat_axis=0, tiled=True)]
    all_gather x1 -> x0, waiting for transfers between devices: 58 us -> none  [local(): zl_blocks = lax.all_gather(features, 'zl', axis=0, tiled=False)]
    psum x0 -> x1, blocking collectives: none -> 53.3 us  [local(): lax.psum(degree_terms.reshape(n_row * span), ROW).reshape(n_row, span)]
    all_to_all x1 -> x3, blocking collectives: 23 us -> 70.6 us  [swap_parts(): return lax.all_to_all(parts, axes, split_axis=0, concat_axis=0, tiled=True)]
    ppermute x4 -> x7, waiting for transfers between devices: 13.6 us -> 37.7 us  [flip(): return lax.ppermute(block, axis, [(0, 1), (1, 0)])]
    ppermute x4 -> x7, starting transfers between devices: 11.9 us -> 31.8 us  [flip(): return lax.ppermute(block, axis, [(0, 1), (1, 0)])]
    reduce_scatter x0 -> x1, waiting for transfers between devices: none -> 10.5 us  [local(): lax.psum_scatter(pair_sum, 'z4', scatter_dimension=0, tiled=False)]
    dot_general x5 -> x0, matrix products: 10.3 us -> none  [the longest x2 5.25 us: forward_terms(): jnp.einsum('sr,sif->rif', place, products, precision=lax.Precision.HIGHEST)]
  transfers between devices with their start and end apart: 14 -> 16, of which waited for: 11 -> 13; matrix products, arithmetic and copies ran while one was open for 4% -> 2% of each run, Pallas kernels for 0% -> 2%
where the time goes in v3:
time: 359 us; the launch traced here: 355 us
  blocking collectives  124 us (35%)
  waiting for transfers between devices  99.7 us (28%)
  starting transfers between devices  87.4 us (24%)
  between operations  15 us (4%)
  other arithmetic  9.39 us (3%)
  local copies, waits for them, and re-layouts  8.7 us (2%)
  Pallas kernels  8.63 us (2%)
    all_to_all x3, blocking collectives, swap_parts(): return lax.all_to_all(parts, axes, split_axis=0, concat_axis=0, tiled=True)  70.6 us
    all_to_all x8, starting transfers between devices, swap_parts(): return lax.all_to_all(parts, axes, split_axis=0, concat_axis=0, tiled=True)  55.5 us
    psum x1, blocking collectives, local(): lax.psum(degree_terms.reshape(n_row * span), ROW).reshape(n_row, span)  53.3 us
    all_to_all x8, waiting for transfers between devices, swap_parts(): return lax.all_to_all(parts, axes, split_axis=0, concat_axis=0, tiled=True)  51.5 us
    ppermute x7, waiting for transfers between devices, flip(): return lax.ppermute(block, axis, [(0, 1), (1, 0)])  37.7 us
    ppermute x7, starting transfers between devices, flip(): return lax.ppermute(block, axis, [(0, 1), (1, 0)])  31.8 us
    reduce_scatter x1, waiting for transfers between devices, local(): lax.psum_scatter(pair_sum, 'z4', scatter_dimension=0, tiled=False)  10.5 us
    pallas_call x3, Pallas kernels, tile_sums(): pl.pallas_call(body, out_shape=(half, half), in_specs=specs + [vmem, vmem...  8.63 us
  transfers between devices with their start and end apart: 16, of which 13 were waited for; matrix products, arithmetic and copies ran while one was open for 2% of the time, Pallas kernels for 2%

profile of v3, /device:TPU:24, one launch (start us, length us, event | category | flops | bytes accessed | tf_op | source)
XLA Modules:
  0.0 355.4 jit_solution(15386392459042959601)
XLA Ops:
  9.0 12.5 %all-to-all-start = ((bf16[8,128,256]{2,1,0:T(8,128)(2,1)}), bf16[8,128,256]{2,1,0:T(8,128)(2,1)S(1)}, u32[]{:S(2)}, u32[]{:S(2)}) async-start(bf16[8,128,256]{2,1,0:T(8,128)(2,1)} %broadcast_in_dim.14), calls=%async_computation | async-start | bytes 1048576 | tf_op jit(solution)/shard_map/all_to_all | solution.py:47
  24.1 53.3 %psum.7 = f32[2048]{0:T(1024)S(1)} all-reduce(f32[2048]{0:T(1024)S(1)} %convolution_bitcast_fusion), channel_id=1, replica_groups=mesh['z4'=4,'z1'=2,'core'=2,'y'=4,'zh'=2,'x'=4] {'z4','z1','core'}, use_global_device_ids=true, to_apply=%region_1.0 | all-reduce | flops 2048 | bytes 16384 | tf_op jit(solution)/shard_map/psum | solution.py:152
  78.3 3.5 all-to-all-start.3
  81.8 1.9 collective-permute-start
  85.6 3.0 shard_map.94
  88.7 19.7 %all-to-all-done.3.first = bf16[8,128,256]{2,1,0:T(8,128)(2,1)S(1)} async-done(((bf16[8,128,256]{2,1,0:T(8,128)(2,1)}), bf16[8,128,256]{2,1,0:T(8,128)(2,1)S(1)}, u32[]{:S(2)}, u32[]{:S(2)}) %all-to-all-start.3) | async-done | bytes 524320 | tf_op jit(solution)/shard_map/all_to_all | solution.py:47
  108.3 7.2 %all-to-all-start.1 = ((bf16[16,128,256]{2,1,0:T(8,128)(2,1)}), bf16[16,128,256]{2,1,0:T(8,128)(2,1)S(1)}, u32[]{:S(2)}, u32[]{:S(2)}) async-start(bf16[16,128,256]{2,1,0:T(8,128)(2,1)} %get-tuple-element.17), calls=%async_computation.1 | async-start | bytes 2097152 | tf_op jit(solution)/shard_map/all_to_all | solution.py:47
  115.5 1.9 collective-permute-start.2
  119.3 3.0 shard_map.95
  122.3 4.3 %all-to-all-done.1 = bf16[16,128,256]{2,1,0:T(8,128)(2,1)S(1)} async-done(((bf16[16,128,256]{2,1,0:T(8,128)(2,1)}), bf16[16,128,256]{2,1,0:T(8,128)(2,1)S(1)}, u32[]{:S(2)}, u32[]{:S(2)}) %all-to-all-start.1) | async-done | bytes 1048608 | tf_op jit(solution)/shard_map/all_to_all | solution.py:47
  126.5 5.9 %all-to-all-start.4 = ((bf16[16,128,256]{2,1,0:T(8,128)(2,1)}), bf16[16,128,256]{2,1,0:T(8,128)(2,1)S(1)}, u32[]{:S(2)}, u32[]{:S(2)}) async-start(bf16[16,128,256]{2,1,0:T(8,128)(2,1)} %get-tuple-element.21), calls=%async_computation.4 | async-start | bytes 2097152 | tf_op jit(solution)/shard_map/all_to_all | solution.py:47
  132.6 13.0 %all-to-all-done.4 = bf16[16,128,256]{2,1,0:T(8,128)(2,1)S(1)} async-done(((bf16[16,128,256]{2,1,0:T(8,128)(2,1)}), bf16[16,128,256]{2,1,0:T(8,128)(2,1)S(1)}, u32[]{:S(2)}, u32[]{:S(2)}) %all-to-all-start.4) | async-done | bytes 1048608 | tf_op jit(solution)/shard_map/all_to_all | solution.py:47
  146.7 6.1 %all-to-all-start.2 = ((bf16[16,128,256]{2,1,0:T(8,128)(2,1)}), bf16[16,128,256]{2,1,0:T(8,128)(2,1)S(1)}, u32[]{:S(2)}, u32[]{:S(2)}) async-start(bf16[16,128,256]{2,1,0:T(8,128)(2,1)} %get-tuple-element.18), calls=%async_computation.2 | async-start | bytes 2097152 | tf_op jit(solution)/shard_map/all_to_all | solution.py:47
  152.7 8.0 %collective-permute-start.1 = (bf16[128,256]{1,0:T(8,128)(2,1)S(1)}, bf16[128,256]{1,0:T(8,128)(2,1)S(1)}, u32[]{:S(2)}, u32[]{:S(2)}) collective-permute-start(bf16[128,256]{1,0:T(8,128)(2,1)S(1)} %reduce_sum.88), channel_id=1, source_target_pairs={{0,4},{4,0},{1,5},{5,1},{2,6},{6,2},{3,7},{7,3},{8,12},{12,8},{9,1... | collective-permute-start | bytes 196616 | tf_op jit(solution)/shard_map/ppermute | solution.py:39
  162.1 6.2 %collective-permute-done.1 = bf16[128,256]{1,0:T(8,128)(2,1)S(1)} collective-permute-done((bf16[128,256]{1,0:T(8,128)(2,1)S(1)}, bf16[128,256]{1,0:T(8,128)(2,1)S(1)}, u32[]{:S(2)}, u32[]{:S(2)}) %collective-permute-start.1) | collective-permute-done | bytes 65568 | tf_op jit(solution)/shard_map/ppermute | solution.py:39
  168.3 7.2 %all-to-all-start.5 = ((bf16[16,128,256]{2,1,0:T(8,128)(2,1)}), bf16[16,128,256]{2,1,0:T(8,128)(2,1)S(1)}, u32[]{:S(2)}, u32[]{:S(2)}) async-start(bf16[16,128,256]{2,1,0:T(8,128)(2,1)} %get-tuple-element.22), calls=%async_computation.5 | async-start | bytes 2097152 | tf_op jit(solution)/shard_map/all_to_all | solution.py:47
  175.6 7.9 %collective-permute-start.3 = (bf16[128,256]{1,0:T(8,128)(2,1)S(1)}, bf16[128,256]{1,0:T(8,128)(2,1)S(1)}, u32[]{:S(2)}, u32[]{:S(2)}) collective-permute-start(bf16[128,256]{1,0:T(8,128)(2,1)S(1)} %reduce_sum.90), channel_id=1, source_target_pairs={{0,4},{4,0},{1,5},{5,1},{2,6},{6,2},{3,7},{7,3},{8,12},{12,8},{9,1... | collective-permute-start | bytes 196616 | tf_op jit(solution)/shard_map/ppermute | solution.py:39
  183.7 2.9 all-to-all-done.5
  186.8 4.5 %collective-permute-done.3 = bf16[128,256]{1,0:T(8,128)(2,1)S(1)} collective-permute-done((bf16[128,256]{1,0:T(8,128)(2,1)S(1)}, bf16[128,256]{1,0:T(8,128)(2,1)S(1)}, u32[]{:S(2)}, u32[]{:S(2)}) %collective-permute-start.3) | collective-permute-done | bytes 65568 | tf_op jit(solution)/shard_map/ppermute | solution.py:39
  195.3 7.2 %all-to-all-start.6 = ((bf16[16,160,512]{2,1,0:T(8,128)(2,1)}), bf16[16,160,512]{2,1,0:T(8,128)(2,1)S(1)}, u32[]{:S(2)}, u32[]{:S(2)}) async-start(bf16[16,160,512]{2,1,0:T(8,128)(2,1)} %pad_maximum_fusion), calls=%async_computation.6 | async-start | bytes 5242880 | tf_op jit(solution)/shard_map/all_to_all | solution.py:47
  202.6 7.1 %collective-permute-start.4 = (bf16[128,512]{1,0:T(8,128)(2,1)S(1)}, bf16[128,512]{1,0:T(8,128)(2,1)}, u32[]{:S(2)}, u32[]{:S(2)}) collective-permute-start(bf16[128,512]{1,0:T(8,128)(2,1)S(1)} %multiply_convert_fusion), channel_id=1, source_target_pairs={{0,4},{4,0},{1,5},{5,1},{2,6},{6,2},{3,7},{7,3},{8,12},{12,8},{9,1... | collective-permute-start | bytes 393224 | tf_op jit(solution)/shard_map/ppermute | solution.py:39
  209.7 11.9 %collective-permute-done.4 = bf16[128,512]{1,0:T(8,128)(2,1)} collective-permute-done((bf16[128,512]{1,0:T(8,128)(2,1)S(1)}, bf16[128,512]{1,0:T(8,128)(2,1)}, u32[]{:S(2)}, u32[]{:S(2)}) %collective-permute-start.4) | collective-permute-done | bytes 131104 | tf_op jit(solution)/shard_map/ppermute | solution.py:39
  221.6 9.7 %all-to-all-done.6.refs_0_ = bf16[16,160,512]{2,1,0:T(8,128)(2,1)S(1)} async-done(((bf16[16,160,512]{2,1,0:T(8,128)(2,1)}), bf16[16,160,512]{2,1,0:T(8,128)(2,1)S(1)}, u32[]{:S(2)}, u32[]{:S(2)}) %all-to-all-start.6) | async-done | bytes 2621472 | tf_op jit(solution)/shard_map/all_to_all | solution.py:47
  232.4 23.7 %all_to_all.55.refs_1_ = bf16[16,128,512]{2,1,0:T(8,128)(2,1)S(1)} all-to-all(bf16[16,128,512]{2,1,0:T(8,128)(2,1)S(1)} %broadcast_in_dim.17), channel_id=1, replica_groups=mesh['z4'=4,'z1'=2,'core'=2,'y'=4,'zh'=2,'x'=4] {'y','x'}, dimensions={0} | all-to-all | bytes 4194304 | tf_op jit(solution)/shard_map/all_to_all | solution.py:47
  256.1 2.6 shard_map.96
  259.7 1.9 collective-permute-start.5
  261.7 29.8 %all_to_all.56 = f32[32,4,128]{2,1,0:T(4,128)S(1)} all-to-all(f32[32,4,128]{2,1,0:T(4,128)S(1)} %reshape.95), channel_id=1, replica_groups=mesh['z4'=4,'z1'=2,'core'=2,'y'=4,'zh'=2,'x'=4] {'z4','z1','core','zh'}, dimensions={0} | all-to-all | bytes 131072 | tf_op jit(solution)/shard_map/all_to_all | solution.py:47
  293.4 3.0 collective-permute-start.6
  296.5 11.9 %collective-permute-done.6 = bf16[4,128,512]{2,1,0:T(8,128)(2,1)S(1)} collective-permute-done((bf16[4,128,512]{2,1,0:T(8,128)(2,1)S(1)}, bf16[4,128,512]{2,1,0:T(8,128)(2,1)S(1)}, u32[]{:S(2)}, u32[]{:S(2)}) %collective-permute-start.6) | collective-permute-done | bytes 524320 | tf_op jit(solution)/shard_map/ppermute | solution.py:39
  309.4 17.1 %all_to_all.57 = f32[32,4,128]{2,1,0:T(4,128)S(1)} all-to-all(f32[32,4,128]{2,1,0:T(4,128)S(1)} %broadcast_in_dim.18), channel_id=1, replica_groups=mesh['z4'=4,'z1'=2,'core'=2,'y'=4,'zh'=2,'x'=4] {'z4','z1','core','zh'}, dimensions={0} | all-to-all | bytes 131072 | tf_op jit(solution)/shard_map/all_to_all | solution.py:47
  327.6 5.9 %all-to-all-start.10 = ((f32[16,32,512]{2,1,0:T(8,128)}), f32[16,32,512]{2,1,0:T(8,128)S(1)}, u32[]{:S(2)}, u32[]{:S(2)}) async-start(f32[16,32,512]{2,1,0:T(8,128)} %broadcast_in_dim.20), calls=%async_computation.10 | async-start | bytes 2097152 | tf_op jit(solution)/shard_map/all_to_all | solution.py:47
  333.5 10.5 %reduce-scatter.2.cloned.1.call-done = bf16[1,128,512]{2,1,0:T(8,128)(2,1)} async-done(((bf16[4,128,512]{2,1,0:T(8,128)(2,1)}), bf16[1,128,512]{2,1,0:T(8,128)(2,1)}) %reduce-scatter.2.cloned.1.call-update) | async-done | bytes 131088 | tf_op jit(solution)/shard_map/reduce_scatter | solution.py:202
  (63 shorter events, 25.9 us)
Async XLA Ops:
  7.2 184.3 %copy-start = (bf16[512,512]{1,0:T(8,128)(2,1)S(1)}, bf16[512,512]{1,0:T(8,128)(2,1)}, u32[]{:S(2)}) copy-start(bf16[512,512]{1,0:T(8,128)(2,1)} %param.8) | copy-start | bytes 1572868
  7.2 78.4 %copy-start.1 = (bf16[1,1,8,128,128]{4,3,2,1,0:T(8,128)(2,1)S(1)}, bf16[1,1,8,128,128]{4,3,2,1,0:T(8,128)(2,1)}, u32[]{:S(2)}) copy-start(bf16[1,1,8,128,128]{4,3,2,1,0:T(8,128)(2,1)} %param.13) | copy-start | bytes 786436
  7.2 74.6 %copy-start.4 = (s32[1,1,8]{2,1,0:T(1,128)S(1)}, s32[1,1,8]{2,1,0:T(1,128)}, u32[]{:S(2)}) copy-start(s32[1,1,8]{2,1,0:T(1,128)} %param.11) | copy-start | bytes 100
  7.2 77.1 %copy-start.6 = (s32[1,1,8]{2,1,0:T(1,128)S(1)}, s32[1,1,8]{2,1,0:T(1,128)}, u32[]{:S(2)}) copy-start(s32[1,1,8]{2,1,0:T(1,128)} %param.10) | copy-start | bytes 100
  9.0 68.5 %all-to-all-start = ((bf16[8,128,256]{2,1,0:T(8,128)(2,1)}), bf16[8,128,256]{2,1,0:T(8,128)(2,1)S(1)}, u32[]{:S(2)}, u32[]{:S(2)}) async-start(bf16[8,128,256]{2,1,0:T(8,128)(2,1)} %broadcast_in_dim.14), calls=%async_computation | async-start | bytes 1048576 | tf_op jit(solution)/shard_map/all_to_all | solution.py:47
  78.3 30.0 %all-to-all-start.3 = ((bf16[8,128,256]{2,1,0:T(8,128)(2,1)}), bf16[8,128,256]{2,1,0:T(8,128)(2,1)S(1)}, u32[]{:S(2)}, u32[]{:S(2)}) async-start(bf16[8,128,256]{2,1,0:T(8,128)(2,1)} %broadcast_in_dim.15), calls=%async_computation.3 | async-start | bytes 1048576 | tf_op jit(solution)/shard_map/all_to_all | solution.py:47
  81.8 3.8 %collective-permute-start = (bf16[8,128,256]{2,1,0:T(8,128)(2,1)S(1)}, bf16[8,128,256]{2,1,0:T(8,128)(2,1)S(1)}, u32[]{:S(2)}, u32[]{:S(2)}) collective-permute-start(bf16[8,128,256]{2,1,0:T(8,128)(2,1)S(1)} %all-to-all-done.first), channel_id=1, source_target_pairs={{0,32},{32,0},{1,33},{33,1},{2,34},{34,2},{3,35},{35,3},{4,36},{36... | collective-permute-start | bytes 1572872 | tf_op jit(solution)/shard_map/ppermute | solution.py:39
  108.3 18.2 %all-to-all-start.1 = ((bf16[16,128,256]{2,1,0:T(8,128)(2,1)}), bf16[16,128,256]{2,1,0:T(8,128)(2,1)S(1)}, u32[]{:S(2)}, u32[]{:S(2)}) async-start(bf16[16,128,256]{2,1,0:T(8,128)(2,1)} %get-tuple-element.17), calls=%async_computation.1 | async-start | bytes 2097152 | tf_op jit(solution)/shard_map/all_to_all | solution.py:47
  115.5 3.8 %collective-permute-start.2 = (bf16[8,128,256]{2,1,0:T(8,128)(2,1)S(1)}, bf16[8,128,256]{2,1,0:T(8,128)(2,1)S(1)}, u32[]{:S(2)}, u32[]{:S(2)}) collective-permute-start(bf16[8,128,256]{2,1,0:T(8,128)(2,1)S(1)} %all-to-all-done.3.first), channel_id=1, source_target_pairs={{0,32},{32,0},{1,33},{33,1},{2,34},{34,2},{3,35},{35,3},{4,36},{36... | collective-permute-start | bytes 1572872 | tf_op jit(solution)/shard_map/ppermute | solution.py:39
  126.5 19.1 %all-to-all-start.4 = ((bf16[16,128,256]{2,1,0:T(8,128)(2,1)}), bf16[16,128,256]{2,1,0:T(8,128)(2,1)S(1)}, u32[]{:S(2)}, u32[]{:S(2)}) async-start(bf16[16,128,256]{2,1,0:T(8,128)(2,1)} %get-tuple-element.21), calls=%async_computation.4 | async-start | bytes 2097152 | tf_op jit(solution)/shard_map/all_to_all | solution.py:47
  145.6 1.0 copy-start.3
  146.7 21.7 %all-to-all-start.2 = ((bf16[16,128,256]{2,1,0:T(8,128)(2,1)}), bf16[16,128,256]{2,1,0:T(8,128)(2,1)S(1)}, u32[]{:S(2)}, u32[]{:S(2)}) async-start(bf16[16,128,256]{2,1,0:T(8,128)(2,1)} %get-tuple-element.18), calls=%async_computation.2 | async-start | bytes 2097152 | tf_op jit(solution)/shard_map/all_to_all | solution.py:47
  152.7 15.6 %collective-permute-start.1 = (bf16[128,256]{1,0:T(8,128)(2,1)S(1)}, bf16[128,256]{1,0:T(8,128)(2,1)S(1)}, u32[]{:S(2)}, u32[]{:S(2)}) collective-permute-start(bf16[128,256]{1,0:T(8,128)(2,1)S(1)} %reduce_sum.88), channel_id=1, source_target_pairs={{0,4},{4,0},{1,5},{5,1},{2,6},{6,2},{3,7},{7,3},{8,12},{12,8},{9,1... | collective-permute-start | bytes 196616 | tf_op jit(solution)/shard_map/ppermute | solution.py:39
  168.3 18.3 %all-to-all-start.5 = ((bf16[16,128,256]{2,1,0:T(8,128)(2,1)}), bf16[16,128,256]{2,1,0:T(8,128)(2,1)S(1)}, u32[]{:S(2)}, u32[]{:S(2)}) async-start(bf16[16,128,256]{2,1,0:T(8,128)(2,1)} %get-tuple-element.22), calls=%async_computation.5 | async-start | bytes 2097152 | tf_op jit(solution)/shard_map/all_to_all | solution.py:47
  175.6 16.8 %copy-start.5 = (bf16[128,512]{1,0:T(8,128)(2,1)S(1)}, bf16[128,512]{1,0:T(8,128)(2,1)}, u32[]{:S(2)}) copy-start(bf16[128,512]{1,0:T(8,128)(2,1)} %param.9) | copy-start | bytes 393220
  175.6 15.7 %collective-permute-start.3 = (bf16[128,256]{1,0:T(8,128)(2,1)S(1)}, bf16[128,256]{1,0:T(8,128)(2,1)S(1)}, u32[]{:S(2)}, u32[]{:S(2)}) collective-permute-start(bf16[128,256]{1,0:T(8,128)(2,1)S(1)} %reduce_sum.90), channel_id=1, source_target_pairs={{0,4},{4,0},{1,5},{5,1},{2,6},{6,2},{3,7},{7,3},{8,12},{12,8},{9,1... | collective-permute-start | bytes 196616 | tf_op jit(solution)/shard_map/ppermute | solution.py:39
  195.3 36.0 %all-to-all-start.6 = ((bf16[16,160,512]{2,1,0:T(8,128)(2,1)}), bf16[16,160,512]{2,1,0:T(8,128)(2,1)S(1)}, u32[]{:S(2)}, u32[]{:S(2)}) async-start(bf16[16,160,512]{2,1,0:T(8,128)(2,1)} %pad_maximum_fusion), calls=%async_computation.6 | async-start | bytes 5242880 | tf_op jit(solution)/shard_map/all_to_all | solution.py:47
  202.5 141.5 %reduce-scatter.2.cloned.1.call-start = ((), (), s32[]{:S(2)}) async-start(), calls=%async_computation.12 | async-start | bytes 655360 | tf_op jit(solution)/shard_map/reduce_scatter | solution.py:202
  202.6 19.0 %collective-permute-start.4 = (bf16[128,512]{1,0:T(8,128)(2,1)S(1)}, bf16[128,512]{1,0:T(8,128)(2,1)}, u32[]{:S(2)}, u32[]{:S(2)}) collective-permute-start(bf16[128,512]{1,0:T(8,128)(2,1)S(1)} %multiply_convert_fusion), channel_id=1, source_target_pairs={{0,4},{4,0},{1,5},{5,1},{2,6},{6,2},{3,7},{7,3},{8,12},{12,8},{9,1... | collective-permute-start | bytes 393224 | tf_op jit(solution)/shard_map/ppermute | solution.py:39
  258.7 1.0 copy-start.2
  259.7 31.9 %collective-permute-start.5 = (bf16[8,128,512]{2,1,0:T(8,128)(2,1)}, bf16[8,128,512]{2,1,0:T(8,128)(2,1)}, u32[]{:S(2)}, u32[]{:S(2)}) collective-permute-start(bf16[8,128,512]{2,1,0:T(8,128)(2,1)} %get-tuple-element.26), channel_id=1, source_target_pairs={{0,32},{32,0},{1,33},{33,1},{2,34},{34,2},{3,35},{35,3},{4,36},{36... | collective-permute-start | bytes 3145736 | tf_op jit(solution)/shard_map/ppermute | solution.py:39
  293.4 15.0 %collective-permute-start.6 = (bf16[4,128,512]{2,1,0:T(8,128)(2,1)S(1)}, bf16[4,128,512]{2,1,0:T(8,128)(2,1)S(1)}, u32[]{:S(2)}, u32[]{:S(2)}) collective-permute-start(bf16[4,128,512]{2,1,0:T(8,128)(2,1)S(1)} %slice.24), channel_id=1, source_target_pairs={{0,64},{64,0},{1,65},{65,1},{2,66},{66,2},{3,67},{67,3},{4,68},{68... | collective-permute-start | bytes 1572872 | tf_op jit(solution)/shard_map/ppermute | solution.py:39
  327.6 20.0 %all-to-all-start.10 = ((f32[16,32,512]{2,1,0:T(8,128)}), f32[16,32,512]{2,1,0:T(8,128)S(1)}, u32[]{:S(2)}, u32[]{:S(2)}) async-start(f32[16,32,512]{2,1,0:T(8,128)} %broadcast_in_dim.20), calls=%async_computation.10 | async-start | bytes 2097152 | tf_op jit(solution)/shard_map/all_to_all | solution.py:47
Sparse Core Ops, SparseCore 0:
  309.5 34.4 reduce-scatter.1

commit v4 on v3

--- a/solution.py
+++ b/solution.py
@@ -14,7 +14,6 @@
 ROW = ("z4", "z1", "core")
 PLANE = ("y", "x")
 DEPTH = ("z4", "z1", "core", "zh")
-CHUNKS = 2
 BF16 = jnp.bfloat16
 F32 = jnp.float32
 
@@ -133,8 +132,6 @@
     my_z1, my_core, my_zh = lax.axis_index("z1"), lax.axis_index("core"), lax.axis_index("zh")
     slots = tile_vals.shape[2]
     nodes = n_row * n_col * span
-    chunk = width // CHUNKS
-    parts = [slice(c * chunk, (c + 1) * chunk) for c in range(CHUNKS)]
     tiles = tile_vals[0, 0]
     count = tile_count[0]
     row_index = tile_rows[0, 0]
@@ -149,33 +146,29 @@
     order_cols = (col_index[:, None] == jnp.arange(n_row, dtype=jnp.int32)[None, :]).astype(F32)
     col_sums = jnp.sum(tiles, axis=1, dtype=F32) * alive[:, None]
     degree_terms = jnp.einsum("sc,sj->cj", order_cols, col_sums, precision=lax.Precision.HIGHEST)
-    col_degree = 1.0 + lax.psum(degree_terms.reshape(n_row * span), ROW).reshape(n_row, span)
-    col_scale = lax.rsqrt(col_degree)
+    high = lax.reduce_precision(degree_terms, 8, 7)
+    middle = lax.reduce_precision(degree_terms - high, 8, 7)
+    pieces = jnp.stack([high, middle, degree_terms - high - middle]).astype(BF16)
+    pieces = pieces.reshape(-1, width)
+    extra = pieces.shape[0]
+    pieces = jnp.pad(pieces, ((0, -extra % 16), (0, 0)))
+    line_blocks = swap_parts(copies_of(jnp.concatenate([features, pieces]), LINE), LINE)
+    other_blocks = flip(line_blocks, "core")
+
+    def degrees(blocks):
+        terms = blocks[:, span : span + extra].astype(F32)
+        return jnp.sum(terms.reshape(n_line * 3, n_row, span), axis=0)
+
+    col_scale = lax.rsqrt(1.0 + degrees(line_blocks) + degrees(other_blocks))
     own_scale = lax.dynamic_index_in_dim(col_scale, my_row, axis=0, keepdims=False)
     slot_scale = col_scale[col_index]
-    first_part, second_part = (features[:, part] for part in parts)
-    line_blocks = [
-        swap_parts(copies_of(part, LINE), LINE)
-        for part in (first_part, after(second_part, col_scale))
-    ]
-
-    near_terms, far_terms = [], []
-    for blocks in line_blocks:
-        near, far = tile_sums(
-            False, col_from, row_place, count, tiles, slot_scale, blocks, flip(blocks, "core"), n_col
-        )
-        near_terms.append(near)
-        far_terms.append(far)
-    far_sums = [
-        jnp.sum(swap_parts(terms, PLANE).astype(F32), axis=0).astype(BF16) for terms in far_terms
-    ]
-    from_far = [flip(total, "zh") for total in far_sums]
-    near_terms[0] = after(near_terms[0], far_sums[0])
-    near_terms[1] = after(near_terms[1], far_sums[1], from_far[0])
-    near_sums = [jnp.sum(swap_parts(terms, PLANE).astype(F32), axis=0) for terms in near_terms]
-    own_total = jnp.concatenate(
-        [near + far.astype(F32) for near, far in zip(near_sums, from_far)], axis=1
-    )
+
+    near_terms, far_terms = tile_sums(
+        False, col_from, row_place, count, tiles, slot_scale, line_blocks, other_blocks, n_col
+    )
+    far_sum = jnp.sum(swap_parts(far_terms, PLANE).astype(F32), axis=0).astype(BF16)
+    near_group = swap_parts(after(near_terms, far_sum), PLANE)
+    own_total = jnp.sum(near_group.astype(F32), axis=0) + flip(far_sum, "zh").astype(F32)
 
     output, normed, grad_pre, grad_own = layer_rows(own_total, cotangent, weight)
 
@@ -188,7 +181,7 @@
 
     depth = n_row * n_zh
     plane_sum = jnp.sum(near_group[:, span:].astype(F32), axis=0)
-    plane_sum = after(plane_sum, far_group)
+    plane_sum, far_group = lax.optimization_barrier((plane_sum, far_group))
     depth_part = swap_parts(plane_sum.reshape(depth, -1, 128), DEPTH)
     depth_sum = jnp.sum(depth_part, axis=0) * (1.0 / math.sqrt(nodes))
 
@@ -196,7 +189,7 @@
         True, row_place, col_to, count, tiles, None, near_group, far_group, n_row
     )
     core_sum = (near.astype(F32) + flip(far, "core").astype(F32)).astype(BF16)
-    pair_far = flip(after(core_sum[n_z4:], depth_sum), "z1")
+    pair_far = flip(core_sum[n_z4:], "z1")
     pair_sum = (core_sum[:n_z4].astype(F32) + pair_far.astype(F32)).astype(BF16)
     depth_sum = after(depth_sum, pair_sum)
     own_grad = lax.psum_scatter(pair_sum, "z4", scatter_dimension=0, tiled=False)

time: 359 us -> 332 us (0.925)
  starting transfers between devices: 87.4 us -> 50.8 us
  blocking collectives: 124 us -> 143 us
  waiting for transfers between devices: 99.7 us -> 92.9 us
    all_to_all x3 -> x4, blocking collectives: 70.6 us -> 143 us  [swap_parts(): return lax.all_to_all(parts, axes, split_axis=0, concat_axis=0, tiled=True)]
    psum x1 -> x0, blocking collectives: 53.3 us -> none  [local(): lax.psum(degree_terms.reshape(n_row * span), ROW).reshape(n_row, span)]
    all_to_all x8 -> x4, starting transfers between devices: 55.5 us -> 24.6 us  [swap_parts(): return lax.all_to_all(parts, axes, split_axis=0, concat_axis=0, tiled=True)]
    ppermute x7 -> x5, waiting for transfers between devices: 37.7 us -> 18.6 us  [flip(): return lax.ppermute(block, axis, [(0, 1), (1, 0)])]
    all_to_all x8 -> x4, waiting for transfers between devices: 51.5 us -> 65 us  [swap_parts(): return lax.all_to_all(parts, axes, split_axis=0, concat_axis=0, tiled=True)]
    ppermute x7 -> x5, starting transfers between devices: 31.8 us -> 26.2 us  [flip(): return lax.ppermute(block, axis, [(0, 1), (1, 0)])]
    pallas_call x3 -> x2, Pallas kernels: 8.63 us -> 7.31 us  [tile_sums(): pl.pallas_call(body, out_shape=(half, half), in_specs=specs + [vmem, vmem...]
  transfers between devices with their start and end apart: 16 -> 10, of which waited for: 13 -> 8; matrix products, arithmetic and copies ran while one was open for 2% -> 2% of each run, Pallas kernels for 2% -> 0%
where the time goes in v4:
time: 332 us; the launch traced here: 329 us
  blocking collectives  143 us (43%)
  waiting for transfers between devices  92.9 us (28%)
  starting transfers between devices  50.8 us (15%)
  between operations  15.1 us (5%)
  other arithmetic  9.59 us (3%)
  Pallas kernels  7.31 us (2%)
  local copies, waits for them, and re-layouts  6.91 us (2%)
    all_to_all x4, blocking collectives, swap_parts(): return lax.all_to_all(parts, axes, split_axis=0, concat_axis=0, tiled=True)  143 us
    all_to_all x4, waiting for transfers between devices, swap_parts(): return lax.all_to_all(parts, axes, split_axis=0, concat_axis=0, tiled=True)  65 us
    ppermute x5, starting transfers between devices, flip(): return lax.ppermute(block, axis, [(0, 1), (1, 0)])  26.2 us
    all_to_all x4, starting transfers between devices, swap_parts(): return lax.all_to_all(parts, axes, split_axis=0, concat_axis=0, tiled=True)  24.6 us
    ppermute x5, waiting for transfers between devices, flip(): return lax.ppermute(block, axis, [(0, 1), (1, 0)])  18.6 us
    reduce_scatter x1, waiting for transfers between devices, local(): lax.psum_scatter(pair_sum, 'z4', scatter_dimension=0, tiled=False)  9.29 us
    pallas_call x2, Pallas kernels, tile_sums(): pl.pallas_call(body, out_shape=(half, half), in_specs=specs + [vmem, vmem...  7.31 us
  transfers between devices with their start and end apart: 10, of which 8 were waited for; matrix products, arithmetic and copies ran while one was open for 2% of the time, Pallas kernels for 0%

profile of v4, /device:TPU:24, one launch (start us, length us, event | category | flops | bytes accessed | tf_op | source)
XLA Modules:
  0.0 328.7 jit_solution(13794641739867280649)
XLA Ops:
  7.9 1.0 convert_reduce_fusion.2
  8.9 1.0 fusion.4
  11.0 69.3 %all_to_all.40.first = bf16[8,144,512]{2,1,0:T(8,128)(2,1)S(1)} all-to-all(bf16[8,144,512]{2,1,0:T(8,128)(2,1)S(1)} %broadcast_in_dim.12), channel_id=1, replica_groups=mesh['z4'=4,'z1'=2,'core'=2,'y'=4,'zh'=2,'x'=4] {'z4','z1'}, dimensions={0} | all-to-all | bytes 2359296 | tf_op jit(solution)/shard_map/all_to_all | solution.py:46
  80.2 1.9 collective-permute-start
  83.0 1.0 reduce_sum.85
  83.9 1.0 collective-permute-done.second
  85.7 1.0 reduce_sum.86
  87.2 4.1 %shard_map.94 = (bf16[16,128,512]{2,1,0:T(8,128)(2,1)}, bf16[16,128,512]{2,1,0:T(8,128)(2,1)S(1)}) custom-call(s32[8]{0:T(128)S(1)} %get-tuple-element.25.source, s32[8]{0:T(128)S(1)} %add_bitcast_fusion.target.s, s32[1]{0:T(128)} %bitcast.34.count, bf16[8,128,128]{2,1,0:T(8,128)(2,1)S(1)} %bitcast.37, f32[8,128]{1,0:T(8,128)S(1)} %gather_fusion, ...), custom_call_target="tpu_custom_call" | custom-call | flops 134217728 | bytes 12582912 | tf_op jit(solution)/shard_map/pallas_call | solution.py:109
  91.4 33.9 %all_to_all.41 = bf16[16,128,512]{2,1,0:T(8,128)(2,1)S(1)} all-to-all(bf16[16,128,512]{2,1,0:T(8,128)(2,1)S(1)} %get-tuple-element.13), channel_id=1, replica_groups=mesh['z4'=4,'z1'=2,'core'=2,'y'=4,'zh'=2,'x'=4] {'y','x'}, dimensions={0} | all-to-all | bytes 4194304 | tf_op jit(solution)/shard_map/all_to_all | solution.py:46
  125.5 6.0 %all-to-all-start.2 = ((bf16[16,128,512]{2,1,0:T(8,128)(2,1)}), bf16[16,128,512]{2,1,0:T(8,128)(2,1)S(1)}, u32[]{:S(2)}, u32[]{:S(2)}) async-start(bf16[16,128,512]{2,1,0:T(8,128)(2,1)} %get-tuple-element.14), calls=%async_computation.2 | async-start | bytes 4194304 | tf_op jit(solution)/shard_map/all_to_all | solution.py:46
  131.5 7.3 %collective-permute-start.1 = (bf16[128,512]{1,0:T(8,128)(2,1)S(1)}, bf16[128,512]{1,0:T(8,128)(2,1)S(1)}, u32[]{:S(2)}, u32[]{:S(2)}) collective-permute-start(bf16[128,512]{1,0:T(8,128)(2,1)S(1)} %reduce_sum.87), channel_id=1, source_target_pairs={{0,4},{4,0},{1,5},{5,1},{2,6},{6,2},{3,7},{7,3},{8,12},{12,8},{9,1... | collective-permute-start | bytes 393224 | tf_op jit(solution)/shard_map/ppermute | solution.py:38
  138.8 20.4 %all-to-all-done.2 = bf16[16,128,512]{2,1,0:T(8,128)(2,1)S(1)} async-done(((bf16[16,128,512]{2,1,0:T(8,128)(2,1)}), bf16[16,128,512]{2,1,0:T(8,128)(2,1)S(1)}, u32[]{:S(2)}, u32[]{:S(2)}) %all-to-all-start.2) | async-done | bytes 2097184 | tf_op jit(solution)/shard_map/all_to_all | solution.py:46
  161.9 1.7 pad_maximum_fusion
  163.6 5.4 %all-to-all-start.3 = ((bf16[16,160,512]{2,1,0:T(8,128)(2,1)}), bf16[16,160,512]{2,1,0:T(8,128)(2,1)S(1)}, u32[]{:S(2)}, u32[]{:S(2)}) async-start(bf16[16,160,512]{2,1,0:T(8,128)(2,1)} %pad_maximum_fusion), calls=%async_computation.3 | async-start | bytes 5242880 | tf_op jit(solution)/shard_map/all_to_all | solution.py:46
  169.0 7.1 %collective-permute-start.2 = (bf16[128,512]{1,0:T(8,128)(2,1)S(1)}, bf16[128,512]{1,0:T(8,128)(2,1)}, u32[]{:S(2)}, u32[]{:S(2)}) collective-permute-start(bf16[128,512]{1,0:T(8,128)(2,1)S(1)} %multiply_convert_fusion), channel_id=1, source_target_pairs={{0,4},{4,0},{1,5},{5,1},{2,6},{6,2},{3,7},{7,3},{8,12},{12,8},{9,1... | collective-permute-start | bytes 393224 | tf_op jit(solution)/shard_map/ppermute | solution.py:38
  176.1 14.9 %collective-permute-done.2 = bf16[128,512]{1,0:T(8,128)(2,1)} collective-permute-done((bf16[128,512]{1,0:T(8,128)(2,1)S(1)}, bf16[128,512]{1,0:T(8,128)(2,1)}, u32[]{:S(2)}, u32[]{:S(2)}) %collective-permute-start.2) | collective-permute-done | bytes 131104 | tf_op jit(solution)/shard_map/ppermute | solution.py:38
  190.9 14.3 %all-to-all-done.3.refs_0_ = bf16[16,160,512]{2,1,0:T(8,128)(2,1)S(1)} async-done(((bf16[16,160,512]{2,1,0:T(8,128)(2,1)}), bf16[16,160,512]{2,1,0:T(8,128)(2,1)S(1)}, u32[]{:S(2)}, u32[]{:S(2)}) %all-to-all-start.3) | async-done | bytes 2621472 | tf_op jit(solution)/shard_map/all_to_all | solution.py:46
  205.2 2.5 broadcast_in_dim.14
  207.7 5.8 %all-to-all-start.4 = ((bf16[16,128,512]{2,1,0:T(8,128)(2,1)}), bf16[16,128,512]{2,1,0:T(8,128)(2,1)}, u32[]{:S(2)}, u32[]{:S(2)}) async-start(bf16[16,128,512]{2,1,0:T(8,128)(2,1)} %broadcast_in_dim.14), calls=%async_computation.4 | async-start | bytes 4194304 | tf_op jit(solution)/shard_map/all_to_all | solution.py:46
  213.6 26.8 %all-to-all-done.4.refs_1_ = bf16[16,128,512]{2,1,0:T(8,128)(2,1)} async-done(((bf16[16,128,512]{2,1,0:T(8,128)(2,1)}), bf16[16,128,512]{2,1,0:T(8,128)(2,1)}, u32[]{:S(2)}, u32[]{:S(2)}) %all-to-all-start.4) | async-done | bytes 2097184 | tf_op jit(solution)/shard_map/all_to_all | solution.py:46
  240.4 3.2 shard_map.95
  243.6 1.9 collective-permute-start.3
  245.5 2.6 collective-permute-done.3
  248.5 8.0 %collective-permute-start.4 = (bf16[4,128,512]{2,1,0:T(8,128)(2,1)S(1)}, bf16[4,128,512]{2,1,0:T(8,128)(2,1)S(1)}, u32[]{:S(2)}, u32[]{:S(2)}) collective-permute-start(bf16[4,128,512]{2,1,0:T(8,128)(2,1)S(1)} %slice.26), channel_id=1, source_target_pairs={{0,64},{64,0},{1,65},{65,1},{2,66},{66,2},{3,67},{67,3},{4,68},{68... | collective-permute-start | bytes 1572872 | tf_op jit(solution)/shard_map/ppermute | solution.py:38
  256.5 18.3 %all_to_all.42 = f32[32,4,128]{2,1,0:T(4,128)S(1)} all-to-all(f32[32,4,128]{2,1,0:T(4,128)S(1)} %reshape.105), channel_id=1, replica_groups=mesh['z4'=4,'z1'=2,'core'=2,'y'=4,'zh'=2,'x'=4] {'z4','z1','core','zh'}, dimensions={0} | all-to-all | bytes 131072 | tf_op jit(solution)/shard_map/all_to_all | solution.py:46
  275.8 22.0 %all_to_all.43 = f32[32,4,128]{2,1,0:T(4,128)S(1)} all-to-all(f32[32,4,128]{2,1,0:T(4,128)S(1)} %broadcast_in_dim.15), channel_id=1, replica_groups=mesh['z4'=4,'z1'=2,'core'=2,'y'=4,'zh'=2,'x'=4] {'z4','z1','core','zh'}, dimensions={0} | all-to-all | bytes 131072 | tf_op jit(solution)/shard_map/all_to_all | solution.py:46
  297.9 1.1 broadcast_in_dim.17
  299.0 7.4 %all-to-all-start.7 = ((f32[16,32,512]{2,1,0:T(8,128)}), f32[16,32,512]{2,1,0:T(8,128)S(1)}, u32[]{:S(2)}, u32[]{:S(2)}) async-start(f32[16,32,512]{2,1,0:T(8,128)} %broadcast_in_dim.17), calls=%async_computation.7 | async-start | bytes 2097152 | tf_op jit(solution)/shard_map/all_to_all | solution.py:46
  306.3 9.3 %reduce-scatter.2.cloned.1.call-done = bf16[1,128,512]{2,1,0:T(8,128)(2,1)} async-done(((bf16[4,128,512]{2,1,0:T(8,128)(2,1)}), bf16[1,128,512]{2,1,0:T(8,128)(2,1)}) %reduce-scatter.2.cloned.1.call-update) | async-done | bytes 131088 | tf_op jit(solution)/shard_map/reduce_scatter | solution.py:195
  315.6 1.7 convert_multiply_fusion
  317.3 3.5 %all-to-all-done.7 = f32[16,32,512]{2,1,0:T(8,128)S(1)} async-done(((f32[16,32,512]{2,1,0:T(8,128)}), f32[16,32,512]{2,1,0:T(8,128)S(1)}, u32[]{:S(2)}, u32[]{:S(2)}) %all-to-all-start.7) | async-done | bytes 1048608 | tf_op jit(solution)/shard_map/all_to_all | solution.py:46
  320.8 1.0 copy.17
  (50 shorter events, 7.5 us)
Async XLA Ops:
  7.2 152.7 %copy-start = (bf16[512,512]{1,0:T(8,128)(2,1)S(1)}, bf16[512,512]{1,0:T(8,128)(2,1)}, u32[]{:S(2)}) copy-start(bf16[512,512]{1,0:T(8,128)(2,1)} %param.8) | copy-start | bytes 1572868
  8.9 73.3 %copy-start.2 = (s32[1,1,8]{2,1,0:T(1,128)S(1)}, s32[1,1,8]{2,1,0:T(1,128)}, u32[]{:S(2)}) copy-start(s32[1,1,8]{2,1,0:T(1,128)} %param.11) | copy-start | bytes 100
  8.9 73.3 %copy-start.4 = (s32[1,1,8]{2,1,0:T(1,128)S(1)}, s32[1,1,8]{2,1,0:T(1,128)}, u32[]{:S(2)}) copy-start(s32[1,1,8]{2,1,0:T(1,128)} %param.10) | copy-start | bytes 100
  11.0 76.3 %copy-start.1 = (bf16[1,1,8,128,128]{4,3,2,1,0:T(8,128)(2,1)S(1)}, bf16[1,1,8,128,128]{4,3,2,1,0:T(8,128)(2,1)}, u32[]{:S(2)}) copy-start(bf16[1,1,8,128,128]{4,3,2,1,0:T(8,128)(2,1)} %param.13) | copy-start | bytes 786436
  80.2 4.7 %collective-permute-start = (bf16[8,144,512]{2,1,0:T(8,128)(2,1)S(1)}, bf16[8,144,512]{2,1,0:T(8,128)(2,1)S(1)}, u32[]{:S(2)}, u32[]{:S(2)}) collective-permute-start(bf16[8,144,512]{2,1,0:T(8,128)(2,1)S(1)} %all_to_all.40.first), channel_id=1, source_target_pairs={{0,32},{32,0},{1,33},{33,1},{2,34},{34,2},{3,35},{35,3},{4,36},{36... | collective-permute-start | bytes 3538952 | tf_op jit(solution)/shard_map/ppermute | solution.py:38
  125.5 33.8 %all-to-all-start.2 = ((bf16[16,128,512]{2,1,0:T(8,128)(2,1)}), bf16[16,128,512]{2,1,0:T(8,128)(2,1)S(1)}, u32[]{:S(2)}, u32[]{:S(2)}) async-start(bf16[16,128,512]{2,1,0:T(8,128)(2,1)} %get-tuple-element.14), calls=%async_computation.2 | async-start | bytes 4194304 | tf_op jit(solution)/shard_map/all_to_all | solution.py:46
  131.5 29.3 %copy-start.3 = (bf16[128,512]{1,0:T(8,128)(2,1)S(1)}, bf16[128,512]{1,0:T(8,128)(2,1)}, u32[]{:S(2)}) copy-start(bf16[128,512]{1,0:T(8,128)(2,1)} %param.9) | copy-start | bytes 393220
  131.5 28.1 %collective-permute-start.1 = (bf16[128,512]{1,0:T(8,128)(2,1)S(1)}, bf16[128,512]{1,0:T(8,128)(2,1)S(1)}, u32[]{:S(2)}, u32[]{:S(2)}) collective-permute-start(bf16[128,512]{1,0:T(8,128)(2,1)S(1)} %reduce_sum.87), channel_id=1, source_target_pairs={{0,4},{4,0},{1,5},{5,1},{2,6},{6,2},{3,7},{7,3},{8,12},{12,8},{9,1... | collective-permute-start | bytes 393224 | tf_op jit(solution)/shard_map/ppermute | solution.py:38
  163.6 41.6 %all-to-all-start.3 = ((bf16[16,160,512]{2,1,0:T(8,128)(2,1)}), bf16[16,160,512]{2,1,0:T(8,128)(2,1)S(1)}, u32[]{:S(2)}, u32[]{:S(2)}) async-start(bf16[16,160,512]{2,1,0:T(8,128)(2,1)} %pad_maximum_fusion), calls=%async_computation.3 | async-start | bytes 5242880 | tf_op jit(solution)/shard_map/all_to_all | solution.py:46
  169.0 22.0 %collective-permute-start.2 = (bf16[128,512]{1,0:T(8,128)(2,1)S(1)}, bf16[128,512]{1,0:T(8,128)(2,1)}, u32[]{:S(2)}, u32[]{:S(2)}) collective-permute-start(bf16[128,512]{1,0:T(8,128)(2,1)S(1)} %multiply_convert_fusion), channel_id=1, source_target_pairs={{0,4},{4,0},{1,5},{5,1},{2,6},{6,2},{3,7},{7,3},{8,12},{12,8},{9,1... | collective-permute-start | bytes 393224 | tf_op jit(solution)/shard_map/ppermute | solution.py:38
  207.7 32.7 %all-to-all-start.4 = ((bf16[16,128,512]{2,1,0:T(8,128)(2,1)}), bf16[16,128,512]{2,1,0:T(8,128)(2,1)}, u32[]{:S(2)}, u32[]{:S(2)}) async-start(bf16[16,128,512]{2,1,0:T(8,128)(2,1)} %broadcast_in_dim.14), calls=%async_computation.4 | async-start | bytes 4194304 | tf_op jit(solution)/shard_map/all_to_all | solution.py:46
  213.5 102.2 %reduce-scatter.2.cloned.1.call-start = ((), (), s32[]{:S(2)}) async-start(), calls=%async_computation.9 | async-start | bytes 655360 | tf_op jit(solution)/shard_map/reduce_scatter | solution.py:195
  243.6 4.6 %collective-permute-start.3 = (bf16[8,128,512]{2,1,0:T(8,128)(2,1)S(1)}, bf16[8,128,512]{2,1,0:T(8,128)(2,1)S(1)}, u32[]{:S(2)}, u32[]{:S(2)}) collective-permute-start(bf16[8,128,512]{2,1,0:T(8,128)(2,1)S(1)} %get-tuple-element.19), channel_id=1, source_target_pairs={{0,32},{32,0},{1,33},{33,1},{2,34},{34,2},{3,35},{35,3},{4,36},{36... | collective-permute-start | bytes 3145736 | tf_op jit(solution)/shard_map/ppermute | solution.py:38
  248.5 26.4 %collective-permute-start.4 = (bf16[4,128,512]{2,1,0:T(8,128)(2,1)S(1)}, bf16[4,128,512]{2,1,0:T(8,128)(2,1)S(1)}, u32[]{:S(2)}, u32[]{:S(2)}) collective-permute-start(bf16[4,128,512]{2,1,0:T(8,128)(2,1)S(1)} %slice.26), channel_id=1, source_target_pairs={{0,64},{64,0},{1,65},{65,1},{2,66},{66,2},{3,67},{67,3},{4,68},{68... | collective-permute-start | bytes 1572872 | tf_op jit(solution)/shard_map/ppermute | solution.py:38
  299.0 21.9 %all-to-all-start.7 = ((f32[16,32,512]{2,1,0:T(8,128)}), f32[16,32,512]{2,1,0:T(8,128)S(1)}, u32[]{:S(2)}, u32[]{:S(2)}) async-start(f32[16,32,512]{2,1,0:T(8,128)} %broadcast_in_dim.17), calls=%async_computation.7 | async-start | bytes 2097152 | tf_op jit(solution)/shard_map/all_to_all | solution.py:46
Sparse Core Ops, SparseCore 0:
  275.9 39.6 reduce-scatter.1

commit v5 on v4

v5 whole, which is shorter than its diff:
```python
import functools
import math

import jax
import jax.numpy as jnp
from jax import lax
from jax.experimental import pallas as pl
from jax.experimental.pallas import tpu as pltpu
from jax.sharding import Mesh
from jax.sharding import PartitionSpec as P

AXES = ("z4", "z1", "core", "y", "zh", "x")
ROW = ("z4", "z1", "core")
PLANE = ("y", "x")
BF16 = jnp.bfloat16
F32 = jnp.float32


def layer_rows(row_total, grad_rows, weight):
    inv_rms = lax.rsqrt(jnp.mean(row_total * row_total, axis=1, keepdims=True) + 1e-06)
    norm_f32 = row_total * inv_rms
    normed = norm_f32.astype(BF16)
    pre_act = jnp.dot(normed, weight, preferred_element_type=F32)
    output = jax.nn.silu(pre_act).astype(BF16)
    sigmoid_pre = jax.nn.sigmoid(pre_act)
    act_slope = sigmoid_pre * (1.0 + pre_act * (1.0 - sigmoid_pre))
    grad_pre = (grad_rows.astype(F32) * act_slope).astype(BF16)
    grad_norm = jnp.einsum("ng,fg->nf", grad_pre, weight, preferred_element_type=F32)
    grad_z = (
        inv_rms * (grad_norm - norm_f32 * jnp.mean(grad_norm * norm_f32, axis=1, keepdims=True))
    ).astype(BF16)
    return (output, normed, grad_pre, grad_z)


def flip(block, axis):
    return lax.ppermute(block, axis, [(0, 1), (1, 0)])


def after(value, *others):
    return lax.optimization_barrier((value,) + others)[0]


def swap_parts(parts, axes):
    return lax.all_to_all(parts, axes, split_axis=0, concat_axis=0, tiled=True)


def copies_of(block, axes):
    return jnp.broadcast_to(block[None], (lax.axis_size(axes),) + block.shape)


def tile_kernel(transposed, scaled, source, target, count, tiles, *refs):
    scale, refs = (refs[0], refs[1:]) if scaled else (None, refs)
    *groups, near, far, total = refs
    slots, size, _ = tiles.shape
    held, near_blocks = groups[0].shape[0], near.shape[0]
    axis = 0 if transposed else 1
    total[...] = jnp.zeros_like(total)
    for slot in range(slots):

        def add(block):
            if scaled:
                row = jnp.broadcast_to(scale[slot : slot + 1, :], (size, size))
                column = jnp.transpose(row)
                lanes = [block[:, i : i + size] for i in range(0, block.shape[1], size)]
                lanes = [(part.astype(F32) * column).astype(BF16) for part in lanes]
                block = jnp.concatenate(lanes, axis=1)
            total[target[slot]] += lax.dot_general(
                tiles[slot], block, (((axis,), (0,)), ((), ())), preferred_element_type=F32
            )

        for number, group in enumerate(groups):
            inside = source[slot] - number * held

            @pl.when((slot < count[0]) & (inside >= 0) & (inside < held))
            def _(group=group, inside=inside):
                add(group[jnp.clip(inside, 0, held - 1), :size, :])

    near[...] = total[:near_blocks].astype(BF16)
    far[...] = total[near_blocks:].astype(BF16)


def tile_sums(transposed, source, target, count, tiles, scale, groups, blocks):
    slots, size, _ = tiles.shape
    width = groups[0].shape[2]
    smem = pl.BlockSpec(memory_space=pltpu.SMEM)
    vmem = pl.BlockSpec(memory_space=pltpu.VMEM)
    half = jax.ShapeDtypeStruct((blocks // 2, size, width), BF16)
    scaled = scale is not None
    operands = [tiles] + [scale] * scaled + list(groups)
    return pl.pallas_call(
        functools.partial(tile_kernel, transposed, scaled),
        out_shape=(half, half),
        in_specs=[smem] * 3 + [vmem] * len(operands),
        out_specs=(vmem, vmem),
        scratch_shapes=[pltpu.VMEM((blocks, size, width), F32)],
        compiler_params=pltpu.CompilerParams(vmem_limit_bytes=40 * 1024 * 1024),
        cost_estimate=pl.CostEstimate(
            flops=2 * slots * size * size * width,
            bytes_accessed=6 * blocks * size * width,
            transcendentals=0,
        ),
    )(source, target, count, *operands)


def local(features, weight, cotangent, tile_rows, tile_cols, tile_count, tile_vals):
    span, width = features.shape
    n_z4, n_z1, n_core = lax.axis_size("z4"), lax.axis_size("z1"), lax.axis_size("core")
    n_y, n_zh, n_x = lax.axis_size("y"), lax.axis_size("zh"), lax.axis_size("x")
    n_line = n_z4 * n_z1
    n_row, n_col = n_line * n_core, n_y * n_zh * n_x
    n_plane = n_y * n_x
    my_row = lax.axis_index(ROW)
    my_z1, my_core, my_zh = lax.axis_index("z1"), lax.axis_index("core"), lax.axis_index("zh")
    slots = tile_vals.shape[2]
    nodes = n_row * n_col * span
    tiles = tile_vals[0, 0]
    count = tile_count[0]
    row_index = tile_rows[0, 0]
    col_index = tile_cols[0, 0]
    col_core = (col_index & 1) ^ my_core
    col_place = col_core * n_line + (((col_index >> 1) & 1) ^ my_z1) * n_z4 + (col_index >> 2)
    row_plane = (row_index >> 3) * n_x + (row_index & 3)
    row_place = (((row_index >> 2) & 1) ^ my_zh) * n_plane + row_plane

    alive = (jnp.arange(slots, dtype=jnp.int32) < count[0]).astype(F32)
    order_cols = (col_index[:, None] == jnp.arange(n_row, dtype=jnp.int32)[None, :]).astype(F32)
    col_sums = jnp.sum(tiles, axis=1, dtype=F32) * alive[:, None]
    degree_terms = jnp.einsum("sc,sj->cj", order_cols, col_sums, precision=lax.Precision.HIGHEST)
    high = lax.reduce_precision(degree_terms, 8, 7)
    middle = lax.reduce_precision(degree_terms - high, 8, 7)
    pieces = jnp.stack([high, middle, degree_terms - high - middle]).astype(BF16)
    pieces = pieces.reshape(-1, width)
    extra = pieces.shape[0]
    pieces = jnp.pad(pieces, ((0, -extra % 16), (0, 0)))
    own_line = swap_parts(copies_of(jnp.concatenate([features, pieces]), "z4"), "z4")
    own_pair = flip(own_line, "z1")
    blocks = [own_line, own_pair, flip(own_line, "core"), flip(own_pair, "core")]

    def degrees(part):
        terms = part[:, span : span + extra].astype(F32)
        return jnp.sum(terms.reshape(n_z4 * 3, n_row, span), axis=0)

    col_scale = lax.rsqrt(1.0 + sum(degrees(part) for part in blocks))
    own_scale = lax.dynamic_index_in_dim(col_scale, my_row, axis=0, keepdims=False)
    slot_scale = col_scale[col_index]

    near_terms, far_terms = tile_sums(
        False, col_place, row_place, count, tiles, slot_scale, blocks, n_col
    )
    far_sum = jnp.sum(swap_parts(far_terms, PLANE).astype(F32), axis=0).astype(BF16)
    near_group = swap_parts(after(near_terms, far_sum), PLANE)
    own_total = jnp.sum(near_group.astype(F32), axis=0) + flip(far_sum, "zh").astype(F32)

    output, normed, grad_pre, grad_own = layer_rows(own_total, cotangent, weight)

    weight_terms = jnp.einsum("nf,ng->fg", normed, grad_pre, preferred_element_type=F32)
    weight_parts = weight_terms.astype(BF16).reshape(n_plane, width // n_plane, width)
    near_group = swap_parts(
        jnp.concatenate([copies_of(grad_own, PLANE), weight_parts], axis=1), PLANE
    )
    far_group = swap_parts(copies_of(after(flip(grad_own, "zh"), near_group), PLANE), PLANE)

    plane_sum = jnp.sum(near_group[:, span:].astype(F32), axis=0)
    for axis in ("core", "z1", "zh"):
        plane_sum = plane_sum + flip(plane_sum, axis)
    far_group = after(far_group, plane_sum)
    line_part = swap_parts(plane_sum.reshape(n_z4, -1, width), "z4")
    line_sum = jnp.sum(line_part, axis=0) * (1.0 / math.sqrt(nodes))

    near, far = tile_sums(
        True, row_place, col_place, count, tiles, None, [near_group, far_group], n_row
    )
    core_sum = (near.astype(F32) + flip(far, "core").astype(F32)).astype(BF16)
    pair_far = flip(core_sum[n_z4:], "z1")
    pair_sum = (core_sum[:n_z4].astype(F32) + pair_far.astype(F32)).astype(BF16)
    line_sum = after(line_sum, pair_sum)
    own_grad = lax.psum_scatter(pair_sum, "z4", scatter_dimension=0, tiled=False)
    feature_grad = own_grad.astype(F32) * own_scale[:, None]

    plane_rows = swap_parts(copies_of(line_sum, "z4"), "z4").reshape(-1, width)
    weight_grad = swap_parts(copies_of(plane_rows, PLANE), PLANE).reshape(width, width)
    return (output, weight_grad, feature_grad)


def solution(mesh):
    fine = Mesh(mesh.devices.reshape(4, 2, 2, 4, 2, 4), AXES)
    nodes, row, col = P(AXES, None), ROW, ("y", "zh", "x")
    in_specs = (
        nodes,
        P(),
        nodes,
        P(row, col, None),
        P(row, col, None),
        P(row, col),
        P(row, col, None, None, None),
    )
    out_specs = (nodes, P(), nodes)
    return jax.shard_map(local, mesh=fine, in_specs=in_specs, out_specs=out_specs, check_vma=False)
```

time: 332 us -> 310 us (0.934)
  blocking collectives: 143 us -> 107 us
  starting transfers between devices: 50.8 us -> 68.5 us
    all_to_all x4, blocking collectives: 143 us -> 107 us  [swap_parts(): return lax.all_to_all(parts, axes, split_axis=0, concat_axis=0, tiled=True)]
    all_to_all x4, waiting for transfers between devices: 65 us -> 37.9 us  [swap_parts(): return lax.all_to_all(parts, axes, split_axis=0, concat_axis=0, tiled=True)]
    ppermute x5 -> x10, waiting for transfers between devices: 18.6 us -> 38.4 us  [flip(): return lax.ppermute(block, axis, [(0, 1), (1, 0)])]
    ppermute x5 -> x10, starting transfers between devices: 26.2 us -> 45.4 us  [flip(): return lax.ppermute(block, axis, [(0, 1), (1, 0)])]
    reduce_scatter x1, waiting for transfers between devices: 9.29 us -> 18.5 us  [local(): lax.psum_scatter(pair_sum, 'z4', scatter_dimension=0, tiled=False)]
  transfers between devices with their start and end apart: 10 -> 15, of which waited for: 8 -> 11; matrix products, arithmetic and copies ran while one was open for 2% -> 1% of each run, Pallas kernels for 0% -> 0%
where the time goes in v5:
time: 310 us; the launch traced here: 309 us
  blocking collectives  107 us (35%)
  waiting for transfers between devices  94.8 us (31%)
  starting transfers between devices  68.5 us (22%)
  between operations  15.2 us (5%)
  Pallas kernels  7.94 us (3%)
  other arithmetic  7.8 us (3%)
  local copies, waits for them, and re-layouts  5.47 us (2%)
    all_to_all x4, blocking collectives, swap_parts(): return lax.all_to_all(parts, axes, split_axis=0, concat_axis=0, tiled=True)  107 us
    ppermute x10, starting transfers between devices, flip(): return lax.ppermute(block, axis, [(0, 1), (1, 0)])  45.4 us
    ppermute x10, waiting for transfers between devices, flip(): return lax.ppermute(block, axis, [(0, 1), (1, 0)])  38.4 us
    all_to_all x4, waiting for transfers between devices, swap_parts(): return lax.all_to_all(parts, axes, split_axis=0, concat_axis=0, tiled=True)  37.9 us
    all_to_all x4, starting transfers between devices, swap_parts(): return lax.all_to_all(parts, axes, split_axis=0, concat_axis=0, tiled=True)  23.1 us
    reduce_scatter x1, waiting for transfers between devices, local(): lax.psum_scatter(pair_sum, 'z4', scatter_dimension=0, tiled=False)  18.5 us
    pallas_call x2, Pallas kernels, tile_sums(): pl.pallas_call(functools.partial(tile_kernel, transposed, scaled), out_sh...  7.94 us
  transfers between devices with their start and end apart: 15, of which 11 were waited for; matrix products, arithmetic and copies ran while one was open for 1% of the time, Pallas kernels for 0%

profile of v5, /device:TPU:24, one launch (start us, length us, event | category | flops | bytes accessed | tf_op | source)
XLA Modules:
  0.0 309.1 jit_solution(12552642800683422524)
XLA Ops:
  10.9 42.6 %all_to_all.40.refs_1_ = bf16[4,144,512]{2,1,0:T(8,128)(2,1)S(1)} all-to-all(bf16[4,144,512]{2,1,0:T(8,128)(2,1)S(1)} %broadcast_in_dim.12), channel_id=1, replica_groups=mesh['z4'=4,'z1'=2,'core'=2,'y'=4,'zh'=2,'x'=4] {'z4'}, dimensions={0} | all-to-all | bytes 1179648 | tf_op jit(solution)/shard_map/all_to_all | solution.py:44
  53.5 1.9 collective-permute-start
  55.5 1.9 collective-permute-start.1
  57.4 11.5 %collective-permute-done.refs_2_ = bf16[4,144,512]{2,1,0:T(8,128)(2,1)S(1)} collective-permute-done((bf16[4,144,512]{2,1,0:T(8,128)(2,1)S(1)}, bf16[4,144,512]{2,1,0:T(8,128)(2,1)S(1)}, u32[]{:S(2)}, u32[]{:S(2)}) %collective-permute-start) | collective-permute-done | bytes 589856 | tf_op jit(solution)/shard_map/ppermute | solution.py:36
  69.0 1.9 collective-permute-start.2
  71.1 1.8 collective-permute-done.2.refs_4_
  73.5 4.5 %shard_map.94 = (bf16[16,128,512]{2,1,0:T(8,128)(2,1)}, bf16[16,128,512]{2,1,0:T(8,128)(2,1)S(1)}) custom-call(s32[8]{0:T(128)S(1)} %shift-right-arithmetic_add_fusion.source.target, s32[8]{0:T(128)S(1)} %add_bitcast_fusion.target.source, s32[1]{0:T(128)} %bitcast.31.count, bf16[8,128,128]{2,1,0:T(8,128)(2,1)S(1)} %bitcast.34, f32[8,128]{1,0:T(8,128)S(1)} %gather_fusion, ...), custom_call_target="tpu_custom_call" | custom-call | flops 134217728 | bytes 12582912 | tf_op jit(solution)/shard_map/pallas_call | solution.py:90
  78.0 33.6 %all_to_all.41 = bf16[16,128,512]{2,1,0:T(8,128)(2,1)S(1)} all-to-all(bf16[16,128,512]{2,1,0:T(8,128)(2,1)S(1)} %get-tuple-element.12), channel_id=1, replica_groups=mesh['z4'=4,'z1'=2,'core'=2,'y'=4,'zh'=2,'x'=4] {'y','x'}, dimensions={0} | all-to-all | bytes 4194304 | tf_op jit(solution)/shard_map/all_to_all | solution.py:44
  111.9 6.0 %all-to-all-start.2 = ((bf16[16,128,512]{2,1,0:T(8,128)(2,1)}), bf16[16,128,512]{2,1,0:T(8,128)(2,1)S(1)}, u32[]{:S(2)}, u32[]{:S(2)}) async-start(bf16[16,128,512]{2,1,0:T(8,128)(2,1)} %get-tuple-element.13), calls=%async_computation.2 | async-start | bytes 4194304 | tf_op jit(solution)/shard_map/all_to_all | solution.py:44
  117.9 10.2 %collective-permute-start.3 = (bf16[128,512]{1,0:T(8,128)(2,1)S(1)}, bf16[128,512]{1,0:T(8,128)(2,1)S(1)}, u32[]{:S(2)}, u32[]{:S(2)}) collective-permute-start(bf16[128,512]{1,0:T(8,128)(2,1)S(1)} %reduce_sum.107), channel_id=1, source_target_pairs={{0,4},{4,0},{1,5},{5,1},{2,6},{6,2},{3,7},{7,3},{8,12},{12,8},{9,1... | collective-permute-start | bytes 393224 | tf_op jit(solution)/shard_map/ppermute | solution.py:36
  128.1 18.6 %all-to-all-done.2 = bf16[16,128,512]{2,1,0:T(8,128)(2,1)S(1)} async-done(((bf16[16,128,512]{2,1,0:T(8,128)(2,1)}), bf16[16,128,512]{2,1,0:T(8,128)(2,1)S(1)}, u32[]{:S(2)}, u32[]{:S(2)}) %all-to-all-start.2) | async-done | bytes 2097184 | tf_op jit(solution)/shard_map/all_to_all | solution.py:44
  149.4 1.7 pad_maximum_fusion
  151.1 5.2 %all-to-all-start.3 = ((bf16[16,160,512]{2,1,0:T(8,128)(2,1)}), bf16[16,160,512]{2,1,0:T(8,128)(2,1)S(1)}, u32[]{:S(2)}, u32[]{:S(2)}) async-start(bf16[16,160,512]{2,1,0:T(8,128)(2,1)} %pad_maximum_fusion), calls=%async_computation.3 | async-start | bytes 5242880 | tf_op jit(solution)/shard_map/all_to_all | solution.py:44
  156.3 9.6 %collective-permute-start.7 = (bf16[128,512]{1,0:T(8,128)(2,1)S(1)}, bf16[128,512]{1,0:T(8,128)(2,1)}, u32[]{:S(2)}, u32[]{:S(2)}) collective-permute-start(bf16[128,512]{1,0:T(8,128)(2,1)S(1)} %multiply_convert_fusion), channel_id=1, source_target_pairs={{0,4},{4,0},{1,5},{5,1},{2,6},{6,2},{3,7},{7,3},{8,12},{12,8},{9,1... | collective-permute-start | bytes 393224 | tf_op jit(solution)/shard_map/ppermute | solution.py:36
  165.9 8.4 %collective-permute-done.7 = bf16[128,512]{1,0:T(8,128)(2,1)} collective-permute-done((bf16[128,512]{1,0:T(8,128)(2,1)S(1)}, bf16[128,512]{1,0:T(8,128)(2,1)}, u32[]{:S(2)}, u32[]{:S(2)}) %collective-permute-start.7) | collective-permute-done | bytes 131104 | tf_op jit(solution)/shard_map/ppermute | solution.py:36
  174.4 19.3 %all-to-all-done.3.refs_0_ = bf16[16,160,512]{2,1,0:T(8,128)(2,1)S(1)} async-done(((bf16[16,160,512]{2,1,0:T(8,128)(2,1)}), bf16[16,160,512]{2,1,0:T(8,128)(2,1)S(1)}, u32[]{:S(2)}, u32[]{:S(2)}) %all-to-all-start.3) | async-done | bytes 2621472 | tf_op jit(solution)/shard_map/all_to_all | solution.py:44
  193.6 2.5 broadcast_in_dim.14
  196.1 5.6 %all-to-all-start.5 = ((bf16[16,128,512]{2,1,0:T(8,128)(2,1)}), bf16[16,128,512]{2,1,0:T(8,128)(2,1)}, u32[]{:S(2)}, u32[]{:S(2)}) async-start(bf16[16,128,512]{2,1,0:T(8,128)(2,1)} %broadcast_in_dim.14), calls=%async_computation.5 | async-start | bytes 4194304 | tf_op jit(solution)/shard_map/all_to_all | solution.py:44
  201.8 1.9 collective-permute-start.4
  205.0 5.6 %collective-permute-start.5 = (f32[32,512]{1,0:T(8,128)S(1)}, f32[32,512]{1,0:T(8,128)S(1)}, u32[]{:S(2)}, u32[]{:S(2)}) collective-permute-start(f32[32,512]{1,0:T(8,128)S(1)} %add.107), channel_id=1, source_target_pairs={{0,64},{64,0},{1,65},{65,1},{2,66},{66,2},{3,67},{67,3},{4,68},{68... | collective-permute-start | bytes 196616 | tf_op jit(solution)/shard_map/ppermute | solution.py:36
  210.6 2.4 collective-permute-done.5
  213.0 6.8 %collective-permute-start.6 = (f32[32,512]{1,0:T(8,128)S(1)}, f32[32,512]{1,0:T(8,128)S(1)}, u32[]{:S(2)}, u32[]{:S(2)}) collective-permute-start(f32[32,512]{1,0:T(8,128)S(1)} %add.108), channel_id=1, source_target_pairs={{0,4},{4,0},{1,5},{5,1},{2,6},{6,2},{3,7},{7,3},{8,12},{12,8},{9,1... | collective-permute-start | bytes 196616 | tf_op jit(solution)/shard_map/ppermute | solution.py:36
  219.8 9.7 %collective-permute-done.6 = f32[32,512]{1,0:T(8,128)S(1)} collective-permute-done((f32[32,512]{1,0:T(8,128)S(1)}, f32[32,512]{1,0:T(8,128)S(1)}, u32[]{:S(2)}, u32[]{:S(2)}) %collective-permute-start.6) | collective-permute-done | bytes 65568 | tf_op jit(solution)/shard_map/ppermute | solution.py:36
  229.5 3.4 %shard_map.95 = (bf16[8,128,512]{2,1,0:T(8,128)(2,1)S(1)}, bf16[8,128,512]{2,1,0:T(8,128)(2,1)S(1)}) custom-call(s32[8]{0:T(128)S(1)} %add_bitcast_fusion.target.source, s32[8]{0:T(128)S(1)} %shift-right-arithmetic_add_fusion.source.target, s32[1]{0:T(128)} %bitcast.32.count, bf16[8,128,128]{2,1,0:T(8,128)(2,1)S(1)} %bitcast.35, ...), custom_call_target="tpu_custom_call" | custom-call | flops 134217728 | bytes 6291456 | tf_op jit(solution)/shard_map/pallas_call | solution.py:90
  232.9 1.9 collective-permute-start.8
  234.8 2.6 collective-permute-done.8
  237.8 3.7 %collective-permute-start.9 = (bf16[4,128,512]{2,1,0:T(8,128)(2,1)S(1)}, bf16[4,128,512]{2,1,0:T(8,128)(2,1)S(1)}, u32[]{:S(2)}, u32[]{:S(2)}) collective-permute-start(bf16[4,128,512]{2,1,0:T(8,128)(2,1)S(1)} %slice.36), channel_id=1, source_target_pairs={{0,64},{64,0},{1,65},{65,1},{2,66},{66,2},{3,67},{67,3},{4,68},{68... | collective-permute-start | bytes 1572872 | tf_op jit(solution)/shard_map/ppermute | solution.py:36
  241.4 12.5 %all_to_all.42 = f32[4,8,512]{2,1,0:T(8,128)S(1)} all-to-all(f32[4,8,512]{2,1,0:T(8,128)S(1)} %bitcast.38), channel_id=1, replica_groups=mesh['z4'=4,'z1'=2,'core'=2,'y'=4,'zh'=2,'x'=4] {'z4'}, dimensions={0} | all-to-all | bytes 131072 | tf_op jit(solution)/shard_map/all_to_all | solution.py:44
  255.7 18.0 %all_to_all.43 = f32[4,8,512]{2,1,0:T(8,128)S(1)} all-to-all(f32[4,8,512]{2,1,0:T(8,128)S(1)} %broadcast_in_dim.15), channel_id=1, replica_groups=mesh['z4'=4,'z1'=2,'core'=2,'y'=4,'zh'=2,'x'=4] {'z4'}, dimensions={0} | all-to-all | bytes 131072 | tf_op jit(solution)/shard_map/all_to_all | solution.py:44
  274.8 6.3 %all-to-all-start.7 = ((f32[16,32,512]{2,1,0:T(8,128)}), f32[16,32,512]{2,1,0:T(8,128)S(1)}, u32[]{:S(2)}, u32[]{:S(2)}) async-start(f32[16,32,512]{2,1,0:T(8,128)} %broadcast_in_dim.17), calls=%async_computation.7 | async-start | bytes 2097152 | tf_op jit(solution)/shard_map/all_to_all | solution.py:44
  281.1 18.5 %reduce-scatter.2.cloned.1.call-done = bf16[1,128,512]{2,1,0:T(8,128)(2,1)} async-done(((bf16[4,128,512]{2,1,0:T(8,128)(2,1)}), bf16[1,128,512]{2,1,0:T(8,128)(2,1)}) %reduce-scatter.2.cloned.1.call-update) | async-done | bytes 131088 | tf_op jit(solution)/shard_map/reduce_scatter | solution.py:177
  299.6 1.7 convert_multiply_fusion
  (67 shorter events, 12.0 us)
Async XLA Ops:
  7.2 140.1 %copy-start = (bf16[512,512]{1,0:T(8,128)(2,1)S(1)}, bf16[512,512]{1,0:T(8,128)(2,1)}, u32[]{:S(2)}) copy-start(bf16[512,512]{1,0:T(8,128)(2,1)} %param.8) | copy-start | bytes 1572868
  7.2 48.2 %copy-start.2 = (s32[1,1,8]{2,1,0:T(1,128)S(1)}, s32[1,1,8]{2,1,0:T(1,128)}, u32[]{:S(2)}) copy-start(s32[1,1,8]{2,1,0:T(1,128)} %param.11) | copy-start | bytes 100
  7.2 50.2 %copy-start.4 = (s32[1,1,8]{2,1,0:T(1,128)S(1)}, s32[1,1,8]{2,1,0:T(1,128)}, u32[]{:S(2)}) copy-start(s32[1,1,8]{2,1,0:T(1,128)} %param.10) | copy-start | bytes 100
  10.8 62.7 %copy-start.1 = (bf16[1,1,8,128,128]{4,3,2,1,0:T(8,128)(2,1)S(1)}, bf16[1,1,8,128,128]{4,3,2,1,0:T(8,128)(2,1)}, u32[]{:S(2)}) copy-start(bf16[1,1,8,128,128]{4,3,2,1,0:T(8,128)(2,1)} %param.13) | copy-start | bytes 786436
  53.5 15.5 %collective-permute-start = (bf16[4,144,512]{2,1,0:T(8,128)(2,1)S(1)}, bf16[4,144,512]{2,1,0:T(8,128)(2,1)S(1)}, u32[]{:S(2)}, u32[]{:S(2)}) collective-permute-start(bf16[4,144,512]{2,1,0:T(8,128)(2,1)S(1)} %all_to_all.40.refs_1_), channel_id=1, source_target_pairs={{0,64},{64,0},{1,65},{65,1},{2,66},{66,2},{3,67},{67,3},{4,68},{68... | collective-permute-start | bytes 1769480 | tf_op jit(solution)/shard_map/ppermute | solution.py:36
  55.5 15.6 %collective-permute-start.1 = (bf16[4,144,512]{2,1,0:T(8,128)(2,1)S(1)}, bf16[4,144,512]{2,1,0:T(8,128)(2,1)S(1)}, u32[]{:S(2)}, u32[]{:S(2)}) collective-permute-start(bf16[4,144,512]{2,1,0:T(8,128)(2,1)S(1)} %all_to_all.40.refs_1_), channel_id=1, source_target_pairs={{0,32},{32,0},{1,33},{33,1},{2,34},{34,2},{3,35},{35,3},{4,36},{36... | collective-permute-start | bytes 1769480 | tf_op jit(solution)/shard_map/ppermute | solution.py:36
  69.0 3.9 %collective-permute-start.2 = (bf16[4,144,512]{2,1,0:T(8,128)(2,1)S(1)}, bf16[4,144,512]{2,1,0:T(8,128)(2,1)S(1)}, u32[]{:S(2)}, u32[]{:S(2)}) collective-permute-start(bf16[4,144,512]{2,1,0:T(8,128)(2,1)S(1)} %collective-permute-done.refs_2_), channel_id=1, source_target_pairs={{0,32},{32,0},{1,33},{33,1},{2,34},{34,2},{3,35},{35,3},{4,36},{36... | collective-permute-start | bytes 1769480 | tf_op jit(solution)/shard_map/ppermute | solution.py:36
  111.9 34.8 %all-to-all-start.2 = ((bf16[16,128,512]{2,1,0:T(8,128)(2,1)}), bf16[16,128,512]{2,1,0:T(8,128)(2,1)S(1)}, u32[]{:S(2)}, u32[]{:S(2)}) async-start(bf16[16,128,512]{2,1,0:T(8,128)(2,1)} %get-tuple-element.13), calls=%async_computation.2 | async-start | bytes 4194304 | tf_op jit(solution)/shard_map/all_to_all | solution.py:44
  117.9 30.3 %copy-start.3 = (bf16[128,512]{1,0:T(8,128)(2,1)S(1)}, bf16[128,512]{1,0:T(8,128)(2,1)}, u32[]{:S(2)}) copy-start(bf16[128,512]{1,0:T(8,128)(2,1)} %param.9) | copy-start | bytes 393220
  117.9 29.1 %collective-permute-start.3 = (bf16[128,512]{1,0:T(8,128)(2,1)S(1)}, bf16[128,512]{1,0:T(8,128)(2,1)S(1)}, u32[]{:S(2)}, u32[]{:S(2)}) collective-permute-start(bf16[128,512]{1,0:T(8,128)(2,1)S(1)} %reduce_sum.107), channel_id=1, source_target_pairs={{0,4},{4,0},{1,5},{5,1},{2,6},{6,2},{3,7},{7,3},{8,12},{12,8},{9,1... | collective-permute-start | bytes 393224 | tf_op jit(solution)/shard_map/ppermute | solution.py:36
  151.1 42.5 %all-to-all-start.3 = ((bf16[16,160,512]{2,1,0:T(8,128)(2,1)}), bf16[16,160,512]{2,1,0:T(8,128)(2,1)S(1)}, u32[]{:S(2)}, u32[]{:S(2)}) async-start(bf16[16,160,512]{2,1,0:T(8,128)(2,1)} %pad_maximum_fusion), calls=%async_computation.3 | async-start | bytes 5242880 | tf_op jit(solution)/shard_map/all_to_all | solution.py:44
  156.3 18.0 %collective-permute-start.7 = (bf16[128,512]{1,0:T(8,128)(2,1)S(1)}, bf16[128,512]{1,0:T(8,128)(2,1)}, u32[]{:S(2)}, u32[]{:S(2)}) collective-permute-start(bf16[128,512]{1,0:T(8,128)(2,1)S(1)} %multiply_convert_fusion), channel_id=1, source_target_pairs={{0,4},{4,0},{1,5},{5,1},{2,6},{6,2},{3,7},{7,3},{8,12},{12,8},{9,1... | collective-permute-start | bytes 393224 | tf_op jit(solution)/shard_map/ppermute | solution.py:36
  196.1 33.4 %all-to-all-start.5 = ((bf16[16,128,512]{2,1,0:T(8,128)(2,1)}), bf16[16,128,512]{2,1,0:T(8,128)(2,1)}, u32[]{:S(2)}, u32[]{:S(2)}) async-start(bf16[16,128,512]{2,1,0:T(8,128)(2,1)} %broadcast_in_dim.14), calls=%async_computation.5 | async-start | bytes 4194304 | tf_op jit(solution)/shard_map/all_to_all | solution.py:44
  201.7 97.9 %reduce-scatter.2.cloned.1.call-start = ((), (), s32[]{:S(2)}) async-start(), calls=%async_computation.9 | async-start | bytes 655360 | tf_op jit(solution)/shard_map/reduce_scatter | solution.py:177
  201.8 3.1 %collective-permute-start.4 = (f32[32,512]{1,0:T(8,128)S(1)}, f32[32,512]{1,0:T(8,128)S(1)}, u32[]{:S(2)}, u32[]{:S(2)}) collective-permute-start(f32[32,512]{1,0:T(8,128)S(1)} %convert_reduce_fusion.1), channel_id=1, source_target_pairs={{0,32},{32,0},{1,33},{33,1},{2,34},{34,2},{3,35},{35,3},{4,36},{36... | collective-permute-start | bytes 196616 | tf_op jit(solution)/shard_map/ppermute | solution.py:36
  205.0 8.0 %collective-permute-start.5 = (f32[32,512]{1,0:T(8,128)S(1)}, f32[32,512]{1,0:T(8,128)S(1)}, u32[]{:S(2)}, u32[]{:S(2)}) collective-permute-start(f32[32,512]{1,0:T(8,128)S(1)} %add.107), channel_id=1, source_target_pairs={{0,64},{64,0},{1,65},{65,1},{2,66},{66,2},{3,67},{67,3},{4,68},{68... | collective-permute-start | bytes 196616 | tf_op jit(solution)/shard_map/ppermute | solution.py:36
  213.0 16.5 %collective-permute-start.6 = (f32[32,512]{1,0:T(8,128)S(1)}, f32[32,512]{1,0:T(8,128)S(1)}, u32[]{:S(2)}, u32[]{:S(2)}) collective-permute-start(f32[32,512]{1,0:T(8,128)S(1)} %add.108), channel_id=1, source_target_pairs={{0,4},{4,0},{1,5},{5,1},{2,6},{6,2},{3,7},{7,3},{8,12},{12,8},{9,1... | collective-permute-start | bytes 196616 | tf_op jit(solution)/shard_map/ppermute | solution.py:36
  232.9 4.6 %collective-permute-start.8 = (bf16[8,128,512]{2,1,0:T(8,128)(2,1)S(1)}, bf16[8,128,512]{2,1,0:T(8,128)(2,1)S(1)}, u32[]{:S(2)}, u32[]{:S(2)}) collective-permute-start(bf16[8,128,512]{2,1,0:T(8,128)(2,1)S(1)} %get-tuple-element.17), channel_id=1, source_target_pairs={{0,32},{32,0},{1,33},{33,1},{2,34},{34,2},{3,35},{35,3},{4,36},{36... | collective-permute-start | bytes 3145736 | tf_op jit(solution)/shard_map/ppermute | solution.py:36
  237.8 16.9 %collective-permute-start.9 = (bf16[4,128,512]{2,1,0:T(8,128)(2,1)S(1)}, bf16[4,128,512]{2,1,0:T(8,128)(2,1)S(1)}, u32[]{:S(2)}, u32[]{:S(2)}) collective-permute-start(bf16[4,128,512]{2,1,0:T(8,128)(2,1)S(1)} %slice.36), channel_id=1, source_target_pairs={{0,64},{64,0},{1,65},{65,1},{2,66},{66,2},{3,67},{67,3},{4,68},{68... | collective-permute-start | bytes 1572872 | tf_op jit(solution)/shard_map/ppermute | solution.py:36
  274.8 26.5 %all-to-all-start.7 = ((f32[16,32,512]{2,1,0:T(8,128)}), f32[16,32,512]{2,1,0:T(8,128)S(1)}, u32[]{:S(2)}, u32[]{:S(2)}) async-start(f32[16,32,512]{2,1,0:T(8,128)} %broadcast_in_dim.17), calls=%async_computation.7 | async-start | bytes 2097152 | tf_op jit(solution)/shard_map/all_to_all | solution.py:44
Sparse Core Ops, SparseCore 0:
  255.8 43.7 reduce-scatter.1

commit v6 on v5

--- a/solution.py
+++ b/solution.py
@@ -9,8 +9,9 @@
 from jax.sharding import Mesh
 from jax.sharding import PartitionSpec as P
 
-AXES = ("z4", "z1", "core", "y", "zh", "x")
-ROW = ("z4", "z1", "core")
+AXES = ("za", "zb", "z1", "core", "y", "zh", "x")
+Z4 = ("za", "zb")
+ROW = ("za", "zb", "z1", "core")
 PLANE = ("y", "x")
 BF16 = jnp.bfloat16
 F32 = jnp.float32
@@ -104,21 +105,23 @@
 
 def local(features, weight, cotangent, tile_rows, tile_cols, tile_count, tile_vals):
     span, width = features.shape
-    n_z4, n_z1, n_core = lax.axis_size("z4"), lax.axis_size("z1"), lax.axis_size("core")
+    n_z4, n_z1, n_core = lax.axis_size(Z4), lax.axis_size("z1"), lax.axis_size("core")
     n_y, n_zh, n_x = lax.axis_size("y"), lax.axis_size("zh"), lax.axis_size("x")
     n_line = n_z4 * n_z1
     n_row, n_col = n_line * n_core, n_y * n_zh * n_x
     n_plane = n_y * n_x
     my_row = lax.axis_index(ROW)
-    my_z1, my_core, my_zh = lax.axis_index("z1"), lax.axis_index("core"), lax.axis_index("zh")
+    my_zh = lax.axis_index("zh")
     slots = tile_vals.shape[2]
     nodes = n_row * n_col * span
     tiles = tile_vals[0, 0]
     count = tile_count[0]
     row_index = tile_rows[0, 0]
     col_index = tile_cols[0, 0]
-    col_core = (col_index & 1) ^ my_core
-    col_place = col_core * n_line + (((col_index >> 1) & 1) ^ my_z1) * n_z4 + (col_index >> 2)
+    col_bits = col_index ^ my_row
+    col_near = (col_bits & 1) * n_line + (col_bits & 2) * (n_z4 // 2)
+    col_from = col_near + (col_index >> 2)
+    col_to = col_near + ((col_bits >> 2) & 1) * 2 + (col_bits >> 3)
     row_plane = (row_index >> 3) * n_x + (row_index & 3)
     row_place = (((row_index >> 2) & 1) ^ my_zh) * n_plane + row_plane
 
@@ -127,25 +130,20 @@
     col_sums = jnp.sum(tiles, axis=1, dtype=F32) * alive[:, None]
     degree_terms = jnp.einsum("sc,sj->cj", order_cols, col_sums, precision=lax.Precision.HIGHEST)
     high = lax.reduce_precision(degree_terms, 8, 7)
-    middle = lax.reduce_precision(degree_terms - high, 8, 7)
-    pieces = jnp.stack([high, middle, degree_terms - high - middle]).astype(BF16)
-    pieces = pieces.reshape(-1, width)
-    extra = pieces.shape[0]
-    pieces = jnp.pad(pieces, ((0, -extra % 16), (0, 0)))
-    own_line = swap_parts(copies_of(jnp.concatenate([features, pieces]), "z4"), "z4")
+    pieces = jnp.stack([high, degree_terms - high]).astype(BF16).reshape(-1, width)
+    own_line = swap_parts(copies_of(jnp.concatenate([features, pieces]), Z4), Z4)
     own_pair = flip(own_line, "z1")
     blocks = [own_line, own_pair, flip(own_line, "core"), flip(own_pair, "core")]
 
     def degrees(part):
-        terms = part[:, span : span + extra].astype(F32)
-        return jnp.sum(terms.reshape(n_z4 * 3, n_row, span), axis=0)
+        return jnp.sum(part[:, span:].astype(F32).reshape(-1, n_row, span), axis=0)
 
     col_scale = lax.rsqrt(1.0 + sum(degrees(part) for part in blocks))
     own_scale = lax.dynamic_index_in_dim(col_scale, my_row, axis=0, keepdims=False)
     slot_scale = col_scale[col_index]
 
     near_terms, far_terms = tile_sums(
-        False, col_place, row_place, count, tiles, slot_scale, blocks, n_col
+        False, col_from, row_place, count, tiles, slot_scale, blocks, n_col
     )
     far_sum = jnp.sum(swap_parts(far_terms, PLANE).astype(F32), axis=0).astype(BF16)
     near_group = swap_parts(after(near_terms, far_sum), PLANE)
@@ -164,26 +162,29 @@
     for axis in ("core", "z1", "zh"):
         plane_sum = plane_sum + flip(plane_sum, axis)
     far_group = after(far_group, plane_sum)
-    line_part = swap_parts(plane_sum.reshape(n_z4, -1, width), "z4")
+    line_part = swap_parts(plane_sum.reshape(n_z4, -1, width), Z4)
     line_sum = jnp.sum(line_part, axis=0) * (1.0 / math.sqrt(nodes))
 
     near, far = tile_sums(
-        True, row_place, col_place, count, tiles, None, [near_group, far_group], n_row
+        True, row_place, col_to, count, tiles, None, [near_group, far_group], n_row
     )
     core_sum = (near.astype(F32) + flip(far, "core").astype(F32)).astype(BF16)
-    pair_far = flip(core_sum[n_z4:], "z1")
-    pair_sum = (core_sum[:n_z4].astype(F32) + pair_far.astype(F32)).astype(BF16)
-    line_sum = after(line_sum, pair_sum)
-    own_grad = lax.psum_scatter(pair_sum, "z4", scatter_dimension=0, tiled=False)
-    feature_grad = own_grad.astype(F32) * own_scale[:, None]
 
-    plane_rows = swap_parts(copies_of(line_sum, "z4"), "z4").reshape(-1, width)
-    weight_grad = swap_parts(copies_of(plane_rows, PLANE), PLANE).reshape(width, width)
+    def halve(total, axis):
+        half = total.shape[0] // 2
+        return total[:half].astype(F32) + flip(total[half:], axis).astype(F32)
+
+    pair_sum = halve(core_sum, "z1").astype(BF16)
+    line_rows = swap_parts(copies_of(after(line_sum, pair_sum), Z4), Z4).reshape(-1, width)
+    quad_sum = halve(pair_sum, "zb").astype(BF16)
+    line_rows = after(line_rows, quad_sum)
+    weight_grad = swap_parts(copies_of(line_rows, PLANE), PLANE).reshape(width, width)
+    feature_grad = halve(quad_sum, "za")[0] * own_scale[:, None]
     return (output, weight_grad, feature_grad)
 
 
 def solution(mesh):
-    fine = Mesh(mesh.devices.reshape(4, 2, 2, 4, 2, 4), AXES)
+    fine = Mesh(mesh.devices.reshape(2, 2, 2, 2, 4, 2, 4), AXES)
     nodes, row, col = P(AXES, None), ROW, ("y", "zh", "x")
     in_specs = (
         nodes,

time: 310 us -> 293 us (0.945)
  blocking collectives: 107 us -> 33.4 us
  waiting for transfers between devices: 94.8 us -> 136 us
  starting transfers between devices: 68.5 us -> 94.8 us
  between operations: 15.2 us -> 1.79 us
    all_to_all x4 -> x1, blocking collectives: 107 us -> 33.4 us  [swap_parts(): return lax.all_to_all(parts, axes, split_axis=0, concat_axis=0, tiled=True)]
    ppermute x10 -> x12, waiting for transfers between devices: 38.4 us -> 73.3 us  [flip(): return lax.ppermute(block, axis, [(0, 1), (1, 0)])]
    all_to_all x4 -> x7, waiting for transfers between devices: 37.9 us -> 62.3 us  [swap_parts(): return lax.all_to_all(parts, axes, split_axis=0, concat_axis=0, tiled=True)]
    all_to_all x4 -> x7, starting transfers between devices: 23.1 us -> 44.4 us  [swap_parts(): return lax.all_to_all(parts, axes, split_axis=0, concat_axis=0, tiled=True)]
    reduce_scatter x1 -> x0, waiting for transfers between devices: 18.5 us -> none  [local(): lax.psum_scatter(pair_sum, 'z4', scatter_dimension=0, tiled=False)]
    ppermute x10 -> x12, starting transfers between devices: 45.4 us -> 50.4 us  [flip(): return lax.ppermute(block, axis, [(0, 1), (1, 0)])]
  transfers between devices with their start and end apart: 15 -> 19, of which waited for: 11 -> 14; matrix products, arithmetic and copies ran while one was open for 1% -> 1% of each run, Pallas kernels for 0% -> 0%
where the time goes in v6:
time: 293 us; the launch traced here: 290 us
  waiting for transfers between devices  136 us (46%)
  starting transfers between devices  94.8 us (32%)
  blocking collectives  33.4 us (11%)
  Pallas kernels  8.41 us (3%)
  local copies, waits for them, and re-layouts  6.85 us (2%)
  other arithmetic  6.74 us (2%)
    ppermute x12, waiting for transfers between devices, flip(): return lax.ppermute(block, axis, [(0, 1), (1, 0)])  73.3 us
    all_to_all x7, waiting for transfers between devices, swap_parts(): return lax.all_to_all(parts, axes, split_axis=0, concat_axis=0, tiled=True)  62.3 us
    ppermute x12, starting transfers between devices, flip(): return lax.ppermute(block, axis, [(0, 1), (1, 0)])  50.4 us
    all_to_all x7, starting transfers between devices, swap_parts(): return lax.all_to_all(parts, axes, split_axis=0, concat_axis=0, tiled=True)  44.4 us
    all_to_all x1, blocking collectives, swap_parts(): return lax.all_to_all(parts, axes, split_axis=0, concat_axis=0, tiled=True)  33.4 us
    pallas_call x2, Pallas kernels, tile_sums(): pl.pallas_call(functools.partial(tile_kernel, transposed, scaled), out_sh...  8.41 us
  transfers between devices with their start and end apart: 19, of which 14 were waited for; matrix products, arithmetic and copies ran while one was open for 1% of the time, Pallas kernels for 0%

profile of v6, /device:TPU:24, one launch (start us, length us, event | category | flops | bytes accessed | tf_op | source)
XLA Modules:
  0.0 290.2 jit_solution(16220595812420739803)
XLA Ops:
  5.1 11.2 %all-to-all-start = ((bf16[4,136,512]{2,1,0:T(8,128)(2,1)}), bf16[4,136,512]{2,1,0:T(8,128)(2,1)S(1)}, u32[]{:S(2)}, u32[]{:S(2)}) async-start(bf16[4,136,512]{2,1,0:T(8,128)(2,1)} %broadcast_in_dim.10), calls=%async_computation | async-start | bytes 1114112 | tf_op jit(solution)/shard_map/all_to_all | solution.py:45
  16.3 30.1 %all-to-all-done.refs_1_ = bf16[4,136,512]{2,1,0:T(8,128)(2,1)S(1)} async-done(((bf16[4,136,512]{2,1,0:T(8,128)(2,1)}), bf16[4,136,512]{2,1,0:T(8,128)(2,1)S(1)}, u32[]{:S(2)}, u32[]{:S(2)}) %all-to-all-start) | async-done | bytes 557088 | tf_op jit(solution)/shard_map/all_to_all | solution.py:45
  48.4 1.9 collective-permute-start.1
  50.3 11.2 %collective-permute-done.refs_2_ = bf16[4,136,512]{2,1,0:T(8,128)(2,1)S(1)} collective-permute-done((bf16[4,136,512]{2,1,0:T(8,128)(2,1)S(1)}, bf16[4,136,512]{2,1,0:T(8,128)(2,1)S(1)}, u32[]{:S(2)}, u32[]{:S(2)}) %collective-permute-start) | collective-permute-done | bytes 557088 | tf_op jit(solution)/shard_map/ppermute | solution.py:37
  66.0 4.8 %shard_map.94 = (bf16[16,128,512]{2,1,0:T(8,128)(2,1)}, bf16[16,128,512]{2,1,0:T(8,128)(2,1)S(1)}) custom-call(s32[8]{0:T(128)S(1)} %get-tuple-element.24.source, s32[8]{0:T(128)S(1)} %add_bitcast_fusion.target.source, s32[1]{0:T(128)} %bitcast.34.count, bf16[8,128,128]{2,1,0:T(8,128)(2,1)S(1)} %bitcast.37, f32[8,128]{1,0:T(8,128)S(1)} %gather_fusion, ...), custom_call_target="tpu_custom_call" | custom-call | flops 134217728 | bytes 12582912 | tf_op jit(solution)/shard_map/pallas_call | solution.py:91
  70.7 33.4 %all_to_all.40 = bf16[16,128,512]{2,1,0:T(8,128)(2,1)S(1)} all-to-all(bf16[16,128,512]{2,1,0:T(8,128)(2,1)S(1)} %get-tuple-element.13), channel_id=1, replica_groups=mesh['za'=2,'zb'=2,'z1'=2,'core'=2,'y'=4,'zh'=2,'x'=4] {'y','x'}, dimensions={0} | all-to-all | bytes 4194304 | tf_op jit(solution)/shard_map/all_to_all | solution.py:45
  104.4 6.0 %all-to-all-start.2 = ((bf16[16,128,512]{2,1,0:T(8,128)(2,1)}), bf16[16,128,512]{2,1,0:T(8,128)(2,1)S(1)}, u32[]{:S(2)}, u32[]{:S(2)}) async-start(bf16[16,128,512]{2,1,0:T(8,128)(2,1)} %get-tuple-element.14), calls=%async_computation.2 | async-start | bytes 4194304 | tf_op jit(solution)/shard_map/all_to_all | solution.py:45
  110.4 9.6 %collective-permute-start.3 = (bf16[128,512]{1,0:T(8,128)(2,1)S(1)}, bf16[128,512]{1,0:T(8,128)(2,1)S(1)}, u32[]{:S(2)}, u32[]{:S(2)}) collective-permute-start(bf16[128,512]{1,0:T(8,128)(2,1)S(1)} %reduce_sum.107), channel_id=1, source_target_pairs={{0,4},{4,0},{1,5},{5,1},{2,6},{6,2},{3,7},{7,3},{8,12},{12,8},{9,1... | collective-permute-start | bytes 393224 | tf_op jit(solution)/shard_map/ppermute | solution.py:37
  120.0 18.5 %all-to-all-done.2 = bf16[16,128,512]{2,1,0:T(8,128)(2,1)S(1)} async-done(((bf16[16,128,512]{2,1,0:T(8,128)(2,1)}), bf16[16,128,512]{2,1,0:T(8,128)(2,1)S(1)}, u32[]{:S(2)}, u32[]{:S(2)}) %all-to-all-start.2) | async-done | bytes 2097184 | tf_op jit(solution)/shard_map/all_to_all | solution.py:45
  142.9 5.3 %all-to-all-start.3 = ((bf16[16,160,512]{2,1,0:T(8,128)(2,1)}), bf16[16,160,512]{2,1,0:T(8,128)(2,1)S(1)}, u32[]{:S(2)}, u32[]{:S(2)}) async-start(bf16[16,160,512]{2,1,0:T(8,128)(2,1)} %pad_maximum_fusion), calls=%async_computation.3 | async-start | bytes 5242880 | tf_op jit(solution)/shard_map/all_to_all | solution.py:45
  148.2 9.5 %collective-permute-start.7 = (bf16[128,512]{1,0:T(8,128)(2,1)S(1)}, bf16[128,512]{1,0:T(8,128)(2,1)}, u32[]{:S(2)}, u32[]{:S(2)}) collective-permute-start(bf16[128,512]{1,0:T(8,128)(2,1)S(1)} %multiply_convert_fusion), channel_id=1, source_target_pairs={{0,4},{4,0},{1,5},{5,1},{2,6},{6,2},{3,7},{7,3},{8,12},{12,8},{9,1... | collective-permute-start | bytes 393224 | tf_op jit(solution)/shard_map/ppermute | solution.py:37
  157.7 13.7 %collective-permute-done.7 = bf16[128,512]{1,0:T(8,128)(2,1)} collective-permute-done((bf16[128,512]{1,0:T(8,128)(2,1)S(1)}, bf16[128,512]{1,0:T(8,128)(2,1)}, u32[]{:S(2)}, u32[]{:S(2)}) %collective-permute-start.7) | collective-permute-done | bytes 131104 | tf_op jit(solution)/shard_map/ppermute | solution.py:37
  171.4 13.0 %all-to-all-done.3.refs_0_ = bf16[16,160,512]{2,1,0:T(8,128)(2,1)S(1)} async-done(((bf16[16,160,512]{2,1,0:T(8,128)(2,1)}), bf16[16,160,512]{2,1,0:T(8,128)(2,1)S(1)}, u32[]{:S(2)}, u32[]{:S(2)}) %all-to-all-start.3) | async-done | bytes 2621472 | tf_op jit(solution)/shard_map/all_to_all | solution.py:45
  184.4 2.4 broadcast_in_dim.12
  186.8 5.8 %all-to-all-start.5 = ((bf16[16,128,512]{2,1,0:T(8,128)(2,1)}), bf16[16,128,512]{2,1,0:T(8,128)(2,1)}, u32[]{:S(2)}, u32[]{:S(2)}) async-start(bf16[16,128,512]{2,1,0:T(8,128)(2,1)} %broadcast_in_dim.12), calls=%async_computation.5 | async-start | bytes 4194304 | tf_op jit(solution)/shard_map/all_to_all | solution.py:45
  192.7 1.9 collective-permute-start.4
  195.8 4.0 %collective-permute-start.5 = (f32[32,512]{1,0:T(8,128)S(1)}, f32[32,512]{1,0:T(8,128)S(1)}, u32[]{:S(2)}, u32[]{:S(2)}) collective-permute-start(f32[32,512]{1,0:T(8,128)S(1)} %add.121), channel_id=1, source_target_pairs={{0,64},{64,0},{1,65},{65,1},{2,66},{66,2},{3,67},{67,3},{4,68},{68... | collective-permute-start | bytes 196616 | tf_op jit(solution)/shard_map/ppermute | solution.py:37
  199.9 2.4 collective-permute-done.5
  202.3 9.8 %collective-permute-start.6 = (f32[32,512]{1,0:T(8,128)S(1)}, f32[32,512]{1,0:T(8,128)S(1)}, u32[]{:S(2)}, u32[]{:S(2)}) collective-permute-start(f32[32,512]{1,0:T(8,128)S(1)} %add.122), channel_id=1, source_target_pairs={{0,4},{4,0},{1,5},{5,1},{2,6},{6,2},{3,7},{7,3},{8,12},{12,8},{9,1... | collective-permute-start | bytes 196616 | tf_op jit(solution)/shard_map/ppermute | solution.py:37
  212.1 8.8 %collective-permute-done.6 = f32[32,512]{1,0:T(8,128)S(1)} collective-permute-done((f32[32,512]{1,0:T(8,128)S(1)}, f32[32,512]{1,0:T(8,128)S(1)}, u32[]{:S(2)}, u32[]{:S(2)}) %collective-permute-start.6) | collective-permute-done | bytes 65568 | tf_op jit(solution)/shard_map/ppermute | solution.py:37
  221.5 3.6 %shard_map.95 = (bf16[8,128,512]{2,1,0:T(8,128)(2,1)S(1)}, bf16[8,128,512]{2,1,0:T(8,128)(2,1)S(1)}) custom-call(s32[8]{0:T(128)S(1)} %add_bitcast_fusion.target.source, s32[8]{0:T(128)S(1)} %get-tuple-element.23.target, s32[1]{0:T(128)} %bitcast.35.count, bf16[8,128,128]{2,1,0:T(8,128)(2,1)S(1)} %bitcast.38, ...), custom_call_target="tpu_custom_call" | custom-call | flops 134217728 | bytes 6291456 | tf_op jit(solution)/shard_map/pallas_call | solution.py:91
  225.2 1.9 collective-permute-start.8
  227.1 2.6 collective-permute-done.8
  230.1 1.9 collective-permute-start.9
  232.0 3.7 %all-to-all-start.4 = ((f32[4,8,512]{2,1,0:T(8,128)}), f32[4,8,512]{2,1,0:T(8,128)S(1)}, u32[]{:S(2)}, u32[]{:S(2)}) async-start(f32[4,8,512]{2,1,0:T(8,128)} %bitcast.10), calls=%async_computation.4 | async-start | bytes 131072 | tf_op jit(solution)/shard_map/all_to_all | solution.py:45
  235.7 11.3 %collective-permute-done.9 = bf16[4,128,512]{2,1,0:T(8,128)(2,1)S(1)} collective-permute-done((bf16[4,128,512]{2,1,0:T(8,128)(2,1)S(1)}, bf16[4,128,512]{2,1,0:T(8,128)(2,1)S(1)}, u32[]{:S(2)}, u32[]{:S(2)}) %collective-permute-start.9) | collective-permute-done | bytes 524320 | tf_op jit(solution)/shard_map/ppermute | solution.py:37
  247.1 1.9 collective-permute-start.10
  249.7 5.1 %all-to-all-start.6 = ((f32[4,8,512]{2,1,0:T(8,128)}), f32[4,8,512]{2,1,0:T(8,128)S(1)}, u32[]{:S(2)}, u32[]{:S(2)}) async-start(f32[4,8,512]{2,1,0:T(8,128)} %broadcast_in_dim.13), calls=%async_computation.6 | async-start | bytes 131072 | tf_op jit(solution)/shard_map/all_to_all | solution.py:45
  254.8 8.9 %collective-permute-done.10 = bf16[2,128,512]{2,1,0:T(8,128)(2,1)S(1)} collective-permute-done((bf16[2,128,512]{2,1,0:T(8,128)(2,1)S(1)}, bf16[2,128,512]{2,1,0:T(8,128)(2,1)S(1)}, u32[]{:S(2)}, u32[]{:S(2)}) %collective-permute-start.10) | collective-permute-done | bytes 262176 | tf_op jit(solution)/shard_map/ppermute | solution.py:37
  265.6 7.3 %all-to-all-start.7 = ((f32[16,32,512]{2,1,0:T(8,128)}), f32[16,32,512]{2,1,0:T(8,128)S(1)}, u32[]{:S(2)}, u32[]{:S(2)}) async-start(f32[16,32,512]{2,1,0:T(8,128)} %broadcast_in_dim.14), calls=%async_computation.7 | async-start | bytes 2097152 | tf_op jit(solution)/shard_map/all_to_all | solution.py:45
  272.9 4.2 %collective-permute-start.11 = (bf16[1,128,512]{2,1,0:T(8,128)(2,1)S(1)}, bf16[1,128,512]{2,1,0:T(8,128)(2,1)S(1)}, u32[]{:S(2)}, u32[]{:S(2)}) collective-permute-start(bf16[1,128,512]{2,1,0:T(8,128)(2,1)S(1)} %slice.56), channel_id=1, source_target_pairs={{0,256},{256,0},{1,257},{257,1},{2,258},{258,2},{3,259},{259,3},{4... | collective-permute-start | bytes 393224 | tf_op jit(solution)/shard_map/ppermute | solution.py:37
  277.1 11.4 %collective-permute-done.11 = bf16[1,128,512]{2,1,0:T(8,128)(2,1)S(1)} collective-permute-done((bf16[1,128,512]{2,1,0:T(8,128)(2,1)S(1)}, bf16[1,128,512]{2,1,0:T(8,128)(2,1)S(1)}, u32[]{:S(2)}, u32[]{:S(2)}) %collective-permute-start.11) | collective-permute-done | bytes 131104 | tf_op jit(solution)/shard_map/ppermute | solution.py:37
  (74 shorter events, 21.3 us)
Async XLA Ops:
  0.6 138.5 %copy-start = (bf16[512,512]{1,0:T(8,128)(2,1)S(1)}, bf16[512,512]{1,0:T(8,128)(2,1)}, u32[]{:S(2)}) copy-start(bf16[512,512]{1,0:T(8,128)(2,1)} %param.8) | copy-start | bytes 1572868
  0.6 65.3 %copy-start.1 = (bf16[1,1,8,128,128]{4,3,2,1,0:T(8,128)(2,1)S(1)}, bf16[1,1,8,128,128]{4,3,2,1,0:T(8,128)(2,1)}, u32[]{:S(2)}) copy-start(bf16[1,1,8,128,128]{4,3,2,1,0:T(8,128)(2,1)} %param.13) | copy-start | bytes 786436
  0.7 15.6 %copy-start.2 = (s32[1,1,8]{2,1,0:T(1,128)S(1)}, s32[1,1,8]{2,1,0:T(1,128)}, u32[]{:S(2)}) copy-start(s32[1,1,8]{2,1,0:T(1,128)} %param.11) | copy-start | bytes 100
  0.7 47.7 %copy-start.4 = (s32[1,1,8]{2,1,0:T(1,128)S(1)}, s32[1,1,8]{2,1,0:T(1,128)}, u32[]{:S(2)}) copy-start(s32[1,1,8]{2,1,0:T(1,128)} %param.10) | copy-start | bytes 100
  5.1 41.3 %all-to-all-start = ((bf16[4,136,512]{2,1,0:T(8,128)(2,1)}), bf16[4,136,512]{2,1,0:T(8,128)(2,1)S(1)}, u32[]{:S(2)}, u32[]{:S(2)}) async-start(bf16[4,136,512]{2,1,0:T(8,128)(2,1)} %broadcast_in_dim.10), calls=%async_computation | async-start | bytes 1114112 | tf_op jit(solution)/shard_map/all_to_all | solution.py:45
  46.4 15.1 %collective-permute-start = (bf16[4,136,512]{2,1,0:T(8,128)(2,1)S(1)}, bf16[4,136,512]{2,1,0:T(8,128)(2,1)S(1)}, u32[]{:S(2)}, u32[]{:S(2)}) collective-permute-start(bf16[4,136,512]{2,1,0:T(8,128)(2,1)S(1)} %all-to-all-done.refs_1_), channel_id=1, source_target_pairs={{0,64},{64,0},{1,65},{65,1},{2,66},{66,2},{3,67},{67,3},{4,68},{68... | collective-permute-start | bytes 1671176 | tf_op jit(solution)/shard_map/ppermute | solution.py:37
  48.4 15.1 %collective-permute-start.1 = (bf16[4,136,512]{2,1,0:T(8,128)(2,1)S(1)}, bf16[4,136,512]{2,1,0:T(8,128)(2,1)S(1)}, u32[]{:S(2)}, u32[]{:S(2)}) collective-permute-start(bf16[4,136,512]{2,1,0:T(8,128)(2,1)S(1)} %all-to-all-done.refs_1_), channel_id=1, source_target_pairs={{0,32},{32,0},{1,33},{33,1},{2,34},{34,2},{3,35},{35,3},{4,36},{36... | collective-permute-start | bytes 1671176 | tf_op jit(solution)/shard_map/ppermute | solution.py:37
  61.5 3.8 %collective-permute-start.2 = (bf16[4,136,512]{2,1,0:T(8,128)(2,1)S(1)}, bf16[4,136,512]{2,1,0:T(8,128)(2,1)S(1)}, u32[]{:S(2)}, u32[]{:S(2)}) collective-permute-start(bf16[4,136,512]{2,1,0:T(8,128)(2,1)S(1)} %collective-permute-done.refs_2_), channel_id=1, source_target_pairs={{0,32},{32,0},{1,33},{33,1},{2,34},{34,2},{3,35},{35,3},{4,36},{36... | collective-permute-start | bytes 1671176 | tf_op jit(solution)/shard_map/ppermute | solution.py:37
  104.4 34.1 %all-to-all-start.2 = ((bf16[16,128,512]{2,1,0:T(8,128)(2,1)}), bf16[16,128,512]{2,1,0:T(8,128)(2,1)S(1)}, u32[]{:S(2)}, u32[]{:S(2)}) async-start(bf16[16,128,512]{2,1,0:T(8,128)(2,1)} %get-tuple-element.14), calls=%async_computation.2 | async-start | bytes 4194304 | tf_op jit(solution)/shard_map/all_to_all | solution.py:45
  110.4 29.6 %copy-start.3 = (bf16[128,512]{1,0:T(8,128)(2,1)S(1)}, bf16[128,512]{1,0:T(8,128)(2,1)}, u32[]{:S(2)}) copy-start(bf16[128,512]{1,0:T(8,128)(2,1)} %param.9) | copy-start | bytes 393220
  110.4 28.4 %collective-permute-start.3 = (bf16[128,512]{1,0:T(8,128)(2,1)S(1)}, bf16[128,512]{1,0:T(8,128)(2,1)S(1)}, u32[]{:S(2)}, u32[]{:S(2)}) collective-permute-start(bf16[128,512]{1,0:T(8,128)(2,1)S(1)} %reduce_sum.107), channel_id=1, source_target_pairs={{0,4},{4,0},{1,5},{5,1},{2,6},{6,2},{3,7},{7,3},{8,12},{12,8},{9,1... | collective-permute-start | bytes 393224 | tf_op jit(solution)/shard_map/ppermute | solution.py:37
  142.9 41.5 %all-to-all-start.3 = ((bf16[16,160,512]{2,1,0:T(8,128)(2,1)}), bf16[16,160,512]{2,1,0:T(8,128)(2,1)S(1)}, u32[]{:S(2)}, u32[]{:S(2)}) async-start(bf16[16,160,512]{2,1,0:T(8,128)(2,1)} %pad_maximum_fusion), calls=%async_computation.3 | async-start | bytes 5242880 | tf_op jit(solution)/shard_map/all_to_all | solution.py:45
  148.2 23.2 %collective-permute-start.7 = (bf16[128,512]{1,0:T(8,128)(2,1)S(1)}, bf16[128,512]{1,0:T(8,128)(2,1)}, u32[]{:S(2)}, u32[]{:S(2)}) collective-permute-start(bf16[128,512]{1,0:T(8,128)(2,1)S(1)} %multiply_convert_fusion), channel_id=1, source_target_pairs={{0,4},{4,0},{1,5},{5,1},{2,6},{6,2},{3,7},{7,3},{8,12},{12,8},{9,1... | collective-permute-start | bytes 393224 | tf_op jit(solution)/shard_map/ppermute | solution.py:37
  186.8 34.7 %all-to-all-start.5 = ((bf16[16,128,512]{2,1,0:T(8,128)(2,1)}), bf16[16,128,512]{2,1,0:T(8,128)(2,1)}, u32[]{:S(2)}, u32[]{:S(2)}) async-start(bf16[16,128,512]{2,1,0:T(8,128)(2,1)} %broadcast_in_dim.12), calls=%async_computation.5 | async-start | bytes 4194304 | tf_op jit(solution)/shard_map/all_to_all | solution.py:45
  192.7 3.1 %collective-permute-start.4 = (f32[32,512]{1,0:T(8,128)S(1)}, f32[32,512]{1,0:T(8,128)S(1)}, u32[]{:S(2)}, u32[]{:S(2)}) collective-permute-start(f32[32,512]{1,0:T(8,128)S(1)} %convert_reduce_fusion.1), channel_id=1, source_target_pairs={{0,32},{32,0},{1,33},{33,1},{2,34},{34,2},{3,35},{35,3},{4,36},{36... | collective-permute-start | bytes 196616 | tf_op jit(solution)/shard_map/ppermute | solution.py:37
  195.8 6.4 %collective-permute-start.5 = (f32[32,512]{1,0:T(8,128)S(1)}, f32[32,512]{1,0:T(8,128)S(1)}, u32[]{:S(2)}, u32[]{:S(2)}) collective-permute-start(f32[32,512]{1,0:T(8,128)S(1)} %add.121), channel_id=1, source_target_pairs={{0,64},{64,0},{1,65},{65,1},{2,66},{66,2},{3,67},{67,3},{4,68},{68... | collective-permute-start | bytes 196616 | tf_op jit(solution)/shard_map/ppermute | solution.py:37
  202.3 18.6 %collective-permute-start.6 = (f32[32,512]{1,0:T(8,128)S(1)}, f32[32,512]{1,0:T(8,128)S(1)}, u32[]{:S(2)}, u32[]{:S(2)}) collective-permute-start(f32[32,512]{1,0:T(8,128)S(1)} %add.122), channel_id=1, source_target_pairs={{0,4},{4,0},{1,5},{5,1},{2,6},{6,2},{3,7},{7,3},{8,12},{12,8},{9,1... | collective-permute-start | bytes 196616 | tf_op jit(solution)/shard_map/ppermute | solution.py:37
  225.2 4.6 %collective-permute-start.8 = (bf16[8,128,512]{2,1,0:T(8,128)(2,1)S(1)}, bf16[8,128,512]{2,1,0:T(8,128)(2,1)S(1)}, u32[]{:S(2)}, u32[]{:S(2)}) collective-permute-start(bf16[8,128,512]{2,1,0:T(8,128)(2,1)S(1)} %get-tuple-element.18), channel_id=1, source_target_pairs={{0,32},{32,0},{1,33},{33,1},{2,34},{34,2},{3,35},{35,3},{4,36},{36... | collective-permute-start | bytes 3145736 | tf_op jit(solution)/shard_map/ppermute | solution.py:37
  230.1 16.9 %collective-permute-start.9 = (bf16[4,128,512]{2,1,0:T(8,128)(2,1)S(1)}, bf16[4,128,512]{2,1,0:T(8,128)(2,1)S(1)}, u32[]{:S(2)}, u32[]{:S(2)}) collective-permute-start(bf16[4,128,512]{2,1,0:T(8,128)(2,1)S(1)} %slice.52), channel_id=1, source_target_pairs={{0,64},{64,0},{1,65},{65,1},{2,66},{66,2},{3,67},{67,3},{4,68},{68... | collective-permute-start | bytes 1572872 | tf_op jit(solution)/shard_map/ppermute | solution.py:37
  232.0 17.1 %all-to-all-start.4 = ((f32[4,8,512]{2,1,0:T(8,128)}), f32[4,8,512]{2,1,0:T(8,128)S(1)}, u32[]{:S(2)}, u32[]{:S(2)}) async-start(f32[4,8,512]{2,1,0:T(8,128)} %bitcast.10), calls=%async_computation.4 | async-start | bytes 131072 | tf_op jit(solution)/shard_map/all_to_all | solution.py:45
  247.1 16.6 %collective-permute-start.10 = (bf16[2,128,512]{2,1,0:T(8,128)(2,1)S(1)}, bf16[2,128,512]{2,1,0:T(8,128)(2,1)S(1)}, u32[]{:S(2)}, u32[]{:S(2)}) collective-permute-start(bf16[2,128,512]{2,1,0:T(8,128)(2,1)S(1)} %slice.54), channel_id=1, source_target_pairs={{0,128},{128,0},{1,129},{129,1},{2,130},{130,2},{3,131},{131,3},{4... | collective-permute-start | bytes 786440 | tf_op jit(solution)/shard_map/ppermute | solution.py:37
  249.7 14.7 %all-to-all-start.6 = ((f32[4,8,512]{2,1,0:T(8,128)}), f32[4,8,512]{2,1,0:T(8,128)S(1)}, u32[]{:S(2)}, u32[]{:S(2)}) async-start(f32[4,8,512]{2,1,0:T(8,128)} %broadcast_in_dim.13), calls=%async_computation.6 | async-start | bytes 131072 | tf_op jit(solution)/shard_map/all_to_all | solution.py:45
  265.6 23.7 %all-to-all-start.7 = ((f32[16,32,512]{2,1,0:T(8,128)}), f32[16,32,512]{2,1,0:T(8,128)S(1)}, u32[]{:S(2)}, u32[]{:S(2)}) async-start(f32[16,32,512]{2,1,0:T(8,128)} %broadcast_in_dim.14), calls=%async_computation.7 | async-start | bytes 2097152 | tf_op jit(solution)/shard_map/all_to_all | solution.py:45
  272.9 15.6 %collective-permute-start.11 = (bf16[1,128,512]{2,1,0:T(8,128)(2,1)S(1)}, bf16[1,128,512]{2,1,0:T(8,128)(2,1)S(1)}, u32[]{:S(2)}, u32[]{:S(2)}) collective-permute-start(bf16[1,128,512]{2,1,0:T(8,128)(2,1)S(1)} %slice.56), channel_id=1, source_target_pairs={{0,256},{256,0},{1,257},{257,1},{2,258},{258,2},{3,259},{259,3},{4... | collective-permute-start | bytes 393224 | tf_op jit(solution)/shard_map/ppermute | solution.py:37

commit v7 on v6

--- a/solution.py
+++ b/solution.py
@@ -49,11 +49,11 @@
     return jnp.broadcast_to(block[None], (lax.axis_size(axes),) + block.shape)
 
 
-def tile_kernel(transposed, scaled, source, target, count, tiles, *refs):
+def tile_kernel(transposed, scaled, sources, places, source, target, count, tiles, *refs):
     scale, refs = (refs[0], refs[1:]) if scaled else (None, refs)
-    *groups, near, far, total = refs
+    total = refs[-1]
+    arrays, outputs = refs[: -1 - len(places)], refs[-1 - len(places) : -1]
     slots, size, _ = tiles.shape
-    held, near_blocks = groups[0].shape[0], near.shape[0]
     axis = 0 if transposed else 1
     total[...] = jnp.zeros_like(total)
     for slot in range(slots):
@@ -69,30 +69,40 @@
                 tiles[slot], block, (((axis,), (0,)), ((), ())), preferred_element_type=F32
             )
 
-        for number, group in enumerate(groups):
-            inside = source[slot] - number * held
+        first = 0
+        for pieces in sources:
+            held = arrays[pieces[0][0]].shape[0]
+            inside = source[slot] - first
+            first += held
 
             @pl.when((slot < count[0]) & (inside >= 0) & (inside < held))
-            def _(group=group, inside=inside):
-                add(group[jnp.clip(inside, 0, held - 1), :size, :])
-
-    near[...] = total[:near_blocks].astype(BF16)
-    far[...] = total[near_blocks:].astype(BF16)
-
-
-def tile_sums(transposed, source, target, count, tiles, scale, groups, blocks):
+            def _(pieces=pieces, inside=jnp.clip(inside, 0, held - 1)):
+                rows = [arrays[number][inside, low:high, :] for number, low, high in pieces]
+                add(rows[0] if len(rows) == 1 else jnp.concatenate(rows, axis=0))
+
+    for output, pieces in zip(outputs, places):
+        row = 0
+        for start, stop, low, high in pieces:
+            output[:, row : row + high - low, :] = total[start:stop, low:high, :].astype(BF16)
+            row += high - low
+
+
+def tile_sums(transposed, source, target, count, tiles, scale, arrays, sources, places, blocks):
     slots, size, _ = tiles.shape
-    width = groups[0].shape[2]
+    width = arrays[0].shape[2]
     smem = pl.BlockSpec(memory_space=pltpu.SMEM)
     vmem = pl.BlockSpec(memory_space=pltpu.VMEM)
-    half = jax.ShapeDtypeStruct((blocks // 2, size, width), BF16)
     scaled = scale is not None
-    operands = [tiles] + [scale] * scaled + list(groups)
+    operands = [tiles] + [scale] * scaled + list(arrays)
+    shapes = [
+        (pieces[0][1] - pieces[0][0], sum(high - low for _, _, low, high in pieces), width)
+        for pieces in places
+    ]
     return pl.pallas_call(
-        functools.partial(tile_kernel, transposed, scaled),
-        out_shape=(half, half),
+        functools.partial(tile_kernel, transposed, scaled, sources, places),
+        out_shape=[jax.ShapeDtypeStruct(shape, BF16) for shape in shapes],
         in_specs=[smem] * 3 + [vmem] * len(operands),
-        out_specs=(vmem, vmem),
+        out_specs=[vmem] * len(shapes),
         scratch_shapes=[pltpu.VMEM((blocks, size, width), F32)],
         compiler_params=pltpu.CompilerParams(vmem_limit_bytes=40 * 1024 * 1024),
         cost_estimate=pl.CostEstimate(
@@ -142,31 +152,57 @@
     own_scale = lax.dynamic_index_in_dim(col_scale, my_row, axis=0, keepdims=False)
     slot_scale = col_scale[col_index]
 
-    near_terms, far_terms = tile_sums(
-        False, col_from, row_place, count, tiles, slot_scale, blocks, n_col
-    )
-    far_sum = jnp.sum(swap_parts(far_terms, PLANE).astype(F32), axis=0).astype(BF16)
-    near_group = swap_parts(after(near_terms, far_sum), PLANE)
-    own_total = jnp.sum(near_group.astype(F32), axis=0) + flip(far_sum, "zh").astype(F32)
+    half = span // 2
+    first_terms, last_terms = tile_sums(
+        False,
+        col_from,
+        row_place,
+        count,
+        tiles,
+        slot_scale,
+        blocks,
+        [[(number, 0, span)] for number in range(4)],
+        [[(n_plane, n_col, 0, span), (0, n_plane, 0, half)], [(0, n_plane, half, span)]],
+        n_col,
+    )
+    first_group = swap_parts(first_terms, PLANE)
+    far_sum = jnp.sum(first_group[:, :span].astype(F32), axis=0).astype(BF16)
+    last_group = swap_parts(after(last_terms, far_sum), PLANE)
+    near_sum = jnp.concatenate(
+        [
+            jnp.sum(first_group[:, span:].astype(F32), axis=0),
+            jnp.sum(last_group.astype(F32), axis=0),
+        ]
+    )
+    own_total = near_sum + flip(far_sum, "zh").astype(F32)
 
     output, normed, grad_pre, grad_own = layer_rows(own_total, cotangent, weight)
 
     weight_terms = jnp.einsum("nf,ng->fg", normed, grad_pre, preferred_element_type=F32)
     weight_parts = weight_terms.astype(BF16).reshape(n_plane, width // n_plane, width)
-    near_group = swap_parts(
-        jnp.concatenate([copies_of(grad_own, PLANE), weight_parts], axis=1), PLANE
-    )
-    far_group = swap_parts(copies_of(after(flip(grad_own, "zh"), near_group), PLANE), PLANE)
-
-    plane_sum = jnp.sum(near_group[:, span:].astype(F32), axis=0)
-    for axis in ("core", "z1", "zh"):
-        plane_sum = plane_sum + flip(plane_sum, axis)
-    far_group = after(far_group, plane_sum)
-    line_part = swap_parts(plane_sum.reshape(n_z4, -1, width), Z4)
-    line_sum = jnp.sum(line_part, axis=0) * (1.0 / math.sqrt(nodes))
+    first_group = swap_parts(
+        jnp.concatenate([copies_of(grad_own[:half], PLANE), weight_parts], axis=1), PLANE
+    )
+    grad_rest = jnp.concatenate([grad_own[half:], flip(grad_own, "zh")])
+    last_group = swap_parts(copies_of(after(grad_rest, first_group), PLANE), PLANE)
+
+    line_rows = jnp.sum(first_group[:, half:].astype(F32), axis=0)
+    for axis in ("core", "z1", "zb", "za", "zh"):
+        line_rows = line_rows + flip(line_rows, axis)
+    line_rows = line_rows * (1.0 / math.sqrt(nodes))
+    last_group = after(last_group, line_rows)
 
     near, far = tile_sums(
-        True, row_place, col_to, count, tiles, None, [near_group, far_group], n_row
+        True,
+        row_place,
+        col_to,
+        count,
+        tiles,
+        None,
+        [first_group, last_group],
+        [[(0, 0, half), (1, 0, half)], [(1, half, half + span)]],
+        [[(0, n_line, 0, span)], [(n_line, n_row, 0, span)]],
+        n_row,
     )
     core_sum = (near.astype(F32) + flip(far, "core").astype(F32)).astype(BF16)
 
@@ -174,11 +210,10 @@
         half = total.shape[0] // 2
         return total[:half].astype(F32) + flip(total[half:], axis).astype(F32)
 
+    line_rows = after(line_rows, core_sum)
+    weight_grad = swap_parts(copies_of(line_rows, PLANE), PLANE).reshape(width, width)
     pair_sum = halve(core_sum, "z1").astype(BF16)
-    line_rows = swap_parts(copies_of(after(line_sum, pair_sum), Z4), Z4).reshape(-1, width)
     quad_sum = halve(pair_sum, "zb").astype(BF16)
-    line_rows = after(line_rows, quad_sum)
-    weight_grad = swap_parts(copies_of(line_rows, PLANE), PLANE).reshape(width, width)
     feature_grad = halve(quad_sum, "za")[0] * own_scale[:, None]
     return (output, weight_grad, feature_grad)
 

time: 293 us -> 295 us (level)
  starting transfers between devices: 94.8 us -> 80.4 us
  blocking collectives: 33.4 us -> 45.5 us
  waiting for transfers between devices: 136 us -> 140 us
    ppermute x12 -> x14, waiting for transfers between devices: 73.3 us -> 102 us  [flip(): return lax.ppermute(block, axis, [(0, 1), (1, 0)])]
    all_to_all x7 -> x5, waiting for transfers between devices: 62.3 us -> 38 us  [swap_parts(): return lax.all_to_all(parts, axes, split_axis=0, concat_axis=0, tiled=True)]
    all_to_all x1, blocking collectives: 33.4 us -> 45.5 us  [swap_parts(): return lax.all_to_all(parts, axes, split_axis=0, concat_axis=0, tiled=True)]
    ppermute x12 -> x14, starting transfers between devices: 50.4 us -> 42.5 us  [flip(): return lax.ppermute(block, axis, [(0, 1), (1, 0)])]
    all_to_all x7 -> x5, starting transfers between devices: 44.4 us -> 37.9 us  [swap_parts(): return lax.all_to_all(parts, axes, split_axis=0, concat_axis=0, tiled=True)]
  transfers between devices with their start and end apart: 19 -> 19, of which waited for: 14 -> 16; matrix products, arithmetic and copies ran while one was open for 1% -> 1% of each run, Pallas kernels for 0% -> 0%
where the time goes in v7:
time: 295 us; the launch traced here: 293 us
  waiting for transfers between devices  140 us (47%)
  starting transfers between devices  80.4 us (27%)
  blocking collectives  45.5 us (15%)
  local copies, waits for them, and re-layouts  8.14 us (3%)
  Pallas kernels  7.38 us (3%)
  other arithmetic  6.87 us (2%)
    ppermute x14, waiting for transfers between devices, flip(): return lax.ppermute(block, axis, [(0, 1), (1, 0)])  102 us
    all_to_all x1, blocking collectives, swap_parts(): return lax.all_to_all(parts, axes, split_axis=0, concat_axis=0, tiled=True)  45.5 us
    ppermute x14, starting transfers between devices, flip(): return lax.ppermute(block, axis, [(0, 1), (1, 0)])  42.5 us
    all_to_all x5, waiting for transfers between devices, swap_parts(): return lax.all_to_all(parts, axes, split_axis=0, concat_axis=0, tiled=True)  38 us
    all_to_all x5, starting transfers between devices, swap_parts(): return lax.all_to_all(parts, axes, split_axis=0, concat_axis=0, tiled=True)  37.9 us
    pallas_call x2, Pallas kernels, tile_sums(): pl.pallas_call(functools.partial(tile_kernel, transposed, scaled, sources...  7.38 us
  transfers between devices with their start and end apart: 19, of which 16 were waited for; matrix products, arithmetic and copies ran while one was open for 1% of the time, Pallas kernels for 0%

profile of v7, /device:TPU:24, one launch (start us, length us, event | category | flops | bytes accessed | tf_op | source)
XLA Modules:
  0.0 292.8 jit_solution(9572858164903646632)
XLA Ops:
  5.1 11.2 %all-to-all-start = ((bf16[4,136,512]{2,1,0:T(8,128)(2,1)}), bf16[4,136,512]{2,1,0:T(8,128)(2,1)S(1)}, u32[]{:S(2)}, u32[]{:S(2)}) async-start(bf16[4,136,512]{2,1,0:T(8,128)(2,1)} %broadcast_in_dim.8), calls=%async_computation | async-start | bytes 1114112 | tf_op jit(solution)/shard_map/all_to_all | solution.py:45
  16.3 30.1 %all-to-all-done.refs_1_ = bf16[4,136,512]{2,1,0:T(8,128)(2,1)S(1)} async-done(((bf16[4,136,512]{2,1,0:T(8,128)(2,1)}), bf16[4,136,512]{2,1,0:T(8,128)(2,1)S(1)}, u32[]{:S(2)}, u32[]{:S(2)}) %all-to-all-start) | async-done | bytes 557088 | tf_op jit(solution)/shard_map/all_to_all | solution.py:45
  48.4 1.9 collective-permute-start.1
  50.3 11.2 %collective-permute-done.refs_2_ = bf16[4,136,512]{2,1,0:T(8,128)(2,1)S(1)} collective-permute-done((bf16[4,136,512]{2,1,0:T(8,128)(2,1)S(1)}, bf16[4,136,512]{2,1,0:T(8,128)(2,1)S(1)}, u32[]{:S(2)}, u32[]{:S(2)}) %collective-permute-start) | collective-permute-done | bytes 557088 | tf_op jit(solution)/shard_map/ppermute | solution.py:37
  66.0 4.0 %shard_map.94 = (bf16[16,192,512]{2,1,0:T(8,128)(2,1)S(1)}, bf16[16,64,512]{2,1,0:T(8,128)(2,1)}) custom-call(s32[8]{0:T(128)S(1)} %get-tuple-element.24.source, s32[8]{0:T(128)S(1)} %add_bitcast_fusion.target.source, s32[1]{0:T(128)} %bitcast.30.count, bf16[8,128,128]{2,1,0:T(8,128)(2,1)S(1)} %bitcast.33, f32[8,128]{1,0:T(8,128)S(1)} %gather_fusion, ...), custom_call_target="tpu_custom_call" | custom-call | flops 134217728 | bytes 12582912 | tf_op jit(solution)/shard_map/pallas_call | solution.py:101
  70.0 45.5 %all_to_all.30 = bf16[16,192,512]{2,1,0:T(8,128)(2,1)S(1)} all-to-all(bf16[16,192,512]{2,1,0:T(8,128)(2,1)S(1)} %get-tuple-element.11), channel_id=1, replica_groups=mesh['za'=2,'zb'=2,'z1'=2,'core'=2,'y'=4,'zh'=2,'x'=4] {'y','x'}, dimensions={0} | all-to-all | bytes 6291456 | tf_op jit(solution)/shard_map/all_to_all | solution.py:45
  117.3 5.9 %all-to-all-start.2 = ((bf16[16,64,512]{2,1,0:T(8,128)(2,1)}), bf16[16,64,512]{2,1,0:T(8,128)(2,1)S(1)}, u32[]{:S(2)}, u32[]{:S(2)}) async-start(bf16[16,64,512]{2,1,0:T(8,128)(2,1)} %get-tuple-element.13), calls=%async_computation.2 | async-start | bytes 2097152 | tf_op jit(solution)/shard_map/all_to_all | solution.py:45
  123.3 9.9 %collective-permute-start.3 = (bf16[128,512]{1,0:T(8,128)(2,1)S(1)}, bf16[128,512]{1,0:T(8,128)(2,1)S(1)}, u32[]{:S(2)}, u32[]{:S(2)}) collective-permute-start(bf16[128,512]{1,0:T(8,128)(2,1)S(1)} %slice_reduce_fusion), channel_id=1, source_target_pairs={{0,4},{4,0},{1,5},{5,1},{2,6},{6,2},{3,7},{7,3},{8,12},{12,8},{9,1... | collective-permute-start | bytes 393224 | tf_op jit(solution)/shard_map/ppermute | solution.py:37
  134.6 3.3 %all-to-all-done.2 = bf16[16,64,512]{2,1,0:T(8,128)(2,1)S(1)} async-done(((bf16[16,64,512]{2,1,0:T(8,128)(2,1)}), bf16[16,64,512]{2,1,0:T(8,128)(2,1)S(1)}, u32[]{:S(2)}, u32[]{:S(2)}) %all-to-all-start.2) | async-done | bytes 1048608 | tf_op jit(solution)/shard_map/all_to_all | solution.py:45
  138.0 8.8 %collective-permute-done.3 = bf16[128,512]{1,0:T(8,128)(2,1)S(1)} collective-permute-done((bf16[128,512]{1,0:T(8,128)(2,1)S(1)}, bf16[128,512]{1,0:T(8,128)(2,1)S(1)}, u32[]{:S(2)}, u32[]{:S(2)}) %collective-permute-start.3) | collective-permute-done | bytes 131104 | tf_op jit(solution)/shard_map/ppermute | solution.py:37
  150.4 7.2 %all-to-all-start.3 = ((bf16[16,96,512]{2,1,0:T(8,128)(2,1)}), bf16[16,96,512]{2,1,0:T(8,128)(2,1)S(1)}, u32[]{:S(2)}, u32[]{:S(2)}) async-start(bf16[16,96,512]{2,1,0:T(8,128)(2,1)} %pad_maximum_fusion), calls=%async_computation.3 | async-start | bytes 3145728 | tf_op jit(solution)/shard_map/all_to_all | solution.py:45
  157.6 4.6 %collective-permute-start.9 = (bf16[128,512]{1,0:T(8,128)(2,1)S(1)}, bf16[128,512]{1,0:T(8,128)(2,1)S(1)}, u32[]{:S(2)}, u32[]{:S(2)}) collective-permute-start(bf16[128,512]{1,0:T(8,128)(2,1)S(1)} %multiply_convert_fusion), channel_id=1, source_target_pairs={{0,4},{4,0},{1,5},{5,1},{2,6},{6,2},{3,7},{7,3},{8,12},{12,8},{9,1... | collective-permute-start | bytes 393224 | tf_op jit(solution)/shard_map/ppermute | solution.py:37
  162.2 12.0 %collective-permute-done.9 = bf16[128,512]{1,0:T(8,128)(2,1)S(1)} collective-permute-done((bf16[128,512]{1,0:T(8,128)(2,1)S(1)}, bf16[128,512]{1,0:T(8,128)(2,1)S(1)}, u32[]{:S(2)}, u32[]{:S(2)}) %collective-permute-start.9) | collective-permute-done | bytes 131104 | tf_op jit(solution)/shard_map/ppermute | solution.py:37
  174.2 4.6 %all-to-all-done.3.refs_0_ = bf16[16,96,512]{2,1,0:T(8,128)(2,1)S(1)} async-done(((bf16[16,96,512]{2,1,0:T(8,128)(2,1)}), bf16[16,96,512]{2,1,0:T(8,128)(2,1)S(1)}, u32[]{:S(2)}, u32[]{:S(2)}) %all-to-all-start.3) | async-done | bytes 1572896 | tf_op jit(solution)/shard_map/all_to_all | solution.py:45
  178.8 2.0 broadcast_in_dim.10
  180.8 6.5 %all-to-all-start.4 = ((bf16[16,192,512]{2,1,0:T(8,128)(2,1)}), bf16[16,192,512]{2,1,0:T(8,128)(2,1)}, u32[]{:S(2)}, u32[]{:S(2)}) async-start(bf16[16,192,512]{2,1,0:T(8,128)(2,1)} %broadcast_in_dim.10), calls=%async_computation.4 | async-start | bytes 6291456 | tf_op jit(solution)/shard_map/all_to_all | solution.py:45
  187.4 1.9 collective-permute-start.4
  190.5 1.9 collective-permute-start.5
  192.5 4.2 %collective-permute-done.5 = f32[32,512]{1,0:T(8,128)S(1)} collective-permute-done((f32[32,512]{1,0:T(8,128)S(1)}, f32[32,512]{1,0:T(8,128)S(1)}, u32[]{:S(2)}, u32[]{:S(2)}) %collective-permute-start.5) | collective-permute-done | bytes 65568 | tf_op jit(solution)/shard_map/ppermute | solution.py:37
  196.7 1.9 collective-permute-start.6
  198.6 5.6 %collective-permute-done.6 = f32[32,512]{1,0:T(8,128)S(1)} collective-permute-done((f32[32,512]{1,0:T(8,128)S(1)}, f32[32,512]{1,0:T(8,128)S(1)}, u32[]{:S(2)}, u32[]{:S(2)}) %collective-permute-start.6) | collective-permute-done | bytes 65568 | tf_op jit(solution)/shard_map/ppermute | solution.py:37
  204.3 1.9 collective-permute-start.7
  206.2 9.9 %collective-permute-done.7 = f32[32,512]{1,0:T(8,128)S(1)} collective-permute-done((f32[32,512]{1,0:T(8,128)S(1)}, f32[32,512]{1,0:T(8,128)S(1)}, u32[]{:S(2)}, u32[]{:S(2)}) %collective-permute-start.7) | collective-permute-done | bytes 65568 | tf_op jit(solution)/shard_map/ppermute | solution.py:37
  216.2 6.1 %collective-permute-start.8 = (f32[32,512]{1,0:T(8,128)S(1)}, f32[32,512]{1,0:T(8,128)S(1)}, u32[]{:S(2)}, u32[]{:S(2)}) collective-permute-start(f32[32,512]{1,0:T(8,128)S(1)} %add.130), channel_id=1, source_target_pairs={{0,4},{4,0},{1,5},{5,1},{2,6},{6,2},{3,7},{7,3},{8,12},{12,8},{9,1... | collective-permute-start | bytes 196616 | tf_op jit(solution)/shard_map/ppermute | solution.py:37
  222.3 10.4 %collective-permute-done.8 = f32[32,512]{1,0:T(8,128)S(1)} collective-permute-done((f32[32,512]{1,0:T(8,128)S(1)}, f32[32,512]{1,0:T(8,128)S(1)}, u32[]{:S(2)}, u32[]{:S(2)}) %collective-permute-start.8) | collective-permute-done | bytes 65568 | tf_op jit(solution)/shard_map/ppermute | solution.py:37
  232.7 3.4 %shard_map.95 = (bf16[8,128,512]{2,1,0:T(8,128)(2,1)S(1)}, bf16[8,128,512]{2,1,0:T(8,128)(2,1)S(1)}) custom-call(s32[8]{0:T(128)S(1)} %add_bitcast_fusion.target.source, s32[8]{0:T(128)S(1)} %get-tuple-element.23.target, s32[1]{0:T(128)} %bitcast.31.count, bf16[8,128,128]{2,1,0:T(8,128)(2,1)S(1)} %bitcast.34, ...), custom_call_target="tpu_custom_call" | custom-call | flops 134217728 | bytes 6291456 | tf_op jit(solution)/shard_map/pallas_call | solution.py:101
  236.1 2.7 collective-permute-start.10
  238.8 2.3 collective-permute-done.10
  245.2 7.1 %all-to-all-start.5 = ((f32[16,32,512]{2,1,0:T(8,128)}), f32[16,32,512]{2,1,0:T(8,128)S(1)}, u32[]{:S(2)}, u32[]{:S(2)}) async-start(f32[16,32,512]{2,1,0:T(8,128)} %broadcast_in_dim.11), calls=%async_computation.5 | async-start | bytes 2097152 | tf_op jit(solution)/shard_map/all_to_all | solution.py:45
  252.3 6.2 %collective-permute-done.11 = bf16[4,128,512]{2,1,0:T(8,128)(2,1)S(1)} collective-permute-done((bf16[4,128,512]{2,1,0:T(8,128)(2,1)}, bf16[4,128,512]{2,1,0:T(8,128)(2,1)S(1)}, u32[]{:S(2)}, u32[]{:S(2)}) %collective-permute-start.11) | collective-permute-done | bytes 524320 | tf_op jit(solution)/shard_map/ppermute | solution.py:37
  260.6 14.2 %collective-permute-done.12 = bf16[2,128,512]{2,1,0:T(8,128)(2,1)S(1)} collective-permute-done((bf16[2,128,512]{2,1,0:T(8,128)(2,1)S(1)}, bf16[2,128,512]{2,1,0:T(8,128)(2,1)S(1)}, u32[]{:S(2)}, u32[]{:S(2)}) %collective-permute-start.12) | collective-permute-done | bytes 262176 | tf_op jit(solution)/shard_map/ppermute | solution.py:37
  276.8 14.2 %collective-permute-done.13 = bf16[1,128,512]{2,1,0:T(8,128)(2,1)S(1)} collective-permute-done((bf16[1,128,512]{2,1,0:T(8,128)(2,1)S(1)}, bf16[1,128,512]{2,1,0:T(8,128)(2,1)S(1)}, u32[]{:S(2)}, u32[]{:S(2)}) %collective-permute-start.13) | collective-permute-done | bytes 131104 | tf_op jit(solution)/shard_map/ppermute | solution.py:37
  (77 shorter events, 28.3 us)
Async XLA Ops:
  0.6 146.4 %copy-start = (bf16[512,512]{1,0:T(8,128)(2,1)S(1)}, bf16[512,512]{1,0:T(8,128)(2,1)}, u32[]{:S(2)}) copy-start(bf16[512,512]{1,0:T(8,128)(2,1)} %param.8) | copy-start | bytes 1572868
  0.6 65.3 %copy-start.1 = (bf16[1,1,8,128,128]{4,3,2,1,0:T(8,128)(2,1)S(1)}, bf16[1,1,8,128,128]{4,3,2,1,0:T(8,128)(2,1)}, u32[]{:S(2)}) copy-start(bf16[1,1,8,128,128]{4,3,2,1,0:T(8,128)(2,1)} %param.13) | copy-start | bytes 786436
  0.7 15.6 %copy-start.3 = (s32[1,1,8]{2,1,0:T(1,128)S(1)}, s32[1,1,8]{2,1,0:T(1,128)}, u32[]{:S(2)}) copy-start(s32[1,1,8]{2,1,0:T(1,128)} %param.11) | copy-start | bytes 100
  0.7 47.7 %copy-start.5 = (s32[1,1,8]{2,1,0:T(1,128)S(1)}, s32[1,1,8]{2,1,0:T(1,128)}, u32[]{:S(2)}) copy-start(s32[1,1,8]{2,1,0:T(1,128)} %param.10) | copy-start | bytes 100
  5.1 41.3 %all-to-all-start = ((bf16[4,136,512]{2,1,0:T(8,128)(2,1)}), bf16[4,136,512]{2,1,0:T(8,128)(2,1)S(1)}, u32[]{:S(2)}, u32[]{:S(2)}) async-start(bf16[4,136,512]{2,1,0:T(8,128)(2,1)} %broadcast_in_dim.8), calls=%async_computation | async-start | bytes 1114112 | tf_op jit(solution)/shard_map/all_to_all | solution.py:45
  46.4 15.1 %collective-permute-start = (bf16[4,136,512]{2,1,0:T(8,128)(2,1)S(1)}, bf16[4,136,512]{2,1,0:T(8,128)(2,1)S(1)}, u32[]{:S(2)}, u32[]{:S(2)}) collective-permute-start(bf16[4,136,512]{2,1,0:T(8,128)(2,1)S(1)} %all-to-all-done.refs_1_), channel_id=1, source_target_pairs={{0,64},{64,0},{1,65},{65,1},{2,66},{66,2},{3,67},{67,3},{4,68},{68... | collective-permute-start | bytes 1671176 | tf_op jit(solution)/shard_map/ppermute | solution.py:37
  48.4 15.1 %collective-permute-start.1 = (bf16[4,136,512]{2,1,0:T(8,128)(2,1)S(1)}, bf16[4,136,512]{2,1,0:T(8,128)(2,1)S(1)}, u32[]{:S(2)}, u32[]{:S(2)}) collective-permute-start(bf16[4,136,512]{2,1,0:T(8,128)(2,1)S(1)} %all-to-all-done.refs_1_), channel_id=1, source_target_pairs={{0,32},{32,0},{1,33},{33,1},{2,34},{34,2},{3,35},{35,3},{4,36},{36... | collective-permute-start | bytes 1671176 | tf_op jit(solution)/shard_map/ppermute | solution.py:37
  61.5 3.8 %collective-permute-start.2 = (bf16[4,136,512]{2,1,0:T(8,128)(2,1)S(1)}, bf16[4,136,512]{2,1,0:T(8,128)(2,1)S(1)}, u32[]{:S(2)}, u32[]{:S(2)}) collective-permute-start(bf16[4,136,512]{2,1,0:T(8,128)(2,1)S(1)} %collective-permute-done.refs_2_), channel_id=1, source_target_pairs={{0,32},{32,0},{1,33},{33,1},{2,34},{34,2},{3,35},{35,3},{4,36},{36... | collective-permute-start | bytes 1671176 | tf_op jit(solution)/shard_map/ppermute | solution.py:37
  115.4 1.6 copy-start.2
  117.3 20.6 %all-to-all-start.2 = ((bf16[16,64,512]{2,1,0:T(8,128)(2,1)}), bf16[16,64,512]{2,1,0:T(8,128)(2,1)S(1)}, u32[]{:S(2)}, u32[]{:S(2)}) async-start(bf16[16,64,512]{2,1,0:T(8,128)(2,1)} %get-tuple-element.13), calls=%async_computation.2 | async-start | bytes 2097152 | tf_op jit(solution)/shard_map/all_to_all | solution.py:45
  123.2 24.8 %copy-start.4 = (bf16[128,512]{1,0:T(8,128)(2,1)S(1)}, bf16[128,512]{1,0:T(8,128)(2,1)}, u32[]{:S(2)}) copy-start(bf16[128,512]{1,0:T(8,128)(2,1)} %param.9) | copy-start | bytes 393220
  123.3 23.6 %collective-permute-start.3 = (bf16[128,512]{1,0:T(8,128)(2,1)S(1)}, bf16[128,512]{1,0:T(8,128)(2,1)S(1)}, u32[]{:S(2)}, u32[]{:S(2)}) collective-permute-start(bf16[128,512]{1,0:T(8,128)(2,1)S(1)} %slice_reduce_fusion), channel_id=1, source_target_pairs={{0,4},{4,0},{1,5},{5,1},{2,6},{6,2},{3,7},{7,3},{8,12},{12,8},{9,1... | collective-permute-start | bytes 393224 | tf_op jit(solution)/shard_map/ppermute | solution.py:37
  150.4 28.4 %all-to-all-start.3 = ((bf16[16,96,512]{2,1,0:T(8,128)(2,1)}), bf16[16,96,512]{2,1,0:T(8,128)(2,1)S(1)}, u32[]{:S(2)}, u32[]{:S(2)}) async-start(bf16[16,96,512]{2,1,0:T(8,128)(2,1)} %pad_maximum_fusion), calls=%async_computation.3 | async-start | bytes 3145728 | tf_op jit(solution)/shard_map/all_to_all | solution.py:45
  157.6 16.6 %collective-permute-start.9 = (bf16[128,512]{1,0:T(8,128)(2,1)S(1)}, bf16[128,512]{1,0:T(8,128)(2,1)S(1)}, u32[]{:S(2)}, u32[]{:S(2)}) collective-permute-start(bf16[128,512]{1,0:T(8,128)(2,1)S(1)} %multiply_convert_fusion), channel_id=1, source_target_pairs={{0,4},{4,0},{1,5},{5,1},{2,6},{6,2},{3,7},{7,3},{8,12},{12,8},{9,1... | collective-permute-start | bytes 393224 | tf_op jit(solution)/shard_map/ppermute | solution.py:37
  180.8 51.9 %all-to-all-start.4 = ((bf16[16,192,512]{2,1,0:T(8,128)(2,1)}), bf16[16,192,512]{2,1,0:T(8,128)(2,1)}, u32[]{:S(2)}, u32[]{:S(2)}) async-start(bf16[16,192,512]{2,1,0:T(8,128)(2,1)} %broadcast_in_dim.10), calls=%async_computation.4 | async-start | bytes 6291456 | tf_op jit(solution)/shard_map/all_to_all | solution.py:45
  187.4 3.1 %collective-permute-start.4 = (f32[32,512]{1,0:T(8,128)S(1)}, f32[32,512]{1,0:T(8,128)S(1)}, u32[]{:S(2)}, u32[]{:S(2)}) collective-permute-start(f32[32,512]{1,0:T(8,128)S(1)} %convert_reduce_fusion.2), channel_id=1, source_target_pairs={{0,32},{32,0},{1,33},{33,1},{2,34},{34,2},{3,35},{35,3},{4,36},{36... | collective-permute-start | bytes 196616 | tf_op jit(solution)/shard_map/ppermute | solution.py:37
  190.5 6.2 %collective-permute-start.5 = (f32[32,512]{1,0:T(8,128)S(1)}, f32[32,512]{1,0:T(8,128)S(1)}, u32[]{:S(2)}, u32[]{:S(2)}) collective-permute-start(f32[32,512]{1,0:T(8,128)S(1)} %add.127), channel_id=1, source_target_pairs={{0,64},{64,0},{1,65},{65,1},{2,66},{66,2},{3,67},{67,3},{4,68},{68... | collective-permute-start | bytes 196616 | tf_op jit(solution)/shard_map/ppermute | solution.py:37
  196.7 7.6 %collective-permute-start.6 = (f32[32,512]{1,0:T(8,128)S(1)}, f32[32,512]{1,0:T(8,128)S(1)}, u32[]{:S(2)}, u32[]{:S(2)}) collective-permute-start(f32[32,512]{1,0:T(8,128)S(1)} %add.128), channel_id=1, source_target_pairs={{0,128},{128,0},{1,129},{129,1},{2,130},{130,2},{3,131},{131,3},{4... | collective-permute-start | bytes 196616 | tf_op jit(solution)/shard_map/ppermute | solution.py:37
  204.3 11.9 %collective-permute-start.7 = (f32[32,512]{1,0:T(8,128)S(1)}, f32[32,512]{1,0:T(8,128)S(1)}, u32[]{:S(2)}, u32[]{:S(2)}) collective-permute-start(f32[32,512]{1,0:T(8,128)S(1)} %add.129), channel_id=1, source_target_pairs={{0,256},{256,0},{1,257},{257,1},{2,258},{258,2},{3,259},{259,3},{4... | collective-permute-start | bytes 196616 | tf_op jit(solution)/shard_map/ppermute | solution.py:37
  216.2 16.5 %collective-permute-start.8 = (f32[32,512]{1,0:T(8,128)S(1)}, f32[32,512]{1,0:T(8,128)S(1)}, u32[]{:S(2)}, u32[]{:S(2)}) collective-permute-start(f32[32,512]{1,0:T(8,128)S(1)} %add.130), channel_id=1, source_target_pairs={{0,4},{4,0},{1,5},{5,1},{2,6},{6,2},{3,7},{7,3},{8,12},{12,8},{9,1... | collective-permute-start | bytes 196616 | tf_op jit(solution)/shard_map/ppermute | solution.py:37
  236.1 5.0 %collective-permute-start.10 = (bf16[8,128,512]{2,1,0:T(8,128)(2,1)S(1)}, bf16[8,128,512]{2,1,0:T(8,128)(2,1)S(1)}, u32[]{:S(2)}, u32[]{:S(2)}) collective-permute-start(bf16[8,128,512]{2,1,0:T(8,128)(2,1)S(1)} %get-tuple-element.17), channel_id=1, source_target_pairs={{0,32},{32,0},{1,33},{33,1},{2,34},{34,2},{3,35},{35,3},{4,36},{36... | collective-permute-start | bytes 3145736 | tf_op jit(solution)/shard_map/ppermute | solution.py:37
  242.2 16.3 %collective-permute-start.11 = (bf16[4,128,512]{2,1,0:T(8,128)(2,1)}, bf16[4,128,512]{2,1,0:T(8,128)(2,1)S(1)}, u32[]{:S(2)}, u32[]{:S(2)}) collective-permute-start(bf16[4,128,512]{2,1,0:T(8,128)(2,1)} %slice.72), channel_id=1, source_target_pairs={{0,64},{64,0},{1,65},{65,1},{2,66},{66,2},{3,67},{67,3},{4,68},{68... | collective-permute-start | bytes 1572872 | tf_op jit(solution)/shard_map/ppermute | solution.py:37
  245.2 46.6 %all-to-all-start.5 = ((f32[16,32,512]{2,1,0:T(8,128)}), f32[16,32,512]{2,1,0:T(8,128)S(1)}, u32[]{:S(2)}, u32[]{:S(2)}) async-start(f32[16,32,512]{2,1,0:T(8,128)} %broadcast_in_dim.11), calls=%async_computation.5 | async-start | bytes 2097152 | tf_op jit(solution)/shard_map/all_to_all | solution.py:45
  258.7 16.1 %collective-permute-start.12 = (bf16[2,128,512]{2,1,0:T(8,128)(2,1)S(1)}, bf16[2,128,512]{2,1,0:T(8,128)(2,1)S(1)}, u32[]{:S(2)}, u32[]{:S(2)}) collective-permute-start(bf16[2,128,512]{2,1,0:T(8,128)(2,1)S(1)} %slice.74), channel_id=1, source_target_pairs={{0,128},{128,0},{1,129},{129,1},{2,130},{130,2},{3,131},{131,3},{4... | collective-permute-start | bytes 786440 | tf_op jit(solution)/shard_map/ppermute | solution.py:37
  274.9 16.1 %collective-permute-start.13 = (bf16[1,128,512]{2,1,0:T(8,128)(2,1)S(1)}, bf16[1,128,512]{2,1,0:T(8,128)(2,1)S(1)}, u32[]{:S(2)}, u32[]{:S(2)}) collective-permute-start(bf16[1,128,512]{2,1,0:T(8,128)(2,1)S(1)} %slice.76), channel_id=1, source_target_pairs={{0,256},{256,0},{1,257},{257,1},{2,258},{258,2},{3,259},{259,3},{4... | collective-permute-start | bytes 393224 | tf_op jit(solution)/shard_map/ppermute | solution.py:37

commit v8 on v7

--- a/solution.py
+++ b/solution.py
@@ -152,8 +152,7 @@
     own_scale = lax.dynamic_index_in_dim(col_scale, my_row, axis=0, keepdims=False)
     slot_scale = col_scale[col_index]
 
-    half = span // 2
-    first_terms, last_terms = tile_sums(
+    near_terms, far_terms = tile_sums(
         False,
         col_from,
         row_place,
@@ -162,35 +161,27 @@
         slot_scale,
         blocks,
         [[(number, 0, span)] for number in range(4)],
-        [[(n_plane, n_col, 0, span), (0, n_plane, 0, half)], [(0, n_plane, half, span)]],
+        [[(0, n_plane, 0, span)], [(n_plane, n_col, 0, span)]],
         n_col,
     )
-    first_group = swap_parts(first_terms, PLANE)
-    far_sum = jnp.sum(first_group[:, :span].astype(F32), axis=0).astype(BF16)
-    last_group = swap_parts(after(last_terms, far_sum), PLANE)
-    near_sum = jnp.concatenate(
-        [
-            jnp.sum(first_group[:, span:].astype(F32), axis=0),
-            jnp.sum(last_group.astype(F32), axis=0),
-        ]
-    )
-    own_total = near_sum + flip(far_sum, "zh").astype(F32)
+    far_sum = jnp.sum(swap_parts(far_terms, PLANE).astype(F32), axis=0).astype(BF16)
+    near_group = swap_parts(after(near_terms, far_sum), PLANE)
+    own_total = jnp.sum(near_group.astype(F32), axis=0) + flip(far_sum, "zh").astype(F32)
 
     output, normed, grad_pre, grad_own = layer_rows(own_total, cotangent, weight)
 
     weight_terms = jnp.einsum("nf,ng->fg", normed, grad_pre, preferred_element_type=F32)
     weight_parts = weight_terms.astype(BF16).reshape(n_plane, width // n_plane, width)
-    first_group = swap_parts(
-        jnp.concatenate([copies_of(grad_own[:half], PLANE), weight_parts], axis=1), PLANE
-    )
-    grad_rest = jnp.concatenate([grad_own[half:], flip(grad_own, "zh")])
-    last_group = swap_parts(copies_of(after(grad_rest, first_group), PLANE), PLANE)
-
-    line_rows = jnp.sum(first_group[:, half:].astype(F32), axis=0)
-    for axis in ("core", "z1", "zb", "za", "zh"):
+    near_group = swap_parts(
+        jnp.concatenate([copies_of(grad_own, PLANE), weight_parts], axis=1), PLANE
+    )
+    far_group = swap_parts(copies_of(after(flip(grad_own, "zh"), near_group), PLANE), PLANE)
+
+    line_rows = jnp.sum(near_group[:, span:].astype(F32), axis=0)
+    for axis in ("core", "z1", "zb", "zh"):
         line_rows = line_rows + flip(line_rows, axis)
     line_rows = line_rows * (1.0 / math.sqrt(nodes))
-    last_group = after(last_group, line_rows)
+    far_group = after(far_group, line_rows)
 
     near, far = tile_sums(
         True,
@@ -199,8 +190,8 @@
         count,
         tiles,
         None,
-        [first_group, last_group],
-        [[(0, 0, half), (1, 0, half)], [(1, half, half + span)]],
+        [near_group, far_group],
+        [[(0, 0, span)], [(1, 0, span)]],
         [[(0, n_line, 0, span)], [(n_line, n_row, 0, span)]],
         n_row,
     )
@@ -211,8 +202,9 @@
         return total[:half].astype(F32) + flip(total[half:], axis).astype(F32)
 
     line_rows = after(line_rows, core_sum)
+    line_rows = line_rows + flip(line_rows, "za")
+    pair_sum = halve(core_sum, "z1").astype(BF16)
     weight_grad = swap_parts(copies_of(line_rows, PLANE), PLANE).reshape(width, width)
-    pair_sum = halve(core_sum, "z1").astype(BF16)
     quad_sum = halve(pair_sum, "zb").astype(BF16)
     feature_grad = halve(quad_sum, "za")[0] * own_scale[:, None]
     return (output, weight_grad, feature_grad)

time: 295 us -> 300 us (1.017)
  waiting for transfers between devices: 140 us -> 153 us
  blocking collectives: 45.5 us -> 33.2 us
  starting transfers between devices: 80.4 us -> 85.2 us
    all_to_all x5, waiting for transfers between devices: 38 us -> 62.6 us  [swap_parts(): return lax.all_to_all(parts, axes, split_axis=0, concat_axis=0, tiled=True)]
    all_to_all x1, blocking collectives: 45.5 us -> 33.2 us  [swap_parts(): return lax.all_to_all(parts, axes, split_axis=0, concat_axis=0, tiled=True)]
    ppermute x14, waiting for transfers between devices: 102 us -> 90.2 us  [flip(): return lax.ppermute(block, axis, [(0, 1), (1, 0)])]
    ppermute x14, starting transfers between devices: 42.5 us -> 50.5 us  [flip(): return lax.ppermute(block, axis, [(0, 1), (1, 0)])]
    all_to_all x5, starting transfers between devices: 37.9 us -> 34.8 us  [swap_parts(): return lax.all_to_all(parts, axes, split_axis=0, concat_axis=0, tiled=True)]
  transfers between devices with their start and end apart: 19 -> 19, of which waited for: 16 -> 14; matrix products, arithmetic and copies ran while one was open for 1% -> 1% of each run, Pallas kernels for 0% -> 0%
where the time goes in v8:
time: 300 us; the launch traced here: 298 us
  waiting for transfers between devices  153 us (51%)
  starting transfers between devices  85.2 us (28%)
  blocking collectives  33.2 us (11%)
  Pallas kernels  8.8 us (3%)
  local copies, waits for them, and re-layouts  7.05 us (2%)
  other arithmetic  6.13 us (2%)
    ppermute x14, waiting for transfers between devices, flip(): return lax.ppermute(block, axis, [(0, 1), (1, 0)])  90.2 us
    all_to_all x5, waiting for transfers between devices, swap_parts(): return lax.all_to_all(parts, axes, split_axis=0, concat_axis=0, tiled=True)  62.6 us
    ppermute x14, starting transfers between devices, flip(): return lax.ppermute(block, axis, [(0, 1), (1, 0)])  50.5 us
    all_to_all x5, starting transfers between devices, swap_parts(): return lax.all_to_all(parts, axes, split_axis=0, concat_axis=0, tiled=True)  34.8 us
    all_to_all x1, blocking collectives, swap_parts(): return lax.all_to_all(parts, axes, split_axis=0, concat_axis=0, tiled=True)  33.2 us
    pallas_call x2, Pallas kernels, tile_sums(): pl.pallas_call(functools.partial(tile_kernel, transposed, scaled, sources...  8.8 us
  transfers between devices with their start and end apart: 19, of which 14 were waited for; matrix products, arithmetic and copies ran while one was open for 1% of the time, Pallas kernels for 0%

profile of v8, /device:TPU:24, one launch (start us, length us, event | category | flops | bytes accessed | tf_op | source)
XLA Modules:
  0.0 297.7 jit_solution(1463026392045544586)
XLA Ops:
  5.1 11.2 %all-to-all-start = ((bf16[4,136,512]{2,1,0:T(8,128)(2,1)}), bf16[4,136,512]{2,1,0:T(8,128)(2,1)S(1)}, u32[]{:S(2)}, u32[]{:S(2)}) async-start(bf16[4,136,512]{2,1,0:T(8,128)(2,1)} %broadcast_in_dim.8), calls=%async_computation | async-start | bytes 1114112 | tf_op jit(solution)/shard_map/all_to_all | solution.py:45
  16.3 30.1 %all-to-all-done.refs_1_ = bf16[4,136,512]{2,1,0:T(8,128)(2,1)S(1)} async-done(((bf16[4,136,512]{2,1,0:T(8,128)(2,1)}), bf16[4,136,512]{2,1,0:T(8,128)(2,1)S(1)}, u32[]{:S(2)}, u32[]{:S(2)}) %all-to-all-start) | async-done | bytes 557088 | tf_op jit(solution)/shard_map/all_to_all | solution.py:45
  48.4 1.9 collective-permute-start.1
  50.3 11.2 %collective-permute-done.refs_2_ = bf16[4,136,512]{2,1,0:T(8,128)(2,1)S(1)} collective-permute-done((bf16[4,136,512]{2,1,0:T(8,128)(2,1)S(1)}, bf16[4,136,512]{2,1,0:T(8,128)(2,1)S(1)}, u32[]{:S(2)}, u32[]{:S(2)}) %collective-permute-start) | collective-permute-done | bytes 557088 | tf_op jit(solution)/shard_map/ppermute | solution.py:37
  66.0 5.1 %shard_map.94 = (bf16[16,128,512]{2,1,0:T(8,128)(2,1)}, bf16[16,128,512]{2,1,0:T(8,128)(2,1)S(1)}) custom-call(s32[8]{0:T(128)S(1)} %get-tuple-element.22.source, s32[8]{0:T(128)S(1)} %add_bitcast_fusion.target.source, s32[1]{0:T(128)} %bitcast.32.count, bf16[8,128,128]{2,1,0:T(8,128)(2,1)S(1)} %bitcast.35, f32[8,128]{1,0:T(8,128)S(1)} %gather_fusion, ...), custom_call_target="tpu_custom_call" | custom-call | flops 134217728 | bytes 12582912 | tf_op jit(solution)/shard_map/pallas_call | solution.py:101
  71.1 33.2 %all_to_all.30 = bf16[16,128,512]{2,1,0:T(8,128)(2,1)S(1)} all-to-all(bf16[16,128,512]{2,1,0:T(8,128)(2,1)S(1)} %get-tuple-element.12), channel_id=1, replica_groups=mesh['za'=2,'zb'=2,'z1'=2,'core'=2,'y'=4,'zh'=2,'x'=4] {'y','x'}, dimensions={0} | all-to-all | bytes 4194304 | tf_op jit(solution)/shard_map/all_to_all | solution.py:45
  104.6 6.0 %all-to-all-start.2 = ((bf16[16,128,512]{2,1,0:T(8,128)(2,1)}), bf16[16,128,512]{2,1,0:T(8,128)(2,1)S(1)}, u32[]{:S(2)}, u32[]{:S(2)}) async-start(bf16[16,128,512]{2,1,0:T(8,128)(2,1)} %get-tuple-element.13), calls=%async_computation.2 | async-start | bytes 4194304 | tf_op jit(solution)/shard_map/all_to_all | solution.py:45
  110.6 9.8 %collective-permute-start.3 = (bf16[128,512]{1,0:T(8,128)(2,1)S(1)}, bf16[128,512]{1,0:T(8,128)(2,1)S(1)}, u32[]{:S(2)}, u32[]{:S(2)}) collective-permute-start(bf16[128,512]{1,0:T(8,128)(2,1)S(1)} %reduce_sum.98), channel_id=1, source_target_pairs={{0,4},{4,0},{1,5},{5,1},{2,6},{6,2},{3,7},{7,3},{8,12},{12,8},{9,1... | collective-permute-start | bytes 393224 | tf_op jit(solution)/shard_map/ppermute | solution.py:37
  120.4 18.9 %all-to-all-done.2 = bf16[16,128,512]{2,1,0:T(8,128)(2,1)S(1)} async-done(((bf16[16,128,512]{2,1,0:T(8,128)(2,1)}), bf16[16,128,512]{2,1,0:T(8,128)(2,1)S(1)}, u32[]{:S(2)}, u32[]{:S(2)}) %all-to-all-start.2) | async-done | bytes 2097184 | tf_op jit(solution)/shard_map/all_to_all | solution.py:45
  143.6 5.2 %all-to-all-start.3 = ((bf16[16,160,512]{2,1,0:T(8,128)(2,1)}), bf16[16,160,512]{2,1,0:T(8,128)(2,1)S(1)}, u32[]{:S(2)}, u32[]{:S(2)}) async-start(bf16[16,160,512]{2,1,0:T(8,128)(2,1)} %pad_maximum_fusion), calls=%async_computation.3 | async-start | bytes 5242880 | tf_op jit(solution)/shard_map/all_to_all | solution.py:45
  148.8 9.5 %collective-permute-start.8 = (bf16[128,512]{1,0:T(8,128)(2,1)S(1)}, bf16[128,512]{1,0:T(8,128)(2,1)}, u32[]{:S(2)}, u32[]{:S(2)}) collective-permute-start(bf16[128,512]{1,0:T(8,128)(2,1)S(1)} %multiply_convert_fusion), channel_id=1, source_target_pairs={{0,4},{4,0},{1,5},{5,1},{2,6},{6,2},{3,7},{7,3},{8,12},{12,8},{9,1... | collective-permute-start | bytes 393224 | tf_op jit(solution)/shard_map/ppermute | solution.py:37
  158.4 13.8 %collective-permute-done.8 = bf16[128,512]{1,0:T(8,128)(2,1)} collective-permute-done((bf16[128,512]{1,0:T(8,128)(2,1)S(1)}, bf16[128,512]{1,0:T(8,128)(2,1)}, u32[]{:S(2)}, u32[]{:S(2)}) %collective-permute-start.8) | collective-permute-done | bytes 131104 | tf_op jit(solution)/shard_map/ppermute | solution.py:37
  172.2 13.6 %all-to-all-done.3.refs_0_ = bf16[16,160,512]{2,1,0:T(8,128)(2,1)S(1)} async-done(((bf16[16,160,512]{2,1,0:T(8,128)(2,1)}), bf16[16,160,512]{2,1,0:T(8,128)(2,1)S(1)}, u32[]{:S(2)}, u32[]{:S(2)}) %all-to-all-start.3) | async-done | bytes 2621472 | tf_op jit(solution)/shard_map/all_to_all | solution.py:45
  185.8 2.4 broadcast_in_dim.10
  188.2 5.6 %all-to-all-start.4 = ((bf16[16,128,512]{2,1,0:T(8,128)(2,1)}), bf16[16,128,512]{2,1,0:T(8,128)(2,1)}, u32[]{:S(2)}, u32[]{:S(2)}) async-start(bf16[16,128,512]{2,1,0:T(8,128)(2,1)} %broadcast_in_dim.10), calls=%async_computation.4 | async-start | bytes 4194304 | tf_op jit(solution)/shard_map/all_to_all | solution.py:45
  193.9 1.9 collective-permute-start.4
  197.1 1.9 collective-permute-start.5
  199.0 4.2 %collective-permute-done.5 = f32[32,512]{1,0:T(8,128)S(1)} collective-permute-done((f32[32,512]{1,0:T(8,128)S(1)}, f32[32,512]{1,0:T(8,128)S(1)}, u32[]{:S(2)}, u32[]{:S(2)}) %collective-permute-start.5) | collective-permute-done | bytes 65568 | tf_op jit(solution)/shard_map/ppermute | solution.py:37
  203.3 1.9 collective-permute-start.6
  205.2 5.6 %collective-permute-done.6 = f32[32,512]{1,0:T(8,128)S(1)} collective-permute-done((f32[32,512]{1,0:T(8,128)S(1)}, f32[32,512]{1,0:T(8,128)S(1)}, u32[]{:S(2)}, u32[]{:S(2)}) %collective-permute-start.6) | collective-permute-done | bytes 65568 | tf_op jit(solution)/shard_map/ppermute | solution.py:37
  210.9 9.3 %collective-permute-start.7 = (f32[32,512]{1,0:T(8,128)S(1)}, f32[32,512]{1,0:T(8,128)S(1)}, u32[]{:S(2)}, u32[]{:S(2)}) collective-permute-start(f32[32,512]{1,0:T(8,128)S(1)} %add.129), channel_id=1, source_target_pairs={{0,4},{4,0},{1,5},{5,1},{2,6},{6,2},{3,7},{7,3},{8,12},{12,8},{9,1... | collective-permute-start | bytes 196616 | tf_op jit(solution)/shard_map/ppermute | solution.py:37
  220.1 9.8 %collective-permute-done.7 = f32[32,512]{1,0:T(8,128)S(1)} collective-permute-done((f32[32,512]{1,0:T(8,128)S(1)}, f32[32,512]{1,0:T(8,128)S(1)}, u32[]{:S(2)}, u32[]{:S(2)}) %collective-permute-start.7) | collective-permute-done | bytes 65568 | tf_op jit(solution)/shard_map/ppermute | solution.py:37
  230.0 3.7 %shard_map.95 = (bf16[8,128,512]{2,1,0:T(8,128)(2,1)S(1)}, bf16[8,128,512]{2,1,0:T(8,128)(2,1)S(1)}) custom-call(s32[8]{0:T(128)S(1)} %add_bitcast_fusion.target.source, s32[8]{0:T(128)S(1)} %get-tuple-element.21.target, s32[1]{0:T(128)} %bitcast.33.count, bf16[8,128,128]{2,1,0:T(8,128)(2,1)S(1)} %bitcast.36, ...), custom_call_target="tpu_custom_call" | custom-call | flops 134217728 | bytes 6291456 | tf_op jit(solution)/shard_map/pallas_call | solution.py:101
  233.7 1.9 collective-permute-start.9
  235.6 2.6 collective-permute-done.9
  241.3 1.9 collective-permute-start.10
  243.2 11.4 %collective-permute-done.10 = f32[32,512]{1,0:T(8,128)S(1)} collective-permute-done((f32[32,512]{1,0:T(8,128)S(1)}, f32[32,512]{1,0:T(8,128)S(1)}, u32[]{:S(2)}, u32[]{:S(2)}) %collective-permute-start.10) | collective-permute-done | bytes 65568 | tf_op jit(solution)/shard_map/ppermute | solution.py:37
  255.7 6.8 %all-to-all-start.5 = ((f32[16,32,512]{2,1,0:T(8,128)}), f32[16,32,512]{2,1,0:T(8,128)S(1)}, u32[]{:S(2)}, u32[]{:S(2)}) async-start(f32[16,32,512]{2,1,0:T(8,128)} %broadcast_in_dim.11), calls=%async_computation.5 | async-start | bytes 2097152 | tf_op jit(solution)/shard_map/all_to_all | solution.py:45
  262.7 1.9 collective-permute-start.12
  264.7 13.8 %collective-permute-done.12 = bf16[2,128,512]{2,1,0:T(8,128)(2,1)S(1)} collective-permute-done((bf16[2,128,512]{2,1,0:T(8,128)(2,1)S(1)}, bf16[2,128,512]{2,1,0:T(8,128)(2,1)S(1)}, u32[]{:S(2)}, u32[]{:S(2)}) %collective-permute-start.12) | collective-permute-done | bytes 262176 | tf_op jit(solution)/shard_map/ppermute | solution.py:37
  278.5 2.7 collective-permute-start.13
  281.2 14.7 %collective-permute-done.13 = bf16[1,128,512]{2,1,0:T(8,128)(2,1)S(1)} collective-permute-done((bf16[1,128,512]{2,1,0:T(8,128)(2,1)S(1)}, bf16[1,128,512]{2,1,0:T(8,128)(2,1)S(1)}, u32[]{:S(2)}, u32[]{:S(2)}) %collective-permute-start.13) | collective-permute-done | bytes 131104 | tf_op jit(solution)/shard_map/ppermute | solution.py:37
  (73 shorter events, 22.1 us)
Async XLA Ops:
  0.6 139.2 %copy-start = (bf16[512,512]{1,0:T(8,128)(2,1)S(1)}, bf16[512,512]{1,0:T(8,128)(2,1)}, u32[]{:S(2)}) copy-start(bf16[512,512]{1,0:T(8,128)(2,1)} %param.8) | copy-start | bytes 1572868
  0.6 65.3 %copy-start.1 = (bf16[1,1,8,128,128]{4,3,2,1,0:T(8,128)(2,1)S(1)}, bf16[1,1,8,128,128]{4,3,2,1,0:T(8,128)(2,1)}, u32[]{:S(2)}) copy-start(bf16[1,1,8,128,128]{4,3,2,1,0:T(8,128)(2,1)} %param.13) | copy-start | bytes 786436
  0.7 15.6 %copy-start.2 = (s32[1,1,8]{2,1,0:T(1,128)S(1)}, s32[1,1,8]{2,1,0:T(1,128)}, u32[]{:S(2)}) copy-start(s32[1,1,8]{2,1,0:T(1,128)} %param.11) | copy-start | bytes 100
  0.7 47.7 %copy-start.4 = (s32[1,1,8]{2,1,0:T(1,128)S(1)}, s32[1,1,8]{2,1,0:T(1,128)}, u32[]{:S(2)}) copy-start(s32[1,1,8]{2,1,0:T(1,128)} %param.10) | copy-start | bytes 100
  5.1 41.3 %all-to-all-start = ((bf16[4,136,512]{2,1,0:T(8,128)(2,1)}), bf16[4,136,512]{2,1,0:T(8,128)(2,1)S(1)}, u32[]{:S(2)}, u32[]{:S(2)}) async-start(bf16[4,136,512]{2,1,0:T(8,128)(2,1)} %broadcast_in_dim.8), calls=%async_computation | async-start | bytes 1114112 | tf_op jit(solution)/shard_map/all_to_all | solution.py:45
  46.4 15.1 %collective-permute-start = (bf16[4,136,512]{2,1,0:T(8,128)(2,1)S(1)}, bf16[4,136,512]{2,1,0:T(8,128)(2,1)S(1)}, u32[]{:S(2)}, u32[]{:S(2)}) collective-permute-start(bf16[4,136,512]{2,1,0:T(8,128)(2,1)S(1)} %all-to-all-done.refs_1_), channel_id=1, source_target_pairs={{0,64},{64,0},{1,65},{65,1},{2,66},{66,2},{3,67},{67,3},{4,68},{68... | collective-permute-start | bytes 1671176 | tf_op jit(solution)/shard_map/ppermute | solution.py:37
  48.4 15.1 %collective-permute-start.1 = (bf16[4,136,512]{2,1,0:T(8,128)(2,1)S(1)}, bf16[4,136,512]{2,1,0:T(8,128)(2,1)S(1)}, u32[]{:S(2)}, u32[]{:S(2)}) collective-permute-start(bf16[4,136,512]{2,1,0:T(8,128)(2,1)S(1)} %all-to-all-done.refs_1_), channel_id=1, source_target_pairs={{0,32},{32,0},{1,33},{33,1},{2,34},{34,2},{3,35},{35,3},{4,36},{36... | collective-permute-start | bytes 1671176 | tf_op jit(solution)/shard_map/ppermute | solution.py:37
  61.5 3.8 %collective-permute-start.2 = (bf16[4,136,512]{2,1,0:T(8,128)(2,1)S(1)}, bf16[4,136,512]{2,1,0:T(8,128)(2,1)S(1)}, u32[]{:S(2)}, u32[]{:S(2)}) collective-permute-start(bf16[4,136,512]{2,1,0:T(8,128)(2,1)S(1)} %collective-permute-done.refs_2_), channel_id=1, source_target_pairs={{0,32},{32,0},{1,33},{33,1},{2,34},{34,2},{3,35},{35,3},{4,36},{36... | collective-permute-start | bytes 1671176 | tf_op jit(solution)/shard_map/ppermute | solution.py:37
  104.6 34.7 %all-to-all-start.2 = ((bf16[16,128,512]{2,1,0:T(8,128)(2,1)}), bf16[16,128,512]{2,1,0:T(8,128)(2,1)S(1)}, u32[]{:S(2)}, u32[]{:S(2)}) async-start(bf16[16,128,512]{2,1,0:T(8,128)(2,1)} %get-tuple-element.13), calls=%async_computation.2 | async-start | bytes 4194304 | tf_op jit(solution)/shard_map/all_to_all | solution.py:45
  110.6 30.2 %copy-start.3 = (bf16[128,512]{1,0:T(8,128)(2,1)S(1)}, bf16[128,512]{1,0:T(8,128)(2,1)}, u32[]{:S(2)}) copy-start(bf16[128,512]{1,0:T(8,128)(2,1)} %param.9) | copy-start | bytes 393220
  110.6 29.0 %collective-permute-start.3 = (bf16[128,512]{1,0:T(8,128)(2,1)S(1)}, bf16[128,512]{1,0:T(8,128)(2,1)S(1)}, u32[]{:S(2)}, u32[]{:S(2)}) collective-permute-start(bf16[128,512]{1,0:T(8,128)(2,1)S(1)} %reduce_sum.98), channel_id=1, source_target_pairs={{0,4},{4,0},{1,5},{5,1},{2,6},{6,2},{3,7},{7,3},{8,12},{12,8},{9,1... | collective-permute-start | bytes 393224 | tf_op jit(solution)/shard_map/ppermute | solution.py:37
  143.6 42.2 %all-to-all-start.3 = ((bf16[16,160,512]{2,1,0:T(8,128)(2,1)}), bf16[16,160,512]{2,1,0:T(8,128)(2,1)S(1)}, u32[]{:S(2)}, u32[]{:S(2)}) async-start(bf16[16,160,512]{2,1,0:T(8,128)(2,1)} %pad_maximum_fusion), calls=%async_computation.3 | async-start | bytes 5242880 | tf_op jit(solution)/shard_map/all_to_all | solution.py:45
  148.8 23.4 %collective-permute-start.8 = (bf16[128,512]{1,0:T(8,128)(2,1)S(1)}, bf16[128,512]{1,0:T(8,128)(2,1)}, u32[]{:S(2)}, u32[]{:S(2)}) collective-permute-start(bf16[128,512]{1,0:T(8,128)(2,1)S(1)} %multiply_convert_fusion), channel_id=1, source_target_pairs={{0,4},{4,0},{1,5},{5,1},{2,6},{6,2},{3,7},{7,3},{8,12},{12,8},{9,1... | collective-permute-start | bytes 393224 | tf_op jit(solution)/shard_map/ppermute | solution.py:37
  188.2 41.7 %all-to-all-start.4 = ((bf16[16,128,512]{2,1,0:T(8,128)(2,1)}), bf16[16,128,512]{2,1,0:T(8,128)(2,1)}, u32[]{:S(2)}, u32[]{:S(2)}) async-start(bf16[16,128,512]{2,1,0:T(8,128)(2,1)} %broadcast_in_dim.10), calls=%async_computation.4 | async-start | bytes 4194304 | tf_op jit(solution)/shard_map/all_to_all | solution.py:45
  193.9 3.1 %collective-permute-start.4 = (f32[32,512]{1,0:T(8,128)S(1)}, f32[32,512]{1,0:T(8,128)S(1)}, u32[]{:S(2)}, u32[]{:S(2)}) collective-permute-start(f32[32,512]{1,0:T(8,128)S(1)} %convert_reduce_fusion.1), channel_id=1, source_target_pairs={{0,32},{32,0},{1,33},{33,1},{2,34},{34,2},{3,35},{35,3},{4,36},{36... | collective-permute-start | bytes 196616 | tf_op jit(solution)/shard_map/ppermute | solution.py:37
  197.1 6.2 %collective-permute-start.5 = (f32[32,512]{1,0:T(8,128)S(1)}, f32[32,512]{1,0:T(8,128)S(1)}, u32[]{:S(2)}, u32[]{:S(2)}) collective-permute-start(f32[32,512]{1,0:T(8,128)S(1)} %add.127), channel_id=1, source_target_pairs={{0,64},{64,0},{1,65},{65,1},{2,66},{66,2},{3,67},{67,3},{4,68},{68... | collective-permute-start | bytes 196616 | tf_op jit(solution)/shard_map/ppermute | solution.py:37
  203.3 7.6 %collective-permute-start.6 = (f32[32,512]{1,0:T(8,128)S(1)}, f32[32,512]{1,0:T(8,128)S(1)}, u32[]{:S(2)}, u32[]{:S(2)}) collective-permute-start(f32[32,512]{1,0:T(8,128)S(1)} %add.128), channel_id=1, source_target_pairs={{0,128},{128,0},{1,129},{129,1},{2,130},{130,2},{3,131},{131,3},{4... | collective-permute-start | bytes 196616 | tf_op jit(solution)/shard_map/ppermute | solution.py:37
  210.9 19.1 %collective-permute-start.7 = (f32[32,512]{1,0:T(8,128)S(1)}, f32[32,512]{1,0:T(8,128)S(1)}, u32[]{:S(2)}, u32[]{:S(2)}) collective-permute-start(f32[32,512]{1,0:T(8,128)S(1)} %add.129), channel_id=1, source_target_pairs={{0,4},{4,0},{1,5},{5,1},{2,6},{6,2},{3,7},{7,3},{8,12},{12,8},{9,1... | collective-permute-start | bytes 196616 | tf_op jit(solution)/shard_map/ppermute | solution.py:37
  233.7 4.6 %collective-permute-start.9 = (bf16[8,128,512]{2,1,0:T(8,128)(2,1)S(1)}, bf16[8,128,512]{2,1,0:T(8,128)(2,1)S(1)}, u32[]{:S(2)}, u32[]{:S(2)}) collective-permute-start(bf16[8,128,512]{2,1,0:T(8,128)(2,1)S(1)} %get-tuple-element.17), channel_id=1, source_target_pairs={{0,32},{32,0},{1,33},{33,1},{2,34},{34,2},{3,35},{35,3},{4,36},{36... | collective-permute-start | bytes 3145736 | tf_op jit(solution)/shard_map/ppermute | solution.py:37
  239.3 23.2 %collective-permute-start.11 = (bf16[4,128,512]{2,1,0:T(8,128)(2,1)}, bf16[4,128,512]{2,1,0:T(8,128)(2,1)S(1)}, u32[]{:S(2)}, u32[]{:S(2)}) collective-permute-start(bf16[4,128,512]{2,1,0:T(8,128)(2,1)} %slice.52), channel_id=1, source_target_pairs={{0,64},{64,0},{1,65},{65,1},{2,66},{66,2},{3,67},{67,3},{4,68},{68... | collective-permute-start | bytes 1572872 | tf_op jit(solution)/shard_map/ppermute | solution.py:37
  241.3 13.4 %collective-permute-start.10 = (f32[32,512]{1,0:T(8,128)S(1)}, f32[32,512]{1,0:T(8,128)S(1)}, u32[]{:S(2)}, u32[]{:S(2)}) collective-permute-start(f32[32,512]{1,0:T(8,128)S(1)} %add_multiply_fusion), channel_id=1, source_target_pairs={{0,256},{256,0},{1,257},{257,1},{2,258},{258,2},{3,259},{259,3},{4... | collective-permute-start | bytes 196616 | tf_op jit(solution)/shard_map/ppermute | solution.py:37
  255.7 41.0 %all-to-all-start.5 = ((f32[16,32,512]{2,1,0:T(8,128)}), f32[16,32,512]{2,1,0:T(8,128)S(1)}, u32[]{:S(2)}, u32[]{:S(2)}) async-start(f32[16,32,512]{2,1,0:T(8,128)} %broadcast_in_dim.11), calls=%async_computation.5 | async-start | bytes 2097152 | tf_op jit(solution)/shard_map/all_to_all | solution.py:45
  262.7 15.7 %collective-permute-start.12 = (bf16[2,128,512]{2,1,0:T(8,128)(2,1)S(1)}, bf16[2,128,512]{2,1,0:T(8,128)(2,1)S(1)}, u32[]{:S(2)}, u32[]{:S(2)}) collective-permute-start(bf16[2,128,512]{2,1,0:T(8,128)(2,1)S(1)} %slice.54), channel_id=1, source_target_pairs={{0,128},{128,0},{1,129},{129,1},{2,130},{130,2},{3,131},{131,3},{4... | collective-permute-start | bytes 786440 | tf_op jit(solution)/shard_map/ppermute | solution.py:37
  278.5 17.4 %collective-permute-start.13 = (bf16[1,128,512]{2,1,0:T(8,128)(2,1)S(1)}, bf16[1,128,512]{2,1,0:T(8,128)(2,1)S(1)}, u32[]{:S(2)}, u32[]{:S(2)}) collective-permute-start(bf16[1,128,512]{2,1,0:T(8,128)(2,1)S(1)} %slice.56), channel_id=1, source_target_pairs={{0,256},{256,0},{1,257},{257,1},{2,258},{258,2},{3,259},{259,3},{4... | collective-permute-start | bytes 393224 | tf_op jit(solution)/shard_map/ppermute | solution.py:37

commit v9 on v8

--- a/solution.py
+++ b/solution.py
@@ -13,6 +13,7 @@
 Z4 = ("za", "zb")
 ROW = ("za", "zb", "z1", "core")
 PLANE = ("y", "x")
+CHUNKS = 2
 BF16 = jnp.bfloat16
 F32 = jnp.float32
 
@@ -58,45 +59,50 @@
     total[...] = jnp.zeros_like(total)
     for slot in range(slots):
 
-        def add(block):
+        def add(block, left):
             if scaled:
                 row = jnp.broadcast_to(scale[slot : slot + 1, :], (size, size))
                 column = jnp.transpose(row)
                 lanes = [block[:, i : i + size] for i in range(0, block.shape[1], size)]
                 lanes = [(part.astype(F32) * column).astype(BF16) for part in lanes]
                 block = jnp.concatenate(lanes, axis=1)
-            total[target[slot]] += lax.dot_general(
+            total[target[slot], :, left : left + block.shape[1]] += lax.dot_general(
                 tiles[slot], block, (((axis,), (0,)), ((), ())), preferred_element_type=F32
             )
 
         first = 0
-        for pieces in sources:
-            held = arrays[pieces[0][0]].shape[0]
+        for chunks in sources:
+            held = arrays[chunks[0][0][0]].shape[0]
             inside = source[slot] - first
             first += held
 
             @pl.when((slot < count[0]) & (inside >= 0) & (inside < held))
-            def _(pieces=pieces, inside=jnp.clip(inside, 0, held - 1)):
-                rows = [arrays[number][inside, low:high, :] for number, low, high in pieces]
-                add(rows[0] if len(rows) == 1 else jnp.concatenate(rows, axis=0))
-
-    for output, pieces in zip(outputs, places):
+            def _(chunks=chunks, inside=jnp.clip(inside, 0, held - 1)):
+                left = 0
+                for pieces in chunks:
+                    rows = [arrays[number][inside, low:high, :] for number, low, high in pieces]
+                    block = rows[0] if len(rows) == 1 else jnp.concatenate(rows, axis=0)
+                    add(block, left)
+                    left += block.shape[1]
+
+    for output, (left, right, pieces) in zip(outputs, places):
         row = 0
         for start, stop, low, high in pieces:
-            output[:, row : row + high - low, :] = total[start:stop, low:high, :].astype(BF16)
+            part = total[start:stop, low:high, left:right]
+            output[:, row : row + high - low, :] = part.astype(BF16)
             row += high - low
 
 
 def tile_sums(transposed, source, target, count, tiles, scale, arrays, sources, places, blocks):
     slots, size, _ = tiles.shape
-    width = arrays[0].shape[2]
+    width = sum(arrays[pieces[0][0]].shape[2] for pieces in sources[0])
     smem = pl.BlockSpec(memory_space=pltpu.SMEM)
     vmem = pl.BlockSpec(memory_space=pltpu.VMEM)
     scaled = scale is not None
     operands = [tiles] + [scale] * scaled + list(arrays)
     shapes = [
-        (pieces[0][1] - pieces[0][0], sum(high - low for _, _, low, high in pieces), width)
-        for pieces in places
+        (pieces[0][1] - pieces[0][0], sum(high - low for _, _, low, high in pieces), right - left)
+        for left, right, pieces in places
     ]
     return pl.pallas_call(
         functools.partial(tile_kernel, transposed, scaled, sources, places),
@@ -129,9 +135,8 @@
     row_index = tile_rows[0, 0]
     col_index = tile_cols[0, 0]
     col_bits = col_index ^ my_row
-    col_near = (col_bits & 1) * n_line + (col_bits & 2) * (n_z4 // 2)
-    col_from = col_near + (col_index >> 2)
-    col_to = col_near + ((col_bits >> 2) & 1) * 2 + (col_bits >> 3)
+    col_place = (col_bits & 1) * n_line + (col_bits & 2) * (n_z4 // 2)
+    col_place = col_place + ((col_bits >> 2) & 1) * 2 + (col_bits >> 3)
     row_plane = (row_index >> 3) * n_x + (row_index & 3)
     row_place = (((row_index >> 2) & 1) ^ my_zh) * n_plane + row_plane
 
@@ -140,28 +145,33 @@
     col_sums = jnp.sum(tiles, axis=1, dtype=F32) * alive[:, None]
     degree_terms = jnp.einsum("sc,sj->cj", order_cols, col_sums, precision=lax.Precision.HIGHEST)
     high = lax.reduce_precision(degree_terms, 8, 7)
-    pieces = jnp.stack([high, degree_terms - high]).astype(BF16).reshape(-1, width)
-    own_line = swap_parts(copies_of(jnp.concatenate([features, pieces]), Z4), Z4)
-    own_pair = flip(own_line, "z1")
-    blocks = [own_line, own_pair, flip(own_line, "core"), flip(own_pair, "core")]
+    pieces = jnp.stack([high, degree_terms - high]).astype(BF16)
+    chunk = width // CHUNKS
+    parts = [slice(c * chunk, (c + 1) * chunk) for c in range(CHUNKS)]
+    held = [features[None, :, part] for part in parts]
+    held[0] = jnp.concatenate([held[0], pieces.reshape(1, -1, chunk)], axis=1)
+    for axis in Z4:
+        held = [jnp.concatenate([part, flip(part, axis)]) for part in held]
+    pairs = [flip(part, "z1") for part in held]
+    groups = [held, pairs] + [[flip(part, "core") for part in group] for group in (held, pairs)]
 
     def degrees(part):
         return jnp.sum(part[:, span:].astype(F32).reshape(-1, n_row, span), axis=0)
 
-    col_scale = lax.rsqrt(1.0 + sum(degrees(part) for part in blocks))
+    col_scale = lax.rsqrt(1.0 + sum(degrees(group[0]) for group in groups))
     own_scale = lax.dynamic_index_in_dim(col_scale, my_row, axis=0, keepdims=False)
     slot_scale = col_scale[col_index]
 
     near_terms, far_terms = tile_sums(
         False,
-        col_from,
+        col_place,
         row_place,
         count,
         tiles,
         slot_scale,
-        blocks,
-        [[(number, 0, span)] for number in range(4)],
-        [[(0, n_plane, 0, span)], [(n_plane, n_col, 0, span)]],
+        sum(groups, []),
+        [[[(g * CHUNKS + c, 0, span)] for c in range(CHUNKS)] for g in range(len(groups))],
+        [(0, width, [(0, n_plane, 0, span)]), (0, width, [(n_plane, n_col, 0, span)])],
         n_col,
     )
     far_sum = jnp.sum(swap_parts(far_terms, PLANE).astype(F32), axis=0).astype(BF16)
@@ -170,43 +180,50 @@
 
     output, normed, grad_pre, grad_own = layer_rows(own_total, cotangent, weight)
 
+    half = span // 2
     weight_terms = jnp.einsum("nf,ng->fg", normed, grad_pre, preferred_element_type=F32)
     weight_parts = weight_terms.astype(BF16).reshape(n_plane, width // n_plane, width)
-    near_group = swap_parts(
-        jnp.concatenate([copies_of(grad_own, PLANE), weight_parts], axis=1), PLANE
-    )
-    far_group = swap_parts(copies_of(after(flip(grad_own, "zh"), near_group), PLANE), PLANE)
-
-    line_rows = jnp.sum(near_group[:, span:].astype(F32), axis=0)
-    for axis in ("core", "z1", "zb", "zh"):
+    first_group = swap_parts(
+        jnp.concatenate([copies_of(grad_own[:half], PLANE), weight_parts], axis=1), PLANE
+    )
+    grad_rest = jnp.concatenate([grad_own[half:], flip(grad_own, "zh")])
+    last_group = swap_parts(copies_of(after(grad_rest, first_group), PLANE), PLANE)
+
+    line_rows = jnp.sum(first_group[:, half:].astype(F32), axis=0)
+    for axis in ("core", "z1", "zb", "za", "zh"):
         line_rows = line_rows + flip(line_rows, axis)
     line_rows = line_rows * (1.0 / math.sqrt(nodes))
-    far_group = after(far_group, line_rows)
-
-    near, far = tile_sums(
+    last_group = after(last_group, line_rows)
+
+    halves = tile_sums(
         True,
         row_place,
-        col_to,
+        col_place,
         count,
         tiles,
         None,
-        [near_group, far_group],
-        [[(0, 0, span)], [(1, 0, span)]],
-        [[(0, n_line, 0, span)], [(n_line, n_row, 0, span)]],
+        [first_group, last_group],
+        [[[(0, 0, half), (1, 0, half)]], [[(1, half, half + span)]]],
+        [
+            (part.start, part.stop, [(first, first + n_line, 0, span)])
+            for first in (0, n_line)
+            for part in parts
+        ],
         n_row,
     )
-    core_sum = (near.astype(F32) + flip(far, "core").astype(F32)).astype(BF16)
-
-    def halve(total, axis):
-        half = total.shape[0] // 2
-        return total[:half].astype(F32) + flip(total[half:], axis).astype(F32)
-
-    line_rows = after(line_rows, core_sum)
-    line_rows = line_rows + flip(line_rows, "za")
-    pair_sum = halve(core_sum, "z1").astype(BF16)
+    totals = [
+        keep.astype(F32) + flip(send, "core").astype(F32)
+        for keep, send in zip(halves[:CHUNKS], halves[CHUNKS:])
+    ]
+    line_rows = after(line_rows, *totals)
     weight_grad = swap_parts(copies_of(line_rows, PLANE), PLANE).reshape(width, width)
-    quad_sum = halve(pair_sum, "zb").astype(BF16)
-    feature_grad = halve(quad_sum, "za")[0] * own_scale[:, None]
+    for axis in ("z1", "zb", "za"):
+        totals = [total.astype(BF16) for total in totals]
+        size = totals[0].shape[0] // 2
+        totals = [
+            total[:size].astype(F32) + flip(total[size:], axis).astype(F32) for total in totals
+        ]
+    feature_grad = jnp.concatenate([total[0] for total in totals], axis=1) * own_scale[:, None]
     return (output, weight_grad, feature_grad)
 
 

time: 300 us -> 285 us (0.950)
  waiting for transfers between devices: 153 us -> 82.1 us
  starting transfers between devices: 85.2 us -> 136 us
  other arithmetic: 6.13 us -> 9.97 us
    ppermute x14 -> x25, starting transfers between devices: 50.5 us -> 111 us  [flip(): return lax.ppermute(block, axis, [(0, 1), (1, 0)])]
    all_to_all x5 -> x4, waiting for transfers between devices: 62.6 us -> 26.6 us  [swap_parts(): return lax.all_to_all(parts, axes, split_axis=0, concat_axis=0, tiled=True)]
    ppermute x14 -> x25, waiting for transfers between devices: 90.2 us -> 55.5 us  [flip(): return lax.ppermute(block, axis, [(0, 1), (1, 0)])]
    all_to_all x5 -> x4, starting transfers between devices: 34.8 us -> 25 us  [swap_parts(): return lax.all_to_all(parts, axes, split_axis=0, concat_axis=0, tiled=True)]
    convert_element_type x3 -> x6, other arithmetic: 0.51 us -> 3.54 us  [local(): totals = [total.astype(BF16) for total in totals]]
  transfers between devices with their start and end apart: 19 -> 29, of which waited for: 14 -> 18; matrix products, arithmetic and copies ran while one was open for 1% -> 3% of each run, Pallas kernels for 0% -> 0%
where the time goes in v9:
time: 285 us; the launch traced here: 283 us
  starting transfers between devices  136 us (48%)
  waiting for transfers between devices  82.1 us (29%)
  blocking collectives  33.4 us (12%)
  Pallas kernels  10.1 us (4%)
  other arithmetic  9.97 us (3%)
  local copies, waits for them, and re-layouts  6.54 us (2%)
    ppermute x25, starting transfers between devices, flip(): return lax.ppermute(block, axis, [(0, 1), (1, 0)])  111 us
    ppermute x25, waiting for transfers between devices, flip(): return lax.ppermute(block, axis, [(0, 1), (1, 0)])  55.5 us
    all_to_all x1, blocking collectives, swap_parts(): return lax.all_to_all(parts, axes, split_axis=0, concat_axis=0, tiled=True)  33.4 us
    all_to_all x4, waiting for transfers between devices, swap_parts(): return lax.all_to_all(parts, axes, split_axis=0, concat_axis=0, tiled=True)  26.6 us
    all_to_all x4, starting transfers between devices, swap_parts(): return lax.all_to_all(parts, axes, split_axis=0, concat_axis=0, tiled=True)  25 us
    pallas_call x2, Pallas kernels, tile_sums(): pl.pallas_call(functools.partial(tile_kernel, transposed, scaled, sources...  10.1 us
  transfers between devices with their start and end apart: 29, of which 18 were waited for; matrix products, arithmetic and copies ran while one was open for 3% of the time, Pallas kernels for 0%

profile of v9, /device:TPU:24, one launch (start us, length us, event | category | flops | bytes accessed | tf_op | source)
XLA Modules:
  0.0 282.6 jit_solution(51320749754502160)
XLA Ops:
  4.2 9.1 %collective-permute-start = (bf16[1,144,256]{2,1,0:T(8,128)(2,1)S(1)}, bf16[1,144,256]{2,1,0:T(8,128)(2,1)S(1)}, u32[]{:S(2)}, u32[]{:S(2)}) collective-permute-start(bf16[1,144,256]{2,1,0:T(8,128)(2,1)S(1)} %pad_maximum_fusion.6), channel_id=1, source_target_pairs={{0,256},{256,0},{1,257},{257,1},{2,258},{258,2},{3,259},{259,3},{4... | collective-permute-start | bytes 221192 | tf_op jit(solution)/shard_map/ppermute | solution.py:38
  16.6 11.0 %collective-permute-done.5 = bf16[1,128,256]{2,1,0:T(8,128)(2,1)S(1)} collective-permute-done((bf16[1,128,256]{2,1,0:T(8,128)(2,1)S(1)}, bf16[1,128,256]{2,1,0:T(8,128)(2,1)S(1)}, u32[]{:S(2)}, u32[]{:S(2)}) %collective-permute-start.5) | collective-permute-done | bytes 65568 | tf_op jit(solution)/shard_map/ppermute | solution.py:38
  29.5 4.8 %collective-permute-start.1 = (bf16[2,144,256]{2,1,0:T(8,128)(2,1)S(1)}, bf16[2,144,256]{2,1,0:T(8,128)(2,1)S(1)}, u32[]{:S(2)}, u32[]{:S(2)}) collective-permute-start(bf16[2,144,256]{2,1,0:T(8,128)(2,1)S(1)} %pad_maximum_fusion.4), channel_id=1, source_target_pairs={{0,128},{128,0},{1,129},{129,1},{2,130},{130,2},{3,131},{131,3},{4... | collective-permute-start | bytes 442376 | tf_op jit(solution)/shard_map/ppermute | solution.py:38
  35.0 5.2 %collective-permute-done.6 = bf16[2,128,256]{2,1,0:T(8,128)(2,1)S(1)} collective-permute-done((bf16[2,128,256]{2,1,0:T(8,128)(2,1)S(1)}, bf16[2,128,256]{2,1,0:T(8,128)(2,1)S(1)}, u32[]{:S(2)}, u32[]{:S(2)}) %collective-permute-start.6) | collective-permute-done | bytes 131104 | tf_op jit(solution)/shard_map/ppermute | solution.py:38
  42.2 3.9 %collective-permute-start.2 = (bf16[4,144,256]{2,1,0:T(8,128)(2,1)S(1)}, bf16[4,144,256]{2,1,0:T(8,128)(2,1)S(1)}, u32[]{:S(2)}, u32[]{:S(2)}) collective-permute-start(bf16[4,144,256]{2,1,0:T(8,128)(2,1)S(1)} %pad_maximum_fusion.1.refs_1_), channel_id=1, source_target_pairs={{0,64},{64,0},{1,65},{65,1},{2,66},{66,2},{3,67},{67,3},{4,68},{68... | collective-permute-start | bytes 884744 | tf_op jit(solution)/shard_map/ppermute | solution.py:38
  48.1 2.4 collective-permute-start.3
  58.1 5.1 %shard_map.94 = (bf16[16,128,512]{2,1,0:T(8,128)(2,1)}, bf16[16,128,512]{2,1,0:T(8,128)(2,1)S(1)}) custom-call(s32[8]{0:T(128)S(1)} %shift-right-arithmetic_add_fusion.source.target, s32[8]{0:T(128)S(1)} %add_bitcast_fusion.2.target.source, s32[1]{0:T(128)} %bitcast.32.count, bf16[8,128,128]{2,1,0:T(8,128)(2,1)S(1)} %bitcast.35, f32[8,128]{1,0:T(8,128)S(1)} %gather_fusion, ...), custom_call_target="tpu_custom_call" | custom-call | flops 134217728 | bytes 12582912 | tf_op jit(solution)/shard_map/pallas_call | solution.py:107
  63.3 33.4 %all_to_all.25 = bf16[16,128,512]{2,1,0:T(8,128)(2,1)S(1)} all-to-all(bf16[16,128,512]{2,1,0:T(8,128)(2,1)S(1)} %get-tuple-element.14), channel_id=1, replica_groups=mesh['za'=2,'zb'=2,'z1'=2,'core'=2,'y'=4,'zh'=2,'x'=4] {'y','x'}, dimensions={0} | all-to-all | bytes 4194304 | tf_op jit(solution)/shard_map/all_to_all | solution.py:46
  96.9 6.0 %all-to-all-start.1 = ((bf16[16,128,512]{2,1,0:T(8,128)(2,1)}), bf16[16,128,512]{2,1,0:T(8,128)(2,1)S(1)}, u32[]{:S(2)}, u32[]{:S(2)}) async-start(bf16[16,128,512]{2,1,0:T(8,128)(2,1)} %get-tuple-element.15), calls=%async_computation.1 | async-start | bytes 4194304 | tf_op jit(solution)/shard_map/all_to_all | solution.py:46
  102.9 12.8 %collective-permute-start.10 = (bf16[128,512]{1,0:T(8,128)(2,1)S(1)}, bf16[128,512]{1,0:T(8,128)(2,1)S(1)}, u32[]{:S(2)}, u32[]{:S(2)}) collective-permute-start(bf16[128,512]{1,0:T(8,128)(2,1)S(1)} %reduce_sum.98), channel_id=1, source_target_pairs={{0,4},{4,0},{1,5},{5,1},{2,6},{6,2},{3,7},{7,3},{8,12},{12,8},{9,1... | collective-permute-start | bytes 393224 | tf_op jit(solution)/shard_map/ppermute | solution.py:38
  115.7 15.5 %all-to-all-done.1 = bf16[16,128,512]{2,1,0:T(8,128)(2,1)S(1)} async-done(((bf16[16,128,512]{2,1,0:T(8,128)(2,1)}), bf16[16,128,512]{2,1,0:T(8,128)(2,1)S(1)}, u32[]{:S(2)}, u32[]{:S(2)}) %all-to-all-start.1) | async-done | bytes 2097184 | tf_op jit(solution)/shard_map/all_to_all | solution.py:46
  135.1 5.3 %all-to-all-start.2 = ((bf16[16,96,512]{2,1,0:T(8,128)(2,1)}), bf16[16,96,512]{2,1,0:T(8,128)(2,1)S(1)}, u32[]{:S(2)}, u32[]{:S(2)}) async-start(bf16[16,96,512]{2,1,0:T(8,128)(2,1)} %pad_maximum_fusion), calls=%async_computation.2 | async-start | bytes 3145728 | tf_op jit(solution)/shard_map/all_to_all | solution.py:46
  140.3 12.3 %collective-permute-start.16 = (bf16[128,512]{1,0:T(8,128)(2,1)S(1)}, bf16[128,512]{1,0:T(8,128)(2,1)S(1)}, u32[]{:S(2)}, u32[]{:S(2)}) collective-permute-start(bf16[128,512]{1,0:T(8,128)(2,1)S(1)} %multiply_convert_fusion), channel_id=1, source_target_pairs={{0,4},{4,0},{1,5},{5,1},{2,6},{6,2},{3,7},{7,3},{8,12},{12,8},{9,1... | collective-permute-start | bytes 393224 | tf_op jit(solution)/shard_map/ppermute | solution.py:38
  152.6 3.5 %collective-permute-done.16 = bf16[128,512]{1,0:T(8,128)(2,1)S(1)} collective-permute-done((bf16[128,512]{1,0:T(8,128)(2,1)S(1)}, bf16[128,512]{1,0:T(8,128)(2,1)S(1)}, u32[]{:S(2)}, u32[]{:S(2)}) %collective-permute-start.16) | collective-permute-done | bytes 131104 | tf_op jit(solution)/shard_map/ppermute | solution.py:38
  156.1 5.2 %all-to-all-done.2.refs_0_ = bf16[16,96,512]{2,1,0:T(8,128)(2,1)S(1)} async-done(((bf16[16,96,512]{2,1,0:T(8,128)(2,1)}), bf16[16,96,512]{2,1,0:T(8,128)(2,1)S(1)}, u32[]{:S(2)}, u32[]{:S(2)}) %all-to-all-start.2) | async-done | bytes 1572896 | tf_op jit(solution)/shard_map/all_to_all | solution.py:46
  163.3 6.5 %all-to-all-start.3 = ((bf16[16,192,512]{2,1,0:T(8,128)(2,1)}), bf16[16,192,512]{2,1,0:T(8,128)(2,1)}, u32[]{:S(2)}, u32[]{:S(2)}) async-start(bf16[16,192,512]{2,1,0:T(8,128)(2,1)} %broadcast_in_dim.13), calls=%async_computation.3 | async-start | bytes 6291456 | tf_op jit(solution)/shard_map/all_to_all | solution.py:46
  173.1 5.8 %collective-permute-start.12 = (f32[32,512]{1,0:T(8,128)S(1)}, f32[32,512]{1,0:T(8,128)S(1)}, u32[]{:S(2)}, u32[]{:S(2)}) collective-permute-start(f32[32,512]{1,0:T(8,128)S(1)} %add.137), channel_id=1, source_target_pairs={{0,64},{64,0},{1,65},{65,1},{2,66},{66,2},{3,67},{67,3},{4,68},{68... | collective-permute-start | bytes 196616 | tf_op jit(solution)/shard_map/ppermute | solution.py:38
  178.9 2.4 collective-permute-done.12
  183.3 5.6 %collective-permute-done.13 = f32[32,512]{1,0:T(8,128)S(1)} collective-permute-done((f32[32,512]{1,0:T(8,128)S(1)}, f32[32,512]{1,0:T(8,128)S(1)}, u32[]{:S(2)}, u32[]{:S(2)}) %collective-permute-start.13) | collective-permute-done | bytes 65568 | tf_op jit(solution)/shard_map/ppermute | solution.py:38
  188.8 6.3 %collective-permute-start.14 = (f32[32,512]{1,0:T(8,128)S(1)}, f32[32,512]{1,0:T(8,128)S(1)}, u32[]{:S(2)}, u32[]{:S(2)}) collective-permute-start(f32[32,512]{1,0:T(8,128)S(1)} %add.139), channel_id=1, source_target_pairs={{0,256},{256,0},{1,257},{257,1},{2,258},{258,2},{3,259},{259,3},{4... | collective-permute-start | bytes 196616 | tf_op jit(solution)/shard_map/ppermute | solution.py:38
  195.2 6.5 %collective-permute-done.14 = f32[32,512]{1,0:T(8,128)S(1)} collective-permute-done((f32[32,512]{1,0:T(8,128)S(1)}, f32[32,512]{1,0:T(8,128)S(1)}, u32[]{:S(2)}, u32[]{:S(2)}) %collective-permute-start.14) | collective-permute-done | bytes 65568 | tf_op jit(solution)/shard_map/ppermute | solution.py:38
  201.7 12.0 %collective-permute-start.15 = (f32[32,512]{1,0:T(8,128)S(1)}, f32[32,512]{1,0:T(8,128)S(1)}, u32[]{:S(2)}, u32[]{:S(2)}) collective-permute-start(f32[32,512]{1,0:T(8,128)S(1)} %add.140), channel_id=1, source_target_pairs={{0,4},{4,0},{1,5},{5,1},{2,6},{6,2},{3,7},{7,3},{8,12},{12,8},{9,1... | collective-permute-start | bytes 196616 | tf_op jit(solution)/shard_map/ppermute | solution.py:38
  213.7 5.0 %collective-permute-done.15 = f32[32,512]{1,0:T(8,128)S(1)} collective-permute-done((f32[32,512]{1,0:T(8,128)S(1)}, f32[32,512]{1,0:T(8,128)S(1)}, u32[]{:S(2)}, u32[]{:S(2)}) %collective-permute-start.15) | collective-permute-done | bytes 65568 | tf_op jit(solution)/shard_map/ppermute | solution.py:38
  218.7 4.9 %shard_map.95 = (bf16[8,128,256]{2,1,0:T(8,128)(2,1)S(1)}, bf16[8,128,256]{2,1,0:T(8,128)(2,1)S(1)}, bf16[8,128,256]{2,1,0:T(8,128)(2,1)}, bf16[8,128,256]{2,1,0:T(8,128)(2,1)S(1)}) custom-call(s32[8]{0:T(128)S(1)} %add_bitcast_fusion.2.target.source, s32[8]{0:T(128)S(1)} %shift-right-arithmetic_add_fusion.source.target, s32[1]{0:T(128)} %bitcast.33.count, ...), custom_call_target="tpu_custom_call" | custom-call | flops 134217728 | bytes 6291456 | tf_op jit(solution)/shard_map/pallas_call | solution.py:107
  227.6 7.2 %all-to-all-start.4 = ((f32[16,32,512]{2,1,0:T(8,128)}), f32[16,32,512]{2,1,0:T(8,128)S(1)}, u32[]{:S(2)}, u32[]{:S(2)}) async-start(f32[16,32,512]{2,1,0:T(8,128)} %broadcast_in_dim.14), calls=%async_computation.4 | async-start | bytes 2097152 | tf_op jit(solution)/shard_map/all_to_all | solution.py:46
  241.2 3.9 %collective-permute-start.22 = (bf16[4,128,256]{2,1,0:T(8,128)(2,1)S(1)}, bf16[4,128,256]{2,1,0:T(8,128)(2,1)S(1)}, u32[]{:S(2)}, u32[]{:S(2)}) collective-permute-start(bf16[4,128,256]{2,1,0:T(8,128)(2,1)S(1)} %slice.100), channel_id=1, source_target_pairs={{0,64},{64,0},{1,65},{65,1},{2,66},{66,2},{3,67},{67,3},{4,68},{68... | collective-permute-start | bytes 786440 | tf_op jit(solution)/shard_map/ppermute | solution.py:38
  245.1 5.9 %all-to-all-done.4 = f32[16,32,512]{2,1,0:T(8,128)S(1)} async-done(((f32[16,32,512]{2,1,0:T(8,128)}), f32[16,32,512]{2,1,0:T(8,128)S(1)}, u32[]{:S(2)}, u32[]{:S(2)}) %all-to-all-start.4) | async-done | bytes 1048608 | tf_op jit(solution)/shard_map/all_to_all | solution.py:46
  254.3 4.6 %collective-permute-start.23 = (bf16[2,128,256]{2,1,0:T(8,128)(2,1)S(1)}, bf16[2,128,256]{2,1,0:T(8,128)(2,1)S(1)}, u32[]{:S(2)}, u32[]{:S(2)}) collective-permute-start(bf16[2,128,256]{2,1,0:T(8,128)(2,1)S(1)} %slice.102), channel_id=1, source_target_pairs={{0,128},{128,0},{1,129},{129,1},{2,130},{130,2},{3,131},{131,3},{4... | collective-permute-start | bytes 393224 | tf_op jit(solution)/shard_map/ppermute | solution.py:38
  258.9 5.2 %collective-permute-done.20 = bf16[2,128,256]{2,1,0:T(8,128)(2,1)S(1)} collective-permute-done((bf16[2,128,256]{2,1,0:T(8,128)(2,1)S(1)}, bf16[2,128,256]{2,1,0:T(8,128)(2,1)S(1)}, u32[]{:S(2)}, u32[]{:S(2)}) %collective-permute-start.20) | collective-permute-done | bytes 131104 | tf_op jit(solution)/shard_map/ppermute | solution.py:38
  264.1 5.5 %collective-permute-start.21 = (bf16[1,128,256]{2,1,0:T(8,128)(2,1)S(1)}, bf16[1,128,256]{2,1,0:T(8,128)(2,1)S(1)}, u32[]{:S(2)}, u32[]{:S(2)}) collective-permute-start(bf16[1,128,256]{2,1,0:T(8,128)(2,1)S(1)} %slice.98), channel_id=1, source_target_pairs={{0,256},{256,0},{1,257},{257,1},{2,258},{258,2},{3,259},{259,3},{4... | collective-permute-start | bytes 196616 | tf_op jit(solution)/shard_map/ppermute | solution.py:38
  269.7 4.3 %collective-permute-start.24 = (bf16[1,128,256]{2,1,0:T(8,128)(2,1)S(1)}, bf16[1,128,256]{2,1,0:T(8,128)(2,1)S(1)}, u32[]{:S(2)}, u32[]{:S(2)}) collective-permute-start(bf16[1,128,256]{2,1,0:T(8,128)(2,1)S(1)} %slice.104), channel_id=1, source_target_pairs={{0,256},{256,0},{1,257},{257,1},{2,258},{258,2},{3,259},{259,3},{4... | collective-permute-start | bytes 196616 | tf_op jit(solution)/shard_map/ppermute | solution.py:38
  276.1 4.6 %collective-permute-done.24 = bf16[1,128,256]{2,1,0:T(8,128)(2,1)S(1)} collective-permute-done((bf16[1,128,256]{2,1,0:T(8,128)(2,1)S(1)}, bf16[1,128,256]{2,1,0:T(8,128)(2,1)S(1)}, u32[]{:S(2)}, u32[]{:S(2)}) %collective-permute-start.24) | collective-permute-done | bytes 65568 | tf_op jit(solution)/shard_map/ppermute | solution.py:38
  (109 shorter events, 48.9 us)
Async XLA Ops:
  0.6 131.1 %copy-start = (bf16[512,512]{1,0:T(8,128)(2,1)S(1)}, bf16[512,512]{1,0:T(8,128)(2,1)}, u32[]{:S(2)}) copy-start(bf16[512,512]{1,0:T(8,128)(2,1)} %param.8) | copy-start | bytes 1572868
  0.6 57.5 %copy-start.1 = (bf16[1,1,8,128,128]{4,3,2,1,0:T(8,128)(2,1)S(1)}, bf16[1,1,8,128,128]{4,3,2,1,0:T(8,128)(2,1)}, u32[]{:S(2)}) copy-start(bf16[1,1,8,128,128]{4,3,2,1,0:T(8,128)(2,1)} %param.13) | copy-start | bytes 786436
  4.2 25.3 %collective-permute-start = (bf16[1,144,256]{2,1,0:T(8,128)(2,1)S(1)}, bf16[1,144,256]{2,1,0:T(8,128)(2,1)S(1)}, u32[]{:S(2)}, u32[]{:S(2)}) collective-permute-start(bf16[1,144,256]{2,1,0:T(8,128)(2,1)S(1)} %pad_maximum_fusion.6), channel_id=1, source_target_pairs={{0,256},{256,0},{1,257},{257,1},{2,258},{258,2},{3,259},{259,3},{4... | collective-permute-start | bytes 221192 | tf_op jit(solution)/shard_map/ppermute | solution.py:38
  13.3 14.2 %collective-permute-start.5 = (bf16[1,128,256]{2,1,0:T(8,128)(2,1)S(1)}, bf16[1,128,256]{2,1,0:T(8,128)(2,1)S(1)}, u32[]{:S(2)}, u32[]{:S(2)}) collective-permute-start(bf16[1,128,256]{2,1,0:T(8,128)(2,1)S(1)} %get-tuple-element.25), channel_id=1, source_target_pairs={{0,256},{256,0},{1,257},{257,1},{2,258},{258,2},{3,259},{259,3},{4... | collective-permute-start | bytes 196616 | tf_op jit(solution)/shard_map/ppermute | solution.py:38
  27.6 12.6 %collective-permute-start.6 = (bf16[2,128,256]{2,1,0:T(8,128)(2,1)S(1)}, bf16[2,128,256]{2,1,0:T(8,128)(2,1)S(1)}, u32[]{:S(2)}, u32[]{:S(2)}) collective-permute-start(bf16[2,128,256]{2,1,0:T(8,128)(2,1)S(1)} %pad_maximum_fusion.5), channel_id=1, source_target_pairs={{0,128},{128,0},{1,129},{129,1},{2,130},{130,2},{3,131},{131,3},{4... | collective-permute-start | bytes 393224 | tf_op jit(solution)/shard_map/ppermute | solution.py:38
  29.5 12.6 %collective-permute-start.1 = (bf16[2,144,256]{2,1,0:T(8,128)(2,1)S(1)}, bf16[2,144,256]{2,1,0:T(8,128)(2,1)S(1)}, u32[]{:S(2)}, u32[]{:S(2)}) collective-permute-start(bf16[2,144,256]{2,1,0:T(8,128)(2,1)S(1)} %pad_maximum_fusion.4), channel_id=1, source_target_pairs={{0,128},{128,0},{1,129},{129,1},{2,130},{130,2},{3,131},{131,3},{4... | collective-permute-start | bytes 442376 | tf_op jit(solution)/shard_map/ppermute | solution.py:38
  40.2 10.6 %collective-permute-start.7 = (bf16[4,128,256]{2,1,0:T(8,128)(2,1)S(1)}, bf16[4,128,256]{2,1,0:T(8,128)(2,1)S(1)}, u32[]{:S(2)}, u32[]{:S(2)}) collective-permute-start(bf16[4,128,256]{2,1,0:T(8,128)(2,1)S(1)} %pad_maximum_fusion.2.refs_2_), channel_id=1, source_target_pairs={{0,64},{64,0},{1,65},{65,1},{2,66},{66,2},{3,67},{67,3},{4,68},{68... | collective-permute-start | bytes 786440 | tf_op jit(solution)/shard_map/ppermute | solution.py:38
  42.2 11.8 %collective-permute-start.2 = (bf16[4,144,256]{2,1,0:T(8,128)(2,1)S(1)}, bf16[4,144,256]{2,1,0:T(8,128)(2,1)S(1)}, u32[]{:S(2)}, u32[]{:S(2)}) collective-permute-start(bf16[4,144,256]{2,1,0:T(8,128)(2,1)S(1)} %pad_maximum_fusion.1.refs_1_), channel_id=1, source_target_pairs={{0,64},{64,0},{1,65},{65,1},{2,66},{66,2},{3,67},{67,3},{4,68},{68... | collective-permute-start | bytes 884744 | tf_op jit(solution)/shard_map/ppermute | solution.py:38
  46.2 12.0 %collective-permute-start.8 = (bf16[4,128,256]{2,1,0:T(8,128)(2,1)S(1)}, bf16[4,128,256]{2,1,0:T(8,128)(2,1)S(1)}, u32[]{:S(2)}, u32[]{:S(2)}) collective-permute-start(bf16[4,128,256]{2,1,0:T(8,128)(2,1)S(1)} %pad_maximum_fusion.2.refs_2_), channel_id=1, source_target_pairs={{0,32},{32,0},{1,33},{33,1},{2,34},{34,2},{3,35},{35,3},{4,36},{36... | collective-permute-start | bytes 786440 | tf_op jit(solution)/shard_map/ppermute | solution.py:38
  48.1 7.9 %collective-permute-start.3 = (bf16[4,144,256]{2,1,0:T(8,128)(2,1)S(1)}, bf16[4,144,256]{2,1,0:T(8,128)(2,1)S(1)}, u32[]{:S(2)}, u32[]{:S(2)}) collective-permute-start(bf16[4,144,256]{2,1,0:T(8,128)(2,1)S(1)} %pad_maximum_fusion.1.refs_1_), channel_id=1, source_target_pairs={{0,32},{32,0},{1,33},{33,1},{2,34},{34,2},{3,35},{35,3},{4,36},{36... | collective-permute-start | bytes 884744 | tf_op jit(solution)/shard_map/ppermute | solution.py:38
  50.9 7.2 %collective-permute-start.9 = (bf16[4,128,256]{2,1,0:T(8,128)(2,1)S(1)}, bf16[4,128,256]{2,1,0:T(8,128)(2,1)S(1)}, u32[]{:S(2)}, u32[]{:S(2)}) collective-permute-start(bf16[4,128,256]{2,1,0:T(8,128)(2,1)S(1)} %collective-permute-done.7.refs_4_), channel_id=1, source_target_pairs={{0,32},{32,0},{1,33},{33,1},{2,34},{34,2},{3,35},{35,3},{4,36},{36... | collective-permute-start | bytes 786440 | tf_op jit(solution)/shard_map/ppermute | solution.py:38
  54.0 3.5 %collective-permute-start.4 = (bf16[4,144,256]{2,1,0:T(8,128)(2,1)S(1)}, bf16[4,144,256]{2,1,0:T(8,128)(2,1)S(1)}, u32[]{:S(2)}, u32[]{:S(2)}) collective-permute-start(bf16[4,144,256]{2,1,0:T(8,128)(2,1)S(1)} %collective-permute-done.2.refs_3_), channel_id=1, source_target_pairs={{0,32},{32,0},{1,33},{33,1},{2,34},{34,2},{3,35},{35,3},{4,36},{36... | collective-permute-start | bytes 884744 | tf_op jit(solution)/shard_map/ppermute | solution.py:38
  96.9 34.3 %all-to-all-start.1 = ((bf16[16,128,512]{2,1,0:T(8,128)(2,1)}), bf16[16,128,512]{2,1,0:T(8,128)(2,1)S(1)}, u32[]{:S(2)}, u32[]{:S(2)}) async-start(bf16[16,128,512]{2,1,0:T(8,128)(2,1)} %get-tuple-element.15), calls=%async_computation.1 | async-start | bytes 4194304 | tf_op jit(solution)/shard_map/all_to_all | solution.py:46
  102.9 29.8 %copy-start.5 = (bf16[128,512]{1,0:T(8,128)(2,1)S(1)}, bf16[128,512]{1,0:T(8,128)(2,1)}, u32[]{:S(2)}) copy-start(bf16[128,512]{1,0:T(8,128)(2,1)} %param.9) | copy-start | bytes 393220
  102.9 28.6 %collective-permute-start.10 = (bf16[128,512]{1,0:T(8,128)(2,1)S(1)}, bf16[128,512]{1,0:T(8,128)(2,1)S(1)}, u32[]{:S(2)}, u32[]{:S(2)}) collective-permute-start(bf16[128,512]{1,0:T(8,128)(2,1)S(1)} %reduce_sum.98), channel_id=1, source_target_pairs={{0,4},{4,0},{1,5},{5,1},{2,6},{6,2},{3,7},{7,3},{8,12},{12,8},{9,1... | collective-permute-start | bytes 393224 | tf_op jit(solution)/shard_map/ppermute | solution.py:38
  135.1 26.3 %all-to-all-start.2 = ((bf16[16,96,512]{2,1,0:T(8,128)(2,1)}), bf16[16,96,512]{2,1,0:T(8,128)(2,1)S(1)}, u32[]{:S(2)}, u32[]{:S(2)}) async-start(bf16[16,96,512]{2,1,0:T(8,128)(2,1)} %pad_maximum_fusion), calls=%async_computation.2 | async-start | bytes 3145728 | tf_op jit(solution)/shard_map/all_to_all | solution.py:46
  140.3 15.8 %collective-permute-start.16 = (bf16[128,512]{1,0:T(8,128)(2,1)S(1)}, bf16[128,512]{1,0:T(8,128)(2,1)S(1)}, u32[]{:S(2)}, u32[]{:S(2)}) collective-permute-start(bf16[128,512]{1,0:T(8,128)(2,1)S(1)} %multiply_convert_fusion), channel_id=1, source_target_pairs={{0,4},{4,0},{1,5},{5,1},{2,6},{6,2},{3,7},{7,3},{8,12},{12,8},{9,1... | collective-permute-start | bytes 393224 | tf_op jit(solution)/shard_map/ppermute | solution.py:38
  163.3 55.4 %all-to-all-start.3 = ((bf16[16,192,512]{2,1,0:T(8,128)(2,1)}), bf16[16,192,512]{2,1,0:T(8,128)(2,1)}, u32[]{:S(2)}, u32[]{:S(2)}) async-start(bf16[16,192,512]{2,1,0:T(8,128)(2,1)} %broadcast_in_dim.13), calls=%async_computation.3 | async-start | bytes 6291456 | tf_op jit(solution)/shard_map/all_to_all | solution.py:46
  170.0 3.1 %collective-permute-start.11 = (f32[32,512]{1,0:T(8,128)S(1)}, f32[32,512]{1,0:T(8,128)S(1)}, u32[]{:S(2)}, u32[]{:S(2)}) collective-permute-start(f32[32,512]{1,0:T(8,128)S(1)} %convert_reduce_fusion.1), channel_id=1, source_target_pairs={{0,32},{32,0},{1,33},{33,1},{2,34},{34,2},{3,35},{35,3},{4,36},{36... | collective-permute-start | bytes 196616 | tf_op jit(solution)/shard_map/ppermute | solution.py:38
  173.1 8.2 %collective-permute-start.12 = (f32[32,512]{1,0:T(8,128)S(1)}, f32[32,512]{1,0:T(8,128)S(1)}, u32[]{:S(2)}, u32[]{:S(2)}) collective-permute-start(f32[32,512]{1,0:T(8,128)S(1)} %add.137), channel_id=1, source_target_pairs={{0,64},{64,0},{1,65},{65,1},{2,66},{66,2},{3,67},{67,3},{4,68},{68... | collective-permute-start | bytes 196616 | tf_op jit(solution)/shard_map/ppermute | solution.py:38
  181.4 7.5 %collective-permute-start.13 = (f32[32,512]{1,0:T(8,128)S(1)}, f32[32,512]{1,0:T(8,128)S(1)}, u32[]{:S(2)}, u32[]{:S(2)}) collective-permute-start(f32[32,512]{1,0:T(8,128)S(1)} %add.138), channel_id=1, source_target_pairs={{0,128},{128,0},{1,129},{129,1},{2,130},{130,2},{3,131},{131,3},{4... | collective-permute-start | bytes 196616 | tf_op jit(solution)/shard_map/ppermute | solution.py:38
  188.8 12.9 %collective-permute-start.14 = (f32[32,512]{1,0:T(8,128)S(1)}, f32[32,512]{1,0:T(8,128)S(1)}, u32[]{:S(2)}, u32[]{:S(2)}) collective-permute-start(f32[32,512]{1,0:T(8,128)S(1)} %add.139), channel_id=1, source_target_pairs={{0,256},{256,0},{1,257},{257,1},{2,258},{258,2},{3,259},{259,3},{4... | collective-permute-start | bytes 196616 | tf_op jit(solution)/shard_map/ppermute | solution.py:38
  201.7 17.0 %collective-permute-start.15 = (f32[32,512]{1,0:T(8,128)S(1)}, f32[32,512]{1,0:T(8,128)S(1)}, u32[]{:S(2)}, u32[]{:S(2)}) collective-permute-start(f32[32,512]{1,0:T(8,128)S(1)} %add.140), channel_id=1, source_target_pairs={{0,4},{4,0},{1,5},{5,1},{2,6},{6,2},{3,7},{7,3},{8,12},{12,8},{9,1... | collective-permute-start | bytes 196616 | tf_op jit(solution)/shard_map/ppermute | solution.py:38
  224.5 12.3 %collective-permute-start.17 = (bf16[8,128,256]{2,1,0:T(8,128)(2,1)}, bf16[8,128,256]{2,1,0:T(8,128)(2,1)}, u32[]{:S(2)}, u32[]{:S(2)}) collective-permute-start(bf16[8,128,256]{2,1,0:T(8,128)(2,1)} %get-tuple-element.19), channel_id=1, source_target_pairs={{0,32},{32,0},{1,33},{33,1},{2,34},{34,2},{3,35},{35,3},{4,36},{36... | collective-permute-start | bytes 1572872 | tf_op jit(solution)/shard_map/ppermute | solution.py:38
  227.6 23.4 %all-to-all-start.4 = ((f32[16,32,512]{2,1,0:T(8,128)}), f32[16,32,512]{2,1,0:T(8,128)S(1)}, u32[]{:S(2)}, u32[]{:S(2)}) async-start(f32[16,32,512]{2,1,0:T(8,128)} %broadcast_in_dim.14), calls=%async_computation.4 | async-start | bytes 2097152 | tf_op jit(solution)/shard_map/all_to_all | solution.py:46
  234.8 5.1 %collective-permute-start.18 = (bf16[8,128,256]{2,1,0:T(8,128)(2,1)S(1)}, bf16[8,128,256]{2,1,0:T(8,128)(2,1)}, u32[]{:S(2)}, u32[]{:S(2)}) collective-permute-start(bf16[8,128,256]{2,1,0:T(8,128)(2,1)S(1)} %copy-done.3), channel_id=1, source_target_pairs={{0,32},{32,0},{1,33},{33,1},{2,34},{34,2},{3,35},{35,3},{4,36},{36... | collective-permute-start | bytes 1572872 | tf_op jit(solution)/shard_map/ppermute | solution.py:38
  238.0 13.0 %collective-permute-start.19 = (bf16[4,128,256]{2,1,0:T(8,128)(2,1)S(1)}, bf16[4,128,256]{2,1,0:T(8,128)(2,1)S(1)}, u32[]{:S(2)}, u32[]{:S(2)}) collective-permute-start(bf16[4,128,256]{2,1,0:T(8,128)(2,1)S(1)} %slice.94), channel_id=1, source_target_pairs={{0,64},{64,0},{1,65},{65,1},{2,66},{66,2},{3,67},{67,3},{4,68},{68... | collective-permute-start | bytes 786440 | tf_op jit(solution)/shard_map/ppermute | solution.py:38
  241.2 13.1 %collective-permute-start.22 = (bf16[4,128,256]{2,1,0:T(8,128)(2,1)S(1)}, bf16[4,128,256]{2,1,0:T(8,128)(2,1)S(1)}, u32[]{:S(2)}, u32[]{:S(2)}) collective-permute-start(bf16[4,128,256]{2,1,0:T(8,128)(2,1)S(1)} %slice.100), channel_id=1, source_target_pairs={{0,64},{64,0},{1,65},{65,1},{2,66},{66,2},{3,67},{67,3},{4,68},{68... | collective-permute-start | bytes 786440 | tf_op jit(solution)/shard_map/ppermute | solution.py:38
  252.1 12.0 %collective-permute-start.20 = (bf16[2,128,256]{2,1,0:T(8,128)(2,1)S(1)}, bf16[2,128,256]{2,1,0:T(8,128)(2,1)S(1)}, u32[]{:S(2)}, u32[]{:S(2)}) collective-permute-start(bf16[2,128,256]{2,1,0:T(8,128)(2,1)S(1)} %slice.96), channel_id=1, source_target_pairs={{0,128},{128,0},{1,129},{129,1},{2,130},{130,2},{3,131},{131,3},{4... | collective-permute-start | bytes 393224 | tf_op jit(solution)/shard_map/ppermute | solution.py:38
  254.3 15.3 %collective-permute-start.23 = (bf16[2,128,256]{2,1,0:T(8,128)(2,1)S(1)}, bf16[2,128,256]{2,1,0:T(8,128)(2,1)S(1)}, u32[]{:S(2)}, u32[]{:S(2)}) collective-permute-start(bf16[2,128,256]{2,1,0:T(8,128)(2,1)S(1)} %slice.102), channel_id=1, source_target_pairs={{0,128},{128,0},{1,129},{129,1},{2,130},{130,2},{3,131},{131,3},{4... | collective-permute-start | bytes 393224 | tf_op jit(solution)/shard_map/ppermute | solution.py:38
  264.1 12.0 %collective-permute-start.21 = (bf16[1,128,256]{2,1,0:T(8,128)(2,1)S(1)}, bf16[1,128,256]{2,1,0:T(8,128)(2,1)S(1)}, u32[]{:S(2)}, u32[]{:S(2)}) collective-permute-start(bf16[1,128,256]{2,1,0:T(8,128)(2,1)S(1)} %slice.98), channel_id=1, source_target_pairs={{0,256},{256,0},{1,257},{257,1},{2,258},{258,2},{3,259},{259,3},{4... | collective-permute-start | bytes 196616 | tf_op jit(solution)/shard_map/ppermute | solution.py:38
  269.7 11.1 %collective-permute-start.24 = (bf16[1,128,256]{2,1,0:T(8,128)(2,1)S(1)}, bf16[1,128,256]{2,1,0:T(8,128)(2,1)S(1)}, u32[]{:S(2)}, u32[]{:S(2)}) collective-permute-start(bf16[1,128,256]{2,1,0:T(8,128)(2,1)S(1)} %slice.104), channel_id=1, source_target_pairs={{0,256},{256,0},{1,257},{257,1},{2,258},{258,2},{3,259},{259,3},{4... | collective-permute-start | bytes 196616 | tf_op jit(solution)/shard_map/ppermute | solution.py:38
  (3 other events, 18.3 us)

commit v10 on v9

--- a/solution.py
+++ b/solution.py
@@ -180,16 +180,16 @@
 
     output, normed, grad_pre, grad_own = layer_rows(own_total, cotangent, weight)
 
-    half = span // 2
+    lead = span // 4
     weight_terms = jnp.einsum("nf,ng->fg", normed, grad_pre, preferred_element_type=F32)
     weight_parts = weight_terms.astype(BF16).reshape(n_plane, width // n_plane, width)
     first_group = swap_parts(
-        jnp.concatenate([copies_of(grad_own[:half], PLANE), weight_parts], axis=1), PLANE
-    )
-    grad_rest = jnp.concatenate([grad_own[half:], flip(grad_own, "zh")])
+        jnp.concatenate([copies_of(grad_own[:lead], PLANE), weight_parts], axis=1), PLANE
+    )
+    grad_rest = jnp.concatenate([grad_own[lead:], flip(grad_own, "zh")])
     last_group = swap_parts(copies_of(after(grad_rest, first_group), PLANE), PLANE)
 
-    line_rows = jnp.sum(first_group[:, half:].astype(F32), axis=0)
+    line_rows = jnp.sum(first_group[:, lead:].astype(F32), axis=0)
     for axis in ("core", "z1", "zb", "za", "zh"):
         line_rows = line_rows + flip(line_rows, axis)
     line_rows = line_rows * (1.0 / math.sqrt(nodes))
@@ -203,7 +203,7 @@
         tiles,
         None,
         [first_group, last_group],
-        [[[(0, 0, half), (1, 0, half)]], [[(1, half, half + span)]]],
+        [[[(0, 0, lead), (1, 0, span - lead)]], [[(1, span - lead, 2 * span - lead)]]],
         [
             (part.start, part.stop, [(first, first + n_line, 0, span)])
             for first in (0, n_line)
@@ -215,8 +215,9 @@
         keep.astype(F32) + flip(send, "core").astype(F32)
         for keep, send in zip(halves[:CHUNKS], halves[CHUNKS:])
     ]
-    line_rows = after(line_rows, *totals)
-    weight_grad = swap_parts(copies_of(line_rows, PLANE), PLANE).reshape(width, width)
+    along = jnp.concatenate([total[0, :8] for total in totals], axis=1)
+    weight_rows = swap_parts(copies_of(jnp.concatenate([line_rows, along]), PLANE), PLANE)
+    weight_grad = weight_rows[:, : line_rows.shape[0]].reshape(width, width)
     for axis in ("z1", "zb", "za"):
         totals = [total.astype(BF16) for total in totals]
         size = totals[0].shape[0] // 2

time: 285 us -> 282 us (0.989)
  waiting for transfers between devices: 82.1 us -> 72.4 us
  starting transfers between devices: 136 us -> 144 us
    all_to_all x4, waiting for transfers between devices: 26.6 us -> 15.5 us  [swap_parts(): return lax.all_to_all(parts, axes, split_axis=0, concat_axis=0, tiled=True)]
    ppermute x25, starting transfers between devices: 111 us -> 120 us  [flip(): return lax.ppermute(block, axis, [(0, 1), (1, 0)])]
  transfers between devices with their start and end apart: 29 -> 29, of which waited for: 18 -> 14; matrix products, arithmetic and copies ran while one was open for 3% -> 3% of each run, Pallas kernels for 0% -> 0%
where the time goes in v10:
time: 282 us; the launch traced here: 279 us
  starting transfers between devices  144 us (51%)
  waiting for transfers between devices  72.4 us (26%)
  blocking collectives  33.5 us (12%)
  Pallas kernels  9.58 us (3%)
  other arithmetic  7.63 us (3%)
  local copies, waits for them, and re-layouts  7.6 us (3%)
    ppermute x25, starting transfers between devices, flip(): return lax.ppermute(block, axis, [(0, 1), (1, 0)])  120 us
    ppermute x25, waiting for transfers between devices, flip(): return lax.ppermute(block, axis, [(0, 1), (1, 0)])  56.9 us
    all_to_all x1, blocking collectives, swap_parts(): return lax.all_to_all(parts, axes, split_axis=0, concat_axis=0, tiled=True)  33.5 us
    all_to_all x4, starting transfers between devices, swap_parts(): return lax.all_to_all(parts, axes, split_axis=0, concat_axis=0, tiled=True)  23.8 us
    all_to_all x4, waiting for transfers between devices, swap_parts(): return lax.all_to_all(parts, axes, split_axis=0, concat_axis=0, tiled=True)  15.5 us
    pallas_call x2, Pallas kernels, tile_sums(): pl.pallas_call(functools.partial(tile_kernel, transposed, scaled, sources...  9.58 us
  transfers between devices with their start and end apart: 29, of which 14 were waited for; matrix products, arithmetic and copies ran while one was open for 3% of the time, Pallas kernels for 0%

profile of v10, /device:TPU:24, one launch (start us, length us, event | category | flops | bytes accessed | tf_op | source)
XLA Modules:
  0.0 279.5 jit_solution(8741399485707465892)
XLA Ops:
  4.2 9.1 %collective-permute-start = (bf16[1,144,256]{2,1,0:T(8,128)(2,1)S(1)}, bf16[1,144,256]{2,1,0:T(8,128)(2,1)S(1)}, u32[]{:S(2)}, u32[]{:S(2)}) collective-permute-start(bf16[1,144,256]{2,1,0:T(8,128)(2,1)S(1)} %pad_maximum_fusion.6), channel_id=1, source_target_pairs={{0,256},{256,0},{1,257},{257,1},{2,258},{258,2},{3,259},{259,3},{4... | collective-permute-start | bytes 221192 | tf_op jit(solution)/shard_map/ppermute | solution.py:38
  16.6 11.0 %collective-permute-done.5 = bf16[1,128,256]{2,1,0:T(8,128)(2,1)S(1)} collective-permute-done((bf16[1,128,256]{2,1,0:T(8,128)(2,1)S(1)}, bf16[1,128,256]{2,1,0:T(8,128)(2,1)S(1)}, u32[]{:S(2)}, u32[]{:S(2)}) %collective-permute-start.5) | collective-permute-done | bytes 65568 | tf_op jit(solution)/shard_map/ppermute | solution.py:38
  29.5 4.8 %collective-permute-start.1 = (bf16[2,144,256]{2,1,0:T(8,128)(2,1)S(1)}, bf16[2,144,256]{2,1,0:T(8,128)(2,1)S(1)}, u32[]{:S(2)}, u32[]{:S(2)}) collective-permute-start(bf16[2,144,256]{2,1,0:T(8,128)(2,1)S(1)} %pad_maximum_fusion.4), channel_id=1, source_target_pairs={{0,128},{128,0},{1,129},{129,1},{2,130},{130,2},{3,131},{131,3},{4... | collective-permute-start | bytes 442376 | tf_op jit(solution)/shard_map/ppermute | solution.py:38
  35.0 5.2 %collective-permute-done.6 = bf16[2,128,256]{2,1,0:T(8,128)(2,1)S(1)} collective-permute-done((bf16[2,128,256]{2,1,0:T(8,128)(2,1)S(1)}, bf16[2,128,256]{2,1,0:T(8,128)(2,1)S(1)}, u32[]{:S(2)}, u32[]{:S(2)}) %collective-permute-start.6) | collective-permute-done | bytes 131104 | tf_op jit(solution)/shard_map/ppermute | solution.py:38
  42.2 3.9 %collective-permute-start.2 = (bf16[4,144,256]{2,1,0:T(8,128)(2,1)S(1)}, bf16[4,144,256]{2,1,0:T(8,128)(2,1)S(1)}, u32[]{:S(2)}, u32[]{:S(2)}) collective-permute-start(bf16[4,144,256]{2,1,0:T(8,128)(2,1)S(1)} %pad_maximum_fusion.1.refs_1_), channel_id=1, source_target_pairs={{0,64},{64,0},{1,65},{65,1},{2,66},{66,2},{3,67},{67,3},{4,68},{68... | collective-permute-start | bytes 884744 | tf_op jit(solution)/shard_map/ppermute | solution.py:38
  48.1 2.4 collective-permute-start.8
  58.1 4.9 %shard_map.94 = (bf16[16,128,512]{2,1,0:T(8,128)(2,1)}, bf16[16,128,512]{2,1,0:T(8,128)(2,1)S(1)}) custom-call(s32[8]{0:T(128)S(1)} %shift-right-arithmetic_add_fusion.source.target, s32[8]{0:T(128)S(1)} %add_bitcast_fusion.2.target.source, s32[1]{0:T(128)} %bitcast.36.count, bf16[8,128,128]{2,1,0:T(8,128)(2,1)S(1)} %bitcast.39, f32[8,128]{1,0:T(8,128)S(1)} %gather_fusion, ...), custom_call_target="tpu_custom_call" | custom-call | flops 134217728 | bytes 12582912 | tf_op jit(solution)/shard_map/pallas_call | solution.py:107
  63.0 33.5 %all_to_all.25 = bf16[16,128,512]{2,1,0:T(8,128)(2,1)S(1)} all-to-all(bf16[16,128,512]{2,1,0:T(8,128)(2,1)S(1)} %get-tuple-element.13), channel_id=1, replica_groups=mesh['za'=2,'zb'=2,'z1'=2,'core'=2,'y'=4,'zh'=2,'x'=4] {'y','x'}, dimensions={0} | all-to-all | bytes 4194304 | tf_op jit(solution)/shard_map/all_to_all | solution.py:46
  96.8 6.0 %all-to-all-start.1 = ((bf16[16,128,512]{2,1,0:T(8,128)(2,1)}), bf16[16,128,512]{2,1,0:T(8,128)(2,1)S(1)}, u32[]{:S(2)}, u32[]{:S(2)}) async-start(bf16[16,128,512]{2,1,0:T(8,128)(2,1)} %get-tuple-element.14), calls=%async_computation.1 | async-start | bytes 4194304 | tf_op jit(solution)/shard_map/all_to_all | solution.py:46
  102.8 13.3 %collective-permute-start.10 = (bf16[128,512]{1,0:T(8,128)(2,1)S(1)}, bf16[128,512]{1,0:T(8,128)(2,1)S(1)}, u32[]{:S(2)}, u32[]{:S(2)}) collective-permute-start(bf16[128,512]{1,0:T(8,128)(2,1)S(1)} %reduce_sum.98), channel_id=1, source_target_pairs={{0,4},{4,0},{1,5},{5,1},{2,6},{6,2},{3,7},{7,3},{8,12},{12,8},{9,1... | collective-permute-start | bytes 393224 | tf_op jit(solution)/shard_map/ppermute | solution.py:38
  116.1 15.5 %all-to-all-done.1 = bf16[16,128,512]{2,1,0:T(8,128)(2,1)S(1)} async-done(((bf16[16,128,512]{2,1,0:T(8,128)(2,1)}), bf16[16,128,512]{2,1,0:T(8,128)(2,1)S(1)}, u32[]{:S(2)}, u32[]{:S(2)}) %all-to-all-start.1) | async-done | bytes 2097184 | tf_op jit(solution)/shard_map/all_to_all | solution.py:46
  135.1 5.1 %all-to-all-start.2 = ((bf16[16,64,512]{2,1,0:T(8,128)(2,1)}), bf16[16,64,512]{2,1,0:T(8,128)(2,1)S(1)}, u32[]{:S(2)}, u32[]{:S(2)}) async-start(bf16[16,64,512]{2,1,0:T(8,128)(2,1)} %pad_maximum_fusion), calls=%async_computation.2 | async-start | bytes 2097152 | tf_op jit(solution)/shard_map/all_to_all | solution.py:46
  140.2 12.6 %collective-permute-start.16 = (bf16[128,512]{1,0:T(8,128)(2,1)S(1)}, bf16[128,512]{1,0:T(8,128)(2,1)S(1)}, u32[]{:S(2)}, u32[]{:S(2)}) collective-permute-start(bf16[128,512]{1,0:T(8,128)(2,1)S(1)} %multiply_convert_fusion), channel_id=1, source_target_pairs={{0,4},{4,0},{1,5},{5,1},{2,6},{6,2},{3,7},{7,3},{8,12},{12,8},{9,1... | collective-permute-start | bytes 393224 | tf_op jit(solution)/shard_map/ppermute | solution.py:38
  152.8 8.5 %collective-permute-done.16 = bf16[128,512]{1,0:T(8,128)(2,1)S(1)} collective-permute-done((bf16[128,512]{1,0:T(8,128)(2,1)S(1)}, bf16[128,512]{1,0:T(8,128)(2,1)S(1)}, u32[]{:S(2)}, u32[]{:S(2)}) %collective-permute-start.16) | collective-permute-done | bytes 131104 | tf_op jit(solution)/shard_map/ppermute | solution.py:38
  163.5 7.2 %all-to-all-start.3 = ((bf16[16,224,512]{2,1,0:T(8,128)(2,1)}), bf16[16,224,512]{2,1,0:T(8,128)(2,1)}, u32[]{:S(2)}, u32[]{:S(2)}) async-start(bf16[16,224,512]{2,1,0:T(8,128)(2,1)} %broadcast_in_dim.13), calls=%async_computation.3 | async-start | bytes 7340032 | tf_op jit(solution)/shard_map/all_to_all | solution.py:46
  174.0 4.2 %collective-permute-start.12 = (f32[32,512]{1,0:T(8,128)S(1)}, f32[32,512]{1,0:T(8,128)S(1)}, u32[]{:S(2)}, u32[]{:S(2)}) collective-permute-start(f32[32,512]{1,0:T(8,128)S(1)} %add.137), channel_id=1, source_target_pairs={{0,64},{64,0},{1,65},{65,1},{2,66},{66,2},{3,67},{67,3},{4,68},{68... | collective-permute-start | bytes 196616 | tf_op jit(solution)/shard_map/ppermute | solution.py:38
  180.6 5.7 %collective-permute-start.13 = (f32[32,512]{1,0:T(8,128)S(1)}, f32[32,512]{1,0:T(8,128)S(1)}, u32[]{:S(2)}, u32[]{:S(2)}) collective-permute-start(f32[32,512]{1,0:T(8,128)S(1)} %add.138), channel_id=1, source_target_pairs={{0,128},{128,0},{1,129},{129,1},{2,130},{130,2},{3,131},{131,3},{4... | collective-permute-start | bytes 196616 | tf_op jit(solution)/shard_map/ppermute | solution.py:38
  186.4 3.6 %collective-permute-done.13 = f32[32,512]{1,0:T(8,128)S(1)} collective-permute-done((f32[32,512]{1,0:T(8,128)S(1)}, f32[32,512]{1,0:T(8,128)S(1)}, u32[]{:S(2)}, u32[]{:S(2)}) %collective-permute-start.13) | collective-permute-done | bytes 65568 | tf_op jit(solution)/shard_map/ppermute | solution.py:38
  190.0 7.2 %collective-permute-start.14 = (f32[32,512]{1,0:T(8,128)S(1)}, f32[32,512]{1,0:T(8,128)S(1)}, u32[]{:S(2)}, u32[]{:S(2)}) collective-permute-start(f32[32,512]{1,0:T(8,128)S(1)} %add.139), channel_id=1, source_target_pairs={{0,256},{256,0},{1,257},{257,1},{2,258},{258,2},{3,259},{259,3},{4... | collective-permute-start | bytes 196616 | tf_op jit(solution)/shard_map/ppermute | solution.py:38
  197.2 5.6 %collective-permute-done.14 = f32[32,512]{1,0:T(8,128)S(1)} collective-permute-done((f32[32,512]{1,0:T(8,128)S(1)}, f32[32,512]{1,0:T(8,128)S(1)}, u32[]{:S(2)}, u32[]{:S(2)}) %collective-permute-start.14) | collective-permute-done | bytes 65568 | tf_op jit(solution)/shard_map/ppermute | solution.py:38
  202.9 10.7 %collective-permute-start.15 = (f32[32,512]{1,0:T(8,128)S(1)}, f32[32,512]{1,0:T(8,128)S(1)}, u32[]{:S(2)}, u32[]{:S(2)}) collective-permute-start(f32[32,512]{1,0:T(8,128)S(1)} %add.140), channel_id=1, source_target_pairs={{0,4},{4,0},{1,5},{5,1},{2,6},{6,2},{3,7},{7,3},{8,12},{12,8},{9,1... | collective-permute-start | bytes 196616 | tf_op jit(solution)/shard_map/ppermute | solution.py:38
  213.5 7.7 %collective-permute-done.15 = f32[32,512]{1,0:T(8,128)S(1)} collective-permute-done((f32[32,512]{1,0:T(8,128)S(1)}, f32[32,512]{1,0:T(8,128)S(1)}, u32[]{:S(2)}, u32[]{:S(2)}) %collective-permute-start.15) | collective-permute-done | bytes 65568 | tf_op jit(solution)/shard_map/ppermute | solution.py:38
  221.3 4.7 %shard_map.95 = (bf16[8,128,256]{2,1,0:T(8,128)(2,1)S(1)}, bf16[8,128,256]{2,1,0:T(8,128)(2,1)S(1)}, bf16[8,128,256]{2,1,0:T(8,128)(2,1)S(1)}, bf16[8,128,256]{2,1,0:T(8,128)(2,1)}) custom-call(s32[8]{0:T(128)S(1)} %add_bitcast_fusion.2.target.source, s32[8]{0:T(128)S(1)} %shift-right-arithmetic_add_fusion.source.target, s32[1]{0:T(128)} %bitcast.37.count, ...), custom_call_target="tpu_custom_call" | custom-call | flops 134217728 | bytes 6291456 | tf_op jit(solution)/shard_map/pallas_call | solution.py:107
  227.9 2.4 collective-permute-start.17
  234.1 3.9 %collective-permute-start.19 = (bf16[4,128,256]{2,1,0:T(8,128)(2,1)}, bf16[4,128,256]{2,1,0:T(8,128)(2,1)}, u32[]{:S(2)}, u32[]{:S(2)}) collective-permute-start(bf16[4,128,256]{2,1,0:T(8,128)(2,1)} %slice.109), channel_id=1, source_target_pairs={{0,64},{64,0},{1,65},{65,1},{2,66},{66,2},{3,67},{67,3},{4,68},{68... | collective-permute-start | bytes 786440 | tf_op jit(solution)/shard_map/ppermute | solution.py:38
  239.3 5.5 %all-to-all-start.4 = ((f32[16,40,512]{2,1,0:T(8,128)}), f32[16,40,512]{2,1,0:T(8,128)S(1)}, u32[]{:S(2)}, u32[]{:S(2)}) async-start(f32[16,40,512]{2,1,0:T(8,128)} %broadcast_in_dim.14), calls=%async_computation.4 | async-start | bytes 2621440 | tf_op jit(solution)/shard_map/all_to_all | solution.py:46
  244.9 3.0 %collective-permute-start.23 = (bf16[2,128,256]{2,1,0:T(8,128)(2,1)S(1)}, bf16[2,128,256]{2,1,0:T(8,128)(2,1)S(1)}, u32[]{:S(2)}, u32[]{:S(2)}) collective-permute-start(bf16[2,128,256]{2,1,0:T(8,128)(2,1)S(1)} %slice.117), channel_id=1, source_target_pairs={{0,128},{128,0},{1,129},{129,1},{2,130},{130,2},{3,131},{131,3},{4... | collective-permute-start | bytes 393224 | tf_op jit(solution)/shard_map/ppermute | solution.py:38
  249.0 3.8 %collective-permute-start.20 = (bf16[2,128,256]{2,1,0:T(8,128)(2,1)S(1)}, bf16[2,128,256]{2,1,0:T(8,128)(2,1)S(1)}, u32[]{:S(2)}, u32[]{:S(2)}) collective-permute-start(bf16[2,128,256]{2,1,0:T(8,128)(2,1)S(1)} %slice.111), channel_id=1, source_target_pairs={{0,128},{128,0},{1,129},{129,1},{2,130},{130,2},{3,131},{131,3},{4... | collective-permute-start | bytes 393224 | tf_op jit(solution)/shard_map/ppermute | solution.py:38
  252.7 3.9 %collective-permute-done.23 = bf16[2,128,256]{2,1,0:T(8,128)(2,1)S(1)} collective-permute-done((bf16[2,128,256]{2,1,0:T(8,128)(2,1)S(1)}, bf16[2,128,256]{2,1,0:T(8,128)(2,1)S(1)}, u32[]{:S(2)}, u32[]{:S(2)}) %collective-permute-start.23) | collective-permute-done | bytes 131104 | tf_op jit(solution)/shard_map/ppermute | solution.py:38
  256.6 10.8 %collective-permute-start.24 = (bf16[1,128,256]{2,1,0:T(8,128)(2,1)S(1)}, bf16[1,128,256]{2,1,0:T(8,128)(2,1)S(1)}, u32[]{:S(2)}, u32[]{:S(2)}) collective-permute-start(bf16[1,128,256]{2,1,0:T(8,128)(2,1)S(1)} %slice.119), channel_id=1, source_target_pairs={{0,256},{256,0},{1,257},{257,1},{2,258},{258,2},{3,259},{259,3},{4... | collective-permute-start | bytes 196616 | tf_op jit(solution)/shard_map/ppermute | solution.py:38
  267.5 5.3 %collective-permute-start.21 = (bf16[1,128,256]{2,1,0:T(8,128)(2,1)S(1)}, bf16[1,128,256]{2,1,0:T(8,128)(2,1)S(1)}, u32[]{:S(2)}, u32[]{:S(2)}) collective-permute-start(bf16[1,128,256]{2,1,0:T(8,128)(2,1)S(1)} %slice.113), channel_id=1, source_target_pairs={{0,256},{256,0},{1,257},{257,1},{2,258},{258,2},{3,259},{259,3},{4... | collective-permute-start | bytes 196616 | tf_op jit(solution)/shard_map/ppermute | solution.py:38
  272.8 4.8 %collective-permute-done.21 = bf16[1,128,256]{2,1,0:T(8,128)(2,1)S(1)} collective-permute-done((bf16[1,128,256]{2,1,0:T(8,128)(2,1)S(1)}, bf16[1,128,256]{2,1,0:T(8,128)(2,1)S(1)}, u32[]{:S(2)}, u32[]{:S(2)}) %collective-permute-start.21) | collective-permute-done | bytes 65568 | tf_op jit(solution)/shard_map/ppermute | solution.py:38
  (111 shorter events, 41.7 us)
Async XLA Ops:
  0.6 131.5 %copy-start = (bf16[512,512]{1,0:T(8,128)(2,1)S(1)}, bf16[512,512]{1,0:T(8,128)(2,1)}, u32[]{:S(2)}) copy-start(bf16[512,512]{1,0:T(8,128)(2,1)} %param.8) | copy-start | bytes 1572868
  0.6 57.5 %copy-start.1 = (bf16[1,1,8,128,128]{4,3,2,1,0:T(8,128)(2,1)S(1)}, bf16[1,1,8,128,128]{4,3,2,1,0:T(8,128)(2,1)}, u32[]{:S(2)}) copy-start(bf16[1,1,8,128,128]{4,3,2,1,0:T(8,128)(2,1)} %param.13) | copy-start | bytes 786436
  4.2 25.3 %collective-permute-start = (bf16[1,144,256]{2,1,0:T(8,128)(2,1)S(1)}, bf16[1,144,256]{2,1,0:T(8,128)(2,1)S(1)}, u32[]{:S(2)}, u32[]{:S(2)}) collective-permute-start(bf16[1,144,256]{2,1,0:T(8,128)(2,1)S(1)} %pad_maximum_fusion.6), channel_id=1, source_target_pairs={{0,256},{256,0},{1,257},{257,1},{2,258},{258,2},{3,259},{259,3},{4... | collective-permute-start | bytes 221192 | tf_op jit(solution)/shard_map/ppermute | solution.py:38
  13.3 14.2 %collective-permute-start.5 = (bf16[1,128,256]{2,1,0:T(8,128)(2,1)S(1)}, bf16[1,128,256]{2,1,0:T(8,128)(2,1)S(1)}, u32[]{:S(2)}, u32[]{:S(2)}) collective-permute-start(bf16[1,128,256]{2,1,0:T(8,128)(2,1)S(1)} %get-tuple-element.25), channel_id=1, source_target_pairs={{0,256},{256,0},{1,257},{257,1},{2,258},{258,2},{3,259},{259,3},{4... | collective-permute-start | bytes 196616 | tf_op jit(solution)/shard_map/ppermute | solution.py:38
  27.6 12.6 %collective-permute-start.6 = (bf16[2,128,256]{2,1,0:T(8,128)(2,1)S(1)}, bf16[2,128,256]{2,1,0:T(8,128)(2,1)S(1)}, u32[]{:S(2)}, u32[]{:S(2)}) collective-permute-start(bf16[2,128,256]{2,1,0:T(8,128)(2,1)S(1)} %pad_maximum_fusion.5), channel_id=1, source_target_pairs={{0,128},{128,0},{1,129},{129,1},{2,130},{130,2},{3,131},{131,3},{4... | collective-permute-start | bytes 393224 | tf_op jit(solution)/shard_map/ppermute | solution.py:38
  29.5 12.6 %collective-permute-start.1 = (bf16[2,144,256]{2,1,0:T(8,128)(2,1)S(1)}, bf16[2,144,256]{2,1,0:T(8,128)(2,1)S(1)}, u32[]{:S(2)}, u32[]{:S(2)}) collective-permute-start(bf16[2,144,256]{2,1,0:T(8,128)(2,1)S(1)} %pad_maximum_fusion.4), channel_id=1, source_target_pairs={{0,128},{128,0},{1,129},{129,1},{2,130},{130,2},{3,131},{131,3},{4... | collective-permute-start | bytes 442376 | tf_op jit(solution)/shard_map/ppermute | solution.py:38
  40.2 10.6 %collective-permute-start.7 = (bf16[4,128,256]{2,1,0:T(8,128)(2,1)S(1)}, bf16[4,128,256]{2,1,0:T(8,128)(2,1)S(1)}, u32[]{:S(2)}, u32[]{:S(2)}) collective-permute-start(bf16[4,128,256]{2,1,0:T(8,128)(2,1)S(1)} %pad_maximum_fusion.2.refs_2_), channel_id=1, source_target_pairs={{0,64},{64,0},{1,65},{65,1},{2,66},{66,2},{3,67},{67,3},{4,68},{68... | collective-permute-start | bytes 786440 | tf_op jit(solution)/shard_map/ppermute | solution.py:38
  42.2 11.8 %collective-permute-start.2 = (bf16[4,144,256]{2,1,0:T(8,128)(2,1)S(1)}, bf16[4,144,256]{2,1,0:T(8,128)(2,1)S(1)}, u32[]{:S(2)}, u32[]{:S(2)}) collective-permute-start(bf16[4,144,256]{2,1,0:T(8,128)(2,1)S(1)} %pad_maximum_fusion.1.refs_1_), channel_id=1, source_target_pairs={{0,64},{64,0},{1,65},{65,1},{2,66},{66,2},{3,67},{67,3},{4,68},{68... | collective-permute-start | bytes 884744 | tf_op jit(solution)/shard_map/ppermute | solution.py:38
  46.1 9.8 %collective-permute-start.3 = (bf16[4,144,256]{2,1,0:T(8,128)(2,1)S(1)}, bf16[4,144,256]{2,1,0:T(8,128)(2,1)S(1)}, u32[]{:S(2)}, u32[]{:S(2)}) collective-permute-start(bf16[4,144,256]{2,1,0:T(8,128)(2,1)S(1)} %pad_maximum_fusion.1.refs_1_), channel_id=1, source_target_pairs={{0,32},{32,0},{1,33},{33,1},{2,34},{34,2},{3,35},{35,3},{4,36},{36... | collective-permute-start | bytes 884744 | tf_op jit(solution)/shard_map/ppermute | solution.py:38
  48.1 10.0 %collective-permute-start.8 = (bf16[4,128,256]{2,1,0:T(8,128)(2,1)S(1)}, bf16[4,128,256]{2,1,0:T(8,128)(2,1)S(1)}, u32[]{:S(2)}, u32[]{:S(2)}) collective-permute-start(bf16[4,128,256]{2,1,0:T(8,128)(2,1)S(1)} %pad_maximum_fusion.2.refs_2_), channel_id=1, source_target_pairs={{0,32},{32,0},{1,33},{33,1},{2,34},{34,2},{3,35},{35,3},{4,36},{36... | collective-permute-start | bytes 786440 | tf_op jit(solution)/shard_map/ppermute | solution.py:38
  50.9 7.2 %collective-permute-start.9 = (bf16[4,128,256]{2,1,0:T(8,128)(2,1)S(1)}, bf16[4,128,256]{2,1,0:T(8,128)(2,1)S(1)}, u32[]{:S(2)}, u32[]{:S(2)}) collective-permute-start(bf16[4,128,256]{2,1,0:T(8,128)(2,1)S(1)} %collective-permute-done.7.refs_4_), channel_id=1, source_target_pairs={{0,32},{32,0},{1,33},{33,1},{2,34},{34,2},{3,35},{35,3},{4,36},{36... | collective-permute-start | bytes 786440 | tf_op jit(solution)/shard_map/ppermute | solution.py:38
  54.0 3.5 %collective-permute-start.4 = (bf16[4,144,256]{2,1,0:T(8,128)(2,1)S(1)}, bf16[4,144,256]{2,1,0:T(8,128)(2,1)S(1)}, u32[]{:S(2)}, u32[]{:S(2)}) collective-permute-start(bf16[4,144,256]{2,1,0:T(8,128)(2,1)S(1)} %collective-permute-done.2.refs_3_), channel_id=1, source_target_pairs={{0,32},{32,0},{1,33},{33,1},{2,34},{34,2},{3,35},{35,3},{4,36},{36... | collective-permute-start | bytes 884744 | tf_op jit(solution)/shard_map/ppermute | solution.py:38
  96.8 34.7 %all-to-all-start.1 = ((bf16[16,128,512]{2,1,0:T(8,128)(2,1)}), bf16[16,128,512]{2,1,0:T(8,128)(2,1)S(1)}, u32[]{:S(2)}, u32[]{:S(2)}) async-start(bf16[16,128,512]{2,1,0:T(8,128)(2,1)} %get-tuple-element.14), calls=%async_computation.1 | async-start | bytes 4194304 | tf_op jit(solution)/shard_map/all_to_all | solution.py:46
  102.8 30.3 %copy-start.4 = (bf16[128,512]{1,0:T(8,128)(2,1)S(1)}, bf16[128,512]{1,0:T(8,128)(2,1)}, u32[]{:S(2)}) copy-start(bf16[128,512]{1,0:T(8,128)(2,1)} %param.9) | copy-start | bytes 393220
  102.8 29.1 %collective-permute-start.10 = (bf16[128,512]{1,0:T(8,128)(2,1)S(1)}, bf16[128,512]{1,0:T(8,128)(2,1)S(1)}, u32[]{:S(2)}, u32[]{:S(2)}) collective-permute-start(bf16[128,512]{1,0:T(8,128)(2,1)S(1)} %reduce_sum.98), channel_id=1, source_target_pairs={{0,4},{4,0},{1,5},{5,1},{2,6},{6,2},{3,7},{7,3},{8,12},{12,8},{9,1... | collective-permute-start | bytes 393224 | tf_op jit(solution)/shard_map/ppermute | solution.py:38
  135.1 26.2 %all-to-all-start.2 = ((bf16[16,64,512]{2,1,0:T(8,128)(2,1)}), bf16[16,64,512]{2,1,0:T(8,128)(2,1)S(1)}, u32[]{:S(2)}, u32[]{:S(2)}) async-start(bf16[16,64,512]{2,1,0:T(8,128)(2,1)} %pad_maximum_fusion), calls=%async_computation.2 | async-start | bytes 2097152 | tf_op jit(solution)/shard_map/all_to_all | solution.py:46
  140.2 21.1 %collective-permute-start.16 = (bf16[128,512]{1,0:T(8,128)(2,1)S(1)}, bf16[128,512]{1,0:T(8,128)(2,1)S(1)}, u32[]{:S(2)}, u32[]{:S(2)}) collective-permute-start(bf16[128,512]{1,0:T(8,128)(2,1)S(1)} %multiply_convert_fusion), channel_id=1, source_target_pairs={{0,4},{4,0},{1,5},{5,1},{2,6},{6,2},{3,7},{7,3},{8,12},{12,8},{9,1... | collective-permute-start | bytes 393224 | tf_op jit(solution)/shard_map/ppermute | solution.py:38
  163.5 57.8 %all-to-all-start.3 = ((bf16[16,224,512]{2,1,0:T(8,128)(2,1)}), bf16[16,224,512]{2,1,0:T(8,128)(2,1)}, u32[]{:S(2)}, u32[]{:S(2)}) async-start(bf16[16,224,512]{2,1,0:T(8,128)(2,1)} %broadcast_in_dim.13), calls=%async_computation.3 | async-start | bytes 7340032 | tf_op jit(solution)/shard_map/all_to_all | solution.py:46
  170.8 3.1 %collective-permute-start.11 = (f32[32,512]{1,0:T(8,128)S(1)}, f32[32,512]{1,0:T(8,128)S(1)}, u32[]{:S(2)}, u32[]{:S(2)}) collective-permute-start(f32[32,512]{1,0:T(8,128)S(1)} %convert_reduce_fusion.1), channel_id=1, source_target_pairs={{0,32},{32,0},{1,33},{33,1},{2,34},{34,2},{3,35},{35,3},{4,36},{36... | collective-permute-start | bytes 196616 | tf_op jit(solution)/shard_map/ppermute | solution.py:38
  174.0 6.6 %collective-permute-start.12 = (f32[32,512]{1,0:T(8,128)S(1)}, f32[32,512]{1,0:T(8,128)S(1)}, u32[]{:S(2)}, u32[]{:S(2)}) collective-permute-start(f32[32,512]{1,0:T(8,128)S(1)} %add.137), channel_id=1, source_target_pairs={{0,64},{64,0},{1,65},{65,1},{2,66},{66,2},{3,67},{67,3},{4,68},{68... | collective-permute-start | bytes 196616 | tf_op jit(solution)/shard_map/ppermute | solution.py:38
  180.6 9.4 %collective-permute-start.13 = (f32[32,512]{1,0:T(8,128)S(1)}, f32[32,512]{1,0:T(8,128)S(1)}, u32[]{:S(2)}, u32[]{:S(2)}) collective-permute-start(f32[32,512]{1,0:T(8,128)S(1)} %add.138), channel_id=1, source_target_pairs={{0,128},{128,0},{1,129},{129,1},{2,130},{130,2},{3,131},{131,3},{4... | collective-permute-start | bytes 196616 | tf_op jit(solution)/shard_map/ppermute | solution.py:38
  190.0 12.9 %collective-permute-start.14 = (f32[32,512]{1,0:T(8,128)S(1)}, f32[32,512]{1,0:T(8,128)S(1)}, u32[]{:S(2)}, u32[]{:S(2)}) collective-permute-start(f32[32,512]{1,0:T(8,128)S(1)} %add.139), channel_id=1, source_target_pairs={{0,256},{256,0},{1,257},{257,1},{2,258},{258,2},{3,259},{259,3},{4... | collective-permute-start | bytes 196616 | tf_op jit(solution)/shard_map/ppermute | solution.py:38
  202.9 18.4 %collective-permute-start.15 = (f32[32,512]{1,0:T(8,128)S(1)}, f32[32,512]{1,0:T(8,128)S(1)}, u32[]{:S(2)}, u32[]{:S(2)}) collective-permute-start(f32[32,512]{1,0:T(8,128)S(1)} %add.140), channel_id=1, source_target_pairs={{0,4},{4,0},{1,5},{5,1},{2,6},{6,2},{3,7},{7,3},{8,12},{12,8},{9,1... | collective-permute-start | bytes 196616 | tf_op jit(solution)/shard_map/ppermute | solution.py:38
  226.0 4.4 %collective-permute-start.18 = (bf16[8,128,256]{2,1,0:T(8,128)(2,1)}, bf16[8,128,256]{2,1,0:T(8,128)(2,1)S(1)}, u32[]{:S(2)}, u32[]{:S(2)}) collective-permute-start(bf16[8,128,256]{2,1,0:T(8,128)(2,1)} %get-tuple-element.20), channel_id=1, source_target_pairs={{0,32},{32,0},{1,33},{33,1},{2,34},{34,2},{3,35},{35,3},{4,36},{36... | collective-permute-start | bytes 1572872 | tf_op jit(solution)/shard_map/ppermute | solution.py:38
  227.9 5.3 %collective-permute-start.17 = (bf16[8,128,256]{2,1,0:T(8,128)(2,1)S(1)}, bf16[8,128,256]{2,1,0:T(8,128)(2,1)S(1)}, u32[]{:S(2)}, u32[]{:S(2)}) collective-permute-start(bf16[8,128,256]{2,1,0:T(8,128)(2,1)S(1)} %get-tuple-element.18), channel_id=1, source_target_pairs={{0,32},{32,0},{1,33},{33,1},{2,34},{34,2},{3,35},{35,3},{4,36},{36... | collective-permute-start | bytes 1572872 | tf_op jit(solution)/shard_map/ppermute | solution.py:38
  231.3 13.5 %collective-permute-start.22 = (bf16[4,128,256]{2,1,0:T(8,128)(2,1)}, bf16[4,128,256]{2,1,0:T(8,128)(2,1)S(1)}, u32[]{:S(2)}, u32[]{:S(2)}) collective-permute-start(bf16[4,128,256]{2,1,0:T(8,128)(2,1)} %slice.115), channel_id=1, source_target_pairs={{0,64},{64,0},{1,65},{65,1},{2,66},{66,2},{3,67},{67,3},{4,68},{68... | collective-permute-start | bytes 786440 | tf_op jit(solution)/shard_map/ppermute | solution.py:38
  234.1 13.8 %collective-permute-start.19 = (bf16[4,128,256]{2,1,0:T(8,128)(2,1)}, bf16[4,128,256]{2,1,0:T(8,128)(2,1)}, u32[]{:S(2)}, u32[]{:S(2)}) collective-permute-start(bf16[4,128,256]{2,1,0:T(8,128)(2,1)} %slice.109), channel_id=1, source_target_pairs={{0,64},{64,0},{1,65},{65,1},{2,66},{66,2},{3,67},{67,3},{4,68},{68... | collective-permute-start | bytes 786440 | tf_op jit(solution)/shard_map/ppermute | solution.py:38
  239.3 39.1 %all-to-all-start.4 = ((f32[16,40,512]{2,1,0:T(8,128)}), f32[16,40,512]{2,1,0:T(8,128)S(1)}, u32[]{:S(2)}, u32[]{:S(2)}) async-start(f32[16,40,512]{2,1,0:T(8,128)} %broadcast_in_dim.14), calls=%async_computation.4 | async-start | bytes 2621440 | tf_op jit(solution)/shard_map/all_to_all | solution.py:46
  244.9 11.7 %collective-permute-start.23 = (bf16[2,128,256]{2,1,0:T(8,128)(2,1)S(1)}, bf16[2,128,256]{2,1,0:T(8,128)(2,1)S(1)}, u32[]{:S(2)}, u32[]{:S(2)}) collective-permute-start(bf16[2,128,256]{2,1,0:T(8,128)(2,1)S(1)} %slice.117), channel_id=1, source_target_pairs={{0,128},{128,0},{1,129},{129,1},{2,130},{130,2},{3,131},{131,3},{4... | collective-permute-start | bytes 393224 | tf_op jit(solution)/shard_map/ppermute | solution.py:38
  249.0 18.5 %collective-permute-start.20 = (bf16[2,128,256]{2,1,0:T(8,128)(2,1)S(1)}, bf16[2,128,256]{2,1,0:T(8,128)(2,1)S(1)}, u32[]{:S(2)}, u32[]{:S(2)}) collective-permute-start(bf16[2,128,256]{2,1,0:T(8,128)(2,1)S(1)} %slice.111), channel_id=1, source_target_pairs={{0,128},{128,0},{1,129},{129,1},{2,130},{130,2},{3,131},{131,3},{4... | collective-permute-start | bytes 393224 | tf_op jit(solution)/shard_map/ppermute | solution.py:38
  256.6 16.1 %collective-permute-start.24 = (bf16[1,128,256]{2,1,0:T(8,128)(2,1)S(1)}, bf16[1,128,256]{2,1,0:T(8,128)(2,1)S(1)}, u32[]{:S(2)}, u32[]{:S(2)}) collective-permute-start(bf16[1,128,256]{2,1,0:T(8,128)(2,1)S(1)} %slice.119), channel_id=1, source_target_pairs={{0,256},{256,0},{1,257},{257,1},{2,258},{258,2},{3,259},{259,3},{4... | collective-permute-start | bytes 196616 | tf_op jit(solution)/shard_map/ppermute | solution.py:38
  267.5 10.1 %collective-permute-start.21 = (bf16[1,128,256]{2,1,0:T(8,128)(2,1)S(1)}, bf16[1,128,256]{2,1,0:T(8,128)(2,1)S(1)}, u32[]{:S(2)}, u32[]{:S(2)}) collective-permute-start(bf16[1,128,256]{2,1,0:T(8,128)(2,1)S(1)} %slice.113), channel_id=1, source_target_pairs={{0,256},{256,0},{1,257},{257,1},{2,258},{258,2},{3,259},{259,3},{4... | collective-permute-start | bytes 196616 | tf_op jit(solution)/shard_map/ppermute | solution.py:38
  (2 other events, 9.7 us)

commit v11 on v10

--- a/solution.py
+++ b/solution.py
@@ -149,7 +149,7 @@
     chunk = width // CHUNKS
     parts = [slice(c * chunk, (c + 1) * chunk) for c in range(CHUNKS)]
     held = [features[None, :, part] for part in parts]
-    held[0] = jnp.concatenate([held[0], pieces.reshape(1, -1, chunk)], axis=1)
+    held[-1] = jnp.concatenate([held[-1], pieces.reshape(1, -1, chunk)], axis=1)
     for axis in Z4:
         held = [jnp.concatenate([part, flip(part, axis)]) for part in held]
     pairs = [flip(part, "z1") for part in held]
@@ -158,7 +158,7 @@
     def degrees(part):
         return jnp.sum(part[:, span:].astype(F32).reshape(-1, n_row, span), axis=0)
 
-    col_scale = lax.rsqrt(1.0 + sum(degrees(group[0]) for group in groups))
+    col_scale = lax.rsqrt(1.0 + sum(degrees(group[-1]) for group in groups))
     own_scale = lax.dynamic_index_in_dim(col_scale, my_row, axis=0, keepdims=False)
     slot_scale = col_scale[col_index]
 
@@ -190,7 +190,7 @@
     last_group = swap_parts(copies_of(after(grad_rest, first_group), PLANE), PLANE)
 
     line_rows = jnp.sum(first_group[:, lead:].astype(F32), axis=0)
-    for axis in ("core", "z1", "zb", "za", "zh"):
+    for axis in ("zh", "core", "za", "zb", "z1"):
         line_rows = line_rows + flip(line_rows, axis)
     line_rows = line_rows * (1.0 / math.sqrt(nodes))
     last_group = after(last_group, line_rows)

time: 282 us -> 281 us (level)
  starting transfers between devices: 144 us -> 158 us
  waiting for transfers between devices: 72.4 us -> 60.2 us
    ppermute x25, starting transfers between devices: 120 us -> 133 us  [flip(): return lax.ppermute(block, axis, [(0, 1), (1, 0)])]
    ppermute x25, waiting for transfers between devices: 56.9 us -> 44.8 us  [flip(): return lax.ppermute(block, axis, [(0, 1), (1, 0)])]
  transfers between devices with their start and end apart: 29 -> 29, of which waited for: 14 -> 17; matrix products, arithmetic and copies ran while one was open for 3% -> 3% of each run, Pallas kernels for 0% -> 0%
where the time goes in v11:
time: 281 us; the launch traced here: 279 us
  starting transfers between devices  158 us (56%)
  waiting for transfers between devices  60.2 us (21%)
  blocking collectives  34.3 us (12%)
  other arithmetic  7.63 us (3%)
  local copies, waits for them, and re-layouts  7.6 us (3%)
  Pallas kernels  7.46 us (3%)
    ppermute x25, starting transfers between devices, flip(): return lax.ppermute(block, axis, [(0, 1), (1, 0)])  133 us
    ppermute x25, waiting for transfers between devices, flip(): return lax.ppermute(block, axis, [(0, 1), (1, 0)])  44.8 us
    all_to_all x1, blocking collectives, swap_parts(): return lax.all_to_all(parts, axes, split_axis=0, concat_axis=0, tiled=True)  34.3 us
    all_to_all x4, starting transfers between devices, swap_parts(): return lax.all_to_all(parts, axes, split_axis=0, concat_axis=0, tiled=True)  24.3 us
    all_to_all x4, waiting for transfers between devices, swap_parts(): return lax.all_to_all(parts, axes, split_axis=0, concat_axis=0, tiled=True)  15.4 us
    pallas_call x2, Pallas kernels, tile_sums(): pl.pallas_call(functools.partial(tile_kernel, transposed, scaled, sources...  7.46 us
  transfers between devices with their start and end apart: 29, of which 17 were waited for; matrix products, arithmetic and copies ran while one was open for 3% of the time, Pallas kernels for 0%

profile of v11, /device:TPU:24, one launch (start us, length us, event | category | flops | bytes accessed | tf_op | source)
XLA Modules:
  0.0 279.5 jit_solution(11960064330582031662)
XLA Ops:
  4.2 9.1 %collective-permute-start = (bf16[1,144,256]{2,1,0:T(8,128)(2,1)S(1)}, bf16[1,144,256]{2,1,0:T(8,128)(2,1)S(1)}, u32[]{:S(2)}, u32[]{:S(2)}) collective-permute-start(bf16[1,144,256]{2,1,0:T(8,128)(2,1)S(1)} %pad_maximum_fusion.6), channel_id=1, source_target_pairs={{0,256},{256,0},{1,257},{257,1},{2,258},{258,2},{3,259},{259,3},{4... | collective-permute-start | bytes 221192 | tf_op jit(solution)/shard_map/ppermute | solution.py:38
  16.6 11.0 %collective-permute-done.5 = bf16[1,128,256]{2,1,0:T(8,128)(2,1)S(1)} collective-permute-done((bf16[1,128,256]{2,1,0:T(8,128)(2,1)S(1)}, bf16[1,128,256]{2,1,0:T(8,128)(2,1)S(1)}, u32[]{:S(2)}, u32[]{:S(2)}) %collective-permute-start.5) | collective-permute-done | bytes 65568 | tf_op jit(solution)/shard_map/ppermute | solution.py:38
  29.5 4.8 %collective-permute-start.1 = (bf16[2,144,256]{2,1,0:T(8,128)(2,1)S(1)}, bf16[2,144,256]{2,1,0:T(8,128)(2,1)S(1)}, u32[]{:S(2)}, u32[]{:S(2)}) collective-permute-start(bf16[2,144,256]{2,1,0:T(8,128)(2,1)S(1)} %pad_maximum_fusion.4), channel_id=1, source_target_pairs={{0,128},{128,0},{1,129},{129,1},{2,130},{130,2},{3,131},{131,3},{4... | collective-permute-start | bytes 442376 | tf_op jit(solution)/shard_map/ppermute | solution.py:38
  35.0 5.2 %collective-permute-done.6 = bf16[2,128,256]{2,1,0:T(8,128)(2,1)S(1)} collective-permute-done((bf16[2,128,256]{2,1,0:T(8,128)(2,1)S(1)}, bf16[2,128,256]{2,1,0:T(8,128)(2,1)S(1)}, u32[]{:S(2)}, u32[]{:S(2)}) %collective-permute-start.6) | collective-permute-done | bytes 131104 | tf_op jit(solution)/shard_map/ppermute | solution.py:38
  42.2 3.9 %collective-permute-start.2 = (bf16[4,144,256]{2,1,0:T(8,128)(2,1)S(1)}, bf16[4,144,256]{2,1,0:T(8,128)(2,1)S(1)}, u32[]{:S(2)}, u32[]{:S(2)}) collective-permute-start(bf16[4,144,256]{2,1,0:T(8,128)(2,1)S(1)} %pad_maximum_fusion.1.refs_2_), channel_id=1, source_target_pairs={{0,64},{64,0},{1,65},{65,1},{2,66},{66,2},{3,67},{67,3},{4,68},{68... | collective-permute-start | bytes 884744 | tf_op jit(solution)/shard_map/ppermute | solution.py:38
  48.1 2.4 collective-permute-start.8
  58.1 3.6 %shard_map.94 = (bf16[16,128,512]{2,1,0:T(8,128)(2,1)}, bf16[16,128,512]{2,1,0:T(8,128)(2,1)S(1)}) custom-call(s32[8]{0:T(128)S(1)} %shift-right-arithmetic_add_fusion.source.target, s32[8]{0:T(128)S(1)} %add_bitcast_fusion.2.target.source, s32[1]{0:T(128)} %bitcast.36.count, bf16[8,128,128]{2,1,0:T(8,128)(2,1)S(1)} %bitcast.39, f32[8,128]{1,0:T(8,128)S(1)} %gather_fusion, ...), custom_call_target="tpu_custom_call" | custom-call | flops 134217728 | bytes 12582912 | tf_op jit(solution)/shard_map/pallas_call | solution.py:107
  61.8 34.3 %all_to_all.25 = bf16[16,128,512]{2,1,0:T(8,128)(2,1)S(1)} all-to-all(bf16[16,128,512]{2,1,0:T(8,128)(2,1)S(1)} %get-tuple-element.13), channel_id=1, replica_groups=mesh['za'=2,'zb'=2,'z1'=2,'core'=2,'y'=4,'zh'=2,'x'=4] {'y','x'}, dimensions={0} | all-to-all | bytes 4194304 | tf_op jit(solution)/shard_map/all_to_all | solution.py:46
  96.4 6.0 %all-to-all-start.1 = ((bf16[16,128,512]{2,1,0:T(8,128)(2,1)}), bf16[16,128,512]{2,1,0:T(8,128)(2,1)S(1)}, u32[]{:S(2)}, u32[]{:S(2)}) async-start(bf16[16,128,512]{2,1,0:T(8,128)(2,1)} %get-tuple-element.14), calls=%async_computation.1 | async-start | bytes 4194304 | tf_op jit(solution)/shard_map/all_to_all | solution.py:46
  102.3 13.6 %collective-permute-start.10 = (bf16[128,512]{1,0:T(8,128)(2,1)S(1)}, bf16[128,512]{1,0:T(8,128)(2,1)S(1)}, u32[]{:S(2)}, u32[]{:S(2)}) collective-permute-start(bf16[128,512]{1,0:T(8,128)(2,1)S(1)} %reduce_sum.98), channel_id=1, source_target_pairs={{0,4},{4,0},{1,5},{5,1},{2,6},{6,2},{3,7},{7,3},{8,12},{12,8},{9,1... | collective-permute-start | bytes 393224 | tf_op jit(solution)/shard_map/ppermute | solution.py:38
  115.9 15.2 %all-to-all-done.1 = bf16[16,128,512]{2,1,0:T(8,128)(2,1)S(1)} async-done(((bf16[16,128,512]{2,1,0:T(8,128)(2,1)}), bf16[16,128,512]{2,1,0:T(8,128)(2,1)S(1)}, u32[]{:S(2)}, u32[]{:S(2)}) %all-to-all-start.1) | async-done | bytes 2097184 | tf_op jit(solution)/shard_map/all_to_all | solution.py:46
  134.6 5.1 %all-to-all-start.2 = ((bf16[16,64,512]{2,1,0:T(8,128)(2,1)}), bf16[16,64,512]{2,1,0:T(8,128)(2,1)S(1)}, u32[]{:S(2)}, u32[]{:S(2)}) async-start(bf16[16,64,512]{2,1,0:T(8,128)(2,1)} %pad_maximum_fusion), calls=%async_computation.2 | async-start | bytes 2097152 | tf_op jit(solution)/shard_map/all_to_all | solution.py:46
  139.7 12.3 %collective-permute-start.16 = (bf16[128,512]{1,0:T(8,128)(2,1)S(1)}, bf16[128,512]{1,0:T(8,128)(2,1)S(1)}, u32[]{:S(2)}, u32[]{:S(2)}) collective-permute-start(bf16[128,512]{1,0:T(8,128)(2,1)S(1)} %multiply_convert_fusion), channel_id=1, source_target_pairs={{0,4},{4,0},{1,5},{5,1},{2,6},{6,2},{3,7},{7,3},{8,12},{12,8},{9,1... | collective-permute-start | bytes 393224 | tf_op jit(solution)/shard_map/ppermute | solution.py:38
  152.1 3.5 %collective-permute-done.16 = bf16[128,512]{1,0:T(8,128)(2,1)S(1)} collective-permute-done((bf16[128,512]{1,0:T(8,128)(2,1)S(1)}, bf16[128,512]{1,0:T(8,128)(2,1)S(1)}, u32[]{:S(2)}, u32[]{:S(2)}) %collective-permute-start.16) | collective-permute-done | bytes 131104 | tf_op jit(solution)/shard_map/ppermute | solution.py:38
  157.8 7.2 %all-to-all-start.3 = ((bf16[16,224,512]{2,1,0:T(8,128)(2,1)}), bf16[16,224,512]{2,1,0:T(8,128)(2,1)}, u32[]{:S(2)}, u32[]{:S(2)}) async-start(bf16[16,224,512]{2,1,0:T(8,128)(2,1)} %broadcast_in_dim.13), calls=%async_computation.3 | async-start | bytes 7340032 | tf_op jit(solution)/shard_map/all_to_all | solution.py:46
  165.1 12.3 %collective-permute-start.11 = (f32[32,512]{1,0:T(8,128)S(1)}, f32[32,512]{1,0:T(8,128)S(1)}, u32[]{:S(2)}, u32[]{:S(2)}) collective-permute-start(f32[32,512]{1,0:T(8,128)S(1)} %convert_reduce_fusion.1), channel_id=1, source_target_pairs={{0,4},{4,0},{1,5},{5,1},{2,6},{6,2},{3,7},{7,3},{8,12},{12,8},{9,1... | collective-permute-start | bytes 196616 | tf_op jit(solution)/shard_map/ppermute | solution.py:38
  177.4 2.6 collective-permute-done.11
  183.2 11.2 %collective-permute-start.13 = (f32[32,512]{1,0:T(8,128)S(1)}, f32[32,512]{1,0:T(8,128)S(1)}, u32[]{:S(2)}, u32[]{:S(2)}) collective-permute-start(f32[32,512]{1,0:T(8,128)S(1)} %add.138), channel_id=1, source_target_pairs={{0,256},{256,0},{1,257},{257,1},{2,258},{258,2},{3,259},{259,3},{4... | collective-permute-start | bytes 196616 | tf_op jit(solution)/shard_map/ppermute | solution.py:38
  194.4 2.4 collective-permute-done.13
  196.8 7.3 %collective-permute-start.14 = (f32[32,512]{1,0:T(8,128)S(1)}, f32[32,512]{1,0:T(8,128)S(1)}, u32[]{:S(2)}, u32[]{:S(2)}) collective-permute-start(f32[32,512]{1,0:T(8,128)S(1)} %add.139), channel_id=1, source_target_pairs={{0,128},{128,0},{1,129},{129,1},{2,130},{130,2},{3,131},{131,3},{4... | collective-permute-start | bytes 196616 | tf_op jit(solution)/shard_map/ppermute | solution.py:38
  204.2 2.2 collective-permute-done.14
  206.4 4.8 %collective-permute-start.15 = (f32[32,512]{1,0:T(8,128)S(1)}, f32[32,512]{1,0:T(8,128)S(1)}, u32[]{:S(2)}, u32[]{:S(2)}) collective-permute-start(f32[32,512]{1,0:T(8,128)S(1)} %add.140), channel_id=1, source_target_pairs={{0,64},{64,0},{1,65},{65,1},{2,66},{66,2},{3,67},{67,3},{4,68},{68... | collective-permute-start | bytes 196616 | tf_op jit(solution)/shard_map/ppermute | solution.py:38
  213.8 3.8 %shard_map.95 = (bf16[8,128,256]{2,1,0:T(8,128)(2,1)S(1)}, bf16[8,128,256]{2,1,0:T(8,128)(2,1)S(1)}, bf16[8,128,256]{2,1,0:T(8,128)(2,1)S(1)}, bf16[8,128,256]{2,1,0:T(8,128)(2,1)}) custom-call(s32[8]{0:T(128)S(1)} %add_bitcast_fusion.2.target.source, s32[8]{0:T(128)S(1)} %shift-right-arithmetic_add_fusion.source.target, s32[1]{0:T(128)} %bitcast.37.count, ...), custom_call_target="tpu_custom_call" | custom-call | flops 134217728 | bytes 6291456 | tf_op jit(solution)/shard_map/pallas_call | solution.py:107
  219.6 2.4 collective-permute-start.17
  223.0 15.5 %collective-permute-start.22 = (bf16[4,128,256]{2,1,0:T(8,128)(2,1)}, bf16[4,128,256]{2,1,0:T(8,128)(2,1)S(1)}, u32[]{:S(2)}, u32[]{:S(2)}) collective-permute-start(bf16[4,128,256]{2,1,0:T(8,128)(2,1)} %slice.115), channel_id=1, source_target_pairs={{0,64},{64,0},{1,65},{65,1},{2,66},{66,2},{3,67},{67,3},{4,68},{68... | collective-permute-start | bytes 786440 | tf_op jit(solution)/shard_map/ppermute | solution.py:38
  242.6 6.1 %all-to-all-start.4 = ((f32[16,40,512]{2,1,0:T(8,128)}), f32[16,40,512]{2,1,0:T(8,128)S(1)}, u32[]{:S(2)}, u32[]{:S(2)}) async-start(f32[16,40,512]{2,1,0:T(8,128)} %broadcast_in_dim.14), calls=%async_computation.4 | async-start | bytes 2621440 | tf_op jit(solution)/shard_map/all_to_all | solution.py:46
  251.9 4.6 %collective-permute-start.20 = (bf16[2,128,256]{2,1,0:T(8,128)(2,1)S(1)}, bf16[2,128,256]{2,1,0:T(8,128)(2,1)S(1)}, u32[]{:S(2)}, u32[]{:S(2)}) collective-permute-start(bf16[2,128,256]{2,1,0:T(8,128)(2,1)S(1)} %slice.111), channel_id=1, source_target_pairs={{0,128},{128,0},{1,129},{129,1},{2,130},{130,2},{3,131},{131,3},{4... | collective-permute-start | bytes 393224 | tf_op jit(solution)/shard_map/ppermute | solution.py:38
  256.5 6.0 %collective-permute-done.23 = bf16[2,128,256]{2,1,0:T(8,128)(2,1)S(1)} collective-permute-done((bf16[2,128,256]{2,1,0:T(8,128)(2,1)S(1)}, bf16[2,128,256]{2,1,0:T(8,128)(2,1)S(1)}, u32[]{:S(2)}, u32[]{:S(2)}) %collective-permute-start.23) | collective-permute-done | bytes 131104 | tf_op jit(solution)/shard_map/ppermute | solution.py:38
  262.5 4.9 %collective-permute-start.24 = (bf16[1,128,256]{2,1,0:T(8,128)(2,1)S(1)}, bf16[1,128,256]{2,1,0:T(8,128)(2,1)S(1)}, u32[]{:S(2)}, u32[]{:S(2)}) collective-permute-start(bf16[1,128,256]{2,1,0:T(8,128)(2,1)S(1)} %slice.119), channel_id=1, source_target_pairs={{0,256},{256,0},{1,257},{257,1},{2,258},{258,2},{3,259},{259,3},{4... | collective-permute-start | bytes 196616 | tf_op jit(solution)/shard_map/ppermute | solution.py:38
  267.5 4.9 %collective-permute-start.21 = (bf16[1,128,256]{2,1,0:T(8,128)(2,1)S(1)}, bf16[1,128,256]{2,1,0:T(8,128)(2,1)S(1)}, u32[]{:S(2)}, u32[]{:S(2)}) collective-permute-start(bf16[1,128,256]{2,1,0:T(8,128)(2,1)S(1)} %slice.113), channel_id=1, source_target_pairs={{0,256},{256,0},{1,257},{257,1},{2,258},{258,2},{3,259},{259,3},{4... | collective-permute-start | bytes 196616 | tf_op jit(solution)/shard_map/ppermute | solution.py:38
  272.4 2.8 %collective-permute-done.24 = bf16[1,128,256]{2,1,0:T(8,128)(2,1)S(1)} collective-permute-done((bf16[1,128,256]{2,1,0:T(8,128)(2,1)S(1)}, bf16[1,128,256]{2,1,0:T(8,128)(2,1)S(1)}, u32[]{:S(2)}, u32[]{:S(2)}) %collective-permute-start.24) | collective-permute-done | bytes 65568 | tf_op jit(solution)/shard_map/ppermute | solution.py:38
  275.2 2.3 collective-permute-done.21
  (111 shorter events, 43.9 us)
Async XLA Ops:
  0.6 131.0 %copy-start = (bf16[512,512]{1,0:T(8,128)(2,1)S(1)}, bf16[512,512]{1,0:T(8,128)(2,1)}, u32[]{:S(2)}) copy-start(bf16[512,512]{1,0:T(8,128)(2,1)} %param.8) | copy-start | bytes 1572868
  0.6 57.5 %copy-start.1 = (bf16[1,1,8,128,128]{4,3,2,1,0:T(8,128)(2,1)S(1)}, bf16[1,1,8,128,128]{4,3,2,1,0:T(8,128)(2,1)}, u32[]{:S(2)}) copy-start(bf16[1,1,8,128,128]{4,3,2,1,0:T(8,128)(2,1)} %param.13) | copy-start | bytes 786436
  4.2 25.3 %collective-permute-start = (bf16[1,144,256]{2,1,0:T(8,128)(2,1)S(1)}, bf16[1,144,256]{2,1,0:T(8,128)(2,1)S(1)}, u32[]{:S(2)}, u32[]{:S(2)}) collective-permute-start(bf16[1,144,256]{2,1,0:T(8,128)(2,1)S(1)} %pad_maximum_fusion.6), channel_id=1, source_target_pairs={{0,256},{256,0},{1,257},{257,1},{2,258},{258,2},{3,259},{259,3},{4... | collective-permute-start | bytes 221192 | tf_op jit(solution)/shard_map/ppermute | solution.py:38
  13.3 14.2 %collective-permute-start.5 = (bf16[1,128,256]{2,1,0:T(8,128)(2,1)S(1)}, bf16[1,128,256]{2,1,0:T(8,128)(2,1)S(1)}, u32[]{:S(2)}, u32[]{:S(2)}) collective-permute-start(bf16[1,128,256]{2,1,0:T(8,128)(2,1)S(1)} %get-tuple-element.25), channel_id=1, source_target_pairs={{0,256},{256,0},{1,257},{257,1},{2,258},{258,2},{3,259},{259,3},{4... | collective-permute-start | bytes 196616 | tf_op jit(solution)/shard_map/ppermute | solution.py:38
  27.6 12.6 %collective-permute-start.6 = (bf16[2,128,256]{2,1,0:T(8,128)(2,1)S(1)}, bf16[2,128,256]{2,1,0:T(8,128)(2,1)S(1)}, u32[]{:S(2)}, u32[]{:S(2)}) collective-permute-start(bf16[2,128,256]{2,1,0:T(8,128)(2,1)S(1)} %pad_maximum_fusion.5), channel_id=1, source_target_pairs={{0,128},{128,0},{1,129},{129,1},{2,130},{130,2},{3,131},{131,3},{4... | collective-permute-start | bytes 393224 | tf_op jit(solution)/shard_map/ppermute | solution.py:38
  29.5 12.6 %collective-permute-start.1 = (bf16[2,144,256]{2,1,0:T(8,128)(2,1)S(1)}, bf16[2,144,256]{2,1,0:T(8,128)(2,1)S(1)}, u32[]{:S(2)}, u32[]{:S(2)}) collective-permute-start(bf16[2,144,256]{2,1,0:T(8,128)(2,1)S(1)} %pad_maximum_fusion.4), channel_id=1, source_target_pairs={{0,128},{128,0},{1,129},{129,1},{2,130},{130,2},{3,131},{131,3},{4... | collective-permute-start | bytes 442376 | tf_op jit(solution)/shard_map/ppermute | solution.py:38
  40.2 10.6 %collective-permute-start.7 = (bf16[4,128,256]{2,1,0:T(8,128)(2,1)S(1)}, bf16[4,128,256]{2,1,0:T(8,128)(2,1)S(1)}, u32[]{:S(2)}, u32[]{:S(2)}) collective-permute-start(bf16[4,128,256]{2,1,0:T(8,128)(2,1)S(1)} %pad_maximum_fusion.2.refs_1_), channel_id=1, source_target_pairs={{0,64},{64,0},{1,65},{65,1},{2,66},{66,2},{3,67},{67,3},{4,68},{68... | collective-permute-start | bytes 786440 | tf_op jit(solution)/shard_map/ppermute | solution.py:38
  42.2 11.8 %collective-permute-start.2 = (bf16[4,144,256]{2,1,0:T(8,128)(2,1)S(1)}, bf16[4,144,256]{2,1,0:T(8,128)(2,1)S(1)}, u32[]{:S(2)}, u32[]{:S(2)}) collective-permute-start(bf16[4,144,256]{2,1,0:T(8,128)(2,1)S(1)} %pad_maximum_fusion.1.refs_2_), channel_id=1, source_target_pairs={{0,64},{64,0},{1,65},{65,1},{2,66},{66,2},{3,67},{67,3},{4,68},{68... | collective-permute-start | bytes 884744 | tf_op jit(solution)/shard_map/ppermute | solution.py:38
  46.1 9.8 %collective-permute-start.3 = (bf16[4,144,256]{2,1,0:T(8,128)(2,1)S(1)}, bf16[4,144,256]{2,1,0:T(8,128)(2,1)S(1)}, u32[]{:S(2)}, u32[]{:S(2)}) collective-permute-start(bf16[4,144,256]{2,1,0:T(8,128)(2,1)S(1)} %pad_maximum_fusion.1.refs_2_), channel_id=1, source_target_pairs={{0,32},{32,0},{1,33},{33,1},{2,34},{34,2},{3,35},{35,3},{4,36},{36... | collective-permute-start | bytes 884744 | tf_op jit(solution)/shard_map/ppermute | solution.py:38
  48.1 10.0 %collective-permute-start.8 = (bf16[4,128,256]{2,1,0:T(8,128)(2,1)S(1)}, bf16[4,128,256]{2,1,0:T(8,128)(2,1)S(1)}, u32[]{:S(2)}, u32[]{:S(2)}) collective-permute-start(bf16[4,128,256]{2,1,0:T(8,128)(2,1)S(1)} %pad_maximum_fusion.2.refs_1_), channel_id=1, source_target_pairs={{0,32},{32,0},{1,33},{33,1},{2,34},{34,2},{3,35},{35,3},{4,36},{36... | collective-permute-start | bytes 786440 | tf_op jit(solution)/shard_map/ppermute | solution.py:38
  50.9 7.2 %collective-permute-start.9 = (bf16[4,128,256]{2,1,0:T(8,128)(2,1)S(1)}, bf16[4,128,256]{2,1,0:T(8,128)(2,1)S(1)}, u32[]{:S(2)}, u32[]{:S(2)}) collective-permute-start(bf16[4,128,256]{2,1,0:T(8,128)(2,1)S(1)} %collective-permute-done.7.refs_3_), channel_id=1, source_target_pairs={{0,32},{32,0},{1,33},{33,1},{2,34},{34,2},{3,35},{35,3},{4,36},{36... | collective-permute-start | bytes 786440 | tf_op jit(solution)/shard_map/ppermute | solution.py:38
  54.0 3.5 %collective-permute-start.4 = (bf16[4,144,256]{2,1,0:T(8,128)(2,1)S(1)}, bf16[4,144,256]{2,1,0:T(8,128)(2,1)S(1)}, u32[]{:S(2)}, u32[]{:S(2)}) collective-permute-start(bf16[4,144,256]{2,1,0:T(8,128)(2,1)S(1)} %collective-permute-done.2.refs_4_), channel_id=1, source_target_pairs={{0,32},{32,0},{1,33},{33,1},{2,34},{34,2},{3,35},{35,3},{4,36},{36... | collective-permute-start | bytes 884744 | tf_op jit(solution)/shard_map/ppermute | solution.py:38
  96.4 34.7 %all-to-all-start.1 = ((bf16[16,128,512]{2,1,0:T(8,128)(2,1)}), bf16[16,128,512]{2,1,0:T(8,128)(2,1)S(1)}, u32[]{:S(2)}, u32[]{:S(2)}) async-start(bf16[16,128,512]{2,1,0:T(8,128)(2,1)} %get-tuple-element.14), calls=%async_computation.1 | async-start | bytes 4194304 | tf_op jit(solution)/shard_map/all_to_all | solution.py:46
  102.3 30.2 %copy-start.4 = (bf16[128,512]{1,0:T(8,128)(2,1)S(1)}, bf16[128,512]{1,0:T(8,128)(2,1)}, u32[]{:S(2)}) copy-start(bf16[128,512]{1,0:T(8,128)(2,1)} %param.9) | copy-start | bytes 393220
  102.3 29.0 %collective-permute-start.10 = (bf16[128,512]{1,0:T(8,128)(2,1)S(1)}, bf16[128,512]{1,0:T(8,128)(2,1)S(1)}, u32[]{:S(2)}, u32[]{:S(2)}) collective-permute-start(bf16[128,512]{1,0:T(8,128)(2,1)S(1)} %reduce_sum.98), channel_id=1, source_target_pairs={{0,4},{4,0},{1,5},{5,1},{2,6},{6,2},{3,7},{7,3},{8,12},{12,8},{9,1... | collective-permute-start | bytes 393224 | tf_op jit(solution)/shard_map/ppermute | solution.py:38
  134.6 21.0 %all-to-all-start.2 = ((bf16[16,64,512]{2,1,0:T(8,128)(2,1)}), bf16[16,64,512]{2,1,0:T(8,128)(2,1)S(1)}, u32[]{:S(2)}, u32[]{:S(2)}) async-start(bf16[16,64,512]{2,1,0:T(8,128)(2,1)} %pad_maximum_fusion), calls=%async_computation.2 | async-start | bytes 2097152 | tf_op jit(solution)/shard_map/all_to_all | solution.py:46
  139.7 15.9 %collective-permute-start.16 = (bf16[128,512]{1,0:T(8,128)(2,1)S(1)}, bf16[128,512]{1,0:T(8,128)(2,1)S(1)}, u32[]{:S(2)}, u32[]{:S(2)}) collective-permute-start(bf16[128,512]{1,0:T(8,128)(2,1)S(1)} %multiply_convert_fusion), channel_id=1, source_target_pairs={{0,4},{4,0},{1,5},{5,1},{2,6},{6,2},{3,7},{7,3},{8,12},{12,8},{9,1... | collective-permute-start | bytes 393224 | tf_op jit(solution)/shard_map/ppermute | solution.py:38
  157.8 56.0 %all-to-all-start.3 = ((bf16[16,224,512]{2,1,0:T(8,128)(2,1)}), bf16[16,224,512]{2,1,0:T(8,128)(2,1)}, u32[]{:S(2)}, u32[]{:S(2)}) async-start(bf16[16,224,512]{2,1,0:T(8,128)(2,1)} %broadcast_in_dim.13), calls=%async_computation.3 | async-start | bytes 7340032 | tf_op jit(solution)/shard_map/all_to_all | solution.py:46
  165.1 14.9 %collective-permute-start.11 = (f32[32,512]{1,0:T(8,128)S(1)}, f32[32,512]{1,0:T(8,128)S(1)}, u32[]{:S(2)}, u32[]{:S(2)}) collective-permute-start(f32[32,512]{1,0:T(8,128)S(1)} %convert_reduce_fusion.1), channel_id=1, source_target_pairs={{0,4},{4,0},{1,5},{5,1},{2,6},{6,2},{3,7},{7,3},{8,12},{12,8},{9,1... | collective-permute-start | bytes 196616 | tf_op jit(solution)/shard_map/ppermute | solution.py:38
  180.0 3.1 %collective-permute-start.12 = (f32[32,512]{1,0:T(8,128)S(1)}, f32[32,512]{1,0:T(8,128)S(1)}, u32[]{:S(2)}, u32[]{:S(2)}) collective-permute-start(f32[32,512]{1,0:T(8,128)S(1)} %add.137), channel_id=1, source_target_pairs={{0,32},{32,0},{1,33},{33,1},{2,34},{34,2},{3,35},{35,3},{4,36},{36... | collective-permute-start | bytes 196616 | tf_op jit(solution)/shard_map/ppermute | solution.py:38
  183.2 13.7 %collective-permute-start.13 = (f32[32,512]{1,0:T(8,128)S(1)}, f32[32,512]{1,0:T(8,128)S(1)}, u32[]{:S(2)}, u32[]{:S(2)}) collective-permute-start(f32[32,512]{1,0:T(8,128)S(1)} %add.138), channel_id=1, source_target_pairs={{0,256},{256,0},{1,257},{257,1},{2,258},{258,2},{3,259},{259,3},{4... | collective-permute-start | bytes 196616 | tf_op jit(solution)/shard_map/ppermute | solution.py:38
  196.8 9.6 %collective-permute-start.14 = (f32[32,512]{1,0:T(8,128)S(1)}, f32[32,512]{1,0:T(8,128)S(1)}, u32[]{:S(2)}, u32[]{:S(2)}) collective-permute-start(f32[32,512]{1,0:T(8,128)S(1)} %add.139), channel_id=1, source_target_pairs={{0,128},{128,0},{1,129},{129,1},{2,130},{130,2},{3,131},{131,3},{4... | collective-permute-start | bytes 196616 | tf_op jit(solution)/shard_map/ppermute | solution.py:38
  206.4 7.1 %collective-permute-start.15 = (f32[32,512]{1,0:T(8,128)S(1)}, f32[32,512]{1,0:T(8,128)S(1)}, u32[]{:S(2)}, u32[]{:S(2)}) collective-permute-start(f32[32,512]{1,0:T(8,128)S(1)} %add.140), channel_id=1, source_target_pairs={{0,64},{64,0},{1,65},{65,1},{2,66},{66,2},{3,67},{67,3},{4,68},{68... | collective-permute-start | bytes 196616 | tf_op jit(solution)/shard_map/ppermute | solution.py:38
  217.7 4.4 %collective-permute-start.18 = (bf16[8,128,256]{2,1,0:T(8,128)(2,1)}, bf16[8,128,256]{2,1,0:T(8,128)(2,1)S(1)}, u32[]{:S(2)}, u32[]{:S(2)}) collective-permute-start(bf16[8,128,256]{2,1,0:T(8,128)(2,1)} %get-tuple-element.20), channel_id=1, source_target_pairs={{0,32},{32,0},{1,33},{33,1},{2,34},{34,2},{3,35},{35,3},{4,36},{36... | collective-permute-start | bytes 1572872 | tf_op jit(solution)/shard_map/ppermute | solution.py:38
  219.6 18.9 %collective-permute-start.17 = (bf16[8,128,256]{2,1,0:T(8,128)(2,1)S(1)}, bf16[8,128,256]{2,1,0:T(8,128)(2,1)S(1)}, u32[]{:S(2)}, u32[]{:S(2)}) collective-permute-start(bf16[8,128,256]{2,1,0:T(8,128)(2,1)S(1)} %get-tuple-element.18), channel_id=1, source_target_pairs={{0,32},{32,0},{1,33},{33,1},{2,34},{34,2},{3,35},{35,3},{4,36},{36... | collective-permute-start | bytes 1572872 | tf_op jit(solution)/shard_map/ppermute | solution.py:38
  223.0 25.6 %collective-permute-start.22 = (bf16[4,128,256]{2,1,0:T(8,128)(2,1)}, bf16[4,128,256]{2,1,0:T(8,128)(2,1)S(1)}, u32[]{:S(2)}, u32[]{:S(2)}) collective-permute-start(bf16[4,128,256]{2,1,0:T(8,128)(2,1)} %slice.115), channel_id=1, source_target_pairs={{0,64},{64,0},{1,65},{65,1},{2,66},{66,2},{3,67},{67,3},{4,68},{68... | collective-permute-start | bytes 786440 | tf_op jit(solution)/shard_map/ppermute | solution.py:38
  239.4 11.5 %collective-permute-start.19 = (bf16[4,128,256]{2,1,0:T(8,128)(2,1)}, bf16[4,128,256]{2,1,0:T(8,128)(2,1)}, u32[]{:S(2)}, u32[]{:S(2)}) collective-permute-start(bf16[4,128,256]{2,1,0:T(8,128)(2,1)} %slice.109), channel_id=1, source_target_pairs={{0,64},{64,0},{1,65},{65,1},{2,66},{66,2},{3,67},{67,3},{4,68},{68... | collective-permute-start | bytes 786440 | tf_op jit(solution)/shard_map/ppermute | solution.py:38
  242.6 35.8 %all-to-all-start.4 = ((f32[16,40,512]{2,1,0:T(8,128)}), f32[16,40,512]{2,1,0:T(8,128)S(1)}, u32[]{:S(2)}, u32[]{:S(2)}) async-start(f32[16,40,512]{2,1,0:T(8,128)} %broadcast_in_dim.14), calls=%async_computation.4 | async-start | bytes 2621440 | tf_op jit(solution)/shard_map/all_to_all | solution.py:46
  248.7 13.8 %collective-permute-start.23 = (bf16[2,128,256]{2,1,0:T(8,128)(2,1)S(1)}, bf16[2,128,256]{2,1,0:T(8,128)(2,1)S(1)}, u32[]{:S(2)}, u32[]{:S(2)}) collective-permute-start(bf16[2,128,256]{2,1,0:T(8,128)(2,1)S(1)} %slice.117), channel_id=1, source_target_pairs={{0,128},{128,0},{1,129},{129,1},{2,130},{130,2},{3,131},{131,3},{4... | collective-permute-start | bytes 393224 | tf_op jit(solution)/shard_map/ppermute | solution.py:38
  251.9 15.6 %collective-permute-start.20 = (bf16[2,128,256]{2,1,0:T(8,128)(2,1)S(1)}, bf16[2,128,256]{2,1,0:T(8,128)(2,1)S(1)}, u32[]{:S(2)}, u32[]{:S(2)}) collective-permute-start(bf16[2,128,256]{2,1,0:T(8,128)(2,1)S(1)} %slice.111), channel_id=1, source_target_pairs={{0,128},{128,0},{1,129},{129,1},{2,130},{130,2},{3,131},{131,3},{4... | collective-permute-start | bytes 393224 | tf_op jit(solution)/shard_map/ppermute | solution.py:38
  262.5 12.7 %collective-permute-start.24 = (bf16[1,128,256]{2,1,0:T(8,128)(2,1)S(1)}, bf16[1,128,256]{2,1,0:T(8,128)(2,1)S(1)}, u32[]{:S(2)}, u32[]{:S(2)}) collective-permute-start(bf16[1,128,256]{2,1,0:T(8,128)(2,1)S(1)} %slice.119), channel_id=1, source_target_pairs={{0,256},{256,0},{1,257},{257,1},{2,258},{258,2},{3,259},{259,3},{4... | collective-permute-start | bytes 196616 | tf_op jit(solution)/shard_map/ppermute | solution.py:38
  267.5 10.1 %collective-permute-start.21 = (bf16[1,128,256]{2,1,0:T(8,128)(2,1)S(1)}, bf16[1,128,256]{2,1,0:T(8,128)(2,1)S(1)}, u32[]{:S(2)}, u32[]{:S(2)}) collective-permute-start(bf16[1,128,256]{2,1,0:T(8,128)(2,1)S(1)} %slice.113), channel_id=1, source_target_pairs={{0,256},{256,0},{1,257},{257,1},{2,258},{258,2},{3,259},{259,3},{4... | collective-permute-start | bytes 196616 | tf_op jit(solution)/shard_map/ppermute | solution.py:38
  (2 other events, 23.8 us)

commit v12 on v11

--- a/solution.py
+++ b/solution.py
@@ -136,7 +136,8 @@
     col_index = tile_cols[0, 0]
     col_bits = col_index ^ my_row
     col_place = (col_bits & 1) * n_line + (col_bits & 2) * (n_z4 // 2)
-    col_place = col_place + ((col_bits >> 2) & 1) * 2 + (col_bits >> 3)
+    col_from = col_place + ((col_bits >> 2) & 1) * 2 + (col_bits >> 3)
+    col_to = col_place + (col_index >> 2)
     row_plane = (row_index >> 3) * n_x + (row_index & 3)
     row_place = (((row_index >> 2) & 1) ^ my_zh) * n_plane + row_plane
 
@@ -164,7 +165,7 @@
 
     near_terms, far_terms = tile_sums(
         False,
-        col_place,
+        col_from,
         row_place,
         count,
         tiles,
@@ -198,7 +199,7 @@
     halves = tile_sums(
         True,
         row_place,
-        col_place,
+        col_to,
         count,
         tiles,
         None,
@@ -215,16 +216,14 @@
         keep.astype(F32) + flip(send, "core").astype(F32)
         for keep, send in zip(halves[:CHUNKS], halves[CHUNKS:])
     ]
-    along = jnp.concatenate([total[0, :8] for total in totals], axis=1)
-    weight_rows = swap_parts(copies_of(jnp.concatenate([line_rows, along]), PLANE), PLANE)
-    weight_grad = weight_rows[:, : line_rows.shape[0]].reshape(width, width)
-    for axis in ("z1", "zb", "za"):
-        totals = [total.astype(BF16) for total in totals]
-        size = totals[0].shape[0] // 2
-        totals = [
-            total[:size].astype(F32) + flip(total[size:], axis).astype(F32) for total in totals
-        ]
-    feature_grad = jnp.concatenate([total[0] for total in totals], axis=1) * own_scale[:, None]
+    weight_grad = swap_parts(copies_of(line_rows, PLANE), PLANE).reshape(width, width)
+    totals = [total.astype(BF16) for total in totals]
+    totals = [
+        total[:n_z4].astype(F32) + flip(total[n_z4:], "z1").astype(F32) for total in totals
+    ]
+    pair_sum = jnp.concatenate([total.astype(BF16) for total in totals], axis=2)
+    own_grad = jnp.sum(swap_parts(pair_sum, Z4).astype(F32), axis=0)
+    feature_grad = own_grad * own_scale[:, None]
     return (output, weight_grad, feature_grad)
 
 

time: 281 us -> 299 us (1.064)
  waiting for transfers between devices: 60.2 us -> 89.5 us
  starting transfers between devices: 158 us -> 145 us
    ppermute x25 -> x21, starting transfers between devices: 133 us -> 103 us  [flip(): return lax.ppermute(block, axis, [(0, 1), (1, 0)])]
    all_to_all x4 -> x5, waiting for transfers between devices: 15.4 us -> 41.3 us  [swap_parts(): return lax.all_to_all(parts, axes, split_axis=0, concat_axis=0, tiled=True)]
    all_to_all x4 -> x5, starting transfers between devices: 24.3 us -> 41.7 us  [swap_parts(): return lax.all_to_all(parts, axes, split_axis=0, concat_axis=0, tiled=True)]
    ppermute x25 -> x21, waiting for transfers between devices: 44.8 us -> 48.3 us  [flip(): return lax.ppermute(block, axis, [(0, 1), (1, 0)])]
  transfers between devices with their start and end apart: 29 -> 26, of which waited for: 17 -> 15; matrix products, arithmetic and copies ran while one was open for 3% -> 3% of each run, Pallas kernels for 0% -> 0%
where the time goes in v12:
time: 299 us; the launch traced here: 297 us
  starting transfers between devices  145 us (48%)
  waiting for transfers between devices  89.5 us (30%)
  blocking collectives  33.8 us (11%)
  other arithmetic  9.56 us (3%)
  Pallas kernels  8.6 us (3%)
  local copies, waits for them, and re-layouts  5.84 us (2%)
    ppermute x21, starting transfers between devices, flip(): return lax.ppermute(block, axis, [(0, 1), (1, 0)])  103 us
    ppermute x21, waiting for transfers between devices, flip(): return lax.ppermute(block, axis, [(0, 1), (1, 0)])  48.3 us
    all_to_all x5, starting transfers between devices, swap_parts(): return lax.all_to_all(parts, axes, split_axis=0, concat_axis=0, tiled=True)  41.7 us
    all_to_all x5, waiting for transfers between devices, swap_parts(): return lax.all_to_all(parts, axes, split_axis=0, concat_axis=0, tiled=True)  41.3 us
    all_to_all x1, blocking collectives, swap_parts(): return lax.all_to_all(parts, axes, split_axis=0, concat_axis=0, tiled=True)  33.8 us
    pallas_call x2, Pallas kernels, tile_sums(): pl.pallas_call(functools.partial(tile_kernel, transposed, scaled, sources...  8.6 us
  transfers between devices with their start and end apart: 26, of which 15 were waited for; matrix products, arithmetic and copies ran while one was open for 3% of the time, Pallas kernels for 0%

profile of v12, /device:TPU:24, one launch (start us, length us, event | category | flops | bytes accessed | tf_op | source)
XLA Modules:
  0.0 296.5 jit_solution(15542436049666331543)
XLA Ops:
  4.2 9.1 %collective-permute-start = (bf16[1,144,256]{2,1,0:T(8,128)(2,1)S(1)}, bf16[1,144,256]{2,1,0:T(8,128)(2,1)S(1)}, u32[]{:S(2)}, u32[]{:S(2)}) collective-permute-start(bf16[1,144,256]{2,1,0:T(8,128)(2,1)S(1)} %pad_maximum_fusion.7), channel_id=1, source_target_pairs={{0,256},{256,0},{1,257},{257,1},{2,258},{258,2},{3,259},{259,3},{4... | collective-permute-start | bytes 221192 | tf_op jit(solution)/shard_map/ppermute | solution.py:38
  16.6 11.0 %collective-permute-done.5 = bf16[1,128,256]{2,1,0:T(8,128)(2,1)S(1)} collective-permute-done((bf16[1,128,256]{2,1,0:T(8,128)(2,1)S(1)}, bf16[1,128,256]{2,1,0:T(8,128)(2,1)S(1)}, u32[]{:S(2)}, u32[]{:S(2)}) %collective-permute-start.5) | collective-permute-done | bytes 65568 | tf_op jit(solution)/shard_map/ppermute | solution.py:38
  29.5 4.8 %collective-permute-start.1 = (bf16[2,144,256]{2,1,0:T(8,128)(2,1)S(1)}, bf16[2,144,256]{2,1,0:T(8,128)(2,1)S(1)}, u32[]{:S(2)}, u32[]{:S(2)}) collective-permute-start(bf16[2,144,256]{2,1,0:T(8,128)(2,1)S(1)} %pad_maximum_fusion.5), channel_id=1, source_target_pairs={{0,128},{128,0},{1,129},{129,1},{2,130},{130,2},{3,131},{131,3},{4... | collective-permute-start | bytes 442376 | tf_op jit(solution)/shard_map/ppermute | solution.py:38
  35.0 5.2 %collective-permute-done.6 = bf16[2,128,256]{2,1,0:T(8,128)(2,1)S(1)} collective-permute-done((bf16[2,128,256]{2,1,0:T(8,128)(2,1)S(1)}, bf16[2,128,256]{2,1,0:T(8,128)(2,1)S(1)}, u32[]{:S(2)}, u32[]{:S(2)}) %collective-permute-start.6) | collective-permute-done | bytes 131104 | tf_op jit(solution)/shard_map/ppermute | solution.py:38
  42.2 3.9 %collective-permute-start.2 = (bf16[4,144,256]{2,1,0:T(8,128)(2,1)S(1)}, bf16[4,144,256]{2,1,0:T(8,128)(2,1)S(1)}, u32[]{:S(2)}, u32[]{:S(2)}) collective-permute-start(bf16[4,144,256]{2,1,0:T(8,128)(2,1)S(1)} %pad_maximum_fusion.2.refs_2_), channel_id=1, source_target_pairs={{0,64},{64,0},{1,65},{65,1},{2,66},{66,2},{3,67},{67,3},{4,68},{68... | collective-permute-start | bytes 884744 | tf_op jit(solution)/shard_map/ppermute | solution.py:38
  48.1 2.4 collective-permute-start.3
  58.1 4.3 %shard_map.94 = (bf16[16,128,512]{2,1,0:T(8,128)(2,1)}, bf16[16,128,512]{2,1,0:T(8,128)(2,1)S(1)}) custom-call(s32[8]{0:T(128)S(1)} %get-tuple-element.26.source, s32[8]{0:T(128)S(1)} %add_bitcast_fusion.target.source, s32[1]{0:T(128)} %bitcast.34.count, bf16[8,128,128]{2,1,0:T(8,128)(2,1)S(1)} %bitcast.37, f32[8,128]{1,0:T(8,128)S(1)} %gather_fusion, ...), custom_call_target="tpu_custom_call" | custom-call | flops 134217728 | bytes 12582912 | tf_op jit(solution)/shard_map/pallas_call | solution.py:107
  62.5 33.8 %all_to_all.30 = bf16[16,128,512]{2,1,0:T(8,128)(2,1)S(1)} all-to-all(bf16[16,128,512]{2,1,0:T(8,128)(2,1)S(1)} %get-tuple-element.13), channel_id=1, replica_groups=mesh['za'=2,'zb'=2,'z1'=2,'core'=2,'y'=4,'zh'=2,'x'=4] {'y','x'}, dimensions={0} | all-to-all | bytes 4194304 | tf_op jit(solution)/shard_map/all_to_all | solution.py:46
  96.5 6.0 %all-to-all-start.1 = ((bf16[16,128,512]{2,1,0:T(8,128)(2,1)}), bf16[16,128,512]{2,1,0:T(8,128)(2,1)S(1)}, u32[]{:S(2)}, u32[]{:S(2)}) async-start(bf16[16,128,512]{2,1,0:T(8,128)(2,1)} %get-tuple-element.14), calls=%async_computation.1 | async-start | bytes 4194304 | tf_op jit(solution)/shard_map/all_to_all | solution.py:46
  102.5 13.9 %collective-permute-start.10 = (bf16[128,512]{1,0:T(8,128)(2,1)S(1)}, bf16[128,512]{1,0:T(8,128)(2,1)S(1)}, u32[]{:S(2)}, u32[]{:S(2)}) collective-permute-start(bf16[128,512]{1,0:T(8,128)(2,1)S(1)} %reduce_sum.107), channel_id=1, source_target_pairs={{0,4},{4,0},{1,5},{5,1},{2,6},{6,2},{3,7},{7,3},{8,12},{12,8},{9,1... | collective-permute-start | bytes 393224 | tf_op jit(solution)/shard_map/ppermute | solution.py:38
  116.4 13.8 %all-to-all-done.1 = bf16[16,128,512]{2,1,0:T(8,128)(2,1)S(1)} async-done(((bf16[16,128,512]{2,1,0:T(8,128)(2,1)}), bf16[16,128,512]{2,1,0:T(8,128)(2,1)S(1)}, u32[]{:S(2)}, u32[]{:S(2)}) %all-to-all-start.1) | async-done | bytes 2097184 | tf_op jit(solution)/shard_map/all_to_all | solution.py:46
  133.8 5.3 %all-to-all-start.2 = ((bf16[16,64,512]{2,1,0:T(8,128)(2,1)}), bf16[16,64,512]{2,1,0:T(8,128)(2,1)S(1)}, u32[]{:S(2)}, u32[]{:S(2)}) async-start(bf16[16,64,512]{2,1,0:T(8,128)(2,1)} %pad_maximum_fusion), calls=%async_computation.2 | async-start | bytes 2097152 | tf_op jit(solution)/shard_map/all_to_all | solution.py:46
  139.2 14.2 %collective-permute-start.16 = (bf16[128,512]{1,0:T(8,128)(2,1)S(1)}, bf16[128,512]{1,0:T(8,128)(2,1)S(1)}, u32[]{:S(2)}, u32[]{:S(2)}) collective-permute-start(bf16[128,512]{1,0:T(8,128)(2,1)S(1)} %multiply_convert_fusion), channel_id=1, source_target_pairs={{0,4},{4,0},{1,5},{5,1},{2,6},{6,2},{3,7},{7,3},{8,12},{12,8},{9,1... | collective-permute-start | bytes 393224 | tf_op jit(solution)/shard_map/ppermute | solution.py:38
  153.4 8.7 %collective-permute-done.16 = bf16[128,512]{1,0:T(8,128)(2,1)S(1)} collective-permute-done((bf16[128,512]{1,0:T(8,128)(2,1)S(1)}, bf16[128,512]{1,0:T(8,128)(2,1)S(1)}, u32[]{:S(2)}, u32[]{:S(2)}) %collective-permute-start.16) | collective-permute-done | bytes 131104 | tf_op jit(solution)/shard_map/ppermute | solution.py:38
  162.1 2.2 broadcast_in_dim.14
  164.3 7.2 %all-to-all-start.4 = ((bf16[16,224,512]{2,1,0:T(8,128)(2,1)}), bf16[16,224,512]{2,1,0:T(8,128)(2,1)}, u32[]{:S(2)}, u32[]{:S(2)}) async-start(bf16[16,224,512]{2,1,0:T(8,128)(2,1)} %broadcast_in_dim.14), calls=%async_computation.4 | async-start | bytes 7340032 | tf_op jit(solution)/shard_map/all_to_all | solution.py:46
  171.6 13.1 %collective-permute-start.11 = (f32[32,512]{1,0:T(8,128)S(1)}, f32[32,512]{1,0:T(8,128)S(1)}, u32[]{:S(2)}, u32[]{:S(2)}) collective-permute-start(f32[32,512]{1,0:T(8,128)S(1)} %convert_reduce_fusion.2), channel_id=1, source_target_pairs={{0,4},{4,0},{1,5},{5,1},{2,6},{6,2},{3,7},{7,3},{8,12},{12,8},{9,1... | collective-permute-start | bytes 196616 | tf_op jit(solution)/shard_map/ppermute | solution.py:38
  184.7 2.5 collective-permute-done.11
  190.3 6.1 %collective-permute-start.13 = (f32[32,512]{1,0:T(8,128)S(1)}, f32[32,512]{1,0:T(8,128)S(1)}, u32[]{:S(2)}, u32[]{:S(2)}) collective-permute-start(f32[32,512]{1,0:T(8,128)S(1)} %add.129), channel_id=1, source_target_pairs={{0,256},{256,0},{1,257},{257,1},{2,258},{258,2},{3,259},{259,3},{4... | collective-permute-start | bytes 196616 | tf_op jit(solution)/shard_map/ppermute | solution.py:38
  196.5 3.9 %collective-permute-done.13 = f32[32,512]{1,0:T(8,128)S(1)} collective-permute-done((f32[32,512]{1,0:T(8,128)S(1)}, f32[32,512]{1,0:T(8,128)S(1)}, u32[]{:S(2)}, u32[]{:S(2)}) %collective-permute-start.13) | collective-permute-done | bytes 65568 | tf_op jit(solution)/shard_map/ppermute | solution.py:38
  200.4 5.9 %collective-permute-start.14 = (f32[32,512]{1,0:T(8,128)S(1)}, f32[32,512]{1,0:T(8,128)S(1)}, u32[]{:S(2)}, u32[]{:S(2)}) collective-permute-start(f32[32,512]{1,0:T(8,128)S(1)} %add.130), channel_id=1, source_target_pairs={{0,128},{128,0},{1,129},{129,1},{2,130},{130,2},{3,131},{131,3},{4... | collective-permute-start | bytes 196616 | tf_op jit(solution)/shard_map/ppermute | solution.py:38
  206.4 2.2 collective-permute-done.14
  208.6 5.8 %collective-permute-start.15 = (f32[32,512]{1,0:T(8,128)S(1)}, f32[32,512]{1,0:T(8,128)S(1)}, u32[]{:S(2)}, u32[]{:S(2)}) collective-permute-start(f32[32,512]{1,0:T(8,128)S(1)} %add.131), channel_id=1, source_target_pairs={{0,64},{64,0},{1,65},{65,1},{2,66},{66,2},{3,67},{67,3},{4,68},{68... | collective-permute-start | bytes 196616 | tf_op jit(solution)/shard_map/ppermute | solution.py:38
  214.4 2.2 collective-permute-done.15
  216.7 4.3 %shard_map.95 = (bf16[8,128,256]{2,1,0:T(8,128)(2,1)S(1)}, bf16[8,128,256]{2,1,0:T(8,128)(2,1)S(1)}, bf16[8,128,256]{2,1,0:T(8,128)(2,1)}, bf16[8,128,256]{2,1,0:T(8,128)(2,1)S(1)}) custom-call(s32[8]{0:T(128)S(1)} %add_bitcast_fusion.target.source, s32[8]{0:T(128)S(1)} %get-tuple-element.25.target, s32[1]{0:T(128)} %bitcast.35.count, ...), custom_call_target="tpu_custom_call" | custom-call | flops 134217728 | bytes 6291456 | tf_op jit(solution)/shard_map/pallas_call | solution.py:107
  222.9 2.4 collective-permute-start.19
  226.4 7.7 %all-to-all-start.3 = ((f32[16,32,512]{2,1,0:T(8,128)}), f32[16,32,512]{2,1,0:T(8,128)S(1)}, u32[]{:S(2)}, u32[]{:S(2)}) async-start(f32[16,32,512]{2,1,0:T(8,128)} %broadcast_in_dim.13), calls=%async_computation.3 | async-start | bytes 2097152 | tf_op jit(solution)/shard_map/all_to_all | solution.py:46
  235.3 4.0 %collective-permute-start.18 = (bf16[4,128,256]{2,1,0:T(8,128)(2,1)S(1)}, bf16[4,128,256]{2,1,0:T(8,128)(2,1)S(1)}, u32[]{:S(2)}, u32[]{:S(2)}) collective-permute-start(bf16[4,128,256]{2,1,0:T(8,128)(2,1)S(1)} %slice.62), channel_id=1, source_target_pairs={{0,64},{64,0},{1,65},{65,1},{2,66},{66,2},{3,67},{67,3},{4,68},{68... | collective-permute-start | bytes 786440 | tf_op jit(solution)/shard_map/ppermute | solution.py:38
  242.5 3.7 %collective-permute-done.18 = bf16[4,128,256]{2,1,0:T(8,128)(2,1)S(1)} collective-permute-done((bf16[4,128,256]{2,1,0:T(8,128)(2,1)S(1)}, bf16[4,128,256]{2,1,0:T(8,128)(2,1)S(1)}, u32[]{:S(2)}, u32[]{:S(2)}) %collective-permute-start.18) | collective-permute-done | bytes 262176 | tf_op jit(solution)/shard_map/ppermute | solution.py:38
  246.2 4.6 %collective-permute-done.20 = bf16[4,128,256]{2,1,0:T(8,128)(2,1)S(1)} collective-permute-done((bf16[4,128,256]{2,1,0:T(8,128)(2,1)S(1)}, bf16[4,128,256]{2,1,0:T(8,128)(2,1)S(1)}, u32[]{:S(2)}, u32[]{:S(2)}) %collective-permute-start.20) | collective-permute-done | bytes 262176 | tf_op jit(solution)/shard_map/ppermute | solution.py:38
  251.8 15.5 %all-to-all-start.5 = ((bf16[4,128,512]{2,1,0:T(8,128)(2,1)}), bf16[4,128,512]{2,1,0:T(8,128)(2,1)S(1)}, u32[]{:S(2)}, u32[]{:S(2)}) async-start(bf16[4,128,512]{2,1,0:T(8,128)(2,1)} %pad_maximum_fusion.1), calls=%async_computation.5 | async-start | bytes 1048576 | tf_op jit(solution)/shard_map/all_to_all | solution.py:46
  267.3 27.4 %all-to-all-done.5 = bf16[4,128,512]{2,1,0:T(8,128)(2,1)S(1)} async-done(((bf16[4,128,512]{2,1,0:T(8,128)(2,1)}), bf16[4,128,512]{2,1,0:T(8,128)(2,1)S(1)}, u32[]{:S(2)}, u32[]{:S(2)}) %all-to-all-start.5) | async-done | bytes 524320 | tf_op jit(solution)/shard_map/all_to_all | solution.py:46
  (92 shorter events, 37.3 us)
Async XLA Ops:
  0.6 130.2 %copy-start = (bf16[512,512]{1,0:T(8,128)(2,1)S(1)}, bf16[512,512]{1,0:T(8,128)(2,1)}, u32[]{:S(2)}) copy-start(bf16[512,512]{1,0:T(8,128)(2,1)} %param.8) | copy-start | bytes 1572868
  0.6 57.5 %copy-start.1 = (bf16[1,1,8,128,128]{4,3,2,1,0:T(8,128)(2,1)S(1)}, bf16[1,1,8,128,128]{4,3,2,1,0:T(8,128)(2,1)}, u32[]{:S(2)}) copy-start(bf16[1,1,8,128,128]{4,3,2,1,0:T(8,128)(2,1)} %param.13) | copy-start | bytes 786436
  4.2 25.3 %collective-permute-start = (bf16[1,144,256]{2,1,0:T(8,128)(2,1)S(1)}, bf16[1,144,256]{2,1,0:T(8,128)(2,1)S(1)}, u32[]{:S(2)}, u32[]{:S(2)}) collective-permute-start(bf16[1,144,256]{2,1,0:T(8,128)(2,1)S(1)} %pad_maximum_fusion.7), channel_id=1, source_target_pairs={{0,256},{256,0},{1,257},{257,1},{2,258},{258,2},{3,259},{259,3},{4... | collective-permute-start | bytes 221192 | tf_op jit(solution)/shard_map/ppermute | solution.py:38
  13.3 14.2 %collective-permute-start.5 = (bf16[1,128,256]{2,1,0:T(8,128)(2,1)S(1)}, bf16[1,128,256]{2,1,0:T(8,128)(2,1)S(1)}, u32[]{:S(2)}, u32[]{:S(2)}) collective-permute-start(bf16[1,128,256]{2,1,0:T(8,128)(2,1)S(1)} %get-tuple-element.21), channel_id=1, source_target_pairs={{0,256},{256,0},{1,257},{257,1},{2,258},{258,2},{3,259},{259,3},{4... | collective-permute-start | bytes 196616 | tf_op jit(solution)/shard_map/ppermute | solution.py:38
  27.6 12.6 %collective-permute-start.6 = (bf16[2,128,256]{2,1,0:T(8,128)(2,1)S(1)}, bf16[2,128,256]{2,1,0:T(8,128)(2,1)S(1)}, u32[]{:S(2)}, u32[]{:S(2)}) collective-permute-start(bf16[2,128,256]{2,1,0:T(8,128)(2,1)S(1)} %pad_maximum_fusion.6), channel_id=1, source_target_pairs={{0,128},{128,0},{1,129},{129,1},{2,130},{130,2},{3,131},{131,3},{4... | collective-permute-start | bytes 393224 | tf_op jit(solution)/shard_map/ppermute | solution.py:38
  29.5 12.6 %collective-permute-start.1 = (bf16[2,144,256]{2,1,0:T(8,128)(2,1)S(1)}, bf16[2,144,256]{2,1,0:T(8,128)(2,1)S(1)}, u32[]{:S(2)}, u32[]{:S(2)}) collective-permute-start(bf16[2,144,256]{2,1,0:T(8,128)(2,1)S(1)} %pad_maximum_fusion.5), channel_id=1, source_target_pairs={{0,128},{128,0},{1,129},{129,1},{2,130},{130,2},{3,131},{131,3},{4... | collective-permute-start | bytes 442376 | tf_op jit(solution)/shard_map/ppermute | solution.py:38
  40.2 10.6 %collective-permute-start.7 = (bf16[4,128,256]{2,1,0:T(8,128)(2,1)S(1)}, bf16[4,128,256]{2,1,0:T(8,128)(2,1)S(1)}, u32[]{:S(2)}, u32[]{:S(2)}) collective-permute-start(bf16[4,128,256]{2,1,0:T(8,128)(2,1)S(1)} %pad_maximum_fusion.3.refs_1_), channel_id=1, source_target_pairs={{0,64},{64,0},{1,65},{65,1},{2,66},{66,2},{3,67},{67,3},{4,68},{68... | collective-permute-start | bytes 786440 | tf_op jit(solution)/shard_map/ppermute | solution.py:38
  42.2 11.8 %collective-permute-start.2 = (bf16[4,144,256]{2,1,0:T(8,128)(2,1)S(1)}, bf16[4,144,256]{2,1,0:T(8,128)(2,1)S(1)}, u32[]{:S(2)}, u32[]{:S(2)}) collective-permute-start(bf16[4,144,256]{2,1,0:T(8,128)(2,1)S(1)} %pad_maximum_fusion.2.refs_2_), channel_id=1, source_target_pairs={{0,64},{64,0},{1,65},{65,1},{2,66},{66,2},{3,67},{67,3},{4,68},{68... | collective-permute-start | bytes 884744 | tf_op jit(solution)/shard_map/ppermute | solution.py:38
  46.2 12.0 %collective-permute-start.8 = (bf16[4,128,256]{2,1,0:T(8,128)(2,1)S(1)}, bf16[4,128,256]{2,1,0:T(8,128)(2,1)S(1)}, u32[]{:S(2)}, u32[]{:S(2)}) collective-permute-start(bf16[4,128,256]{2,1,0:T(8,128)(2,1)S(1)} %pad_maximum_fusion.3.refs_1_), channel_id=1, source_target_pairs={{0,32},{32,0},{1,33},{33,1},{2,34},{34,2},{3,35},{35,3},{4,36},{36... | collective-permute-start | bytes 786440 | tf_op jit(solution)/shard_map/ppermute | solution.py:38
  48.1 7.9 %collective-permute-start.3 = (bf16[4,144,256]{2,1,0:T(8,128)(2,1)S(1)}, bf16[4,144,256]{2,1,0:T(8,128)(2,1)S(1)}, u32[]{:S(2)}, u32[]{:S(2)}) collective-permute-start(bf16[4,144,256]{2,1,0:T(8,128)(2,1)S(1)} %pad_maximum_fusion.2.refs_2_), channel_id=1, source_target_pairs={{0,32},{32,0},{1,33},{33,1},{2,34},{34,2},{3,35},{35,3},{4,36},{36... | collective-permute-start | bytes 884744 | tf_op jit(solution)/shard_map/ppermute | solution.py:38
  50.9 7.2 %collective-permute-start.9 = (bf16[4,128,256]{2,1,0:T(8,128)(2,1)S(1)}, bf16[4,128,256]{2,1,0:T(8,128)(2,1)S(1)}, u32[]{:S(2)}, u32[]{:S(2)}) collective-permute-start(bf16[4,128,256]{2,1,0:T(8,128)(2,1)S(1)} %collective-permute-done.7.refs_3_), channel_id=1, source_target_pairs={{0,32},{32,0},{1,33},{33,1},{2,34},{34,2},{3,35},{35,3},{4,36},{36... | collective-permute-start | bytes 786440 | tf_op jit(solution)/shard_map/ppermute | solution.py:38
  54.0 3.5 %collective-permute-start.4 = (bf16[4,144,256]{2,1,0:T(8,128)(2,1)S(1)}, bf16[4,144,256]{2,1,0:T(8,128)(2,1)S(1)}, u32[]{:S(2)}, u32[]{:S(2)}) collective-permute-start(bf16[4,144,256]{2,1,0:T(8,128)(2,1)S(1)} %collective-permute-done.2.refs_4_), channel_id=1, source_target_pairs={{0,32},{32,0},{1,33},{33,1},{2,34},{34,2},{3,35},{35,3},{4,36},{36... | collective-permute-start | bytes 884744 | tf_op jit(solution)/shard_map/ppermute | solution.py:38
  96.5 33.8 %all-to-all-start.1 = ((bf16[16,128,512]{2,1,0:T(8,128)(2,1)}), bf16[16,128,512]{2,1,0:T(8,128)(2,1)S(1)}, u32[]{:S(2)}, u32[]{:S(2)}) async-start(bf16[16,128,512]{2,1,0:T(8,128)(2,1)} %get-tuple-element.14), calls=%async_computation.1 | async-start | bytes 4194304 | tf_op jit(solution)/shard_map/all_to_all | solution.py:46
  102.5 29.3 %copy-start.2 = (bf16[128,512]{1,0:T(8,128)(2,1)S(1)}, bf16[128,512]{1,0:T(8,128)(2,1)}, u32[]{:S(2)}) copy-start(bf16[128,512]{1,0:T(8,128)(2,1)} %param.9) | copy-start | bytes 393220
  102.5 28.1 %collective-permute-start.10 = (bf16[128,512]{1,0:T(8,128)(2,1)S(1)}, bf16[128,512]{1,0:T(8,128)(2,1)S(1)}, u32[]{:S(2)}, u32[]{:S(2)}) collective-permute-start(bf16[128,512]{1,0:T(8,128)(2,1)S(1)} %reduce_sum.107), channel_id=1, source_target_pairs={{0,4},{4,0},{1,5},{5,1},{2,6},{6,2},{3,7},{7,3},{8,12},{12,8},{9,1... | collective-permute-start | bytes 393224 | tf_op jit(solution)/shard_map/ppermute | solution.py:38
  133.8 28.3 %all-to-all-start.2 = ((bf16[16,64,512]{2,1,0:T(8,128)(2,1)}), bf16[16,64,512]{2,1,0:T(8,128)(2,1)S(1)}, u32[]{:S(2)}, u32[]{:S(2)}) async-start(bf16[16,64,512]{2,1,0:T(8,128)(2,1)} %pad_maximum_fusion), calls=%async_computation.2 | async-start | bytes 2097152 | tf_op jit(solution)/shard_map/all_to_all | solution.py:46
  139.2 22.9 %collective-permute-start.16 = (bf16[128,512]{1,0:T(8,128)(2,1)S(1)}, bf16[128,512]{1,0:T(8,128)(2,1)S(1)}, u32[]{:S(2)}, u32[]{:S(2)}) collective-permute-start(bf16[128,512]{1,0:T(8,128)(2,1)S(1)} %multiply_convert_fusion), channel_id=1, source_target_pairs={{0,4},{4,0},{1,5},{5,1},{2,6},{6,2},{3,7},{7,3},{8,12},{12,8},{9,1... | collective-permute-start | bytes 393224 | tf_op jit(solution)/shard_map/ppermute | solution.py:38
  164.3 52.4 %all-to-all-start.4 = ((bf16[16,224,512]{2,1,0:T(8,128)(2,1)}), bf16[16,224,512]{2,1,0:T(8,128)(2,1)}, u32[]{:S(2)}, u32[]{:S(2)}) async-start(bf16[16,224,512]{2,1,0:T(8,128)(2,1)} %broadcast_in_dim.14), calls=%async_computation.4 | async-start | bytes 7340032 | tf_op jit(solution)/shard_map/all_to_all | solution.py:46
  171.6 15.6 %collective-permute-start.11 = (f32[32,512]{1,0:T(8,128)S(1)}, f32[32,512]{1,0:T(8,128)S(1)}, u32[]{:S(2)}, u32[]{:S(2)}) collective-permute-start(f32[32,512]{1,0:T(8,128)S(1)} %convert_reduce_fusion.2), channel_id=1, source_target_pairs={{0,4},{4,0},{1,5},{5,1},{2,6},{6,2},{3,7},{7,3},{8,12},{12,8},{9,1... | collective-permute-start | bytes 196616 | tf_op jit(solution)/shard_map/ppermute | solution.py:38
  187.2 3.1 %collective-permute-start.12 = (f32[32,512]{1,0:T(8,128)S(1)}, f32[32,512]{1,0:T(8,128)S(1)}, u32[]{:S(2)}, u32[]{:S(2)}) collective-permute-start(f32[32,512]{1,0:T(8,128)S(1)} %add.128), channel_id=1, source_target_pairs={{0,32},{32,0},{1,33},{33,1},{2,34},{34,2},{3,35},{35,3},{4,36},{36... | collective-permute-start | bytes 196616 | tf_op jit(solution)/shard_map/ppermute | solution.py:38
  190.3 10.1 %collective-permute-start.13 = (f32[32,512]{1,0:T(8,128)S(1)}, f32[32,512]{1,0:T(8,128)S(1)}, u32[]{:S(2)}, u32[]{:S(2)}) collective-permute-start(f32[32,512]{1,0:T(8,128)S(1)} %add.129), channel_id=1, source_target_pairs={{0,256},{256,0},{1,257},{257,1},{2,258},{258,2},{3,259},{259,3},{4... | collective-permute-start | bytes 196616 | tf_op jit(solution)/shard_map/ppermute | solution.py:38
  200.4 8.2 %collective-permute-start.14 = (f32[32,512]{1,0:T(8,128)S(1)}, f32[32,512]{1,0:T(8,128)S(1)}, u32[]{:S(2)}, u32[]{:S(2)}) collective-permute-start(f32[32,512]{1,0:T(8,128)S(1)} %add.130), channel_id=1, source_target_pairs={{0,128},{128,0},{1,129},{129,1},{2,130},{130,2},{3,131},{131,3},{4... | collective-permute-start | bytes 196616 | tf_op jit(solution)/shard_map/ppermute | solution.py:38
  208.6 8.0 %collective-permute-start.15 = (f32[32,512]{1,0:T(8,128)S(1)}, f32[32,512]{1,0:T(8,128)S(1)}, u32[]{:S(2)}, u32[]{:S(2)}) collective-permute-start(f32[32,512]{1,0:T(8,128)S(1)} %add.131), channel_id=1, source_target_pairs={{0,64},{64,0},{1,65},{65,1},{2,66},{66,2},{3,67},{67,3},{4,68},{68... | collective-permute-start | bytes 196616 | tf_op jit(solution)/shard_map/ppermute | solution.py:38
  220.9 13.1 %collective-permute-start.17 = (bf16[8,128,256]{2,1,0:T(8,128)(2,1)}, bf16[8,128,256]{2,1,0:T(8,128)(2,1)}, u32[]{:S(2)}, u32[]{:S(2)}) collective-permute-start(bf16[8,128,256]{2,1,0:T(8,128)(2,1)} %get-tuple-element.18), channel_id=1, source_target_pairs={{0,32},{32,0},{1,33},{33,1},{2,34},{34,2},{3,35},{35,3},{4,36},{36... | collective-permute-start | bytes 1572872 | tf_op jit(solution)/shard_map/ppermute | solution.py:38
  222.9 16.5 %collective-permute-start.19 = (bf16[8,128,256]{2,1,0:T(8,128)(2,1)S(1)}, bf16[8,128,256]{2,1,0:T(8,128)(2,1)}, u32[]{:S(2)}, u32[]{:S(2)}) collective-permute-start(bf16[8,128,256]{2,1,0:T(8,128)(2,1)S(1)} %get-tuple-element.20), channel_id=1, source_target_pairs={{0,32},{32,0},{1,33},{33,1},{2,34},{34,2},{3,35},{35,3},{4,36},{36... | collective-permute-start | bytes 1572872 | tf_op jit(solution)/shard_map/ppermute | solution.py:38
  226.4 25.4 %all-to-all-start.3 = ((f32[16,32,512]{2,1,0:T(8,128)}), f32[16,32,512]{2,1,0:T(8,128)S(1)}, u32[]{:S(2)}, u32[]{:S(2)}) async-start(f32[16,32,512]{2,1,0:T(8,128)} %broadcast_in_dim.13), calls=%async_computation.3 | async-start | bytes 2097152 | tf_op jit(solution)/shard_map/all_to_all | solution.py:46
  235.3 10.9 %collective-permute-start.18 = (bf16[4,128,256]{2,1,0:T(8,128)(2,1)S(1)}, bf16[4,128,256]{2,1,0:T(8,128)(2,1)S(1)}, u32[]{:S(2)}, u32[]{:S(2)}) collective-permute-start(bf16[4,128,256]{2,1,0:T(8,128)(2,1)S(1)} %slice.62), channel_id=1, source_target_pairs={{0,64},{64,0},{1,65},{65,1},{2,66},{66,2},{3,67},{67,3},{4,68},{68... | collective-permute-start | bytes 786440 | tf_op jit(solution)/shard_map/ppermute | solution.py:38
  240.6 10.3 %collective-permute-start.20 = (bf16[4,128,256]{2,1,0:T(8,128)(2,1)S(1)}, bf16[4,128,256]{2,1,0:T(8,128)(2,1)S(1)}, u32[]{:S(2)}, u32[]{:S(2)}) collective-permute-start(bf16[4,128,256]{2,1,0:T(8,128)(2,1)S(1)} %slice.64), channel_id=1, source_target_pairs={{0,64},{64,0},{1,65},{65,1},{2,66},{66,2},{3,67},{67,3},{4,68},{68... | collective-permute-start | bytes 786440 | tf_op jit(solution)/shard_map/ppermute | solution.py:38
  251.8 42.9 %all-to-all-start.5 = ((bf16[4,128,512]{2,1,0:T(8,128)(2,1)}), bf16[4,128,512]{2,1,0:T(8,128)(2,1)S(1)}, u32[]{:S(2)}, u32[]{:S(2)}) async-start(bf16[4,128,512]{2,1,0:T(8,128)(2,1)} %pad_maximum_fusion.1), calls=%async_computation.5 | async-start | bytes 1048576 | tf_op jit(solution)/shard_map/all_to_all | solution.py:46

commit v13 on v10

--- a/solution.py
+++ b/solution.py
@@ -56,7 +56,16 @@
     arrays, outputs = refs[: -1 - len(places)], refs[-1 - len(places) : -1]
     slots, size, _ = tiles.shape
     axis = 0 if transposed else 1
+    for output in outputs:
+        output[...] = jnp.zeros_like(output)
     total[...] = jnp.zeros_like(total)
+    owners = []
+    for slot in range(slots):
+        owner = jnp.int32(slot)
+        for earlier in reversed(range(slot)):
+            owner = jnp.where(target[earlier] == target[slot], earlier, owner)
+        owners.append(owner)
+
     for slot in range(slots):
 
         def add(block, left):
@@ -66,7 +75,7 @@
                 lanes = [block[:, i : i + size] for i in range(0, block.shape[1], size)]
                 lanes = [(part.astype(F32) * column).astype(BF16) for part in lanes]
                 block = jnp.concatenate(lanes, axis=1)
-            total[target[slot], :, left : left + block.shape[1]] += lax.dot_general(
+            total[owners[slot], :, left : left + block.shape[1]] += lax.dot_general(
                 tiles[slot], block, (((axis,), (0,)), ((), ())), preferred_element_type=F32
             )
 
@@ -85,35 +94,35 @@
                     add(block, left)
                     left += block.shape[1]
 
-    for output, (left, right, pieces) in zip(outputs, places):
-        row = 0
-        for start, stop, low, high in pieces:
-            part = total[start:stop, low:high, left:right]
-            output[:, row : row + high - low, :] = part.astype(BF16)
-            row += high - low
-
-
-def tile_sums(transposed, source, target, count, tiles, scale, arrays, sources, places, blocks):
+    for slot in range(slots):
+        for output, (left, right, start, stop) in zip(outputs, places):
+            place = target[slot] - start
+            held = (place >= 0) & (place < stop - start)
+
+            @pl.when((slot < count[0]) & (owners[slot] == slot) & held)
+            def _(output=output, left=left, right=right, place=jnp.clip(place, 0, stop - start - 1)):
+                output[place] = total[slot, :, left:right].astype(BF16)
+
+
+def tile_sums(transposed, source, target, count, tiles, scale, arrays, sources, places):
     slots, size, _ = tiles.shape
     width = sum(arrays[pieces[0][0]].shape[2] for pieces in sources[0])
     smem = pl.BlockSpec(memory_space=pltpu.SMEM)
     vmem = pl.BlockSpec(memory_space=pltpu.VMEM)
     scaled = scale is not None
     operands = [tiles] + [scale] * scaled + list(arrays)
-    shapes = [
-        (pieces[0][1] - pieces[0][0], sum(high - low for _, _, low, high in pieces), right - left)
-        for left, right, pieces in places
-    ]
+    shapes = [(stop - start, size, right - left) for left, right, start, stop in places]
+    moved = sum(math.prod(shape) for shape in shapes) + sum(array.size for array in arrays)
     return pl.pallas_call(
         functools.partial(tile_kernel, transposed, scaled, sources, places),
         out_shape=[jax.ShapeDtypeStruct(shape, BF16) for shape in shapes],
         in_specs=[smem] * 3 + [vmem] * len(operands),
         out_specs=[vmem] * len(shapes),
-        scratch_shapes=[pltpu.VMEM((blocks, size, width), F32)],
+        scratch_shapes=[pltpu.VMEM((slots, size, width), F32)],
         compiler_params=pltpu.CompilerParams(vmem_limit_bytes=40 * 1024 * 1024),
         cost_estimate=pl.CostEstimate(
             flops=2 * slots * size * size * width,
-            bytes_accessed=6 * blocks * size * width,
+            bytes_accessed=2 * moved,
             transcendentals=0,
         ),
     )(source, target, count, *operands)
@@ -171,8 +180,7 @@
         slot_scale,
         sum(groups, []),
         [[[(g * CHUNKS + c, 0, span)] for c in range(CHUNKS)] for g in range(len(groups))],
-        [(0, width, [(0, n_plane, 0, span)]), (0, width, [(n_plane, n_col, 0, span)])],
-        n_col,
+        [(0, width, 0, n_plane), (0, width, n_plane, n_col)],
     )
     far_sum = jnp.sum(swap_parts(far_terms, PLANE).astype(F32), axis=0).astype(BF16)
     near_group = swap_parts(after(near_terms, far_sum), PLANE)
@@ -204,12 +212,7 @@
         None,
         [first_group, last_group],
         [[[(0, 0, lead), (1, 0, span - lead)]], [[(1, span - lead, 2 * span - lead)]]],
-        [
-            (part.start, part.stop, [(first, first + n_line, 0, span)])
-            for first in (0, n_line)
-            for part in parts
-        ],
-        n_row,
+        [(part.start, part.stop, first, first + n_line) for first in (0, n_line) for part in parts],
     )
     totals = [
         keep.astype(F32) + flip(send, "core").astype(F32)

time: 282 us -> 283 us (level)
  starting transfers between devices: 144 us -> 147 us
  transfers between devices with their start and end apart: 29 -> 29, of which waited for: 14 -> 16; matrix products, arithmetic and copies ran while one was open for 3% -> 3% of each run, Pallas kernels for 0% -> 0%
where the time goes in v13:
time: 283 us; the launch traced here: 281 us
  starting transfers between devices  147 us (52%)
  waiting for transfers between devices  70.9 us (25%)
  blocking collectives  33.1 us (12%)
  Pallas kernels  10.2 us (4%)
  other arithmetic  7.63 us (3%)
  local copies, waits for them, and re-layouts  7.6 us (3%)
    ppermute x25, starting transfers between devices, flip(): return lax.ppermute(block, axis, [(0, 1), (1, 0)])  122 us
    ppermute x25, waiting for transfers between devices, flip(): return lax.ppermute(block, axis, [(0, 1), (1, 0)])  56.6 us
    all_to_all x1, blocking collectives, swap_parts(): return lax.all_to_all(parts, axes, split_axis=0, concat_axis=0, tiled=True)  33.1 us
    all_to_all x4, starting transfers between devices, swap_parts(): return lax.all_to_all(parts, axes, split_axis=0, concat_axis=0, tiled=True)  25.4 us
    all_to_all x4, waiting for transfers between devices, swap_parts(): return lax.all_to_all(parts, axes, split_axis=0, concat_axis=0, tiled=True)  14.2 us
    pallas_call x2, Pallas kernels, tile_sums(): pl.pallas_call(functools.partial(tile_kernel, transposed, scaled, sources...  10.2 us
  transfers between devices with their start and end apart: 29, of which 16 were waited for; matrix products, arithmetic and copies ran while one was open for 3% of the time, Pallas kernels for 0%

profile of v13, /device:TPU:24, one launch (start us, length us, event | category | flops | bytes accessed | tf_op | source)
XLA Modules:
  0.0 281.5 jit_solution(3565862669455003355)
XLA Ops:
  4.2 9.1 %collective-permute-start = (bf16[1,144,256]{2,1,0:T(8,128)(2,1)S(1)}, bf16[1,144,256]{2,1,0:T(8,128)(2,1)S(1)}, u32[]{:S(2)}, u32[]{:S(2)}) collective-permute-start(bf16[1,144,256]{2,1,0:T(8,128)(2,1)S(1)} %pad_maximum_fusion.6), channel_id=1, source_target_pairs={{0,256},{256,0},{1,257},{257,1},{2,258},{258,2},{3,259},{259,3},{4... | collective-permute-start | bytes 221192 | tf_op jit(solution)/shard_map/ppermute | solution.py:38
  16.6 11.0 %collective-permute-done.5 = bf16[1,128,256]{2,1,0:T(8,128)(2,1)S(1)} collective-permute-done((bf16[1,128,256]{2,1,0:T(8,128)(2,1)S(1)}, bf16[1,128,256]{2,1,0:T(8,128)(2,1)S(1)}, u32[]{:S(2)}, u32[]{:S(2)}) %collective-permute-start.5) | collective-permute-done | bytes 65568 | tf_op jit(solution)/shard_map/ppermute | solution.py:38
  29.5 4.8 %collective-permute-start.1 = (bf16[2,144,256]{2,1,0:T(8,128)(2,1)S(1)}, bf16[2,144,256]{2,1,0:T(8,128)(2,1)S(1)}, u32[]{:S(2)}, u32[]{:S(2)}) collective-permute-start(bf16[2,144,256]{2,1,0:T(8,128)(2,1)S(1)} %pad_maximum_fusion.4), channel_id=1, source_target_pairs={{0,128},{128,0},{1,129},{129,1},{2,130},{130,2},{3,131},{131,3},{4... | collective-permute-start | bytes 442376 | tf_op jit(solution)/shard_map/ppermute | solution.py:38
  35.0 5.2 %collective-permute-done.6 = bf16[2,128,256]{2,1,0:T(8,128)(2,1)S(1)} collective-permute-done((bf16[2,128,256]{2,1,0:T(8,128)(2,1)S(1)}, bf16[2,128,256]{2,1,0:T(8,128)(2,1)S(1)}, u32[]{:S(2)}, u32[]{:S(2)}) %collective-permute-start.6) | collective-permute-done | bytes 131104 | tf_op jit(solution)/shard_map/ppermute | solution.py:38
  42.2 3.9 %collective-permute-start.2 = (bf16[4,144,256]{2,1,0:T(8,128)(2,1)S(1)}, bf16[4,144,256]{2,1,0:T(8,128)(2,1)S(1)}, u32[]{:S(2)}, u32[]{:S(2)}) collective-permute-start(bf16[4,144,256]{2,1,0:T(8,128)(2,1)S(1)} %pad_maximum_fusion.1.refs_1_), channel_id=1, source_target_pairs={{0,64},{64,0},{1,65},{65,1},{2,66},{66,2},{3,67},{67,3},{4,68},{68... | collective-permute-start | bytes 884744 | tf_op jit(solution)/shard_map/ppermute | solution.py:38
  48.1 2.4 collective-permute-start.8
  58.1 4.9 %shard_map.94 = (bf16[16,128,512]{2,1,0:T(8,128)(2,1)}, bf16[16,128,512]{2,1,0:T(8,128)(2,1)S(1)}) custom-call(s32[8]{0:T(128)S(1)} %shift-right-arithmetic_add_fusion.source.target, s32[8]{0:T(128)S(1)} %add_bitcast_fusion.2.target.source, s32[1]{0:T(128)} %bitcast.36.count, bf16[8,128,128]{2,1,0:T(8,128)(2,1)S(1)} %bitcast.39, f32[8,128]{1,0:T(8,128)S(1)} %gather_fusion, ...), custom_call_target="tpu_custom_call" | custom-call | flops 134217728 | bytes 6422528 | tf_op jit(solution)/shard_map/pallas_call | solution.py:116
  63.0 33.1 %all_to_all.25 = bf16[16,128,512]{2,1,0:T(8,128)(2,1)S(1)} all-to-all(bf16[16,128,512]{2,1,0:T(8,128)(2,1)S(1)} %get-tuple-element.13), channel_id=1, replica_groups=mesh['za'=2,'zb'=2,'z1'=2,'core'=2,'y'=4,'zh'=2,'x'=4] {'y','x'}, dimensions={0} | all-to-all | bytes 4194304 | tf_op jit(solution)/shard_map/all_to_all | solution.py:46
  96.4 6.0 %all-to-all-start.1 = ((bf16[16,128,512]{2,1,0:T(8,128)(2,1)}), bf16[16,128,512]{2,1,0:T(8,128)(2,1)S(1)}, u32[]{:S(2)}, u32[]{:S(2)}) async-start(bf16[16,128,512]{2,1,0:T(8,128)(2,1)} %get-tuple-element.14), calls=%async_computation.1 | async-start | bytes 4194304 | tf_op jit(solution)/shard_map/all_to_all | solution.py:46
  102.4 14.1 %collective-permute-start.10 = (bf16[128,512]{1,0:T(8,128)(2,1)S(1)}, bf16[128,512]{1,0:T(8,128)(2,1)S(1)}, u32[]{:S(2)}, u32[]{:S(2)}) collective-permute-start(bf16[128,512]{1,0:T(8,128)(2,1)S(1)} %reduce_sum.98), channel_id=1, source_target_pairs={{0,4},{4,0},{1,5},{5,1},{2,6},{6,2},{3,7},{7,3},{8,12},{12,8},{9,1... | collective-permute-start | bytes 393224 | tf_op jit(solution)/shard_map/ppermute | solution.py:38
  116.5 14.2 %all-to-all-done.1 = bf16[16,128,512]{2,1,0:T(8,128)(2,1)S(1)} async-done(((bf16[16,128,512]{2,1,0:T(8,128)(2,1)}), bf16[16,128,512]{2,1,0:T(8,128)(2,1)S(1)}, u32[]{:S(2)}, u32[]{:S(2)}) %all-to-all-start.1) | async-done | bytes 2097184 | tf_op jit(solution)/shard_map/all_to_all | solution.py:46
  134.3 5.2 %all-to-all-start.2 = ((bf16[16,64,512]{2,1,0:T(8,128)(2,1)}), bf16[16,64,512]{2,1,0:T(8,128)(2,1)S(1)}, u32[]{:S(2)}, u32[]{:S(2)}) async-start(bf16[16,64,512]{2,1,0:T(8,128)(2,1)} %pad_maximum_fusion), calls=%async_computation.2 | async-start | bytes 2097152 | tf_op jit(solution)/shard_map/all_to_all | solution.py:46
  139.5 13.9 %collective-permute-start.16 = (bf16[128,512]{1,0:T(8,128)(2,1)S(1)}, bf16[128,512]{1,0:T(8,128)(2,1)S(1)}, u32[]{:S(2)}, u32[]{:S(2)}) collective-permute-start(bf16[128,512]{1,0:T(8,128)(2,1)S(1)} %multiply_convert_fusion), channel_id=1, source_target_pairs={{0,4},{4,0},{1,5},{5,1},{2,6},{6,2},{3,7},{7,3},{8,12},{12,8},{9,1... | collective-permute-start | bytes 393224 | tf_op jit(solution)/shard_map/ppermute | solution.py:38
  153.4 6.3 %collective-permute-done.16 = bf16[128,512]{1,0:T(8,128)(2,1)S(1)} collective-permute-done((bf16[128,512]{1,0:T(8,128)(2,1)S(1)}, bf16[128,512]{1,0:T(8,128)(2,1)S(1)}, u32[]{:S(2)}, u32[]{:S(2)}) %collective-permute-start.16) | collective-permute-done | bytes 131104 | tf_op jit(solution)/shard_map/ppermute | solution.py:38
  162.0 7.2 %all-to-all-start.3 = ((bf16[16,224,512]{2,1,0:T(8,128)(2,1)}), bf16[16,224,512]{2,1,0:T(8,128)(2,1)}, u32[]{:S(2)}, u32[]{:S(2)}) async-start(bf16[16,224,512]{2,1,0:T(8,128)(2,1)} %broadcast_in_dim.13), calls=%async_computation.3 | async-start | bytes 7340032 | tf_op jit(solution)/shard_map/all_to_all | solution.py:46
  172.4 2.6 collective-permute-start.12
  175.1 3.5 %collective-permute-done.12 = f32[32,512]{1,0:T(8,128)S(1)} collective-permute-done((f32[32,512]{1,0:T(8,128)S(1)}, f32[32,512]{1,0:T(8,128)S(1)}, u32[]{:S(2)}, u32[]{:S(2)}) %collective-permute-start.12) | collective-permute-done | bytes 65568 | tf_op jit(solution)/shard_map/ppermute | solution.py:38
  178.6 9.3 %collective-permute-start.13 = (f32[32,512]{1,0:T(8,128)S(1)}, f32[32,512]{1,0:T(8,128)S(1)}, u32[]{:S(2)}, u32[]{:S(2)}) collective-permute-start(f32[32,512]{1,0:T(8,128)S(1)} %add.138), channel_id=1, source_target_pairs={{0,128},{128,0},{1,129},{129,1},{2,130},{130,2},{3,131},{131,3},{4... | collective-permute-start | bytes 196616 | tf_op jit(solution)/shard_map/ppermute | solution.py:38
  187.9 3.0 %collective-permute-done.13 = f32[32,512]{1,0:T(8,128)S(1)} collective-permute-done((f32[32,512]{1,0:T(8,128)S(1)}, f32[32,512]{1,0:T(8,128)S(1)}, u32[]{:S(2)}, u32[]{:S(2)}) %collective-permute-start.13) | collective-permute-done | bytes 65568 | tf_op jit(solution)/shard_map/ppermute | solution.py:38
  190.9 6.4 %collective-permute-start.14 = (f32[32,512]{1,0:T(8,128)S(1)}, f32[32,512]{1,0:T(8,128)S(1)}, u32[]{:S(2)}, u32[]{:S(2)}) collective-permute-start(f32[32,512]{1,0:T(8,128)S(1)} %add.139), channel_id=1, source_target_pairs={{0,256},{256,0},{1,257},{257,1},{2,258},{258,2},{3,259},{259,3},{4... | collective-permute-start | bytes 196616 | tf_op jit(solution)/shard_map/ppermute | solution.py:38
  197.3 6.7 %collective-permute-done.14 = f32[32,512]{1,0:T(8,128)S(1)} collective-permute-done((f32[32,512]{1,0:T(8,128)S(1)}, f32[32,512]{1,0:T(8,128)S(1)}, u32[]{:S(2)}, u32[]{:S(2)}) %collective-permute-start.14) | collective-permute-done | bytes 65568 | tf_op jit(solution)/shard_map/ppermute | solution.py:38
  204.0 9.5 %collective-permute-start.15 = (f32[32,512]{1,0:T(8,128)S(1)}, f32[32,512]{1,0:T(8,128)S(1)}, u32[]{:S(2)}, u32[]{:S(2)}) collective-permute-start(f32[32,512]{1,0:T(8,128)S(1)} %add.140), channel_id=1, source_target_pairs={{0,4},{4,0},{1,5},{5,1},{2,6},{6,2},{3,7},{7,3},{8,12},{12,8},{9,1... | collective-permute-start | bytes 196616 | tf_op jit(solution)/shard_map/ppermute | solution.py:38
  213.6 5.8 %collective-permute-done.15 = f32[32,512]{1,0:T(8,128)S(1)} collective-permute-done((f32[32,512]{1,0:T(8,128)S(1)}, f32[32,512]{1,0:T(8,128)S(1)}, u32[]{:S(2)}, u32[]{:S(2)}) %collective-permute-start.15) | collective-permute-done | bytes 65568 | tf_op jit(solution)/shard_map/ppermute | solution.py:38
  219.4 5.3 %shard_map.95 = (bf16[8,128,256]{2,1,0:T(8,128)(2,1)S(1)}, bf16[8,128,256]{2,1,0:T(8,128)(2,1)S(1)}, bf16[8,128,256]{2,1,0:T(8,128)(2,1)S(1)}, bf16[8,128,256]{2,1,0:T(8,128)(2,1)}) custom-call(s32[8]{0:T(128)S(1)} %add_bitcast_fusion.2.target.source, s32[8]{0:T(128)S(1)} %shift-right-arithmetic_add_fusion.source.target, s32[1]{0:T(128)} %bitcast.37.count, ...), custom_call_target="tpu_custom_call" | custom-call | flops 134217728 | bytes 6815744 | tf_op jit(solution)/shard_map/pallas_call | solution.py:116
  226.6 2.4 collective-permute-start.17
  232.9 3.9 %collective-permute-start.19 = (bf16[4,128,256]{2,1,0:T(8,128)(2,1)}, bf16[4,128,256]{2,1,0:T(8,128)(2,1)}, u32[]{:S(2)}, u32[]{:S(2)}) collective-permute-start(bf16[4,128,256]{2,1,0:T(8,128)(2,1)} %slice.109), channel_id=1, source_target_pairs={{0,64},{64,0},{1,65},{65,1},{2,66},{66,2},{3,67},{67,3},{4,68},{68... | collective-permute-start | bytes 786440 | tf_op jit(solution)/shard_map/ppermute | solution.py:38
  238.1 7.0 %all-to-all-start.4 = ((f32[16,40,512]{2,1,0:T(8,128)}), f32[16,40,512]{2,1,0:T(8,128)S(1)}, u32[]{:S(2)}, u32[]{:S(2)}) async-start(f32[16,40,512]{2,1,0:T(8,128)} %broadcast_in_dim.14), calls=%async_computation.4 | async-start | bytes 2621440 | tf_op jit(solution)/shard_map/all_to_all | solution.py:46
  245.2 9.4 %collective-permute-start.23 = (bf16[2,128,256]{2,1,0:T(8,128)(2,1)S(1)}, bf16[2,128,256]{2,1,0:T(8,128)(2,1)S(1)}, u32[]{:S(2)}, u32[]{:S(2)}) collective-permute-start(bf16[2,128,256]{2,1,0:T(8,128)(2,1)S(1)} %slice.117), channel_id=1, source_target_pairs={{0,128},{128,0},{1,129},{129,1},{2,130},{130,2},{3,131},{131,3},{4... | collective-permute-start | bytes 393224 | tf_op jit(solution)/shard_map/ppermute | solution.py:38
  255.7 3.6 %collective-permute-start.20 = (bf16[2,128,256]{2,1,0:T(8,128)(2,1)S(1)}, bf16[2,128,256]{2,1,0:T(8,128)(2,1)S(1)}, u32[]{:S(2)}, u32[]{:S(2)}) collective-permute-start(bf16[2,128,256]{2,1,0:T(8,128)(2,1)S(1)} %slice.111), channel_id=1, source_target_pairs={{0,128},{128,0},{1,129},{129,1},{2,130},{130,2},{3,131},{131,3},{4... | collective-permute-start | bytes 393224 | tf_op jit(solution)/shard_map/ppermute | solution.py:38
  259.3 3.9 %collective-permute-done.23 = bf16[2,128,256]{2,1,0:T(8,128)(2,1)S(1)} collective-permute-done((bf16[2,128,256]{2,1,0:T(8,128)(2,1)S(1)}, bf16[2,128,256]{2,1,0:T(8,128)(2,1)S(1)}, u32[]{:S(2)}, u32[]{:S(2)}) %collective-permute-start.23) | collective-permute-done | bytes 131104 | tf_op jit(solution)/shard_map/ppermute | solution.py:38
  265.8 7.3 %collective-permute-start.21 = (bf16[1,128,256]{2,1,0:T(8,128)(2,1)S(1)}, bf16[1,128,256]{2,1,0:T(8,128)(2,1)S(1)}, u32[]{:S(2)}, u32[]{:S(2)}) collective-permute-start(bf16[1,128,256]{2,1,0:T(8,128)(2,1)S(1)} %slice.113), channel_id=1, source_target_pairs={{0,256},{256,0},{1,257},{257,1},{2,258},{258,2},{3,259},{259,3},{4... | collective-permute-start | bytes 196616 | tf_op jit(solution)/shard_map/ppermute | solution.py:38
  273.2 4.9 %collective-permute-done.24 = bf16[1,128,256]{2,1,0:T(8,128)(2,1)S(1)} collective-permute-done((bf16[1,128,256]{2,1,0:T(8,128)(2,1)S(1)}, bf16[1,128,256]{2,1,0:T(8,128)(2,1)S(1)}, u32[]{:S(2)}, u32[]{:S(2)}) %collective-permute-start.24) | collective-permute-done | bytes 65568 | tf_op jit(solution)/shard_map/ppermute | solution.py:38
  (111 shorter events, 43.3 us)
Async XLA Ops:
  0.6 130.6 %copy-start = (bf16[512,512]{1,0:T(8,128)(2,1)S(1)}, bf16[512,512]{1,0:T(8,128)(2,1)}, u32[]{:S(2)}) copy-start(bf16[512,512]{1,0:T(8,128)(2,1)} %param.8) | copy-start | bytes 1572868
  0.6 57.5 %copy-start.1 = (bf16[1,1,8,128,128]{4,3,2,1,0:T(8,128)(2,1)S(1)}, bf16[1,1,8,128,128]{4,3,2,1,0:T(8,128)(2,1)}, u32[]{:S(2)}) copy-start(bf16[1,1,8,128,128]{4,3,2,1,0:T(8,128)(2,1)} %param.13) | copy-start | bytes 786436
  4.2 25.3 %collective-permute-start = (bf16[1,144,256]{2,1,0:T(8,128)(2,1)S(1)}, bf16[1,144,256]{2,1,0:T(8,128)(2,1)S(1)}, u32[]{:S(2)}, u32[]{:S(2)}) collective-permute-start(bf16[1,144,256]{2,1,0:T(8,128)(2,1)S(1)} %pad_maximum_fusion.6), channel_id=1, source_target_pairs={{0,256},{256,0},{1,257},{257,1},{2,258},{258,2},{3,259},{259,3},{4... | collective-permute-start | bytes 221192 | tf_op jit(solution)/shard_map/ppermute | solution.py:38
  13.3 14.2 %collective-permute-start.5 = (bf16[1,128,256]{2,1,0:T(8,128)(2,1)S(1)}, bf16[1,128,256]{2,1,0:T(8,128)(2,1)S(1)}, u32[]{:S(2)}, u32[]{:S(2)}) collective-permute-start(bf16[1,128,256]{2,1,0:T(8,128)(2,1)S(1)} %get-tuple-element.25), channel_id=1, source_target_pairs={{0,256},{256,0},{1,257},{257,1},{2,258},{258,2},{3,259},{259,3},{4... | collective-permute-start | bytes 196616 | tf_op jit(solution)/shard_map/ppermute | solution.py:38
  27.6 12.6 %collective-permute-start.6 = (bf16[2,128,256]{2,1,0:T(8,128)(2,1)S(1)}, bf16[2,128,256]{2,1,0:T(8,128)(2,1)S(1)}, u32[]{:S(2)}, u32[]{:S(2)}) collective-permute-start(bf16[2,128,256]{2,1,0:T(8,128)(2,1)S(1)} %pad_maximum_fusion.5), channel_id=1, source_target_pairs={{0,128},{128,0},{1,129},{129,1},{2,130},{130,2},{3,131},{131,3},{4... | collective-permute-start | bytes 393224 | tf_op jit(solution)/shard_map/ppermute | solution.py:38
  29.5 12.6 %collective-permute-start.1 = (bf16[2,144,256]{2,1,0:T(8,128)(2,1)S(1)}, bf16[2,144,256]{2,1,0:T(8,128)(2,1)S(1)}, u32[]{:S(2)}, u32[]{:S(2)}) collective-permute-start(bf16[2,144,256]{2,1,0:T(8,128)(2,1)S(1)} %pad_maximum_fusion.4), channel_id=1, source_target_pairs={{0,128},{128,0},{1,129},{129,1},{2,130},{130,2},{3,131},{131,3},{4... | collective-permute-start | bytes 442376 | tf_op jit(solution)/shard_map/ppermute | solution.py:38
  40.2 10.6 %collective-permute-start.7 = (bf16[4,128,256]{2,1,0:T(8,128)(2,1)S(1)}, bf16[4,128,256]{2,1,0:T(8,128)(2,1)S(1)}, u32[]{:S(2)}, u32[]{:S(2)}) collective-permute-start(bf16[4,128,256]{2,1,0:T(8,128)(2,1)S(1)} %pad_maximum_fusion.2.refs_2_), channel_id=1, source_target_pairs={{0,64},{64,0},{1,65},{65,1},{2,66},{66,2},{3,67},{67,3},{4,68},{68... | collective-permute-start | bytes 786440 | tf_op jit(solution)/shard_map/ppermute | solution.py:38
  42.2 11.8 %collective-permute-start.2 = (bf16[4,144,256]{2,1,0:T(8,128)(2,1)S(1)}, bf16[4,144,256]{2,1,0:T(8,128)(2,1)S(1)}, u32[]{:S(2)}, u32[]{:S(2)}) collective-permute-start(bf16[4,144,256]{2,1,0:T(8,128)(2,1)S(1)} %pad_maximum_fusion.1.refs_1_), channel_id=1, source_target_pairs={{0,64},{64,0},{1,65},{65,1},{2,66},{66,2},{3,67},{67,3},{4,68},{68... | collective-permute-start | bytes 884744 | tf_op jit(solution)/shard_map/ppermute | solution.py:38
  46.1 9.8 %collective-permute-start.3 = (bf16[4,144,256]{2,1,0:T(8,128)(2,1)S(1)}, bf16[4,144,256]{2,1,0:T(8,128)(2,1)S(1)}, u32[]{:S(2)}, u32[]{:S(2)}) collective-permute-start(bf16[4,144,256]{2,1,0:T(8,128)(2,1)S(1)} %pad_maximum_fusion.1.refs_1_), channel_id=1, source_target_pairs={{0,32},{32,0},{1,33},{33,1},{2,34},{34,2},{3,35},{35,3},{4,36},{36... | collective-permute-start | bytes 884744 | tf_op jit(solution)/shard_map/ppermute | solution.py:38
  48.1 10.0 %collective-permute-start.8 = (bf16[4,128,256]{2,1,0:T(8,128)(2,1)S(1)}, bf16[4,128,256]{2,1,0:T(8,128)(2,1)S(1)}, u32[]{:S(2)}, u32[]{:S(2)}) collective-permute-start(bf16[4,128,256]{2,1,0:T(8,128)(2,1)S(1)} %pad_maximum_fusion.2.refs_2_), channel_id=1, source_target_pairs={{0,32},{32,0},{1,33},{33,1},{2,34},{34,2},{3,35},{35,3},{4,36},{36... | collective-permute-start | bytes 786440 | tf_op jit(solution)/shard_map/ppermute | solution.py:38
  50.9 7.2 %collective-permute-start.9 = (bf16[4,128,256]{2,1,0:T(8,128)(2,1)S(1)}, bf16[4,128,256]{2,1,0:T(8,128)(2,1)S(1)}, u32[]{:S(2)}, u32[]{:S(2)}) collective-permute-start(bf16[4,128,256]{2,1,0:T(8,128)(2,1)S(1)} %collective-permute-done.7.refs_4_), channel_id=1, source_target_pairs={{0,32},{32,0},{1,33},{33,1},{2,34},{34,2},{3,35},{35,3},{4,36},{36... | collective-permute-start | bytes 786440 | tf_op jit(solution)/shard_map/ppermute | solution.py:38
  54.0 3.5 %collective-permute-start.4 = (bf16[4,144,256]{2,1,0:T(8,128)(2,1)S(1)}, bf16[4,144,256]{2,1,0:T(8,128)(2,1)S(1)}, u32[]{:S(2)}, u32[]{:S(2)}) collective-permute-start(bf16[4,144,256]{2,1,0:T(8,128)(2,1)S(1)} %collective-permute-done.2.refs_3_), channel_id=1, source_target_pairs={{0,32},{32,0},{1,33},{33,1},{2,34},{34,2},{3,35},{35,3},{4,36},{36... | collective-permute-start | bytes 884744 | tf_op jit(solution)/shard_map/ppermute | solution.py:38
  96.4 34.3 %all-to-all-start.1 = ((bf16[16,128,512]{2,1,0:T(8,128)(2,1)}), bf16[16,128,512]{2,1,0:T(8,128)(2,1)S(1)}, u32[]{:S(2)}, u32[]{:S(2)}) async-start(bf16[16,128,512]{2,1,0:T(8,128)(2,1)} %get-tuple-element.14), calls=%async_computation.1 | async-start | bytes 4194304 | tf_op jit(solution)/shard_map/all_to_all | solution.py:46
  102.4 29.8 %copy-start.4 = (bf16[128,512]{1,0:T(8,128)(2,1)S(1)}, bf16[128,512]{1,0:T(8,128)(2,1)}, u32[]{:S(2)}) copy-start(bf16[128,512]{1,0:T(8,128)(2,1)} %param.9) | copy-start | bytes 393220
  102.4 28.6 %collective-permute-start.10 = (bf16[128,512]{1,0:T(8,128)(2,1)S(1)}, bf16[128,512]{1,0:T(8,128)(2,1)S(1)}, u32[]{:S(2)}, u32[]{:S(2)}) collective-permute-start(bf16[128,512]{1,0:T(8,128)(2,1)S(1)} %reduce_sum.98), channel_id=1, source_target_pairs={{0,4},{4,0},{1,5},{5,1},{2,6},{6,2},{3,7},{7,3},{8,12},{12,8},{9,1... | collective-permute-start | bytes 393224 | tf_op jit(solution)/shard_map/ppermute | solution.py:38
  134.3 25.5 %all-to-all-start.2 = ((bf16[16,64,512]{2,1,0:T(8,128)(2,1)}), bf16[16,64,512]{2,1,0:T(8,128)(2,1)S(1)}, u32[]{:S(2)}, u32[]{:S(2)}) async-start(bf16[16,64,512]{2,1,0:T(8,128)(2,1)} %pad_maximum_fusion), calls=%async_computation.2 | async-start | bytes 2097152 | tf_op jit(solution)/shard_map/all_to_all | solution.py:46
  139.5 20.2 %collective-permute-start.16 = (bf16[128,512]{1,0:T(8,128)(2,1)S(1)}, bf16[128,512]{1,0:T(8,128)(2,1)S(1)}, u32[]{:S(2)}, u32[]{:S(2)}) collective-permute-start(bf16[128,512]{1,0:T(8,128)(2,1)S(1)} %multiply_convert_fusion), channel_id=1, source_target_pairs={{0,4},{4,0},{1,5},{5,1},{2,6},{6,2},{3,7},{7,3},{8,12},{12,8},{9,1... | collective-permute-start | bytes 393224 | tf_op jit(solution)/shard_map/ppermute | solution.py:38
  162.0 57.4 %all-to-all-start.3 = ((bf16[16,224,512]{2,1,0:T(8,128)(2,1)}), bf16[16,224,512]{2,1,0:T(8,128)(2,1)}, u32[]{:S(2)}, u32[]{:S(2)}) async-start(bf16[16,224,512]{2,1,0:T(8,128)(2,1)} %broadcast_in_dim.13), calls=%async_computation.3 | async-start | bytes 7340032 | tf_op jit(solution)/shard_map/all_to_all | solution.py:46
  169.3 3.1 %collective-permute-start.11 = (f32[32,512]{1,0:T(8,128)S(1)}, f32[32,512]{1,0:T(8,128)S(1)}, u32[]{:S(2)}, u32[]{:S(2)}) collective-permute-start(f32[32,512]{1,0:T(8,128)S(1)} %convert_reduce_fusion.1), channel_id=1, source_target_pairs={{0,32},{32,0},{1,33},{33,1},{2,34},{34,2},{3,35},{35,3},{4,36},{36... | collective-permute-start | bytes 196616 | tf_op jit(solution)/shard_map/ppermute | solution.py:38
  172.4 6.2 %collective-permute-start.12 = (f32[32,512]{1,0:T(8,128)S(1)}, f32[32,512]{1,0:T(8,128)S(1)}, u32[]{:S(2)}, u32[]{:S(2)}) collective-permute-start(f32[32,512]{1,0:T(8,128)S(1)} %add.137), channel_id=1, source_target_pairs={{0,64},{64,0},{1,65},{65,1},{2,66},{66,2},{3,67},{67,3},{4,68},{68... | collective-permute-start | bytes 196616 | tf_op jit(solution)/shard_map/ppermute | solution.py:38
  178.6 12.3 %collective-permute-start.13 = (f32[32,512]{1,0:T(8,128)S(1)}, f32[32,512]{1,0:T(8,128)S(1)}, u32[]{:S(2)}, u32[]{:S(2)}) collective-permute-start(f32[32,512]{1,0:T(8,128)S(1)} %add.138), channel_id=1, source_target_pairs={{0,128},{128,0},{1,129},{129,1},{2,130},{130,2},{3,131},{131,3},{4... | collective-permute-start | bytes 196616 | tf_op jit(solution)/shard_map/ppermute | solution.py:38
  190.9 13.1 %collective-permute-start.14 = (f32[32,512]{1,0:T(8,128)S(1)}, f32[32,512]{1,0:T(8,128)S(1)}, u32[]{:S(2)}, u32[]{:S(2)}) collective-permute-start(f32[32,512]{1,0:T(8,128)S(1)} %add.139), channel_id=1, source_target_pairs={{0,256},{256,0},{1,257},{257,1},{2,258},{258,2},{3,259},{259,3},{4... | collective-permute-start | bytes 196616 | tf_op jit(solution)/shard_map/ppermute | solution.py:38
  204.0 15.3 %collective-permute-start.15 = (f32[32,512]{1,0:T(8,128)S(1)}, f32[32,512]{1,0:T(8,128)S(1)}, u32[]{:S(2)}, u32[]{:S(2)}) collective-permute-start(f32[32,512]{1,0:T(8,128)S(1)} %add.140), channel_id=1, source_target_pairs={{0,4},{4,0},{1,5},{5,1},{2,6},{6,2},{3,7},{7,3},{8,12},{12,8},{9,1... | collective-permute-start | bytes 196616 | tf_op jit(solution)/shard_map/ppermute | solution.py:38
  224.7 4.4 %collective-permute-start.18 = (bf16[8,128,256]{2,1,0:T(8,128)(2,1)}, bf16[8,128,256]{2,1,0:T(8,128)(2,1)S(1)}, u32[]{:S(2)}, u32[]{:S(2)}) collective-permute-start(bf16[8,128,256]{2,1,0:T(8,128)(2,1)} %get-tuple-element.20), channel_id=1, source_target_pairs={{0,32},{32,0},{1,33},{33,1},{2,34},{34,2},{3,35},{35,3},{4,36},{36... | collective-permute-start | bytes 1572872 | tf_op jit(solution)/shard_map/ppermute | solution.py:38
  226.6 5.3 %collective-permute-start.17 = (bf16[8,128,256]{2,1,0:T(8,128)(2,1)S(1)}, bf16[8,128,256]{2,1,0:T(8,128)(2,1)S(1)}, u32[]{:S(2)}, u32[]{:S(2)}) collective-permute-start(bf16[8,128,256]{2,1,0:T(8,128)(2,1)S(1)} %get-tuple-element.18), channel_id=1, source_target_pairs={{0,32},{32,0},{1,33},{33,1},{2,34},{34,2},{3,35},{35,3},{4,36},{36... | collective-permute-start | bytes 1572872 | tf_op jit(solution)/shard_map/ppermute | solution.py:38
  230.0 15.0 %collective-permute-start.22 = (bf16[4,128,256]{2,1,0:T(8,128)(2,1)}, bf16[4,128,256]{2,1,0:T(8,128)(2,1)S(1)}, u32[]{:S(2)}, u32[]{:S(2)}) collective-permute-start(bf16[4,128,256]{2,1,0:T(8,128)(2,1)} %slice.115), channel_id=1, source_target_pairs={{0,64},{64,0},{1,65},{65,1},{2,66},{66,2},{3,67},{67,3},{4,68},{68... | collective-permute-start | bytes 786440 | tf_op jit(solution)/shard_map/ppermute | solution.py:38
  232.9 21.8 %collective-permute-start.19 = (bf16[4,128,256]{2,1,0:T(8,128)(2,1)}, bf16[4,128,256]{2,1,0:T(8,128)(2,1)}, u32[]{:S(2)}, u32[]{:S(2)}) collective-permute-start(bf16[4,128,256]{2,1,0:T(8,128)(2,1)} %slice.109), channel_id=1, source_target_pairs={{0,64},{64,0},{1,65},{65,1},{2,66},{66,2},{3,67},{67,3},{4,68},{68... | collective-permute-start | bytes 786440 | tf_op jit(solution)/shard_map/ppermute | solution.py:38
  238.1 42.3 %all-to-all-start.4 = ((f32[16,40,512]{2,1,0:T(8,128)}), f32[16,40,512]{2,1,0:T(8,128)S(1)}, u32[]{:S(2)}, u32[]{:S(2)}) async-start(f32[16,40,512]{2,1,0:T(8,128)} %broadcast_in_dim.14), calls=%async_computation.4 | async-start | bytes 2621440 | tf_op jit(solution)/shard_map/all_to_all | solution.py:46
  245.2 18.1 %collective-permute-start.23 = (bf16[2,128,256]{2,1,0:T(8,128)(2,1)S(1)}, bf16[2,128,256]{2,1,0:T(8,128)(2,1)S(1)}, u32[]{:S(2)}, u32[]{:S(2)}) collective-permute-start(bf16[2,128,256]{2,1,0:T(8,128)(2,1)S(1)} %slice.117), channel_id=1, source_target_pairs={{0,128},{128,0},{1,129},{129,1},{2,130},{130,2},{3,131},{131,3},{4... | collective-permute-start | bytes 393224 | tf_op jit(solution)/shard_map/ppermute | solution.py:38
  255.7 10.1 %collective-permute-start.20 = (bf16[2,128,256]{2,1,0:T(8,128)(2,1)S(1)}, bf16[2,128,256]{2,1,0:T(8,128)(2,1)S(1)}, u32[]{:S(2)}, u32[]{:S(2)}) collective-permute-start(bf16[2,128,256]{2,1,0:T(8,128)(2,1)S(1)} %slice.111), channel_id=1, source_target_pairs={{0,128},{128,0},{1,129},{129,1},{2,130},{130,2},{3,131},{131,3},{4... | collective-permute-start | bytes 393224 | tf_op jit(solution)/shard_map/ppermute | solution.py:38
  263.3 14.8 %collective-permute-start.24 = (bf16[1,128,256]{2,1,0:T(8,128)(2,1)S(1)}, bf16[1,128,256]{2,1,0:T(8,128)(2,1)S(1)}, u32[]{:S(2)}, u32[]{:S(2)}) collective-permute-start(bf16[1,128,256]{2,1,0:T(8,128)(2,1)S(1)} %slice.119), channel_id=1, source_target_pairs={{0,256},{256,0},{1,257},{257,1},{2,258},{258,2},{3,259},{259,3},{4... | collective-permute-start | bytes 196616 | tf_op jit(solution)/shard_map/ppermute | solution.py:38
  265.8 13.8 %collective-permute-start.21 = (bf16[1,128,256]{2,1,0:T(8,128)(2,1)S(1)}, bf16[1,128,256]{2,1,0:T(8,128)(2,1)S(1)}, u32[]{:S(2)}, u32[]{:S(2)}) collective-permute-start(bf16[1,128,256]{2,1,0:T(8,128)(2,1)S(1)} %slice.113), channel_id=1, source_target_pairs={{0,256},{256,0},{1,257},{257,1},{2,258},{258,2},{3,259},{259,3},{4... | collective-permute-start | bytes 196616 | tf_op jit(solution)/shard_map/ppermute | solution.py:38
  (2 other events, 11.2 us)

commit v14 on v13

--- a/solution.py
+++ b/solution.py
@@ -188,7 +188,7 @@
 
     output, normed, grad_pre, grad_own = layer_rows(own_total, cotangent, weight)
 
-    lead = span // 4
+    lead = span * 3 // 8
     weight_terms = jnp.einsum("nf,ng->fg", normed, grad_pre, preferred_element_type=F32)
     weight_parts = weight_terms.astype(BF16).reshape(n_plane, width // n_plane, width)
     first_group = swap_parts(

time: 283 us -> 279 us (0.986)
  waiting for transfers between devices: 70.9 us -> 67.8 us
  transfers between devices with their start and end apart: 29 -> 29, of which waited for: 16 -> 15; matrix products, arithmetic and copies ran while one was open for 3% -> 3% of each run, Pallas kernels for 0% -> 0%
where the time goes in v14:
time: 279 us; the launch traced here: 278 us
  starting transfers between devices  148 us (53%)
  waiting for transfers between devices  67.8 us (24%)
  blocking collectives  32.3 us (12%)
  Pallas kernels  9.72 us (3%)
  local copies, waits for them, and re-layouts  8.31 us (3%)
  other arithmetic  7.76 us (3%)
    ppermute x25, starting transfers between devices, flip(): return lax.ppermute(block, axis, [(0, 1), (1, 0)])  123 us
    ppermute x25, waiting for transfers between devices, flip(): return lax.ppermute(block, axis, [(0, 1), (1, 0)])  55.5 us
    all_to_all x1, blocking collectives, swap_parts(): return lax.all_to_all(parts, axes, split_axis=0, concat_axis=0, tiled=True)  32.3 us
    all_to_all x4, starting transfers between devices, swap_parts(): return lax.all_to_all(parts, axes, split_axis=0, concat_axis=0, tiled=True)  25 us
    all_to_all x4, waiting for transfers between devices, swap_parts(): return lax.all_to_all(parts, axes, split_axis=0, concat_axis=0, tiled=True)  12.3 us
    pallas_call x2, Pallas kernels, tile_sums(): pl.pallas_call(functools.partial(tile_kernel, transposed, scaled, sources...  9.72 us
  transfers between devices with their start and end apart: 29, of which 15 were waited for; matrix products, arithmetic and copies ran while one was open for 3% of the time, Pallas kernels for 0%

profile of v14, /device:TPU:24, one launch (start us, length us, event | category | flops | bytes accessed | tf_op | source)
XLA Modules:
  0.0 278.4 jit_solution(11231993225222036782)
XLA Ops:
  4.2 9.1 %collective-permute-start = (bf16[1,144,256]{2,1,0:T(8,128)(2,1)S(1)}, bf16[1,144,256]{2,1,0:T(8,128)(2,1)S(1)}, u32[]{:S(2)}, u32[]{:S(2)}) collective-permute-start(bf16[1,144,256]{2,1,0:T(8,128)(2,1)S(1)} %pad_maximum_fusion.6), channel_id=1, source_target_pairs={{0,256},{256,0},{1,257},{257,1},{2,258},{258,2},{3,259},{259,3},{4... | collective-permute-start | bytes 221192 | tf_op jit(solution)/shard_map/ppermute | solution.py:38
  16.6 11.0 %collective-permute-done.5 = bf16[1,128,256]{2,1,0:T(8,128)(2,1)S(1)} collective-permute-done((bf16[1,128,256]{2,1,0:T(8,128)(2,1)S(1)}, bf16[1,128,256]{2,1,0:T(8,128)(2,1)S(1)}, u32[]{:S(2)}, u32[]{:S(2)}) %collective-permute-start.5) | collective-permute-done | bytes 65568 | tf_op jit(solution)/shard_map/ppermute | solution.py:38
  29.5 4.8 %collective-permute-start.1 = (bf16[2,144,256]{2,1,0:T(8,128)(2,1)S(1)}, bf16[2,144,256]{2,1,0:T(8,128)(2,1)S(1)}, u32[]{:S(2)}, u32[]{:S(2)}) collective-permute-start(bf16[2,144,256]{2,1,0:T(8,128)(2,1)S(1)} %pad_maximum_fusion.4), channel_id=1, source_target_pairs={{0,128},{128,0},{1,129},{129,1},{2,130},{130,2},{3,131},{131,3},{4... | collective-permute-start | bytes 442376 | tf_op jit(solution)/shard_map/ppermute | solution.py:38
  35.0 5.2 %collective-permute-done.6 = bf16[2,128,256]{2,1,0:T(8,128)(2,1)S(1)} collective-permute-done((bf16[2,128,256]{2,1,0:T(8,128)(2,1)S(1)}, bf16[2,128,256]{2,1,0:T(8,128)(2,1)S(1)}, u32[]{:S(2)}, u32[]{:S(2)}) %collective-permute-start.6) | collective-permute-done | bytes 131104 | tf_op jit(solution)/shard_map/ppermute | solution.py:38
  42.2 3.9 %collective-permute-start.2 = (bf16[4,144,256]{2,1,0:T(8,128)(2,1)S(1)}, bf16[4,144,256]{2,1,0:T(8,128)(2,1)S(1)}, u32[]{:S(2)}, u32[]{:S(2)}) collective-permute-start(bf16[4,144,256]{2,1,0:T(8,128)(2,1)S(1)} %pad_maximum_fusion.1.refs_1_), channel_id=1, source_target_pairs={{0,64},{64,0},{1,65},{65,1},{2,66},{66,2},{3,67},{67,3},{4,68},{68... | collective-permute-start | bytes 884744 | tf_op jit(solution)/shard_map/ppermute | solution.py:38
  48.1 2.4 collective-permute-start.8
  58.1 4.6 %shard_map.94 = (bf16[16,128,512]{2,1,0:T(8,128)(2,1)}, bf16[16,128,512]{2,1,0:T(8,128)(2,1)S(1)}) custom-call(s32[8]{0:T(128)S(1)} %shift-right-arithmetic_add_fusion.source.target, s32[8]{0:T(128)S(1)} %add_bitcast_fusion.2.target.source, s32[1]{0:T(128)} %bitcast.36.count, bf16[8,128,128]{2,1,0:T(8,128)(2,1)S(1)} %bitcast.39, f32[8,128]{1,0:T(8,128)S(1)} %gather_fusion, ...), custom_call_target="tpu_custom_call" | custom-call | flops 134217728 | bytes 6422528 | tf_op jit(solution)/shard_map/pallas_call | solution.py:116
  62.8 32.3 %all_to_all.25 = bf16[16,128,512]{2,1,0:T(8,128)(2,1)S(1)} all-to-all(bf16[16,128,512]{2,1,0:T(8,128)(2,1)S(1)} %get-tuple-element.13), channel_id=1, replica_groups=mesh['za'=2,'zb'=2,'z1'=2,'core'=2,'y'=4,'zh'=2,'x'=4] {'y','x'}, dimensions={0} | all-to-all | bytes 4194304 | tf_op jit(solution)/shard_map/all_to_all | solution.py:46
  95.4 6.0 %all-to-all-start.1 = ((bf16[16,128,512]{2,1,0:T(8,128)(2,1)}), bf16[16,128,512]{2,1,0:T(8,128)(2,1)S(1)}, u32[]{:S(2)}, u32[]{:S(2)}) async-start(bf16[16,128,512]{2,1,0:T(8,128)(2,1)} %get-tuple-element.14), calls=%async_computation.1 | async-start | bytes 4194304 | tf_op jit(solution)/shard_map/all_to_all | solution.py:46
  101.4 15.3 %collective-permute-start.10 = (bf16[128,512]{1,0:T(8,128)(2,1)S(1)}, bf16[128,512]{1,0:T(8,128)(2,1)S(1)}, u32[]{:S(2)}, u32[]{:S(2)}) collective-permute-start(bf16[128,512]{1,0:T(8,128)(2,1)S(1)} %reduce_sum.98), channel_id=1, source_target_pairs={{0,4},{4,0},{1,5},{5,1},{2,6},{6,2},{3,7},{7,3},{8,12},{12,8},{9,1... | collective-permute-start | bytes 393224 | tf_op jit(solution)/shard_map/ppermute | solution.py:38
  116.7 12.3 %all-to-all-done.1 = bf16[16,128,512]{2,1,0:T(8,128)(2,1)S(1)} async-done(((bf16[16,128,512]{2,1,0:T(8,128)(2,1)}), bf16[16,128,512]{2,1,0:T(8,128)(2,1)S(1)}, u32[]{:S(2)}, u32[]{:S(2)}) %all-to-all-start.1) | async-done | bytes 2097184 | tf_op jit(solution)/shard_map/all_to_all | solution.py:46
  132.7 5.5 %all-to-all-start.2 = ((bf16[16,80,512]{2,1,0:T(8,128)(2,1)}), bf16[16,80,512]{2,1,0:T(8,128)(2,1)S(1)}, u32[]{:S(2)}, u32[]{:S(2)}) async-start(bf16[16,80,512]{2,1,0:T(8,128)(2,1)} %pad_maximum_fusion), calls=%async_computation.2 | async-start | bytes 2621440 | tf_op jit(solution)/shard_map/all_to_all | solution.py:46
  138.1 16.6 %collective-permute-start.16 = (bf16[128,512]{1,0:T(8,128)(2,1)S(1)}, bf16[128,512]{1,0:T(8,128)(2,1)S(1)}, u32[]{:S(2)}, u32[]{:S(2)}) collective-permute-start(bf16[128,512]{1,0:T(8,128)(2,1)S(1)} %multiply_convert_fusion), channel_id=1, source_target_pairs={{0,4},{4,0},{1,5},{5,1},{2,6},{6,2},{3,7},{7,3},{8,12},{12,8},{9,1... | collective-permute-start | bytes 393224 | tf_op jit(solution)/shard_map/ppermute | solution.py:38
  154.7 6.4 %collective-permute-done.16 = bf16[128,512]{1,0:T(8,128)(2,1)S(1)} collective-permute-done((bf16[128,512]{1,0:T(8,128)(2,1)S(1)}, bf16[128,512]{1,0:T(8,128)(2,1)S(1)}, u32[]{:S(2)}, u32[]{:S(2)}) %collective-permute-start.16) | collective-permute-done | bytes 131104 | tf_op jit(solution)/shard_map/ppermute | solution.py:38
  161.1 2.1 broadcast_in_dim.13
  163.2 7.2 %all-to-all-start.3 = ((bf16[16,208,512]{2,1,0:T(8,128)(2,1)}), bf16[16,208,512]{2,1,0:T(8,128)(2,1)}, u32[]{:S(2)}, u32[]{:S(2)}) async-start(bf16[16,208,512]{2,1,0:T(8,128)(2,1)} %broadcast_in_dim.13), calls=%async_computation.3 | async-start | bytes 6815744 | tf_op jit(solution)/shard_map/all_to_all | solution.py:46
  173.7 6.1 %collective-permute-start.12 = (f32[32,512]{1,0:T(8,128)S(1)}, f32[32,512]{1,0:T(8,128)S(1)}, u32[]{:S(2)}, u32[]{:S(2)}) collective-permute-start(f32[32,512]{1,0:T(8,128)S(1)} %add.137), channel_id=1, source_target_pairs={{0,64},{64,0},{1,65},{65,1},{2,66},{66,2},{3,67},{67,3},{4,68},{68... | collective-permute-start | bytes 196616 | tf_op jit(solution)/shard_map/ppermute | solution.py:38
  179.8 2.4 collective-permute-done.12
  184.1 5.6 %collective-permute-done.13 = f32[32,512]{1,0:T(8,128)S(1)} collective-permute-done((f32[32,512]{1,0:T(8,128)S(1)}, f32[32,512]{1,0:T(8,128)S(1)}, u32[]{:S(2)}, u32[]{:S(2)}) %collective-permute-start.13) | collective-permute-done | bytes 65568 | tf_op jit(solution)/shard_map/ppermute | solution.py:38
  189.7 5.4 %collective-permute-start.14 = (f32[32,512]{1,0:T(8,128)S(1)}, f32[32,512]{1,0:T(8,128)S(1)}, u32[]{:S(2)}, u32[]{:S(2)}) collective-permute-start(f32[32,512]{1,0:T(8,128)S(1)} %add.139), channel_id=1, source_target_pairs={{0,256},{256,0},{1,257},{257,1},{2,258},{258,2},{3,259},{259,3},{4... | collective-permute-start | bytes 196616 | tf_op jit(solution)/shard_map/ppermute | solution.py:38
  195.1 6.9 %collective-permute-done.14 = f32[32,512]{1,0:T(8,128)S(1)} collective-permute-done((f32[32,512]{1,0:T(8,128)S(1)}, f32[32,512]{1,0:T(8,128)S(1)}, u32[]{:S(2)}, u32[]{:S(2)}) %collective-permute-start.14) | collective-permute-done | bytes 65568 | tf_op jit(solution)/shard_map/ppermute | solution.py:38
  202.0 12.6 %collective-permute-start.15 = (f32[32,512]{1,0:T(8,128)S(1)}, f32[32,512]{1,0:T(8,128)S(1)}, u32[]{:S(2)}, u32[]{:S(2)}) collective-permute-start(f32[32,512]{1,0:T(8,128)S(1)} %add.140), channel_id=1, source_target_pairs={{0,4},{4,0},{1,5},{5,1},{2,6},{6,2},{3,7},{7,3},{8,12},{12,8},{9,1... | collective-permute-start | bytes 196616 | tf_op jit(solution)/shard_map/ppermute | solution.py:38
  214.6 3.0 %collective-permute-done.15 = f32[32,512]{1,0:T(8,128)S(1)} collective-permute-done((f32[32,512]{1,0:T(8,128)S(1)}, f32[32,512]{1,0:T(8,128)S(1)}, u32[]{:S(2)}, u32[]{:S(2)}) %collective-permute-start.15) | collective-permute-done | bytes 65568 | tf_op jit(solution)/shard_map/ppermute | solution.py:38
  217.6 5.1 %shard_map.95 = (bf16[8,128,256]{2,1,0:T(8,128)(2,1)S(1)}, bf16[8,128,256]{2,1,0:T(8,128)(2,1)S(1)}, bf16[8,128,256]{2,1,0:T(8,128)(2,1)S(1)}, bf16[8,128,256]{2,1,0:T(8,128)(2,1)}) custom-call(s32[8]{0:T(128)S(1)} %add_bitcast_fusion.2.target.source, s32[8]{0:T(128)S(1)} %shift-right-arithmetic_add_fusion.source.target, s32[1]{0:T(128)} %bitcast.37.count, ...), custom_call_target="tpu_custom_call" | custom-call | flops 134217728 | bytes 6815744 | tf_op jit(solution)/shard_map/pallas_call | solution.py:116
  225.4 2.4 collective-permute-start.17
  228.8 8.5 %collective-permute-start.22 = (bf16[4,128,256]{2,1,0:T(8,128)(2,1)}, bf16[4,128,256]{2,1,0:T(8,128)(2,1)S(1)}, u32[]{:S(2)}, u32[]{:S(2)}) collective-permute-start(bf16[4,128,256]{2,1,0:T(8,128)(2,1)} %slice.115), channel_id=1, source_target_pairs={{0,64},{64,0},{1,65},{65,1},{2,66},{66,2},{3,67},{67,3},{4,68},{68... | collective-permute-start | bytes 786440 | tf_op jit(solution)/shard_map/ppermute | solution.py:38
  241.4 6.3 %all-to-all-start.4 = ((f32[16,40,512]{2,1,0:T(8,128)}), f32[16,40,512]{2,1,0:T(8,128)S(1)}, u32[]{:S(2)}, u32[]{:S(2)}) async-start(f32[16,40,512]{2,1,0:T(8,128)} %broadcast_in_dim.14), calls=%async_computation.4 | async-start | bytes 2621440 | tf_op jit(solution)/shard_map/all_to_all | solution.py:46
  250.8 4.8 %collective-permute-start.20 = (bf16[2,128,256]{2,1,0:T(8,128)(2,1)S(1)}, bf16[2,128,256]{2,1,0:T(8,128)(2,1)S(1)}, u32[]{:S(2)}, u32[]{:S(2)}) collective-permute-start(bf16[2,128,256]{2,1,0:T(8,128)(2,1)S(1)} %slice.111), channel_id=1, source_target_pairs={{0,128},{128,0},{1,129},{129,1},{2,130},{130,2},{3,131},{131,3},{4... | collective-permute-start | bytes 393224 | tf_op jit(solution)/shard_map/ppermute | solution.py:38
  255.7 6.1 %collective-permute-done.23 = bf16[2,128,256]{2,1,0:T(8,128)(2,1)S(1)} collective-permute-done((bf16[2,128,256]{2,1,0:T(8,128)(2,1)S(1)}, bf16[2,128,256]{2,1,0:T(8,128)(2,1)S(1)}, u32[]{:S(2)}, u32[]{:S(2)}) %collective-permute-start.23) | collective-permute-done | bytes 131104 | tf_op jit(solution)/shard_map/ppermute | solution.py:38
  261.8 2.6 collective-permute-start.24
  264.5 7.2 %collective-permute-start.21 = (bf16[1,128,256]{2,1,0:T(8,128)(2,1)S(1)}, bf16[1,128,256]{2,1,0:T(8,128)(2,1)S(1)}, u32[]{:S(2)}, u32[]{:S(2)}) collective-permute-start(bf16[1,128,256]{2,1,0:T(8,128)(2,1)S(1)} %slice.113), channel_id=1, source_target_pairs={{0,256},{256,0},{1,257},{257,1},{2,258},{258,2},{3,259},{259,3},{4... | collective-permute-start | bytes 196616 | tf_op jit(solution)/shard_map/ppermute | solution.py:38
  271.7 4.1 %collective-permute-done.24 = bf16[1,128,256]{2,1,0:T(8,128)(2,1)S(1)} collective-permute-done((bf16[1,128,256]{2,1,0:T(8,128)(2,1)S(1)}, bf16[1,128,256]{2,1,0:T(8,128)(2,1)S(1)}, u32[]{:S(2)}, u32[]{:S(2)}) %collective-permute-start.24) | collective-permute-done | bytes 65568 | tf_op jit(solution)/shard_map/ppermute | solution.py:38
  (113 shorter events, 42.6 us)
Async XLA Ops:
  0.6 128.9 %copy-start = (bf16[512,512]{1,0:T(8,128)(2,1)S(1)}, bf16[512,512]{1,0:T(8,128)(2,1)}, u32[]{:S(2)}) copy-start(bf16[512,512]{1,0:T(8,128)(2,1)} %param.8) | copy-start | bytes 1572868
  0.6 57.5 %copy-start.1 = (bf16[1,1,8,128,128]{4,3,2,1,0:T(8,128)(2,1)S(1)}, bf16[1,1,8,128,128]{4,3,2,1,0:T(8,128)(2,1)}, u32[]{:S(2)}) copy-start(bf16[1,1,8,128,128]{4,3,2,1,0:T(8,128)(2,1)} %param.13) | copy-start | bytes 786436
  4.2 25.3 %collective-permute-start = (bf16[1,144,256]{2,1,0:T(8,128)(2,1)S(1)}, bf16[1,144,256]{2,1,0:T(8,128)(2,1)S(1)}, u32[]{:S(2)}, u32[]{:S(2)}) collective-permute-start(bf16[1,144,256]{2,1,0:T(8,128)(2,1)S(1)} %pad_maximum_fusion.6), channel_id=1, source_target_pairs={{0,256},{256,0},{1,257},{257,1},{2,258},{258,2},{3,259},{259,3},{4... | collective-permute-start | bytes 221192 | tf_op jit(solution)/shard_map/ppermute | solution.py:38
  13.3 14.2 %collective-permute-start.5 = (bf16[1,128,256]{2,1,0:T(8,128)(2,1)S(1)}, bf16[1,128,256]{2,1,0:T(8,128)(2,1)S(1)}, u32[]{:S(2)}, u32[]{:S(2)}) collective-permute-start(bf16[1,128,256]{2,1,0:T(8,128)(2,1)S(1)} %get-tuple-element.25), channel_id=1, source_target_pairs={{0,256},{256,0},{1,257},{257,1},{2,258},{258,2},{3,259},{259,3},{4... | collective-permute-start | bytes 196616 | tf_op jit(solution)/shard_map/ppermute | solution.py:38
  27.6 12.6 %collective-permute-start.6 = (bf16[2,128,256]{2,1,0:T(8,128)(2,1)S(1)}, bf16[2,128,256]{2,1,0:T(8,128)(2,1)S(1)}, u32[]{:S(2)}, u32[]{:S(2)}) collective-permute-start(bf16[2,128,256]{2,1,0:T(8,128)(2,1)S(1)} %pad_maximum_fusion.5), channel_id=1, source_target_pairs={{0,128},{128,0},{1,129},{129,1},{2,130},{130,2},{3,131},{131,3},{4... | collective-permute-start | bytes 393224 | tf_op jit(solution)/shard_map/ppermute | solution.py:38
  29.5 12.6 %collective-permute-start.1 = (bf16[2,144,256]{2,1,0:T(8,128)(2,1)S(1)}, bf16[2,144,256]{2,1,0:T(8,128)(2,1)S(1)}, u32[]{:S(2)}, u32[]{:S(2)}) collective-permute-start(bf16[2,144,256]{2,1,0:T(8,128)(2,1)S(1)} %pad_maximum_fusion.4), channel_id=1, source_target_pairs={{0,128},{128,0},{1,129},{129,1},{2,130},{130,2},{3,131},{131,3},{4... | collective-permute-start | bytes 442376 | tf_op jit(solution)/shard_map/ppermute | solution.py:38
  40.2 10.6 %collective-permute-start.7 = (bf16[4,128,256]{2,1,0:T(8,128)(2,1)S(1)}, bf16[4,128,256]{2,1,0:T(8,128)(2,1)S(1)}, u32[]{:S(2)}, u32[]{:S(2)}) collective-permute-start(bf16[4,128,256]{2,1,0:T(8,128)(2,1)S(1)} %pad_maximum_fusion.2.refs_2_), channel_id=1, source_target_pairs={{0,64},{64,0},{1,65},{65,1},{2,66},{66,2},{3,67},{67,3},{4,68},{68... | collective-permute-start | bytes 786440 | tf_op jit(solution)/shard_map/ppermute | solution.py:38
  42.2 11.8 %collective-permute-start.2 = (bf16[4,144,256]{2,1,0:T(8,128)(2,1)S(1)}, bf16[4,144,256]{2,1,0:T(8,128)(2,1)S(1)}, u32[]{:S(2)}, u32[]{:S(2)}) collective-permute-start(bf16[4,144,256]{2,1,0:T(8,128)(2,1)S(1)} %pad_maximum_fusion.1.refs_1_), channel_id=1, source_target_pairs={{0,64},{64,0},{1,65},{65,1},{2,66},{66,2},{3,67},{67,3},{4,68},{68... | collective-permute-start | bytes 884744 | tf_op jit(solution)/shard_map/ppermute | solution.py:38
  46.1 9.8 %collective-permute-start.3 = (bf16[4,144,256]{2,1,0:T(8,128)(2,1)S(1)}, bf16[4,144,256]{2,1,0:T(8,128)(2,1)S(1)}, u32[]{:S(2)}, u32[]{:S(2)}) collective-permute-start(bf16[4,144,256]{2,1,0:T(8,128)(2,1)S(1)} %pad_maximum_fusion.1.refs_1_), channel_id=1, source_target_pairs={{0,32},{32,0},{1,33},{33,1},{2,34},{34,2},{3,35},{35,3},{4,36},{36... | collective-permute-start | bytes 884744 | tf_op jit(solution)/shard_map/ppermute | solution.py:38
  48.1 10.0 %collective-permute-start.8 = (bf16[4,128,256]{2,1,0:T(8,128)(2,1)S(1)}, bf16[4,128,256]{2,1,0:T(8,128)(2,1)S(1)}, u32[]{:S(2)}, u32[]{:S(2)}) collective-permute-start(bf16[4,128,256]{2,1,0:T(8,128)(2,1)S(1)} %pad_maximum_fusion.2.refs_2_), channel_id=1, source_target_pairs={{0,32},{32,0},{1,33},{33,1},{2,34},{34,2},{3,35},{35,3},{4,36},{36... | collective-permute-start | bytes 786440 | tf_op jit(solution)/shard_map/ppermute | solution.py:38
  50.9 7.2 %collective-permute-start.9 = (bf16[4,128,256]{2,1,0:T(8,128)(2,1)S(1)}, bf16[4,128,256]{2,1,0:T(8,128)(2,1)S(1)}, u32[]{:S(2)}, u32[]{:S(2)}) collective-permute-start(bf16[4,128,256]{2,1,0:T(8,128)(2,1)S(1)} %collective-permute-done.7.refs_4_), channel_id=1, source_target_pairs={{0,32},{32,0},{1,33},{33,1},{2,34},{34,2},{3,35},{35,3},{4,36},{36... | collective-permute-start | bytes 786440 | tf_op jit(solution)/shard_map/ppermute | solution.py:38
  54.0 3.5 %collective-permute-start.4 = (bf16[4,144,256]{2,1,0:T(8,128)(2,1)S(1)}, bf16[4,144,256]{2,1,0:T(8,128)(2,1)S(1)}, u32[]{:S(2)}, u32[]{:S(2)}) collective-permute-start(bf16[4,144,256]{2,1,0:T(8,128)(2,1)S(1)} %collective-permute-done.2.refs_3_), channel_id=1, source_target_pairs={{0,32},{32,0},{1,33},{33,1},{2,34},{34,2},{3,35},{35,3},{4,36},{36... | collective-permute-start | bytes 884744 | tf_op jit(solution)/shard_map/ppermute | solution.py:38
  95.4 33.5 %all-to-all-start.1 = ((bf16[16,128,512]{2,1,0:T(8,128)(2,1)}), bf16[16,128,512]{2,1,0:T(8,128)(2,1)S(1)}, u32[]{:S(2)}, u32[]{:S(2)}) async-start(bf16[16,128,512]{2,1,0:T(8,128)(2,1)} %get-tuple-element.14), calls=%async_computation.1 | async-start | bytes 4194304 | tf_op jit(solution)/shard_map/all_to_all | solution.py:46
  101.4 29.1 %copy-start.5 = (bf16[128,512]{1,0:T(8,128)(2,1)S(1)}, bf16[128,512]{1,0:T(8,128)(2,1)}, u32[]{:S(2)}) copy-start(bf16[128,512]{1,0:T(8,128)(2,1)} %param.9) | copy-start | bytes 393220
  101.4 27.9 %collective-permute-start.10 = (bf16[128,512]{1,0:T(8,128)(2,1)S(1)}, bf16[128,512]{1,0:T(8,128)(2,1)S(1)}, u32[]{:S(2)}, u32[]{:S(2)}) collective-permute-start(bf16[128,512]{1,0:T(8,128)(2,1)S(1)} %reduce_sum.98), channel_id=1, source_target_pairs={{0,4},{4,0},{1,5},{5,1},{2,6},{6,2},{3,7},{7,3},{8,12},{12,8},{9,1... | collective-permute-start | bytes 393224 | tf_op jit(solution)/shard_map/ppermute | solution.py:38
  132.7 28.5 %all-to-all-start.2 = ((bf16[16,80,512]{2,1,0:T(8,128)(2,1)}), bf16[16,80,512]{2,1,0:T(8,128)(2,1)S(1)}, u32[]{:S(2)}, u32[]{:S(2)}) async-start(bf16[16,80,512]{2,1,0:T(8,128)(2,1)} %pad_maximum_fusion), calls=%async_computation.2 | async-start | bytes 2621440 | tf_op jit(solution)/shard_map/all_to_all | solution.py:46
  138.1 23.0 %collective-permute-start.16 = (bf16[128,512]{1,0:T(8,128)(2,1)S(1)}, bf16[128,512]{1,0:T(8,128)(2,1)S(1)}, u32[]{:S(2)}, u32[]{:S(2)}) collective-permute-start(bf16[128,512]{1,0:T(8,128)(2,1)S(1)} %multiply_convert_fusion), channel_id=1, source_target_pairs={{0,4},{4,0},{1,5},{5,1},{2,6},{6,2},{3,7},{7,3},{8,12},{12,8},{9,1... | collective-permute-start | bytes 393224 | tf_op jit(solution)/shard_map/ppermute | solution.py:38
  163.2 54.4 %all-to-all-start.3 = ((bf16[16,208,512]{2,1,0:T(8,128)(2,1)}), bf16[16,208,512]{2,1,0:T(8,128)(2,1)}, u32[]{:S(2)}, u32[]{:S(2)}) async-start(bf16[16,208,512]{2,1,0:T(8,128)(2,1)} %broadcast_in_dim.13), calls=%async_computation.3 | async-start | bytes 6815744 | tf_op jit(solution)/shard_map/all_to_all | solution.py:46
  170.5 3.1 %collective-permute-start.11 = (f32[32,512]{1,0:T(8,128)S(1)}, f32[32,512]{1,0:T(8,128)S(1)}, u32[]{:S(2)}, u32[]{:S(2)}) collective-permute-start(f32[32,512]{1,0:T(8,128)S(1)} %convert_reduce_fusion.1), channel_id=1, source_target_pairs={{0,32},{32,0},{1,33},{33,1},{2,34},{34,2},{3,35},{35,3},{4,36},{36... | collective-permute-start | bytes 196616 | tf_op jit(solution)/shard_map/ppermute | solution.py:38
  173.7 8.5 %collective-permute-start.12 = (f32[32,512]{1,0:T(8,128)S(1)}, f32[32,512]{1,0:T(8,128)S(1)}, u32[]{:S(2)}, u32[]{:S(2)}) collective-permute-start(f32[32,512]{1,0:T(8,128)S(1)} %add.137), channel_id=1, source_target_pairs={{0,64},{64,0},{1,65},{65,1},{2,66},{66,2},{3,67},{67,3},{4,68},{68... | collective-permute-start | bytes 196616 | tf_op jit(solution)/shard_map/ppermute | solution.py:38
  182.2 7.5 %collective-permute-start.13 = (f32[32,512]{1,0:T(8,128)S(1)}, f32[32,512]{1,0:T(8,128)S(1)}, u32[]{:S(2)}, u32[]{:S(2)}) collective-permute-start(f32[32,512]{1,0:T(8,128)S(1)} %add.138), channel_id=1, source_target_pairs={{0,128},{128,0},{1,129},{129,1},{2,130},{130,2},{3,131},{131,3},{4... | collective-permute-start | bytes 196616 | tf_op jit(solution)/shard_map/ppermute | solution.py:38
  189.7 12.3 %collective-permute-start.14 = (f32[32,512]{1,0:T(8,128)S(1)}, f32[32,512]{1,0:T(8,128)S(1)}, u32[]{:S(2)}, u32[]{:S(2)}) collective-permute-start(f32[32,512]{1,0:T(8,128)S(1)} %add.139), channel_id=1, source_target_pairs={{0,256},{256,0},{1,257},{257,1},{2,258},{258,2},{3,259},{259,3},{4... | collective-permute-start | bytes 196616 | tf_op jit(solution)/shard_map/ppermute | solution.py:38
  202.0 15.6 %collective-permute-start.15 = (f32[32,512]{1,0:T(8,128)S(1)}, f32[32,512]{1,0:T(8,128)S(1)}, u32[]{:S(2)}, u32[]{:S(2)}) collective-permute-start(f32[32,512]{1,0:T(8,128)S(1)} %add.140), channel_id=1, source_target_pairs={{0,4},{4,0},{1,5},{5,1},{2,6},{6,2},{3,7},{7,3},{8,12},{12,8},{9,1... | collective-permute-start | bytes 196616 | tf_op jit(solution)/shard_map/ppermute | solution.py:38
  223.5 4.4 %collective-permute-start.18 = (bf16[8,128,256]{2,1,0:T(8,128)(2,1)}, bf16[8,128,256]{2,1,0:T(8,128)(2,1)S(1)}, u32[]{:S(2)}, u32[]{:S(2)}) collective-permute-start(bf16[8,128,256]{2,1,0:T(8,128)(2,1)} %get-tuple-element.20), channel_id=1, source_target_pairs={{0,32},{32,0},{1,33},{33,1},{2,34},{34,2},{3,35},{35,3},{4,36},{36... | collective-permute-start | bytes 1572872 | tf_op jit(solution)/shard_map/ppermute | solution.py:38
  225.4 11.9 %collective-permute-start.17 = (bf16[8,128,256]{2,1,0:T(8,128)(2,1)}, bf16[8,128,256]{2,1,0:T(8,128)(2,1)S(1)}, u32[]{:S(2)}, u32[]{:S(2)}) collective-permute-start(bf16[8,128,256]{2,1,0:T(8,128)(2,1)} %copy-done.2), channel_id=1, source_target_pairs={{0,32},{32,0},{1,33},{33,1},{2,34},{34,2},{3,35},{35,3},{4,36},{36... | collective-permute-start | bytes 1572872 | tf_op jit(solution)/shard_map/ppermute | solution.py:38
  228.8 19.0 %collective-permute-start.22 = (bf16[4,128,256]{2,1,0:T(8,128)(2,1)}, bf16[4,128,256]{2,1,0:T(8,128)(2,1)S(1)}, u32[]{:S(2)}, u32[]{:S(2)}) collective-permute-start(bf16[4,128,256]{2,1,0:T(8,128)(2,1)} %slice.115), channel_id=1, source_target_pairs={{0,64},{64,0},{1,65},{65,1},{2,66},{66,2},{3,67},{67,3},{4,68},{68... | collective-permute-start | bytes 786440 | tf_op jit(solution)/shard_map/ppermute | solution.py:38
  238.2 11.6 %collective-permute-start.19 = (bf16[4,128,256]{2,1,0:T(8,128)(2,1)}, bf16[4,128,256]{2,1,0:T(8,128)(2,1)}, u32[]{:S(2)}, u32[]{:S(2)}) collective-permute-start(bf16[4,128,256]{2,1,0:T(8,128)(2,1)} %slice.109), channel_id=1, source_target_pairs={{0,64},{64,0},{1,65},{65,1},{2,66},{66,2},{3,67},{67,3},{4,68},{68... | collective-permute-start | bytes 786440 | tf_op jit(solution)/shard_map/ppermute | solution.py:38
  241.4 35.9 %all-to-all-start.4 = ((f32[16,40,512]{2,1,0:T(8,128)}), f32[16,40,512]{2,1,0:T(8,128)S(1)}, u32[]{:S(2)}, u32[]{:S(2)}) async-start(f32[16,40,512]{2,1,0:T(8,128)} %broadcast_in_dim.14), calls=%async_computation.4 | async-start | bytes 2621440 | tf_op jit(solution)/shard_map/all_to_all | solution.py:46
  247.9 13.9 %collective-permute-start.23 = (bf16[2,128,256]{2,1,0:T(8,128)(2,1)S(1)}, bf16[2,128,256]{2,1,0:T(8,128)(2,1)S(1)}, u32[]{:S(2)}, u32[]{:S(2)}) collective-permute-start(bf16[2,128,256]{2,1,0:T(8,128)(2,1)S(1)} %slice.117), channel_id=1, source_target_pairs={{0,128},{128,0},{1,129},{129,1},{2,130},{130,2},{3,131},{131,3},{4... | collective-permute-start | bytes 393224 | tf_op jit(solution)/shard_map/ppermute | solution.py:38
  250.8 13.6 %collective-permute-start.20 = (bf16[2,128,256]{2,1,0:T(8,128)(2,1)S(1)}, bf16[2,128,256]{2,1,0:T(8,128)(2,1)S(1)}, u32[]{:S(2)}, u32[]{:S(2)}) collective-permute-start(bf16[2,128,256]{2,1,0:T(8,128)(2,1)S(1)} %slice.111), channel_id=1, source_target_pairs={{0,128},{128,0},{1,129},{129,1},{2,130},{130,2},{3,131},{131,3},{4... | collective-permute-start | bytes 393224 | tf_op jit(solution)/shard_map/ppermute | solution.py:38
  261.8 13.9 %collective-permute-start.24 = (bf16[1,128,256]{2,1,0:T(8,128)(2,1)S(1)}, bf16[1,128,256]{2,1,0:T(8,128)(2,1)S(1)}, u32[]{:S(2)}, u32[]{:S(2)}) collective-permute-start(bf16[1,128,256]{2,1,0:T(8,128)(2,1)S(1)} %slice.119), channel_id=1, source_target_pairs={{0,256},{256,0},{1,257},{257,1},{2,258},{258,2},{3,259},{259,3},{4... | collective-permute-start | bytes 196616 | tf_op jit(solution)/shard_map/ppermute | solution.py:38
  264.5 12.0 %collective-permute-start.21 = (bf16[1,128,256]{2,1,0:T(8,128)(2,1)S(1)}, bf16[1,128,256]{2,1,0:T(8,128)(2,1)S(1)}, u32[]{:S(2)}, u32[]{:S(2)}) collective-permute-start(bf16[1,128,256]{2,1,0:T(8,128)(2,1)S(1)} %slice.113), channel_id=1, source_target_pairs={{0,256},{256,0},{1,257},{257,1},{2,258},{258,2},{3,259},{259,3},{4... | collective-permute-start | bytes 196616 | tf_op jit(solution)/shard_map/ppermute | solution.py:38
  (3 other events, 17.9 us)

commit v15 on v14

--- a/solution.py
+++ b/solution.py
@@ -198,7 +198,7 @@
     last_group = swap_parts(copies_of(after(grad_rest, first_group), PLANE), PLANE)
 
     line_rows = jnp.sum(first_group[:, lead:].astype(F32), axis=0)
-    for axis in ("core", "z1", "zb", "za", "zh"):
+    for axis in ("core", "zh", "z1", "zb", "za"):
         line_rows = line_rows + flip(line_rows, axis)
     line_rows = line_rows * (1.0 / math.sqrt(nodes))
     last_group = after(last_group, line_rows)

time: 279 us -> 282 us (1.011)
  starting transfers between devices: 148 us -> 156 us
  waiting for transfers between devices: 67.8 us -> 60.6 us
    ppermute x25, waiting for transfers between devices: 55.5 us -> 47.1 us  [flip(): return lax.ppermute(block, axis, [(0, 1), (1, 0)])]
    ppermute x25, starting transfers between devices: 123 us -> 129 us  [flip(): return lax.ppermute(block, axis, [(0, 1), (1, 0)])]
  transfers between devices with their start and end apart: 29 -> 29, of which waited for: 15 -> 16; matrix products, arithmetic and copies ran while one was open for 3% -> 3% of each run, Pallas kernels for 0% -> 0%
where the time goes in v15:
time: 282 us; the launch traced here: 279 us
  starting transfers between devices  156 us (55%)
  waiting for transfers between devices  60.6 us (21%)
  blocking collectives  33.9 us (12%)
  Pallas kernels  8.6 us (3%)
  local copies, waits for them, and re-layouts  8.31 us (3%)
  other arithmetic  7.76 us (3%)
    ppermute x25, starting transfers between devices, flip(): return lax.ppermute(block, axis, [(0, 1), (1, 0)])  129 us
    ppermute x25, waiting for transfers between devices, flip(): return lax.ppermute(block, axis, [(0, 1), (1, 0)])  47.1 us
    all_to_all x1, blocking collectives, swap_parts(): return lax.all_to_all(parts, axes, split_axis=0, concat_axis=0, tiled=True)  33.9 us
    all_to_all x4, starting transfers between devices, swap_parts(): return lax.all_to_all(parts, axes, split_axis=0, concat_axis=0, tiled=True)  26.4 us
    all_to_all x4, waiting for transfers between devices, swap_parts(): return lax.all_to_all(parts, axes, split_axis=0, concat_axis=0, tiled=True)  13.5 us
    pallas_call x2, Pallas kernels, tile_sums(): pl.pallas_call(functools.partial(tile_kernel, transposed, scaled, sources...  8.6 us
  transfers between devices with their start and end apart: 29, of which 16 were waited for; matrix products, arithmetic and copies ran while one was open for 3% of the time, Pallas kernels for 0%

profile of v15, /device:TPU:24, one launch (start us, length us, event | category | flops | bytes accessed | tf_op | source)
XLA Modules:
  0.0 279.3 jit_solution(2869851834632478747)
XLA Ops:
  4.2 9.1 %collective-permute-start = (bf16[1,144,256]{2,1,0:T(8,128)(2,1)S(1)}, bf16[1,144,256]{2,1,0:T(8,128)(2,1)S(1)}, u32[]{:S(2)}, u32[]{:S(2)}) collective-permute-start(bf16[1,144,256]{2,1,0:T(8,128)(2,1)S(1)} %pad_maximum_fusion.6), channel_id=1, source_target_pairs={{0,256},{256,0},{1,257},{257,1},{2,258},{258,2},{3,259},{259,3},{4... | collective-permute-start | bytes 221192 | tf_op jit(solution)/shard_map/ppermute | solution.py:38
  16.6 11.0 %collective-permute-done.5 = bf16[1,128,256]{2,1,0:T(8,128)(2,1)S(1)} collective-permute-done((bf16[1,128,256]{2,1,0:T(8,128)(2,1)S(1)}, bf16[1,128,256]{2,1,0:T(8,128)(2,1)S(1)}, u32[]{:S(2)}, u32[]{:S(2)}) %collective-permute-start.5) | collective-permute-done | bytes 65568 | tf_op jit(solution)/shard_map/ppermute | solution.py:38
  29.5 4.8 %collective-permute-start.1 = (bf16[2,144,256]{2,1,0:T(8,128)(2,1)S(1)}, bf16[2,144,256]{2,1,0:T(8,128)(2,1)S(1)}, u32[]{:S(2)}, u32[]{:S(2)}) collective-permute-start(bf16[2,144,256]{2,1,0:T(8,128)(2,1)S(1)} %pad_maximum_fusion.4), channel_id=1, source_target_pairs={{0,128},{128,0},{1,129},{129,1},{2,130},{130,2},{3,131},{131,3},{4... | collective-permute-start | bytes 442376 | tf_op jit(solution)/shard_map/ppermute | solution.py:38
  35.0 5.2 %collective-permute-done.6 = bf16[2,128,256]{2,1,0:T(8,128)(2,1)S(1)} collective-permute-done((bf16[2,128,256]{2,1,0:T(8,128)(2,1)S(1)}, bf16[2,128,256]{2,1,0:T(8,128)(2,1)S(1)}, u32[]{:S(2)}, u32[]{:S(2)}) %collective-permute-start.6) | collective-permute-done | bytes 131104 | tf_op jit(solution)/shard_map/ppermute | solution.py:38
  42.2 3.9 %collective-permute-start.2 = (bf16[4,144,256]{2,1,0:T(8,128)(2,1)S(1)}, bf16[4,144,256]{2,1,0:T(8,128)(2,1)S(1)}, u32[]{:S(2)}, u32[]{:S(2)}) collective-permute-start(bf16[4,144,256]{2,1,0:T(8,128)(2,1)S(1)} %pad_maximum_fusion.1.refs_1_), channel_id=1, source_target_pairs={{0,64},{64,0},{1,65},{65,1},{2,66},{66,2},{3,67},{67,3},{4,68},{68... | collective-permute-start | bytes 884744 | tf_op jit(solution)/shard_map/ppermute | solution.py:38
  48.1 2.4 collective-permute-start.8
  58.1 4.1 %shard_map.94 = (bf16[16,128,512]{2,1,0:T(8,128)(2,1)}, bf16[16,128,512]{2,1,0:T(8,128)(2,1)S(1)}) custom-call(s32[8]{0:T(128)S(1)} %shift-right-arithmetic_add_fusion.source.target, s32[8]{0:T(128)S(1)} %add_bitcast_fusion.2.target.source, s32[1]{0:T(128)} %bitcast.36.count, bf16[8,128,128]{2,1,0:T(8,128)(2,1)S(1)} %bitcast.39, f32[8,128]{1,0:T(8,128)S(1)} %gather_fusion, ...), custom_call_target="tpu_custom_call" | custom-call | flops 134217728 | bytes 6422528 | tf_op jit(solution)/shard_map/pallas_call | solution.py:116
  62.3 33.9 %all_to_all.25 = bf16[16,128,512]{2,1,0:T(8,128)(2,1)S(1)} all-to-all(bf16[16,128,512]{2,1,0:T(8,128)(2,1)S(1)} %get-tuple-element.13), channel_id=1, replica_groups=mesh['za'=2,'zb'=2,'z1'=2,'core'=2,'y'=4,'zh'=2,'x'=4] {'y','x'}, dimensions={0} | all-to-all | bytes 4194304 | tf_op jit(solution)/shard_map/all_to_all | solution.py:46
  96.4 6.0 %all-to-all-start.1 = ((bf16[16,128,512]{2,1,0:T(8,128)(2,1)}), bf16[16,128,512]{2,1,0:T(8,128)(2,1)S(1)}, u32[]{:S(2)}, u32[]{:S(2)}) async-start(bf16[16,128,512]{2,1,0:T(8,128)(2,1)} %get-tuple-element.14), calls=%async_computation.1 | async-start | bytes 4194304 | tf_op jit(solution)/shard_map/all_to_all | solution.py:46
  102.4 14.4 %collective-permute-start.10 = (bf16[128,512]{1,0:T(8,128)(2,1)S(1)}, bf16[128,512]{1,0:T(8,128)(2,1)S(1)}, u32[]{:S(2)}, u32[]{:S(2)}) collective-permute-start(bf16[128,512]{1,0:T(8,128)(2,1)S(1)} %reduce_sum.98), channel_id=1, source_target_pairs={{0,4},{4,0},{1,5},{5,1},{2,6},{6,2},{3,7},{7,3},{8,12},{12,8},{9,1... | collective-permute-start | bytes 393224 | tf_op jit(solution)/shard_map/ppermute | solution.py:38
  116.8 13.5 %all-to-all-done.1 = bf16[16,128,512]{2,1,0:T(8,128)(2,1)S(1)} async-done(((bf16[16,128,512]{2,1,0:T(8,128)(2,1)}), bf16[16,128,512]{2,1,0:T(8,128)(2,1)S(1)}, u32[]{:S(2)}, u32[]{:S(2)}) %all-to-all-start.1) | async-done | bytes 2097184 | tf_op jit(solution)/shard_map/all_to_all | solution.py:46
  134.0 5.4 %all-to-all-start.2 = ((bf16[16,80,512]{2,1,0:T(8,128)(2,1)}), bf16[16,80,512]{2,1,0:T(8,128)(2,1)S(1)}, u32[]{:S(2)}, u32[]{:S(2)}) async-start(bf16[16,80,512]{2,1,0:T(8,128)(2,1)} %pad_maximum_fusion), calls=%async_computation.2 | async-start | bytes 2621440 | tf_op jit(solution)/shard_map/all_to_all | solution.py:46
  139.3 14.9 %collective-permute-start.16 = (bf16[128,512]{1,0:T(8,128)(2,1)S(1)}, bf16[128,512]{1,0:T(8,128)(2,1)S(1)}, u32[]{:S(2)}, u32[]{:S(2)}) collective-permute-start(bf16[128,512]{1,0:T(8,128)(2,1)S(1)} %multiply_convert_fusion), channel_id=1, source_target_pairs={{0,4},{4,0},{1,5},{5,1},{2,6},{6,2},{3,7},{7,3},{8,12},{12,8},{9,1... | collective-permute-start | bytes 393224 | tf_op jit(solution)/shard_map/ppermute | solution.py:38
  154.2 4.8 %collective-permute-done.16 = bf16[128,512]{1,0:T(8,128)(2,1)S(1)} collective-permute-done((bf16[128,512]{1,0:T(8,128)(2,1)S(1)}, bf16[128,512]{1,0:T(8,128)(2,1)S(1)}, u32[]{:S(2)}, u32[]{:S(2)}) %collective-permute-start.16) | collective-permute-done | bytes 131104 | tf_op jit(solution)/shard_map/ppermute | solution.py:38
  161.2 7.2 %all-to-all-start.3 = ((bf16[16,208,512]{2,1,0:T(8,128)(2,1)}), bf16[16,208,512]{2,1,0:T(8,128)(2,1)}, u32[]{:S(2)}, u32[]{:S(2)}) async-start(bf16[16,208,512]{2,1,0:T(8,128)(2,1)} %broadcast_in_dim.13), calls=%async_computation.3 | async-start | bytes 6815744 | tf_op jit(solution)/shard_map/all_to_all | solution.py:46
  171.6 13.2 %collective-permute-start.12 = (f32[32,512]{1,0:T(8,128)S(1)}, f32[32,512]{1,0:T(8,128)S(1)}, u32[]{:S(2)}, u32[]{:S(2)}) collective-permute-start(f32[32,512]{1,0:T(8,128)S(1)} %add.137), channel_id=1, source_target_pairs={{0,4},{4,0},{1,5},{5,1},{2,6},{6,2},{3,7},{7,3},{8,12},{12,8},{9,1... | collective-permute-start | bytes 196616 | tf_op jit(solution)/shard_map/ppermute | solution.py:38
  184.8 2.8 %collective-permute-done.12 = f32[32,512]{1,0:T(8,128)S(1)} collective-permute-done((f32[32,512]{1,0:T(8,128)S(1)}, f32[32,512]{1,0:T(8,128)S(1)}, u32[]{:S(2)}, u32[]{:S(2)}) %collective-permute-start.12) | collective-permute-done | bytes 65568 | tf_op jit(solution)/shard_map/ppermute | solution.py:38
  187.6 5.3 %collective-permute-start.13 = (f32[32,512]{1,0:T(8,128)S(1)}, f32[32,512]{1,0:T(8,128)S(1)}, u32[]{:S(2)}, u32[]{:S(2)}) collective-permute-start(f32[32,512]{1,0:T(8,128)S(1)} %add.138), channel_id=1, source_target_pairs={{0,64},{64,0},{1,65},{65,1},{2,66},{66,2},{3,67},{67,3},{4,68},{68... | collective-permute-start | bytes 196616 | tf_op jit(solution)/shard_map/ppermute | solution.py:38
  193.0 2.2 collective-permute-done.13
  195.2 7.8 %collective-permute-start.14 = (f32[32,512]{1,0:T(8,128)S(1)}, f32[32,512]{1,0:T(8,128)S(1)}, u32[]{:S(2)}, u32[]{:S(2)}) collective-permute-start(f32[32,512]{1,0:T(8,128)S(1)} %add.139), channel_id=1, source_target_pairs={{0,128},{128,0},{1,129},{129,1},{2,130},{130,2},{3,131},{131,3},{4... | collective-permute-start | bytes 196616 | tf_op jit(solution)/shard_map/ppermute | solution.py:38
  203.1 2.4 collective-permute-done.14
  205.5 6.7 %collective-permute-start.15 = (f32[32,512]{1,0:T(8,128)S(1)}, f32[32,512]{1,0:T(8,128)S(1)}, u32[]{:S(2)}, u32[]{:S(2)}) collective-permute-start(f32[32,512]{1,0:T(8,128)S(1)} %add.140), channel_id=1, source_target_pairs={{0,256},{256,0},{1,257},{257,1},{2,258},{258,2},{3,259},{259,3},{4... | collective-permute-start | bytes 196616 | tf_op jit(solution)/shard_map/ppermute | solution.py:38
  212.1 4.1 %collective-permute-done.15 = f32[32,512]{1,0:T(8,128)S(1)} collective-permute-done((f32[32,512]{1,0:T(8,128)S(1)}, f32[32,512]{1,0:T(8,128)S(1)}, u32[]{:S(2)}, u32[]{:S(2)}) %collective-permute-start.15) | collective-permute-done | bytes 65568 | tf_op jit(solution)/shard_map/ppermute | solution.py:38
  216.3 4.5 %shard_map.95 = (bf16[8,128,256]{2,1,0:T(8,128)(2,1)S(1)}, bf16[8,128,256]{2,1,0:T(8,128)(2,1)S(1)}, bf16[8,128,256]{2,1,0:T(8,128)(2,1)S(1)}, bf16[8,128,256]{2,1,0:T(8,128)(2,1)}) custom-call(s32[8]{0:T(128)S(1)} %add_bitcast_fusion.2.target.source, s32[8]{0:T(128)S(1)} %shift-right-arithmetic_add_fusion.source.target, s32[1]{0:T(128)} %bitcast.37.count, ...), custom_call_target="tpu_custom_call" | custom-call | flops 134217728 | bytes 6815744 | tf_op jit(solution)/shard_map/pallas_call | solution.py:116
  223.4 2.4 collective-permute-start.17
  229.6 3.9 %collective-permute-start.19 = (bf16[4,128,256]{2,1,0:T(8,128)(2,1)}, bf16[4,128,256]{2,1,0:T(8,128)(2,1)}, u32[]{:S(2)}, u32[]{:S(2)}) collective-permute-start(bf16[4,128,256]{2,1,0:T(8,128)(2,1)} %slice.109), channel_id=1, source_target_pairs={{0,64},{64,0},{1,65},{65,1},{2,66},{66,2},{3,67},{67,3},{4,68},{68... | collective-permute-start | bytes 786440 | tf_op jit(solution)/shard_map/ppermute | solution.py:38
  234.8 7.8 %all-to-all-start.4 = ((f32[16,40,512]{2,1,0:T(8,128)}), f32[16,40,512]{2,1,0:T(8,128)S(1)}, u32[]{:S(2)}, u32[]{:S(2)}) async-start(f32[16,40,512]{2,1,0:T(8,128)} %broadcast_in_dim.14), calls=%async_computation.4 | async-start | bytes 2621440 | tf_op jit(solution)/shard_map/all_to_all | solution.py:46
  242.8 9.7 %collective-permute-start.23 = (bf16[2,128,256]{2,1,0:T(8,128)(2,1)S(1)}, bf16[2,128,256]{2,1,0:T(8,128)(2,1)S(1)}, u32[]{:S(2)}, u32[]{:S(2)}) collective-permute-start(bf16[2,128,256]{2,1,0:T(8,128)(2,1)S(1)} %slice.117), channel_id=1, source_target_pairs={{0,128},{128,0},{1,129},{129,1},{2,130},{130,2},{3,131},{131,3},{4... | collective-permute-start | bytes 393224 | tf_op jit(solution)/shard_map/ppermute | solution.py:38
  253.6 4.1 %collective-permute-start.20 = (bf16[2,128,256]{2,1,0:T(8,128)(2,1)S(1)}, bf16[2,128,256]{2,1,0:T(8,128)(2,1)S(1)}, u32[]{:S(2)}, u32[]{:S(2)}) collective-permute-start(bf16[2,128,256]{2,1,0:T(8,128)(2,1)S(1)} %slice.111), channel_id=1, source_target_pairs={{0,128},{128,0},{1,129},{129,1},{2,130},{130,2},{3,131},{131,3},{4... | collective-permute-start | bytes 393224 | tf_op jit(solution)/shard_map/ppermute | solution.py:38
  257.7 3.3 %collective-permute-done.23 = bf16[2,128,256]{2,1,0:T(8,128)(2,1)S(1)} collective-permute-done((bf16[2,128,256]{2,1,0:T(8,128)(2,1)S(1)}, bf16[2,128,256]{2,1,0:T(8,128)(2,1)S(1)}, u32[]{:S(2)}, u32[]{:S(2)}) %collective-permute-start.23) | collective-permute-done | bytes 131104 | tf_op jit(solution)/shard_map/ppermute | solution.py:38
  263.5 7.4 %collective-permute-start.21 = (bf16[1,128,256]{2,1,0:T(8,128)(2,1)S(1)}, bf16[1,128,256]{2,1,0:T(8,128)(2,1)S(1)}, u32[]{:S(2)}, u32[]{:S(2)}) collective-permute-start(bf16[1,128,256]{2,1,0:T(8,128)(2,1)S(1)} %slice.113), channel_id=1, source_target_pairs={{0,256},{256,0},{1,257},{257,1},{2,258},{258,2},{3,259},{259,3},{4... | collective-permute-start | bytes 196616 | tf_op jit(solution)/shard_map/ppermute | solution.py:38
  270.9 4.8 %collective-permute-done.24 = bf16[1,128,256]{2,1,0:T(8,128)(2,1)S(1)} collective-permute-done((bf16[1,128,256]{2,1,0:T(8,128)(2,1)S(1)}, bf16[1,128,256]{2,1,0:T(8,128)(2,1)S(1)}, u32[]{:S(2)}, u32[]{:S(2)}) %collective-permute-start.24) | collective-permute-done | bytes 65568 | tf_op jit(solution)/shard_map/ppermute | solution.py:38
  (113 shorter events, 44.3 us)
Async XLA Ops:
  0.6 130.2 %copy-start = (bf16[512,512]{1,0:T(8,128)(2,1)S(1)}, bf16[512,512]{1,0:T(8,128)(2,1)}, u32[]{:S(2)}) copy-start(bf16[512,512]{1,0:T(8,128)(2,1)} %param.8) | copy-start | bytes 1572868
  0.6 57.5 %copy-start.1 = (bf16[1,1,8,128,128]{4,3,2,1,0:T(8,128)(2,1)S(1)}, bf16[1,1,8,128,128]{4,3,2,1,0:T(8,128)(2,1)}, u32[]{:S(2)}) copy-start(bf16[1,1,8,128,128]{4,3,2,1,0:T(8,128)(2,1)} %param.13) | copy-start | bytes 786436
  4.2 25.3 %collective-permute-start = (bf16[1,144,256]{2,1,0:T(8,128)(2,1)S(1)}, bf16[1,144,256]{2,1,0:T(8,128)(2,1)S(1)}, u32[]{:S(2)}, u32[]{:S(2)}) collective-permute-start(bf16[1,144,256]{2,1,0:T(8,128)(2,1)S(1)} %pad_maximum_fusion.6), channel_id=1, source_target_pairs={{0,256},{256,0},{1,257},{257,1},{2,258},{258,2},{3,259},{259,3},{4... | collective-permute-start | bytes 221192 | tf_op jit(solution)/shard_map/ppermute | solution.py:38
  13.3 14.2 %collective-permute-start.5 = (bf16[1,128,256]{2,1,0:T(8,128)(2,1)S(1)}, bf16[1,128,256]{2,1,0:T(8,128)(2,1)S(1)}, u32[]{:S(2)}, u32[]{:S(2)}) collective-permute-start(bf16[1,128,256]{2,1,0:T(8,128)(2,1)S(1)} %get-tuple-element.25), channel_id=1, source_target_pairs={{0,256},{256,0},{1,257},{257,1},{2,258},{258,2},{3,259},{259,3},{4... | collective-permute-start | bytes 196616 | tf_op jit(solution)/shard_map/ppermute | solution.py:38
  27.6 12.6 %collective-permute-start.6 = (bf16[2,128,256]{2,1,0:T(8,128)(2,1)S(1)}, bf16[2,128,256]{2,1,0:T(8,128)(2,1)S(1)}, u32[]{:S(2)}, u32[]{:S(2)}) collective-permute-start(bf16[2,128,256]{2,1,0:T(8,128)(2,1)S(1)} %pad_maximum_fusion.5), channel_id=1, source_target_pairs={{0,128},{128,0},{1,129},{129,1},{2,130},{130,2},{3,131},{131,3},{4... | collective-permute-start | bytes 393224 | tf_op jit(solution)/shard_map/ppermute | solution.py:38
  29.5 12.6 %collective-permute-start.1 = (bf16[2,144,256]{2,1,0:T(8,128)(2,1)S(1)}, bf16[2,144,256]{2,1,0:T(8,128)(2,1)S(1)}, u32[]{:S(2)}, u32[]{:S(2)}) collective-permute-start(bf16[2,144,256]{2,1,0:T(8,128)(2,1)S(1)} %pad_maximum_fusion.4), channel_id=1, source_target_pairs={{0,128},{128,0},{1,129},{129,1},{2,130},{130,2},{3,131},{131,3},{4... | collective-permute-start | bytes 442376 | tf_op jit(solution)/shard_map/ppermute | solution.py:38
  40.2 10.6 %collective-permute-start.7 = (bf16[4,128,256]{2,1,0:T(8,128)(2,1)S(1)}, bf16[4,128,256]{2,1,0:T(8,128)(2,1)S(1)}, u32[]{:S(2)}, u32[]{:S(2)}) collective-permute-start(bf16[4,128,256]{2,1,0:T(8,128)(2,1)S(1)} %pad_maximum_fusion.2.refs_2_), channel_id=1, source_target_pairs={{0,64},{64,0},{1,65},{65,1},{2,66},{66,2},{3,67},{67,3},{4,68},{68... | collective-permute-start | bytes 786440 | tf_op jit(solution)/shard_map/ppermute | solution.py:38
  42.2 11.8 %collective-permute-start.2 = (bf16[4,144,256]{2,1,0:T(8,128)(2,1)S(1)}, bf16[4,144,256]{2,1,0:T(8,128)(2,1)S(1)}, u32[]{:S(2)}, u32[]{:S(2)}) collective-permute-start(bf16[4,144,256]{2,1,0:T(8,128)(2,1)S(1)} %pad_maximum_fusion.1.refs_1_), channel_id=1, source_target_pairs={{0,64},{64,0},{1,65},{65,1},{2,66},{66,2},{3,67},{67,3},{4,68},{68... | collective-permute-start | bytes 884744 | tf_op jit(solution)/shard_map/ppermute | solution.py:38
  46.1 9.8 %collective-permute-start.3 = (bf16[4,144,256]{2,1,0:T(8,128)(2,1)S(1)}, bf16[4,144,256]{2,1,0:T(8,128)(2,1)S(1)}, u32[]{:S(2)}, u32[]{:S(2)}) collective-permute-start(bf16[4,144,256]{2,1,0:T(8,128)(2,1)S(1)} %pad_maximum_fusion.1.refs_1_), channel_id=1, source_target_pairs={{0,32},{32,0},{1,33},{33,1},{2,34},{34,2},{3,35},{35,3},{4,36},{36... | collective-permute-start | bytes 884744 | tf_op jit(solution)/shard_map/ppermute | solution.py:38
  48.1 10.0 %collective-permute-start.8 = (bf16[4,128,256]{2,1,0:T(8,128)(2,1)S(1)}, bf16[4,128,256]{2,1,0:T(8,128)(2,1)S(1)}, u32[]{:S(2)}, u32[]{:S(2)}) collective-permute-start(bf16[4,128,256]{2,1,0:T(8,128)(2,1)S(1)} %pad_maximum_fusion.2.refs_2_), channel_id=1, source_target_pairs={{0,32},{32,0},{1,33},{33,1},{2,34},{34,2},{3,35},{35,3},{4,36},{36... | collective-permute-start | bytes 786440 | tf_op jit(solution)/shard_map/ppermute | solution.py:38
  50.9 7.2 %collective-permute-start.9 = (bf16[4,128,256]{2,1,0:T(8,128)(2,1)S(1)}, bf16[4,128,256]{2,1,0:T(8,128)(2,1)S(1)}, u32[]{:S(2)}, u32[]{:S(2)}) collective-permute-start(bf16[4,128,256]{2,1,0:T(8,128)(2,1)S(1)} %collective-permute-done.7.refs_4_), channel_id=1, source_target_pairs={{0,32},{32,0},{1,33},{33,1},{2,34},{34,2},{3,35},{35,3},{4,36},{36... | collective-permute-start | bytes 786440 | tf_op jit(solution)/shard_map/ppermute | solution.py:38
  54.0 3.5 %collective-permute-start.4 = (bf16[4,144,256]{2,1,0:T(8,128)(2,1)S(1)}, bf16[4,144,256]{2,1,0:T(8,128)(2,1)S(1)}, u32[]{:S(2)}, u32[]{:S(2)}) collective-permute-start(bf16[4,144,256]{2,1,0:T(8,128)(2,1)S(1)} %collective-permute-done.2.refs_3_), channel_id=1, source_target_pairs={{0,32},{32,0},{1,33},{33,1},{2,34},{34,2},{3,35},{35,3},{4,36},{36... | collective-permute-start | bytes 884744 | tf_op jit(solution)/shard_map/ppermute | solution.py:38
  96.4 33.8 %all-to-all-start.1 = ((bf16[16,128,512]{2,1,0:T(8,128)(2,1)}), bf16[16,128,512]{2,1,0:T(8,128)(2,1)S(1)}, u32[]{:S(2)}, u32[]{:S(2)}) async-start(bf16[16,128,512]{2,1,0:T(8,128)(2,1)} %get-tuple-element.14), calls=%async_computation.1 | async-start | bytes 4194304 | tf_op jit(solution)/shard_map/all_to_all | solution.py:46
  102.4 29.4 %copy-start.5 = (bf16[128,512]{1,0:T(8,128)(2,1)S(1)}, bf16[128,512]{1,0:T(8,128)(2,1)}, u32[]{:S(2)}) copy-start(bf16[128,512]{1,0:T(8,128)(2,1)} %param.9) | copy-start | bytes 393220
  102.4 28.2 %collective-permute-start.10 = (bf16[128,512]{1,0:T(8,128)(2,1)S(1)}, bf16[128,512]{1,0:T(8,128)(2,1)S(1)}, u32[]{:S(2)}, u32[]{:S(2)}) collective-permute-start(bf16[128,512]{1,0:T(8,128)(2,1)S(1)} %reduce_sum.98), channel_id=1, source_target_pairs={{0,4},{4,0},{1,5},{5,1},{2,6},{6,2},{3,7},{7,3},{8,12},{12,8},{9,1... | collective-permute-start | bytes 393224 | tf_op jit(solution)/shard_map/ppermute | solution.py:38
  134.0 25.1 %all-to-all-start.2 = ((bf16[16,80,512]{2,1,0:T(8,128)(2,1)}), bf16[16,80,512]{2,1,0:T(8,128)(2,1)S(1)}, u32[]{:S(2)}, u32[]{:S(2)}) async-start(bf16[16,80,512]{2,1,0:T(8,128)(2,1)} %pad_maximum_fusion), calls=%async_computation.2 | async-start | bytes 2621440 | tf_op jit(solution)/shard_map/all_to_all | solution.py:46
  139.3 19.7 %collective-permute-start.16 = (bf16[128,512]{1,0:T(8,128)(2,1)S(1)}, bf16[128,512]{1,0:T(8,128)(2,1)S(1)}, u32[]{:S(2)}, u32[]{:S(2)}) collective-permute-start(bf16[128,512]{1,0:T(8,128)(2,1)S(1)} %multiply_convert_fusion), channel_id=1, source_target_pairs={{0,4},{4,0},{1,5},{5,1},{2,6},{6,2},{3,7},{7,3},{8,12},{12,8},{9,1... | collective-permute-start | bytes 393224 | tf_op jit(solution)/shard_map/ppermute | solution.py:38
  161.2 55.1 %all-to-all-start.3 = ((bf16[16,208,512]{2,1,0:T(8,128)(2,1)}), bf16[16,208,512]{2,1,0:T(8,128)(2,1)}, u32[]{:S(2)}, u32[]{:S(2)}) async-start(bf16[16,208,512]{2,1,0:T(8,128)(2,1)} %broadcast_in_dim.13), calls=%async_computation.3 | async-start | bytes 6815744 | tf_op jit(solution)/shard_map/all_to_all | solution.py:46
  168.5 3.1 %collective-permute-start.11 = (f32[32,512]{1,0:T(8,128)S(1)}, f32[32,512]{1,0:T(8,128)S(1)}, u32[]{:S(2)}, u32[]{:S(2)}) collective-permute-start(f32[32,512]{1,0:T(8,128)S(1)} %convert_reduce_fusion.1), channel_id=1, source_target_pairs={{0,32},{32,0},{1,33},{33,1},{2,34},{34,2},{3,35},{35,3},{4,36},{36... | collective-permute-start | bytes 196616 | tf_op jit(solution)/shard_map/ppermute | solution.py:38
  171.6 16.0 %collective-permute-start.12 = (f32[32,512]{1,0:T(8,128)S(1)}, f32[32,512]{1,0:T(8,128)S(1)}, u32[]{:S(2)}, u32[]{:S(2)}) collective-permute-start(f32[32,512]{1,0:T(8,128)S(1)} %add.137), channel_id=1, source_target_pairs={{0,4},{4,0},{1,5},{5,1},{2,6},{6,2},{3,7},{7,3},{8,12},{12,8},{9,1... | collective-permute-start | bytes 196616 | tf_op jit(solution)/shard_map/ppermute | solution.py:38
  187.6 7.6 %collective-permute-start.13 = (f32[32,512]{1,0:T(8,128)S(1)}, f32[32,512]{1,0:T(8,128)S(1)}, u32[]{:S(2)}, u32[]{:S(2)}) collective-permute-start(f32[32,512]{1,0:T(8,128)S(1)} %add.138), channel_id=1, source_target_pairs={{0,64},{64,0},{1,65},{65,1},{2,66},{66,2},{3,67},{67,3},{4,68},{68... | collective-permute-start | bytes 196616 | tf_op jit(solution)/shard_map/ppermute | solution.py:38
  195.2 10.2 %collective-permute-start.14 = (f32[32,512]{1,0:T(8,128)S(1)}, f32[32,512]{1,0:T(8,128)S(1)}, u32[]{:S(2)}, u32[]{:S(2)}) collective-permute-start(f32[32,512]{1,0:T(8,128)S(1)} %add.139), channel_id=1, source_target_pairs={{0,128},{128,0},{1,129},{129,1},{2,130},{130,2},{3,131},{131,3},{4... | collective-permute-start | bytes 196616 | tf_op jit(solution)/shard_map/ppermute | solution.py:38
  205.5 10.8 %collective-permute-start.15 = (f32[32,512]{1,0:T(8,128)S(1)}, f32[32,512]{1,0:T(8,128)S(1)}, u32[]{:S(2)}, u32[]{:S(2)}) collective-permute-start(f32[32,512]{1,0:T(8,128)S(1)} %add.140), channel_id=1, source_target_pairs={{0,256},{256,0},{1,257},{257,1},{2,258},{258,2},{3,259},{259,3},{4... | collective-permute-start | bytes 196616 | tf_op jit(solution)/shard_map/ppermute | solution.py:38
  221.5 4.4 %collective-permute-start.18 = (bf16[8,128,256]{2,1,0:T(8,128)(2,1)}, bf16[8,128,256]{2,1,0:T(8,128)(2,1)S(1)}, u32[]{:S(2)}, u32[]{:S(2)}) collective-permute-start(bf16[8,128,256]{2,1,0:T(8,128)(2,1)} %get-tuple-element.20), channel_id=1, source_target_pairs={{0,32},{32,0},{1,33},{33,1},{2,34},{34,2},{3,35},{35,3},{4,36},{36... | collective-permute-start | bytes 1572872 | tf_op jit(solution)/shard_map/ppermute | solution.py:38
  223.4 5.3 %collective-permute-start.17 = (bf16[8,128,256]{2,1,0:T(8,128)(2,1)}, bf16[8,128,256]{2,1,0:T(8,128)(2,1)S(1)}, u32[]{:S(2)}, u32[]{:S(2)}) collective-permute-start(bf16[8,128,256]{2,1,0:T(8,128)(2,1)} %copy-done.2), channel_id=1, source_target_pairs={{0,32},{32,0},{1,33},{33,1},{2,34},{34,2},{3,35},{35,3},{4,36},{36... | collective-permute-start | bytes 1572872 | tf_op jit(solution)/shard_map/ppermute | solution.py:38
  226.8 15.9 %collective-permute-start.22 = (bf16[4,128,256]{2,1,0:T(8,128)(2,1)}, bf16[4,128,256]{2,1,0:T(8,128)(2,1)S(1)}, u32[]{:S(2)}, u32[]{:S(2)}) collective-permute-start(bf16[4,128,256]{2,1,0:T(8,128)(2,1)} %slice.115), channel_id=1, source_target_pairs={{0,64},{64,0},{1,65},{65,1},{2,66},{66,2},{3,67},{67,3},{4,68},{68... | collective-permute-start | bytes 786440 | tf_op jit(solution)/shard_map/ppermute | solution.py:38
  229.6 22.9 %collective-permute-start.19 = (bf16[4,128,256]{2,1,0:T(8,128)(2,1)}, bf16[4,128,256]{2,1,0:T(8,128)(2,1)}, u32[]{:S(2)}, u32[]{:S(2)}) collective-permute-start(bf16[4,128,256]{2,1,0:T(8,128)(2,1)} %slice.109), channel_id=1, source_target_pairs={{0,64},{64,0},{1,65},{65,1},{2,66},{66,2},{3,67},{67,3},{4,68},{68... | collective-permute-start | bytes 786440 | tf_op jit(solution)/shard_map/ppermute | solution.py:38
  234.8 43.4 %all-to-all-start.4 = ((f32[16,40,512]{2,1,0:T(8,128)}), f32[16,40,512]{2,1,0:T(8,128)S(1)}, u32[]{:S(2)}, u32[]{:S(2)}) async-start(f32[16,40,512]{2,1,0:T(8,128)} %broadcast_in_dim.14), calls=%async_computation.4 | async-start | bytes 2621440 | tf_op jit(solution)/shard_map/all_to_all | solution.py:46
  242.8 18.2 %collective-permute-start.23 = (bf16[2,128,256]{2,1,0:T(8,128)(2,1)S(1)}, bf16[2,128,256]{2,1,0:T(8,128)(2,1)S(1)}, u32[]{:S(2)}, u32[]{:S(2)}) collective-permute-start(bf16[2,128,256]{2,1,0:T(8,128)(2,1)S(1)} %slice.117), channel_id=1, source_target_pairs={{0,128},{128,0},{1,129},{129,1},{2,130},{130,2},{3,131},{131,3},{4... | collective-permute-start | bytes 393224 | tf_op jit(solution)/shard_map/ppermute | solution.py:38
  253.6 9.9 %collective-permute-start.20 = (bf16[2,128,256]{2,1,0:T(8,128)(2,1)S(1)}, bf16[2,128,256]{2,1,0:T(8,128)(2,1)S(1)}, u32[]{:S(2)}, u32[]{:S(2)}) collective-permute-start(bf16[2,128,256]{2,1,0:T(8,128)(2,1)S(1)} %slice.111), channel_id=1, source_target_pairs={{0,128},{128,0},{1,129},{129,1},{2,130},{130,2},{3,131},{131,3},{4... | collective-permute-start | bytes 393224 | tf_op jit(solution)/shard_map/ppermute | solution.py:38
  261.0 14.6 %collective-permute-start.24 = (bf16[1,128,256]{2,1,0:T(8,128)(2,1)S(1)}, bf16[1,128,256]{2,1,0:T(8,128)(2,1)S(1)}, u32[]{:S(2)}, u32[]{:S(2)}) collective-permute-start(bf16[1,128,256]{2,1,0:T(8,128)(2,1)S(1)} %slice.119), channel_id=1, source_target_pairs={{0,256},{256,0},{1,257},{257,1},{2,258},{258,2},{3,259},{259,3},{4... | collective-permute-start | bytes 196616 | tf_op jit(solution)/shard_map/ppermute | solution.py:38
  263.5 13.9 %collective-permute-start.21 = (bf16[1,128,256]{2,1,0:T(8,128)(2,1)S(1)}, bf16[1,128,256]{2,1,0:T(8,128)(2,1)S(1)}, u32[]{:S(2)}, u32[]{:S(2)}) collective-permute-start(bf16[1,128,256]{2,1,0:T(8,128)(2,1)S(1)} %slice.113), channel_id=1, source_target_pairs={{0,256},{256,0},{1,257},{257,1},{2,258},{258,2},{3,259},{259,3},{4... | collective-permute-start | bytes 196616 | tf_op jit(solution)/shard_map/ppermute | solution.py:38
  (3 other events, 12.8 us)

commit v16 on v15

--- a/solution.py
+++ b/solution.py
@@ -198,7 +198,7 @@
     last_group = swap_parts(copies_of(after(grad_rest, first_group), PLANE), PLANE)
 
     line_rows = jnp.sum(first_group[:, lead:].astype(F32), axis=0)
-    for axis in ("core", "zh", "z1", "zb", "za"):
+    for axis in ("core", "z1", "za", "zb", "zh"):
         line_rows = line_rows + flip(line_rows, axis)
     line_rows = line_rows * (1.0 / math.sqrt(nodes))
     last_group = after(last_group, line_rows)

time: 282 us -> 280 us (level)
  starting transfers between devices: 156 us -> 126 us
  waiting for transfers between devices: 60.6 us -> 89.3 us
    ppermute x25, starting transfers between devices: 129 us -> 99.6 us  [flip(): return lax.ppermute(block, axis, [(0, 1), (1, 0)])]
    ppermute x25, waiting for transfers between devices: 47.1 us -> 71.8 us  [flip(): return lax.ppermute(block, axis, [(0, 1), (1, 0)])]
    all_to_all x4, waiting for transfers between devices: 13.5 us -> 17.5 us  [swap_parts(): return lax.all_to_all(parts, axes, split_axis=0, concat_axis=0, tiled=True)]
  transfers between devices with their start and end apart: 29 -> 29, of which waited for: 16 -> 15; matrix products, arithmetic and copies ran while one was open for 3% -> 3% of each run, Pallas kernels for 0% -> 0%
where the time goes in v16:
time: 280 us; the launch traced here: 278 us
  starting transfers between devices  126 us (45%)
  waiting for transfers between devices  89.3 us (32%)
  blocking collectives  35.1 us (13%)
  local copies, waits for them, and re-layouts  8.31 us (3%)
  other arithmetic  7.76 us (3%)
  Pallas kernels  7.12 us (3%)
    ppermute x25, starting transfers between devices, flip(): return lax.ppermute(block, axis, [(0, 1), (1, 0)])  99.6 us
    ppermute x25, waiting for transfers between devices, flip(): return lax.ppermute(block, axis, [(0, 1), (1, 0)])  71.8 us
    all_to_all x1, blocking collectives, swap_parts(): return lax.all_to_all(parts, axes, split_axis=0, concat_axis=0, tiled=True)  35.1 us
    all_to_all x4, starting transfers between devices, swap_parts(): return lax.all_to_all(parts, axes, split_axis=0, concat_axis=0, tiled=True)  26.2 us
    all_to_all x4, waiting for transfers between devices, swap_parts(): return lax.all_to_all(parts, axes, split_axis=0, concat_axis=0, tiled=True)  17.5 us
    pallas_call x2, Pallas kernels, tile_sums(): pl.pallas_call(functools.partial(tile_kernel, transposed, scaled, sources...  7.12 us
  transfers between devices with their start and end apart: 29, of which 15 were waited for; matrix products, arithmetic and copies ran while one was open for 3% of the time, Pallas kernels for 0%

profile of v16, /device:TPU:24, one launch (start us, length us, event | category | flops | bytes accessed | tf_op | source)
XLA Modules:
  0.0 278.1 jit_solution(3654806050138919289)
XLA Ops:
  4.2 9.1 %collective-permute-start = (bf16[1,144,256]{2,1,0:T(8,128)(2,1)S(1)}, bf16[1,144,256]{2,1,0:T(8,128)(2,1)S(1)}, u32[]{:S(2)}, u32[]{:S(2)}) collective-permute-start(bf16[1,144,256]{2,1,0:T(8,128)(2,1)S(1)} %pad_maximum_fusion.6), channel_id=1, source_target_pairs={{0,256},{256,0},{1,257},{257,1},{2,258},{258,2},{3,259},{259,3},{4... | collective-permute-start | bytes 221192 | tf_op jit(solution)/shard_map/ppermute | solution.py:38
  16.6 11.0 %collective-permute-done.5 = bf16[1,128,256]{2,1,0:T(8,128)(2,1)S(1)} collective-permute-done((bf16[1,128,256]{2,1,0:T(8,128)(2,1)S(1)}, bf16[1,128,256]{2,1,0:T(8,128)(2,1)S(1)}, u32[]{:S(2)}, u32[]{:S(2)}) %collective-permute-start.5) | collective-permute-done | bytes 65568 | tf_op jit(solution)/shard_map/ppermute | solution.py:38
  29.5 4.8 %collective-permute-start.1 = (bf16[2,144,256]{2,1,0:T(8,128)(2,1)S(1)}, bf16[2,144,256]{2,1,0:T(8,128)(2,1)S(1)}, u32[]{:S(2)}, u32[]{:S(2)}) collective-permute-start(bf16[2,144,256]{2,1,0:T(8,128)(2,1)S(1)} %pad_maximum_fusion.4), channel_id=1, source_target_pairs={{0,128},{128,0},{1,129},{129,1},{2,130},{130,2},{3,131},{131,3},{4... | collective-permute-start | bytes 442376 | tf_op jit(solution)/shard_map/ppermute | solution.py:38
  35.0 5.2 %collective-permute-done.6 = bf16[2,128,256]{2,1,0:T(8,128)(2,1)S(1)} collective-permute-done((bf16[2,128,256]{2,1,0:T(8,128)(2,1)S(1)}, bf16[2,128,256]{2,1,0:T(8,128)(2,1)S(1)}, u32[]{:S(2)}, u32[]{:S(2)}) %collective-permute-start.6) | collective-permute-done | bytes 131104 | tf_op jit(solution)/shard_map/ppermute | solution.py:38
  42.2 3.9 %collective-permute-start.2 = (bf16[4,144,256]{2,1,0:T(8,128)(2,1)S(1)}, bf16[4,144,256]{2,1,0:T(8,128)(2,1)S(1)}, u32[]{:S(2)}, u32[]{:S(2)}) collective-permute-start(bf16[4,144,256]{2,1,0:T(8,128)(2,1)S(1)} %pad_maximum_fusion.1.refs_1_), channel_id=1, source_target_pairs={{0,64},{64,0},{1,65},{65,1},{2,66},{66,2},{3,67},{67,3},{4,68},{68... | collective-permute-start | bytes 884744 | tf_op jit(solution)/shard_map/ppermute | solution.py:38
  48.1 2.4 collective-permute-start.8
  58.1 3.3 %shard_map.94 = (bf16[16,128,512]{2,1,0:T(8,128)(2,1)}, bf16[16,128,512]{2,1,0:T(8,128)(2,1)S(1)}) custom-call(s32[8]{0:T(128)S(1)} %shift-right-arithmetic_add_fusion.source.target, s32[8]{0:T(128)S(1)} %add_bitcast_fusion.2.target.source, s32[1]{0:T(128)} %bitcast.36.count, bf16[8,128,128]{2,1,0:T(8,128)(2,1)S(1)} %bitcast.39, f32[8,128]{1,0:T(8,128)S(1)} %gather_fusion, ...), custom_call_target="tpu_custom_call" | custom-call | flops 134217728 | bytes 6422528 | tf_op jit(solution)/shard_map/pallas_call | solution.py:116
  61.4 35.1 %all_to_all.25 = bf16[16,128,512]{2,1,0:T(8,128)(2,1)S(1)} all-to-all(bf16[16,128,512]{2,1,0:T(8,128)(2,1)S(1)} %get-tuple-element.13), channel_id=1, replica_groups=mesh['za'=2,'zb'=2,'z1'=2,'core'=2,'y'=4,'zh'=2,'x'=4] {'y','x'}, dimensions={0} | all-to-all | bytes 4194304 | tf_op jit(solution)/shard_map/all_to_all | solution.py:46
  96.8 6.0 %all-to-all-start.1 = ((bf16[16,128,512]{2,1,0:T(8,128)(2,1)}), bf16[16,128,512]{2,1,0:T(8,128)(2,1)S(1)}, u32[]{:S(2)}, u32[]{:S(2)}) async-start(bf16[16,128,512]{2,1,0:T(8,128)(2,1)} %get-tuple-element.14), calls=%async_computation.1 | async-start | bytes 4194304 | tf_op jit(solution)/shard_map/all_to_all | solution.py:46
  102.8 13.6 %collective-permute-start.10 = (bf16[128,512]{1,0:T(8,128)(2,1)S(1)}, bf16[128,512]{1,0:T(8,128)(2,1)S(1)}, u32[]{:S(2)}, u32[]{:S(2)}) collective-permute-start(bf16[128,512]{1,0:T(8,128)(2,1)S(1)} %reduce_sum.98), channel_id=1, source_target_pairs={{0,4},{4,0},{1,5},{5,1},{2,6},{6,2},{3,7},{7,3},{8,12},{12,8},{9,1... | collective-permute-start | bytes 393224 | tf_op jit(solution)/shard_map/ppermute | solution.py:38
  116.4 17.5 %all-to-all-done.1 = bf16[16,128,512]{2,1,0:T(8,128)(2,1)S(1)} async-done(((bf16[16,128,512]{2,1,0:T(8,128)(2,1)}), bf16[16,128,512]{2,1,0:T(8,128)(2,1)S(1)}, u32[]{:S(2)}, u32[]{:S(2)}) %all-to-all-start.1) | async-done | bytes 2097184 | tf_op jit(solution)/shard_map/all_to_all | solution.py:46
  137.6 5.1 %all-to-all-start.2 = ((bf16[16,80,512]{2,1,0:T(8,128)(2,1)}), bf16[16,80,512]{2,1,0:T(8,128)(2,1)S(1)}, u32[]{:S(2)}, u32[]{:S(2)}) async-start(bf16[16,80,512]{2,1,0:T(8,128)(2,1)} %pad_maximum_fusion), calls=%async_computation.2 | async-start | bytes 2621440 | tf_op jit(solution)/shard_map/all_to_all | solution.py:46
  142.7 11.0 %collective-permute-start.16 = (bf16[128,512]{1,0:T(8,128)(2,1)S(1)}, bf16[128,512]{1,0:T(8,128)(2,1)S(1)}, u32[]{:S(2)}, u32[]{:S(2)}) collective-permute-start(bf16[128,512]{1,0:T(8,128)(2,1)S(1)} %multiply_convert_fusion), channel_id=1, source_target_pairs={{0,4},{4,0},{1,5},{5,1},{2,6},{6,2},{3,7},{7,3},{8,12},{12,8},{9,1... | collective-permute-start | bytes 393224 | tf_op jit(solution)/shard_map/ppermute | solution.py:38
  153.7 11.0 %collective-permute-done.16 = bf16[128,512]{1,0:T(8,128)(2,1)S(1)} collective-permute-done((bf16[128,512]{1,0:T(8,128)(2,1)S(1)}, bf16[128,512]{1,0:T(8,128)(2,1)S(1)}, u32[]{:S(2)}, u32[]{:S(2)}) %collective-permute-start.16) | collective-permute-done | bytes 131104 | tf_op jit(solution)/shard_map/ppermute | solution.py:38
  164.7 2.1 broadcast_in_dim.13
  166.7 7.2 %all-to-all-start.3 = ((bf16[16,208,512]{2,1,0:T(8,128)(2,1)}), bf16[16,208,512]{2,1,0:T(8,128)(2,1)}, u32[]{:S(2)}, u32[]{:S(2)}) async-start(bf16[16,208,512]{2,1,0:T(8,128)(2,1)} %broadcast_in_dim.13), calls=%async_computation.3 | async-start | bytes 6815744 | tf_op jit(solution)/shard_map/all_to_all | solution.py:46
  179.1 4.2 %collective-permute-done.12 = f32[32,512]{1,0:T(8,128)S(1)} collective-permute-done((f32[32,512]{1,0:T(8,128)S(1)}, f32[32,512]{1,0:T(8,128)S(1)}, u32[]{:S(2)}, u32[]{:S(2)}) %collective-permute-start.12) | collective-permute-done | bytes 65568 | tf_op jit(solution)/shard_map/ppermute | solution.py:38
  183.4 2.9 %collective-permute-start.13 = (f32[32,512]{1,0:T(8,128)S(1)}, f32[32,512]{1,0:T(8,128)S(1)}, u32[]{:S(2)}, u32[]{:S(2)}) collective-permute-start(f32[32,512]{1,0:T(8,128)S(1)} %add.138), channel_id=1, source_target_pairs={{0,256},{256,0},{1,257},{257,1},{2,258},{258,2},{3,259},{259,3},{4... | collective-permute-start | bytes 196616 | tf_op jit(solution)/shard_map/ppermute | solution.py:38
  186.2 9.8 %collective-permute-done.13 = f32[32,512]{1,0:T(8,128)S(1)} collective-permute-done((f32[32,512]{1,0:T(8,128)S(1)}, f32[32,512]{1,0:T(8,128)S(1)}, u32[]{:S(2)}, u32[]{:S(2)}) %collective-permute-start.13) | collective-permute-done | bytes 65568 | tf_op jit(solution)/shard_map/ppermute | solution.py:38
  198.0 5.2 %collective-permute-done.14 = f32[32,512]{1,0:T(8,128)S(1)} collective-permute-done((f32[32,512]{1,0:T(8,128)S(1)}, f32[32,512]{1,0:T(8,128)S(1)}, u32[]{:S(2)}, u32[]{:S(2)}) %collective-permute-start.14) | collective-permute-done | bytes 65568 | tf_op jit(solution)/shard_map/ppermute | solution.py:38
  203.2 8.0 %collective-permute-start.15 = (f32[32,512]{1,0:T(8,128)S(1)}, f32[32,512]{1,0:T(8,128)S(1)}, u32[]{:S(2)}, u32[]{:S(2)}) collective-permute-start(f32[32,512]{1,0:T(8,128)S(1)} %add.140), channel_id=1, source_target_pairs={{0,4},{4,0},{1,5},{5,1},{2,6},{6,2},{3,7},{7,3},{8,12},{12,8},{9,1... | collective-permute-start | bytes 196616 | tf_op jit(solution)/shard_map/ppermute | solution.py:38
  211.2 10.5 %collective-permute-done.15 = f32[32,512]{1,0:T(8,128)S(1)} collective-permute-done((f32[32,512]{1,0:T(8,128)S(1)}, f32[32,512]{1,0:T(8,128)S(1)}, u32[]{:S(2)}, u32[]{:S(2)}) %collective-permute-start.15) | collective-permute-done | bytes 65568 | tf_op jit(solution)/shard_map/ppermute | solution.py:38
  221.8 3.8 %shard_map.95 = (bf16[8,128,256]{2,1,0:T(8,128)(2,1)S(1)}, bf16[8,128,256]{2,1,0:T(8,128)(2,1)S(1)}, bf16[8,128,256]{2,1,0:T(8,128)(2,1)S(1)}, bf16[8,128,256]{2,1,0:T(8,128)(2,1)}) custom-call(s32[8]{0:T(128)S(1)} %add_bitcast_fusion.2.target.source, s32[8]{0:T(128)S(1)} %shift-right-arithmetic_add_fusion.source.target, s32[1]{0:T(128)} %bitcast.37.count, ...), custom_call_target="tpu_custom_call" | custom-call | flops 134217728 | bytes 6815744 | tf_op jit(solution)/shard_map/pallas_call | solution.py:116
  228.3 2.4 collective-permute-start.17
  231.7 3.1 %collective-permute-start.22 = (bf16[4,128,256]{2,1,0:T(8,128)(2,1)}, bf16[4,128,256]{2,1,0:T(8,128)(2,1)S(1)}, u32[]{:S(2)}, u32[]{:S(2)}) collective-permute-start(bf16[4,128,256]{2,1,0:T(8,128)(2,1)} %slice.115), channel_id=1, source_target_pairs={{0,64},{64,0},{1,65},{65,1},{2,66},{66,2},{3,67},{67,3},{4,68},{68... | collective-permute-start | bytes 786440 | tf_op jit(solution)/shard_map/ppermute | solution.py:38
  235.8 2.7 collective-permute-start.19
  239.7 7.9 %all-to-all-start.4 = ((f32[16,40,512]{2,1,0:T(8,128)}), f32[16,40,512]{2,1,0:T(8,128)S(1)}, u32[]{:S(2)}, u32[]{:S(2)}) async-start(f32[16,40,512]{2,1,0:T(8,128)} %broadcast_in_dim.14), calls=%async_computation.4 | async-start | bytes 2621440 | tf_op jit(solution)/shard_map/all_to_all | solution.py:46
  250.8 4.8 %collective-permute-start.20 = (bf16[2,128,256]{2,1,0:T(8,128)(2,1)S(1)}, bf16[2,128,256]{2,1,0:T(8,128)(2,1)S(1)}, u32[]{:S(2)}, u32[]{:S(2)}) collective-permute-start(bf16[2,128,256]{2,1,0:T(8,128)(2,1)S(1)} %slice.111), channel_id=1, source_target_pairs={{0,128},{128,0},{1,129},{129,1},{2,130},{130,2},{3,131},{131,3},{4... | collective-permute-start | bytes 393224 | tf_op jit(solution)/shard_map/ppermute | solution.py:38
  255.6 5.1 %collective-permute-done.23 = bf16[2,128,256]{2,1,0:T(8,128)(2,1)S(1)} collective-permute-done((bf16[2,128,256]{2,1,0:T(8,128)(2,1)S(1)}, bf16[2,128,256]{2,1,0:T(8,128)(2,1)S(1)}, u32[]{:S(2)}, u32[]{:S(2)}) %collective-permute-start.23) | collective-permute-done | bytes 131104 | tf_op jit(solution)/shard_map/ppermute | solution.py:38
  260.7 3.5 %collective-permute-start.24 = (bf16[1,128,256]{2,1,0:T(8,128)(2,1)S(1)}, bf16[1,128,256]{2,1,0:T(8,128)(2,1)S(1)}, u32[]{:S(2)}, u32[]{:S(2)}) collective-permute-start(bf16[1,128,256]{2,1,0:T(8,128)(2,1)S(1)} %slice.119), channel_id=1, source_target_pairs={{0,256},{256,0},{1,257},{257,1},{2,258},{258,2},{3,259},{259,3},{4... | collective-permute-start | bytes 196616 | tf_op jit(solution)/shard_map/ppermute | solution.py:38
  264.3 6.3 %collective-permute-start.21 = (bf16[1,128,256]{2,1,0:T(8,128)(2,1)S(1)}, bf16[1,128,256]{2,1,0:T(8,128)(2,1)S(1)}, u32[]{:S(2)}, u32[]{:S(2)}) collective-permute-start(bf16[1,128,256]{2,1,0:T(8,128)(2,1)S(1)} %slice.113), channel_id=1, source_target_pairs={{0,256},{256,0},{1,257},{257,1},{2,258},{258,2},{3,259},{259,3},{4... | collective-permute-start | bytes 196616 | tf_op jit(solution)/shard_map/ppermute | solution.py:38
  270.5 3.6 %collective-permute-done.24 = bf16[1,128,256]{2,1,0:T(8,128)(2,1)S(1)} collective-permute-done((bf16[1,128,256]{2,1,0:T(8,128)(2,1)S(1)}, bf16[1,128,256]{2,1,0:T(8,128)(2,1)S(1)}, u32[]{:S(2)}, u32[]{:S(2)}) %collective-permute-start.24) | collective-permute-done | bytes 65568 | tf_op jit(solution)/shard_map/ppermute | solution.py:38
  (113 shorter events, 43.9 us)
Async XLA Ops:
  0.6 133.8 %copy-start = (bf16[512,512]{1,0:T(8,128)(2,1)S(1)}, bf16[512,512]{1,0:T(8,128)(2,1)}, u32[]{:S(2)}) copy-start(bf16[512,512]{1,0:T(8,128)(2,1)} %param.8) | copy-start | bytes 1572868
  0.6 57.5 %copy-start.1 = (bf16[1,1,8,128,128]{4,3,2,1,0:T(8,128)(2,1)S(1)}, bf16[1,1,8,128,128]{4,3,2,1,0:T(8,128)(2,1)}, u32[]{:S(2)}) copy-start(bf16[1,1,8,128,128]{4,3,2,1,0:T(8,128)(2,1)} %param.13) | copy-start | bytes 786436
  4.2 25.3 %collective-permute-start = (bf16[1,144,256]{2,1,0:T(8,128)(2,1)S(1)}, bf16[1,144,256]{2,1,0:T(8,128)(2,1)S(1)}, u32[]{:S(2)}, u32[]{:S(2)}) collective-permute-start(bf16[1,144,256]{2,1,0:T(8,128)(2,1)S(1)} %pad_maximum_fusion.6), channel_id=1, source_target_pairs={{0,256},{256,0},{1,257},{257,1},{2,258},{258,2},{3,259},{259,3},{4... | collective-permute-start | bytes 221192 | tf_op jit(solution)/shard_map/ppermute | solution.py:38
  13.3 14.2 %collective-permute-start.5 = (bf16[1,128,256]{2,1,0:T(8,128)(2,1)S(1)}, bf16[1,128,256]{2,1,0:T(8,128)(2,1)S(1)}, u32[]{:S(2)}, u32[]{:S(2)}) collective-permute-start(bf16[1,128,256]{2,1,0:T(8,128)(2,1)S(1)} %get-tuple-element.25), channel_id=1, source_target_pairs={{0,256},{256,0},{1,257},{257,1},{2,258},{258,2},{3,259},{259,3},{4... | collective-permute-start | bytes 196616 | tf_op jit(solution)/shard_map/ppermute | solution.py:38
  27.6 12.6 %collective-permute-start.6 = (bf16[2,128,256]{2,1,0:T(8,128)(2,1)S(1)}, bf16[2,128,256]{2,1,0:T(8,128)(2,1)S(1)}, u32[]{:S(2)}, u32[]{:S(2)}) collective-permute-start(bf16[2,128,256]{2,1,0:T(8,128)(2,1)S(1)} %pad_maximum_fusion.5), channel_id=1, source_target_pairs={{0,128},{128,0},{1,129},{129,1},{2,130},{130,2},{3,131},{131,3},{4... | collective-permute-start | bytes 393224 | tf_op jit(solution)/shard_map/ppermute | solution.py:38
  29.5 12.6 %collective-permute-start.1 = (bf16[2,144,256]{2,1,0:T(8,128)(2,1)S(1)}, bf16[2,144,256]{2,1,0:T(8,128)(2,1)S(1)}, u32[]{:S(2)}, u32[]{:S(2)}) collective-permute-start(bf16[2,144,256]{2,1,0:T(8,128)(2,1)S(1)} %pad_maximum_fusion.4), channel_id=1, source_target_pairs={{0,128},{128,0},{1,129},{129,1},{2,130},{130,2},{3,131},{131,3},{4... | collective-permute-start | bytes 442376 | tf_op jit(solution)/shard_map/ppermute | solution.py:38
  40.2 10.6 %collective-permute-start.7 = (bf16[4,128,256]{2,1,0:T(8,128)(2,1)S(1)}, bf16[4,128,256]{2,1,0:T(8,128)(2,1)S(1)}, u32[]{:S(2)}, u32[]{:S(2)}) collective-permute-start(bf16[4,128,256]{2,1,0:T(8,128)(2,1)S(1)} %pad_maximum_fusion.2.refs_2_), channel_id=1, source_target_pairs={{0,64},{64,0},{1,65},{65,1},{2,66},{66,2},{3,67},{67,3},{4,68},{68... | collective-permute-start | bytes 786440 | tf_op jit(solution)/shard_map/ppermute | solution.py:38
  42.2 11.8 %collective-permute-start.2 = (bf16[4,144,256]{2,1,0:T(8,128)(2,1)S(1)}, bf16[4,144,256]{2,1,0:T(8,128)(2,1)S(1)}, u32[]{:S(2)}, u32[]{:S(2)}) collective-permute-start(bf16[4,144,256]{2,1,0:T(8,128)(2,1)S(1)} %pad_maximum_fusion.1.refs_1_), channel_id=1, source_target_pairs={{0,64},{64,0},{1,65},{65,1},{2,66},{66,2},{3,67},{67,3},{4,68},{68... | collective-permute-start | bytes 884744 | tf_op jit(solution)/shard_map/ppermute | solution.py:38
  46.1 9.8 %collective-permute-start.3 = (bf16[4,144,256]{2,1,0:T(8,128)(2,1)S(1)}, bf16[4,144,256]{2,1,0:T(8,128)(2,1)S(1)}, u32[]{:S(2)}, u32[]{:S(2)}) collective-permute-start(bf16[4,144,256]{2,1,0:T(8,128)(2,1)S(1)} %pad_maximum_fusion.1.refs_1_), channel_id=1, source_target_pairs={{0,32},{32,0},{1,33},{33,1},{2,34},{34,2},{3,35},{35,3},{4,36},{36... | collective-permute-start | bytes 884744 | tf_op jit(solution)/shard_map/ppermute | solution.py:38
  48.1 10.0 %collective-permute-start.8 = (bf16[4,128,256]{2,1,0:T(8,128)(2,1)S(1)}, bf16[4,128,256]{2,1,0:T(8,128)(2,1)S(1)}, u32[]{:S(2)}, u32[]{:S(2)}) collective-permute-start(bf16[4,128,256]{2,1,0:T(8,128)(2,1)S(1)} %pad_maximum_fusion.2.refs_2_), channel_id=1, source_target_pairs={{0,32},{32,0},{1,33},{33,1},{2,34},{34,2},{3,35},{35,3},{4,36},{36... | collective-permute-start | bytes 786440 | tf_op jit(solution)/shard_map/ppermute | solution.py:38
  50.9 7.2 %collective-permute-start.9 = (bf16[4,128,256]{2,1,0:T(8,128)(2,1)S(1)}, bf16[4,128,256]{2,1,0:T(8,128)(2,1)S(1)}, u32[]{:S(2)}, u32[]{:S(2)}) collective-permute-start(bf16[4,128,256]{2,1,0:T(8,128)(2,1)S(1)} %collective-permute-done.7.refs_4_), channel_id=1, source_target_pairs={{0,32},{32,0},{1,33},{33,1},{2,34},{34,2},{3,35},{35,3},{4,36},{36... | collective-permute-start | bytes 786440 | tf_op jit(solution)/shard_map/ppermute | solution.py:38
  54.0 3.5 %collective-permute-start.4 = (bf16[4,144,256]{2,1,0:T(8,128)(2,1)S(1)}, bf16[4,144,256]{2,1,0:T(8,128)(2,1)S(1)}, u32[]{:S(2)}, u32[]{:S(2)}) collective-permute-start(bf16[4,144,256]{2,1,0:T(8,128)(2,1)S(1)} %collective-permute-done.2.refs_3_), channel_id=1, source_target_pairs={{0,32},{32,0},{1,33},{33,1},{2,34},{34,2},{3,35},{35,3},{4,36},{36... | collective-permute-start | bytes 884744 | tf_op jit(solution)/shard_map/ppermute | solution.py:38
  96.8 37.0 %all-to-all-start.1 = ((bf16[16,128,512]{2,1,0:T(8,128)(2,1)}), bf16[16,128,512]{2,1,0:T(8,128)(2,1)S(1)}, u32[]{:S(2)}, u32[]{:S(2)}) async-start(bf16[16,128,512]{2,1,0:T(8,128)(2,1)} %get-tuple-element.14), calls=%async_computation.1 | async-start | bytes 4194304 | tf_op jit(solution)/shard_map/all_to_all | solution.py:46
  102.8 32.6 %copy-start.5 = (bf16[128,512]{1,0:T(8,128)(2,1)S(1)}, bf16[128,512]{1,0:T(8,128)(2,1)}, u32[]{:S(2)}) copy-start(bf16[128,512]{1,0:T(8,128)(2,1)} %param.9) | copy-start | bytes 393220
  102.8 31.4 %collective-permute-start.10 = (bf16[128,512]{1,0:T(8,128)(2,1)S(1)}, bf16[128,512]{1,0:T(8,128)(2,1)S(1)}, u32[]{:S(2)}, u32[]{:S(2)}) collective-permute-start(bf16[128,512]{1,0:T(8,128)(2,1)S(1)} %reduce_sum.98), channel_id=1, source_target_pairs={{0,4},{4,0},{1,5},{5,1},{2,6},{6,2},{3,7},{7,3},{8,12},{12,8},{9,1... | collective-permute-start | bytes 393224 | tf_op jit(solution)/shard_map/ppermute | solution.py:38
  137.6 27.1 %all-to-all-start.2 = ((bf16[16,80,512]{2,1,0:T(8,128)(2,1)}), bf16[16,80,512]{2,1,0:T(8,128)(2,1)S(1)}, u32[]{:S(2)}, u32[]{:S(2)}) async-start(bf16[16,80,512]{2,1,0:T(8,128)(2,1)} %pad_maximum_fusion), calls=%async_computation.2 | async-start | bytes 2621440 | tf_op jit(solution)/shard_map/all_to_all | solution.py:46
  142.7 22.0 %collective-permute-start.16 = (bf16[128,512]{1,0:T(8,128)(2,1)S(1)}, bf16[128,512]{1,0:T(8,128)(2,1)S(1)}, u32[]{:S(2)}, u32[]{:S(2)}) collective-permute-start(bf16[128,512]{1,0:T(8,128)(2,1)S(1)} %multiply_convert_fusion), channel_id=1, source_target_pairs={{0,4},{4,0},{1,5},{5,1},{2,6},{6,2},{3,7},{7,3},{8,12},{12,8},{9,1... | collective-permute-start | bytes 393224 | tf_op jit(solution)/shard_map/ppermute | solution.py:38
  166.7 55.0 %all-to-all-start.3 = ((bf16[16,208,512]{2,1,0:T(8,128)(2,1)}), bf16[16,208,512]{2,1,0:T(8,128)(2,1)}, u32[]{:S(2)}, u32[]{:S(2)}) async-start(bf16[16,208,512]{2,1,0:T(8,128)(2,1)} %broadcast_in_dim.13), calls=%async_computation.3 | async-start | bytes 6815744 | tf_op jit(solution)/shard_map/all_to_all | solution.py:46
  174.1 3.1 %collective-permute-start.11 = (f32[32,512]{1,0:T(8,128)S(1)}, f32[32,512]{1,0:T(8,128)S(1)}, u32[]{:S(2)}, u32[]{:S(2)}) collective-permute-start(f32[32,512]{1,0:T(8,128)S(1)} %convert_reduce_fusion.1), channel_id=1, source_target_pairs={{0,32},{32,0},{1,33},{33,1},{2,34},{34,2},{3,35},{35,3},{4,36},{36... | collective-permute-start | bytes 196616 | tf_op jit(solution)/shard_map/ppermute | solution.py:38
  177.2 6.2 %collective-permute-start.12 = (f32[32,512]{1,0:T(8,128)S(1)}, f32[32,512]{1,0:T(8,128)S(1)}, u32[]{:S(2)}, u32[]{:S(2)}) collective-permute-start(f32[32,512]{1,0:T(8,128)S(1)} %add.137), channel_id=1, source_target_pairs={{0,64},{64,0},{1,65},{65,1},{2,66},{66,2},{3,67},{67,3},{4,68},{68... | collective-permute-start | bytes 196616 | tf_op jit(solution)/shard_map/ppermute | solution.py:38
  183.4 12.7 %collective-permute-start.13 = (f32[32,512]{1,0:T(8,128)S(1)}, f32[32,512]{1,0:T(8,128)S(1)}, u32[]{:S(2)}, u32[]{:S(2)}) collective-permute-start(f32[32,512]{1,0:T(8,128)S(1)} %add.138), channel_id=1, source_target_pairs={{0,256},{256,0},{1,257},{257,1},{2,258},{258,2},{3,259},{259,3},{4... | collective-permute-start | bytes 196616 | tf_op jit(solution)/shard_map/ppermute | solution.py:38
  196.1 7.2 %collective-permute-start.14 = (f32[32,512]{1,0:T(8,128)S(1)}, f32[32,512]{1,0:T(8,128)S(1)}, u32[]{:S(2)}, u32[]{:S(2)}) collective-permute-start(f32[32,512]{1,0:T(8,128)S(1)} %add.139), channel_id=1, source_target_pairs={{0,128},{128,0},{1,129},{129,1},{2,130},{130,2},{3,131},{131,3},{4... | collective-permute-start | bytes 196616 | tf_op jit(solution)/shard_map/ppermute | solution.py:38
  203.2 18.5 %collective-permute-start.15 = (f32[32,512]{1,0:T(8,128)S(1)}, f32[32,512]{1,0:T(8,128)S(1)}, u32[]{:S(2)}, u32[]{:S(2)}) collective-permute-start(f32[32,512]{1,0:T(8,128)S(1)} %add.140), channel_id=1, source_target_pairs={{0,4},{4,0},{1,5},{5,1},{2,6},{6,2},{3,7},{7,3},{8,12},{12,8},{9,1... | collective-permute-start | bytes 196616 | tf_op jit(solution)/shard_map/ppermute | solution.py:38
  226.4 4.4 %collective-permute-start.18 = (bf16[8,128,256]{2,1,0:T(8,128)(2,1)}, bf16[8,128,256]{2,1,0:T(8,128)(2,1)S(1)}, u32[]{:S(2)}, u32[]{:S(2)}) collective-permute-start(bf16[8,128,256]{2,1,0:T(8,128)(2,1)} %get-tuple-element.20), channel_id=1, source_target_pairs={{0,32},{32,0},{1,33},{33,1},{2,34},{34,2},{3,35},{35,3},{4,36},{36... | collective-permute-start | bytes 1572872 | tf_op jit(solution)/shard_map/ppermute | solution.py:38
  228.3 6.5 %collective-permute-start.17 = (bf16[8,128,256]{2,1,0:T(8,128)(2,1)}, bf16[8,128,256]{2,1,0:T(8,128)(2,1)S(1)}, u32[]{:S(2)}, u32[]{:S(2)}) collective-permute-start(bf16[8,128,256]{2,1,0:T(8,128)(2,1)} %copy-done.2), channel_id=1, source_target_pairs={{0,32},{32,0},{1,33},{33,1},{2,34},{34,2},{3,35},{35,3},{4,36},{36... | collective-permute-start | bytes 1572872 | tf_op jit(solution)/shard_map/ppermute | solution.py:38
  231.7 16.0 %collective-permute-start.22 = (bf16[4,128,256]{2,1,0:T(8,128)(2,1)}, bf16[4,128,256]{2,1,0:T(8,128)(2,1)S(1)}, u32[]{:S(2)}, u32[]{:S(2)}) collective-permute-start(bf16[4,128,256]{2,1,0:T(8,128)(2,1)} %slice.115), channel_id=1, source_target_pairs={{0,64},{64,0},{1,65},{65,1},{2,66},{66,2},{3,67},{67,3},{4,68},{68... | collective-permute-start | bytes 786440 | tf_op jit(solution)/shard_map/ppermute | solution.py:38
  235.8 13.9 %collective-permute-start.19 = (bf16[4,128,256]{2,1,0:T(8,128)(2,1)}, bf16[4,128,256]{2,1,0:T(8,128)(2,1)}, u32[]{:S(2)}, u32[]{:S(2)}) collective-permute-start(bf16[4,128,256]{2,1,0:T(8,128)(2,1)} %slice.109), channel_id=1, source_target_pairs={{0,64},{64,0},{1,65},{65,1},{2,66},{66,2},{3,67},{67,3},{4,68},{68... | collective-permute-start | bytes 786440 | tf_op jit(solution)/shard_map/ppermute | solution.py:38
  239.7 37.3 %all-to-all-start.4 = ((f32[16,40,512]{2,1,0:T(8,128)}), f32[16,40,512]{2,1,0:T(8,128)S(1)}, u32[]{:S(2)}, u32[]{:S(2)}) async-start(f32[16,40,512]{2,1,0:T(8,128)} %broadcast_in_dim.14), calls=%async_computation.4 | async-start | bytes 2621440 | tf_op jit(solution)/shard_map/all_to_all | solution.py:46
  247.8 12.9 %collective-permute-start.23 = (bf16[2,128,256]{2,1,0:T(8,128)(2,1)S(1)}, bf16[2,128,256]{2,1,0:T(8,128)(2,1)S(1)}, u32[]{:S(2)}, u32[]{:S(2)}) collective-permute-start(bf16[2,128,256]{2,1,0:T(8,128)(2,1)S(1)} %slice.117), channel_id=1, source_target_pairs={{0,128},{128,0},{1,129},{129,1},{2,130},{130,2},{3,131},{131,3},{4... | collective-permute-start | bytes 393224 | tf_op jit(solution)/shard_map/ppermute | solution.py:38
  250.8 13.4 %collective-permute-start.20 = (bf16[2,128,256]{2,1,0:T(8,128)(2,1)S(1)}, bf16[2,128,256]{2,1,0:T(8,128)(2,1)S(1)}, u32[]{:S(2)}, u32[]{:S(2)}) collective-permute-start(bf16[2,128,256]{2,1,0:T(8,128)(2,1)S(1)} %slice.111), channel_id=1, source_target_pairs={{0,128},{128,0},{1,129},{129,1},{2,130},{130,2},{3,131},{131,3},{4... | collective-permute-start | bytes 393224 | tf_op jit(solution)/shard_map/ppermute | solution.py:38
  260.7 13.5 %collective-permute-start.24 = (bf16[1,128,256]{2,1,0:T(8,128)(2,1)S(1)}, bf16[1,128,256]{2,1,0:T(8,128)(2,1)S(1)}, u32[]{:S(2)}, u32[]{:S(2)}) collective-permute-start(bf16[1,128,256]{2,1,0:T(8,128)(2,1)S(1)} %slice.119), channel_id=1, source_target_pairs={{0,256},{256,0},{1,257},{257,1},{2,258},{258,2},{3,259},{259,3},{4... | collective-permute-start | bytes 196616 | tf_op jit(solution)/shard_map/ppermute | solution.py:38
  264.3 11.9 %collective-permute-start.21 = (bf16[1,128,256]{2,1,0:T(8,128)(2,1)S(1)}, bf16[1,128,256]{2,1,0:T(8,128)(2,1)S(1)}, u32[]{:S(2)}, u32[]{:S(2)}) collective-permute-start(bf16[1,128,256]{2,1,0:T(8,128)(2,1)S(1)} %slice.113), channel_id=1, source_target_pairs={{0,256},{256,0},{1,257},{257,1},{2,258},{258,2},{3,259},{259,3},{4... | collective-permute-start | bytes 196616 | tf_op jit(solution)/shard_map/ppermute | solution.py:38
  (3 other events, 14.1 us)
